TPU v7x, 256 devices: a whole 4x4x8 slice. The times are simulated.
256 devices in a mesh: plan: 32 (over z_hi, x, core), layer: 8 (over z_lo, y).
Axes of the slice: x: 4, y: 4, z: 8 (z_hi: 4, z_lo: 2; z = z_hi * 2 + z_lo), core: 2. Of those that a mesh axis runs over, the one named last changes fastest.
Arguments:
- dual_block: float32 [8, 32, 1024, 1024], P('layer', 'plan'), may hold values from -1 to 6, as said below
- start: float32 [8, 32, 8, 1024], P('layer', 'plan'), may hold values from -6 to 6
- load: float32 [8, 32, 8, 1024], P('layer', 'plan'), may hold values from -40 to 40
- partners: int32 [32, 6], P('plan'), may hold values from 0 to 31, as said below
- jump_rows: int32 [8, 32, 6, 32], P('layer', 'plan'), may hold values from 128 to 895, as said below
- counts: int32 [8, 32, 6], P('layer', 'plan'), may hold values from 16 to 32, as said below
- contact: int32 [8, 32, 1024], P('layer', 'plan'), may hold values 0 or 1
Outputs:
- multipliers: float32 [8, 32, 8, 1024], P('layer', 'plan')
- gradient: float32 [8, 32, 8, 1024], P('layer', 'plan')
Inputs may be any that keep to these rules, and one draw needn't show every extreme that they name: `dual_block`: every block is symmetric positive definite. In every round the partners form a perfect matching of the 32 subdomains with nobody paired to itself, and no pair meets in two rounds. `jump_rows`: the 192 rows of one subdomain are distinct and lie outside its first and last 128 rows; row k of a subdomain's block for round r meets row k of its partner's block. `counts`: both partners of a round have the same count; rows at position count or beyond are padding; every count of round 0 is 32.
All inputs are finite; a program needn't handle non-finite values. No bound on the sum of `contact` on one device may be relied on, other than what follows from the above.
Results may differ from a plain program's by a relative error of at most 0.0001.
Values sent between devices are 32-bit elements; how exact they have to be, the bound alone decides.
No kernel may reach another device: no remote copies, remote signals or barrier semaphores. Data moves between devices by JAX's collectives and lax.ppermute only.
A program may use at most 64 MiB of HBM per device.

v0:
```python
import jax
import jax.numpy as jnp
from jax import lax
from jax.sharding import PartitionSpec as P

FACE = 128
JR = 32
ROUNDS = 6
ITERS = 4


highest = lax.Precision.HIGHEST
coupling = 1.0


def with_halo(shard, sides, width):
    for axis, dim in sides:
        peers, length = (lax.axis_size(axis), shard.shape[dim])
        up = [(i, (i + 1) % peers) for i in range(peers - 1)]
        down = [(j, i) for i, j in up]
        last = lax.slice_in_dim(shard, length - width, length, axis=dim)
        initial = lax.slice_in_dim(shard, 0, width, axis=dim)
        before = lax.ppermute(last, axis, up)
        after = lax.ppermute(initial, axis, down)
        shard = jnp.concatenate([before, shard, after], axis=dim)
    return shard


def swap_rows(packed, onehot):
    received = []
    for round_id in range(ROUNDS):
        outgoing = onehot[round_id][:, None] * packed[round_id][None, :]
        incoming = lax.all_to_all(outgoing, "plan", split_axis=0, concat_axis=0, tiled=True)
        received.append(jnp.dot(onehot[round_id], incoming, precision=highest))
    return jnp.stack(received)


def apply_dual(field, dual_block, onehot, row_list, valid_mask):
    load_count, width = field.shape
    padded = with_halo(field, (("layer", 1),), FACE)
    gathered = field[:, row_list].reshape(load_count, ROUNDS, JR)
    packed = jnp.transpose(gathered, (1, 0, 2)).reshape(ROUNDS, load_count * JR)
    received = swap_rows(packed, onehot)
    received = jnp.transpose(received.reshape(ROUNDS, load_count, JR), (1, 0, 2))
    local_term = jnp.dot(field, dual_block, precision=highest)
    from_below = padded[:, :FACE]
    from_above = padded[:, width + FACE :]
    middle = jnp.zeros((load_count, width - 2 * FACE), jnp.float32)
    neighbour = jnp.concatenate([from_below, middle, from_above], axis=1)
    positions = jnp.arange(width)
    edge_mask = (positions < FACE) | (positions >= width - FACE)
    face_term = jnp.where(edge_mask, field, 0.0) - neighbour
    jump_diff = (gathered - received) * valid_mask[None, :, :]
    jump_term = (
        jnp.zeros_like(field).at[:, row_list].add(jump_diff.reshape(load_count, ROUNDS * JR))
    )
    return local_term + coupling * (face_term + jump_term)


def shards(dual_block, start, load, partners, jump_rows, counts, contact):
    local_block = dual_block[0, 0]
    multipliers = start[0, 0]
    target = load[0, 0]
    row_list = jump_rows[0, 0].reshape(ROUNDS * JR)
    plan_size = lax.axis_size("plan")
    onehot = (partners[0][:, None] == jnp.arange(plan_size, dtype=jnp.int32)[None, :]).astype(
        jnp.float32
    )
    valid_mask = (jnp.arange(JR)[None, :] < counts[0, 0][:, None]).astype(jnp.float32)
    is_contact = (contact[0, 0] == 1)[None, :]
    gradient = multipliers
    for iteration in range(ITERS):
        gradient = apply_dual(multipliers, local_block, onehot, row_list, valid_mask) - target
        image = apply_dual(gradient, local_block, onehot, row_list, valid_mask)
        grad_sq, curvature = lax.psum(
            (jnp.sum(gradient * gradient, axis=1), jnp.sum(gradient * image, axis=1)),
            ("plan", "layer"),
        )
        step_size = (grad_sq + 1e-06) / (curvature + 1e-06)
        moved = multipliers - step_size[:, None] * gradient
        multipliers = jnp.where(is_contact, jnp.maximum(moved, 0.0), moved)
    return (multipliers[None, None], gradient[None, None])


def solution(mesh):
    in_specs = (
        P("layer", "plan", None, None),
        P("layer", "plan", None, None),
        P("layer", "plan", None, None),
        P("plan", None),
        P("layer", "plan", None, None),
        P("layer", "plan", None),
        P("layer", "plan", None),
    )
    out_specs = (P("layer", "plan", None, None), P("layer", "plan", None, None))
    return jax.shard_map(shards, mesh=mesh, in_specs=in_specs, out_specs=out_specs, check_vma=False)
```

profile of v0, /device:TPU:1, one launch (start us, length us, event | category | flops | bytes accessed | tf_op | source)
XLA Modules:
  0.0 1098.2 jit_solution(12531134191439685076)
XLA Ops:
  10.7 12.0 %all-to-all-start.5 = ((f32[32,1,256]{2,1,0:T(1,128)}), f32[32,1,256]{2,1,0:T(1,128)S(1)}, u32[]{:S(2)}, u32[]{:S(2)}) async-start(f32[32,1,256]{2,1,0:T(1,128)} %broadcast_multiply_fusion.42), calls=%async_computation.5 | async-start | bytes 65536 | tf_op jit(solution)/shard_map/all_to_all | solution.py:33
  32.5 5.5 all-to-all-start.4
  52.9 9.2 all-to-all-done.3
  66.3 9.6 all-to-all-done.2
  80.0 9.6 all-to-all-done.1
  93.8 9.6 all-to-all-done
  136.1 9.4 all-to-all-done.10
  149.9 9.6 all-to-all-done.9
  163.7 9.6 all-to-all-done.8
  177.4 9.6 all-to-all-done.7
  191.1 9.6 all-to-all-done.6
  203.4 77.4 %all-reduce.3 = (f32[8]{0:T(128)S(1)}, f32[8]{0:T(128)S(1)}) all-reduce(f32[8]{0:T(128)S(1)} %get-tuple-element.9, f32[8]{0:T(128)S(1)} %get-tuple-element.8), channel_id=1, replica_groups=mesh['plan'=32,'layer'=8] {'plan','layer'}, use_global_device_ids=true, to_apply=%region_5.6 | all-reduce | flops 16 | bytes 128 | tf_op jit(solution)/shard_map/psum | solution.py:75
  290.1 6.4 all-to-all-start.17
  311.1 9.4 all-to-all-done.16
  324.7 9.6 all-to-all-done.15
  338.4 9.6 all-to-all-done.14
  352.2 9.6 all-to-all-done.13
  365.9 9.6 all-to-all-done.12
  408.6 9.4 all-to-all-done.22
  422.2 9.6 all-to-all-done.21
  436.0 9.6 all-to-all-done.20
  449.7 9.6 all-to-all-done.19
  463.4 9.6 all-to-all-done.18
  475.7 77.4 %all-reduce.2 = (f32[8]{0:T(128)S(1)}, f32[8]{0:T(128)S(1)}) all-reduce(f32[8]{0:T(128)S(1)} %get-tuple-element.7, f32[8]{0:T(128)S(1)} %get-tuple-element.6), channel_id=1, replica_groups=mesh['plan'=32,'layer'=8] {'plan','layer'}, use_global_device_ids=true, to_apply=%region_11.12 | all-reduce | flops 16 | bytes 128 | tf_op jit(solution)/shard_map/psum | solution.py:75
  562.4 6.4 all-to-all-start.29
  583.4 9.4 all-to-all-done.28
  597.0 9.6 all-to-all-done.27
  610.7 9.6 all-to-all-done.26
  624.5 9.6 all-to-all-done.25
  638.2 9.6 all-to-all-done.24
  680.5 9.4 all-to-all-done.34
  694.1 9.6 all-to-all-done.33
  707.8 9.6 all-to-all-done.32
  721.6 9.6 all-to-all-done.31
  735.3 9.6 all-to-all-done.30
  747.6 77.6 %all-reduce.1 = (f32[8]{0:T(128)S(1)}, f32[8]{0:T(128)S(1)}) all-reduce(f32[8]{0:T(128)S(1)} %get-tuple-element.5, f32[8]{0:T(128)S(1)} %get-tuple-element.4), channel_id=1, replica_groups=mesh['plan'=32,'layer'=8] {'plan','layer'}, use_global_device_ids=true, to_apply=%region_17.18 | all-reduce | flops 16 | bytes 128 | tf_op jit(solution)/shard_map/psum | solution.py:75
  834.5 6.4 all-to-all-start.41
  855.5 9.4 all-to-all-done.40
  869.1 9.6 all-to-all-done.39
  882.8 9.6 all-to-all-done.38
  896.6 9.6 all-to-all-done.37
  910.3 9.6 all-to-all-done.36
  952.6 9.4 all-to-all-done.46
  966.1 9.6 all-to-all-done.45
  979.9 9.6 all-to-all-done.44
  993.6 9.6 all-to-all-done.43
  1007.4 9.6 all-to-all-done.42
  1019.6 77.4 %all-reduce = (f32[8]{0:T(128)S(1)}, f32[8]{0:T(128)S(1)}) all-reduce(f32[8]{0:T(128)S(1)} %get-tuple-element.3, f32[8]{0:T(128)S(1)} %get-tuple-element.2), channel_id=1, replica_groups=mesh['plan'=32,'layer'=8] {'plan','layer'}, use_global_device_ids=true, to_apply=%region_23.24 | all-reduce | flops 16 | bytes 128 | tf_op jit(solution)/shard_map/psum | solution.py:75
  (509 shorter events, 376.6 us)
Async XLA Ops:
  1.3 36.7 %collective-permute-start = (f32[8,128]{1,0:T(8,128)S(1)}, f32[8,128]{1,0:T(8,128)S(1)}, u32[]{:S(2)}, u32[]{:S(2)}) collective-permute-start(f32[8,128]{1,0:T(8,128)S(1)} %get-tuple-element.32), channel_id=1, source_target_pairs={{0,1},{1,2},{2,3},{3,4},{4,5},{5,6},{6,7},{8,9},{9,10},{10,11},{11... | collective-permute-start | bytes 12296 | tf_op jit(solution)/shard_map/ppermute | solution.py:23
  5.4 32.6 %collective-permute-start.1 = (f32[8,128]{1,0:T(8,128)S(1)}, f32[8,128]{1,0:T(8,128)S(1)}, u32[]{:S(2)}, u32[]{:S(2)}) collective-permute-start(f32[8,128]{1,0:T(8,128)S(1)} %get-tuple-element.33), channel_id=1, source_target_pairs={{1,0},{2,1},{3,2},{4,3},{5,4},{6,5},{7,6},{9,8},{10,9},{11,10},{12... | collective-permute-start | bytes 12296 | tf_op jit(solution)/shard_map/ppermute | solution.py:24
  10.7 21.7 %all-to-all-start.5 = ((f32[32,1,256]{2,1,0:T(1,128)}), f32[32,1,256]{2,1,0:T(1,128)S(1)}, u32[]{:S(2)}, u32[]{:S(2)}) async-start(f32[32,1,256]{2,1,0:T(1,128)} %broadcast_multiply_fusion.42), calls=%async_computation.5 | async-start | bytes 65536 | tf_op jit(solution)/shard_map/all_to_all | solution.py:33
  32.5 15.2 %all-to-all-start.4 = ((f32[32,1,256]{2,1,0:T(1,128)}), f32[32,1,256]{2,1,0:T(1,128)S(1)}, u32[]{:S(2)}, u32[]{:S(2)}) async-start(f32[32,1,256]{2,1,0:T(1,128)} %broadcast_multiply_fusion.43), calls=%async_computation.4 | async-start | bytes 65536 | tf_op jit(solution)/shard_map/all_to_all | solution.py:33
  47.7 14.4 %all-to-all-start.3 = ((f32[32,1,256]{2,1,0:T(1,128)}), f32[32,1,256]{2,1,0:T(1,128)S(1)}, u32[]{:S(2)}, u32[]{:S(2)}) async-start(f32[32,1,256]{2,1,0:T(1,128)} %broadcast_multiply_fusion.44), calls=%async_computation.3 | async-start | bytes 65536 | tf_op jit(solution)/shard_map/all_to_all | solution.py:33
  62.1 13.7 %all-to-all-start.2 = ((f32[32,1,256]{2,1,0:T(1,128)}), f32[32,1,256]{2,1,0:T(1,128)S(1)}, u32[]{:S(2)}, u32[]{:S(2)}) async-start(f32[32,1,256]{2,1,0:T(1,128)} %broadcast_multiply_fusion.45), calls=%async_computation.2 | async-start | bytes 65536 | tf_op jit(solution)/shard_map/all_to_all | solution.py:33
  75.8 13.7 %all-to-all-start.1 = ((f32[32,1,256]{2,1,0:T(1,128)}), f32[32,1,256]{2,1,0:T(1,128)S(1)}, u32[]{:S(2)}, u32[]{:S(2)}) async-start(f32[32,1,256]{2,1,0:T(1,128)} %broadcast_multiply_fusion.46), calls=%async_computation.1 | async-start | bytes 65536 | tf_op jit(solution)/shard_map/all_to_all | solution.py:33
  89.6 13.7 %all-to-all-start = ((f32[32,1,256]{2,1,0:T(1,128)}), f32[32,1,256]{2,1,0:T(1,128)S(1)}, u32[]{:S(2)}, u32[]{:S(2)}) async-start(f32[32,1,256]{2,1,0:T(1,128)} %broadcast_multiply_fusion.47), calls=%async_computation | async-start | bytes 65536 | tf_op jit(solution)/shard_map/all_to_all | solution.py:33
  106.1 15.3 %collective-permute-start.2 = (f32[8,128]{1,0:T(8,128)S(1)}, f32[8,128]{1,0:T(8,128)S(1)}, u32[]{:S(2)}, u32[]{:S(2)}) collective-permute-start(f32[8,128]{1,0:T(8,128)S(1)} %get-tuple-element.30), channel_id=1, source_target_pairs={{0,1},{1,2},{2,3},{3,4},{4,5},{5,6},{6,7},{8,9},{9,10},{10,11},{11... | collective-permute-start | bytes 12296 | tf_op jit(solution)/shard_map/ppermute | solution.py:23
  117.2 14.0 %all-to-all-start.11 = ((f32[32,1,256]{2,1,0:T(1,128)}), f32[32,1,256]{2,1,0:T(1,128)S(1)}, u32[]{:S(2)}, u32[]{:S(2)}) async-start(f32[32,1,256]{2,1,0:T(1,128)} %broadcast_multiply_fusion.36), calls=%async_computation.11 | async-start | bytes 65536 | tf_op jit(solution)/shard_map/all_to_all | solution.py:33
  131.2 14.3 %all-to-all-start.10 = ((f32[32,1,256]{2,1,0:T(1,128)}), f32[32,1,256]{2,1,0:T(1,128)S(1)}, u32[]{:S(2)}, u32[]{:S(2)}) async-start(f32[32,1,256]{2,1,0:T(1,128)} %broadcast_multiply_fusion.37), calls=%async_computation.10 | async-start | bytes 65536 | tf_op jit(solution)/shard_map/all_to_all | solution.py:33
  145.5 14.0 %all-to-all-start.9 = ((f32[32,1,256]{2,1,0:T(1,128)}), f32[32,1,256]{2,1,0:T(1,128)S(1)}, u32[]{:S(2)}, u32[]{:S(2)}) async-start(f32[32,1,256]{2,1,0:T(1,128)} %broadcast_multiply_fusion.38), calls=%async_computation.9 | async-start | bytes 65536 | tf_op jit(solution)/shard_map/all_to_all | solution.py:33
  159.5 13.7 %all-to-all-start.8 = ((f32[32,1,256]{2,1,0:T(1,128)}), f32[32,1,256]{2,1,0:T(1,128)S(1)}, u32[]{:S(2)}, u32[]{:S(2)}) async-start(f32[32,1,256]{2,1,0:T(1,128)} %broadcast_multiply_fusion.39), calls=%async_computation.8 | async-start | bytes 65536 | tf_op jit(solution)/shard_map/all_to_all | solution.py:33
  173.2 13.7 %all-to-all-start.7 = ((f32[32,1,256]{2,1,0:T(1,128)}), f32[32,1,256]{2,1,0:T(1,128)S(1)}, u32[]{:S(2)}, u32[]{:S(2)}) async-start(f32[32,1,256]{2,1,0:T(1,128)} %broadcast_multiply_fusion.40), calls=%async_computation.7 | async-start | bytes 65536 | tf_op jit(solution)/shard_map/all_to_all | solution.py:33
  187.0 13.7 %all-to-all-start.6 = ((f32[32,1,256]{2,1,0:T(1,128)}), f32[32,1,256]{2,1,0:T(1,128)S(1)}, u32[]{:S(2)}, u32[]{:S(2)}) async-start(f32[32,1,256]{2,1,0:T(1,128)} %broadcast_multiply_fusion.41), calls=%async_computation.6 | async-start | bytes 65536 | tf_op jit(solution)/shard_map/all_to_all | solution.py:33
  281.1 15.4 %collective-permute-start.4 = (f32[8,128]{1,0:T(8,128)S(1)}, f32[8,128]{1,0:T(8,128)S(1)}, u32[]{:S(2)}, u32[]{:S(2)}) collective-permute-start(f32[8,128]{1,0:T(8,128)S(1)} %get-tuple-element.28), channel_id=1, source_target_pairs={{0,1},{1,2},{2,3},{3,4},{4,5},{5,6},{6,7},{8,9},{9,10},{10,11},{11... | collective-permute-start | bytes 12296 | tf_op jit(solution)/shard_map/ppermute | solution.py:23
  290.1 16.1 %all-to-all-start.17 = ((f32[32,1,256]{2,1,0:T(1,128)}), f32[32,1,256]{2,1,0:T(1,128)S(1)}, u32[]{:S(2)}, u32[]{:S(2)}) async-start(f32[32,1,256]{2,1,0:T(1,128)} %broadcast_multiply_fusion.30), calls=%async_computation.17 | async-start | bytes 65536 | tf_op jit(solution)/shard_map/all_to_all | solution.py:33
  306.2 14.3 %all-to-all-start.16 = ((f32[32,1,256]{2,1,0:T(1,128)}), f32[32,1,256]{2,1,0:T(1,128)S(1)}, u32[]{:S(2)}, u32[]{:S(2)}) async-start(f32[32,1,256]{2,1,0:T(1,128)} %broadcast_multiply_fusion.31), calls=%async_computation.16 | async-start | bytes 65536 | tf_op jit(solution)/shard_map/all_to_all | solution.py:33
  334.2 13.7 %all-to-all-start.14 = ((f32[32,1,256]{2,1,0:T(1,128)}), f32[32,1,256]{2,1,0:T(1,128)S(1)}, u32[]{:S(2)}, u32[]{:S(2)}) async-start(f32[32,1,256]{2,1,0:T(1,128)} %broadcast_multiply_fusion.33), calls=%async_computation.14 | async-start | bytes 65536 | tf_op jit(solution)/shard_map/all_to_all | solution.py:33
  348.0 13.7 %all-to-all-start.13 = ((f32[32,1,256]{2,1,0:T(1,128)}), f32[32,1,256]{2,1,0:T(1,128)S(1)}, u32[]{:S(2)}, u32[]{:S(2)}) async-start(f32[32,1,256]{2,1,0:T(1,128)} %broadcast_multiply_fusion.34), calls=%async_computation.13 | async-start | bytes 65536 | tf_op jit(solution)/shard_map/all_to_all | solution.py:33
  361.7 13.7 %all-to-all-start.12 = ((f32[32,1,256]{2,1,0:T(1,128)}), f32[32,1,256]{2,1,0:T(1,128)S(1)}, u32[]{:S(2)}, u32[]{:S(2)}) async-start(f32[32,1,256]{2,1,0:T(1,128)} %broadcast_multiply_fusion.35), calls=%async_computation.12 | async-start | bytes 65536 | tf_op jit(solution)/shard_map/all_to_all | solution.py:33
  378.2 15.7 %collective-permute-start.6 = (f32[8,128]{1,0:T(8,128)S(1)}, f32[8,128]{1,0:T(8,128)S(1)}, u32[]{:S(2)}, u32[]{:S(2)}) collective-permute-start(f32[8,128]{1,0:T(8,128)S(1)} %get-tuple-element.26), channel_id=1, source_target_pairs={{0,1},{1,2},{2,3},{3,4},{4,5},{5,6},{6,7},{8,9},{9,10},{10,11},{11... | collective-permute-start | bytes 12296 | tf_op jit(solution)/shard_map/ppermute | solution.py:23
  389.7 14.0 %all-to-all-start.23 = ((f32[32,1,256]{2,1,0:T(1,128)}), f32[32,1,256]{2,1,0:T(1,128)S(1)}, u32[]{:S(2)}, u32[]{:S(2)}) async-start(f32[32,1,256]{2,1,0:T(1,128)} %broadcast_multiply_fusion.24), calls=%async_computation.23 | async-start | bytes 65536 | tf_op jit(solution)/shard_map/all_to_all | solution.py:33
  403.7 14.3 %all-to-all-start.22 = ((f32[32,1,256]{2,1,0:T(1,128)}), f32[32,1,256]{2,1,0:T(1,128)S(1)}, u32[]{:S(2)}, u32[]{:S(2)}) async-start(f32[32,1,256]{2,1,0:T(1,128)} %broadcast_multiply_fusion.25), calls=%async_computation.22 | async-start | bytes 65536 | tf_op jit(solution)/shard_map/all_to_all | solution.py:33
  431.8 13.8 %all-to-all-start.20 = ((f32[32,1,256]{2,1,0:T(1,128)}), f32[32,1,256]{2,1,0:T(1,128)S(1)}, u32[]{:S(2)}, u32[]{:S(2)}) async-start(f32[32,1,256]{2,1,0:T(1,128)} %broadcast_multiply_fusion.27), calls=%async_computation.20 | async-start | bytes 65536 | tf_op jit(solution)/shard_map/all_to_all | solution.py:33
  445.5 13.7 %all-to-all-start.19 = ((f32[32,1,256]{2,1,0:T(1,128)}), f32[32,1,256]{2,1,0:T(1,128)S(1)}, u32[]{:S(2)}, u32[]{:S(2)}) async-start(f32[32,1,256]{2,1,0:T(1,128)} %broadcast_multiply_fusion.28), calls=%async_computation.19 | async-start | bytes 65536 | tf_op jit(solution)/shard_map/all_to_all | solution.py:33
  553.4 15.4 %collective-permute-start.8 = (f32[8,128]{1,0:T(8,128)S(1)}, f32[8,128]{1,0:T(8,128)S(1)}, u32[]{:S(2)}, u32[]{:S(2)}) collective-permute-start(f32[8,128]{1,0:T(8,128)S(1)} %get-tuple-element.24), channel_id=1, source_target_pairs={{0,1},{1,2},{2,3},{3,4},{4,5},{5,6},{6,7},{8,9},{9,10},{10,11},{11... | collective-permute-start | bytes 12296 | tf_op jit(solution)/shard_map/ppermute | solution.py:23
  562.4 16.1 %all-to-all-start.29 = ((f32[32,1,256]{2,1,0:T(1,128)}), f32[32,1,256]{2,1,0:T(1,128)S(1)}, u32[]{:S(2)}, u32[]{:S(2)}) async-start(f32[32,1,256]{2,1,0:T(1,128)} %broadcast_multiply_fusion.18), calls=%async_computation.29 | async-start | bytes 65536 | tf_op jit(solution)/shard_map/all_to_all | solution.py:33
  578.5 14.3 %all-to-all-start.28 = ((f32[32,1,256]{2,1,0:T(1,128)}), f32[32,1,256]{2,1,0:T(1,128)S(1)}, u32[]{:S(2)}, u32[]{:S(2)}) async-start(f32[32,1,256]{2,1,0:T(1,128)} %broadcast_multiply_fusion.19), calls=%async_computation.28 | async-start | bytes 65536 | tf_op jit(solution)/shard_map/all_to_all | solution.py:33
  606.5 13.7 %all-to-all-start.26 = ((f32[32,1,256]{2,1,0:T(1,128)}), f32[32,1,256]{2,1,0:T(1,128)S(1)}, u32[]{:S(2)}, u32[]{:S(2)}) async-start(f32[32,1,256]{2,1,0:T(1,128)} %broadcast_multiply_fusion.21), calls=%async_computation.26 | async-start | bytes 65536 | tf_op jit(solution)/shard_map/all_to_all | solution.py:33
  620.3 13.7 %all-to-all-start.25 = ((f32[32,1,256]{2,1,0:T(1,128)}), f32[32,1,256]{2,1,0:T(1,128)S(1)}, u32[]{:S(2)}, u32[]{:S(2)}) async-start(f32[32,1,256]{2,1,0:T(1,128)} %broadcast_multiply_fusion.22), calls=%async_computation.25 | async-start | bytes 65536 | tf_op jit(solution)/shard_map/all_to_all | solution.py:33
  650.5 15.3 %collective-permute-start.10 = (f32[8,128]{1,0:T(8,128)S(1)}, f32[8,128]{1,0:T(8,128)S(1)}, u32[]{:S(2)}, u32[]{:S(2)}) collective-permute-start(f32[8,128]{1,0:T(8,128)S(1)} %get-tuple-element.22), channel_id=1, source_target_pairs={{0,1},{1,2},{2,3},{3,4},{4,5},{5,6},{6,7},{8,9},{9,10},{10,11},{11... | collective-permute-start | bytes 12296 | tf_op jit(solution)/shard_map/ppermute | solution.py:23
  661.6 14.0 %all-to-all-start.35 = ((f32[32,1,256]{2,1,0:T(1,128)}), f32[32,1,256]{2,1,0:T(1,128)S(1)}, u32[]{:S(2)}, u32[]{:S(2)}) async-start(f32[32,1,256]{2,1,0:T(1,128)} %broadcast_multiply_fusion.12), calls=%async_computation.35 | async-start | bytes 65536 | tf_op jit(solution)/shard_map/all_to_all | solution.py:33
  675.6 14.3 %all-to-all-start.34 = ((f32[32,1,256]{2,1,0:T(1,128)}), f32[32,1,256]{2,1,0:T(1,128)S(1)}, u32[]{:S(2)}, u32[]{:S(2)}) async-start(f32[32,1,256]{2,1,0:T(1,128)} %broadcast_multiply_fusion.13), calls=%async_computation.34 | async-start | bytes 65536 | tf_op jit(solution)/shard_map/all_to_all | solution.py:33
  689.9 13.7 %all-to-all-start.33 = ((f32[32,1,256]{2,1,0:T(1,128)}), f32[32,1,256]{2,1,0:T(1,128)S(1)}, u32[]{:S(2)}, u32[]{:S(2)}) async-start(f32[32,1,256]{2,1,0:T(1,128)} %broadcast_multiply_fusion.14), calls=%async_computation.33 | async-start | bytes 65536 | tf_op jit(solution)/shard_map/all_to_all | solution.py:33
  703.6 13.7 %all-to-all-start.32 = ((f32[32,1,256]{2,1,0:T(1,128)}), f32[32,1,256]{2,1,0:T(1,128)S(1)}, u32[]{:S(2)}, u32[]{:S(2)}) async-start(f32[32,1,256]{2,1,0:T(1,128)} %broadcast_multiply_fusion.15), calls=%async_computation.32 | async-start | bytes 65536 | tf_op jit(solution)/shard_map/all_to_all | solution.py:33
  717.4 13.7 %all-to-all-start.31 = ((f32[32,1,256]{2,1,0:T(1,128)}), f32[32,1,256]{2,1,0:T(1,128)S(1)}, u32[]{:S(2)}, u32[]{:S(2)}) async-start(f32[32,1,256]{2,1,0:T(1,128)} %broadcast_multiply_fusion.16), calls=%async_computation.31 | async-start | bytes 65536 | tf_op jit(solution)/shard_map/all_to_all | solution.py:33
  731.1 13.7 %all-to-all-start.30 = ((f32[32,1,256]{2,1,0:T(1,128)}), f32[32,1,256]{2,1,0:T(1,128)S(1)}, u32[]{:S(2)}, u32[]{:S(2)}) async-start(f32[32,1,256]{2,1,0:T(1,128)} %broadcast_multiply_fusion.17), calls=%async_computation.30 | async-start | bytes 65536 | tf_op jit(solution)/shard_map/all_to_all | solution.py:33
  825.5 15.4 %collective-permute-start.12 = (f32[8,128]{1,0:T(8,128)S(1)}, f32[8,128]{1,0:T(8,128)S(1)}, u32[]{:S(2)}, u32[]{:S(2)}) collective-permute-start(f32[8,128]{1,0:T(8,128)S(1)} %get-tuple-element.20), channel_id=1, source_target_pairs={{0,1},{1,2},{2,3},{3,4},{4,5},{5,6},{6,7},{8,9},{9,10},{10,11},{11... | collective-permute-start | bytes 12296 | tf_op jit(solution)/shard_map/ppermute | solution.py:23
  834.5 16.1 %all-to-all-start.41 = ((f32[32,1,256]{2,1,0:T(1,128)}), f32[32,1,256]{2,1,0:T(1,128)S(1)}, u32[]{:S(2)}, u32[]{:S(2)}) async-start(f32[32,1,256]{2,1,0:T(1,128)} %broadcast_multiply_fusion.6), calls=%async_computation.41 | async-start | bytes 65536 | tf_op jit(solution)/shard_map/all_to_all | solution.py:33
  850.6 14.3 %all-to-all-start.40 = ((f32[32,1,256]{2,1,0:T(1,128)}), f32[32,1,256]{2,1,0:T(1,128)S(1)}, u32[]{:S(2)}, u32[]{:S(2)}) async-start(f32[32,1,256]{2,1,0:T(1,128)} %broadcast_multiply_fusion.7), calls=%async_computation.40 | async-start | bytes 65536 | tf_op jit(solution)/shard_map/all_to_all | solution.py:33
  878.6 13.7 %all-to-all-start.38 = ((f32[32,1,256]{2,1,0:T(1,128)}), f32[32,1,256]{2,1,0:T(1,128)S(1)}, u32[]{:S(2)}, u32[]{:S(2)}) async-start(f32[32,1,256]{2,1,0:T(1,128)} %broadcast_multiply_fusion.9), calls=%async_computation.38 | async-start | bytes 65536 | tf_op jit(solution)/shard_map/all_to_all | solution.py:33
  906.1 13.7 %all-to-all-start.36 = ((f32[32,1,256]{2,1,0:T(1,128)}), f32[32,1,256]{2,1,0:T(1,128)S(1)}, u32[]{:S(2)}, u32[]{:S(2)}) async-start(f32[32,1,256]{2,1,0:T(1,128)} %broadcast_multiply_fusion.11), calls=%async_computation.36 | async-start | bytes 65536 | tf_op jit(solution)/shard_map/all_to_all | solution.py:33
  922.6 15.2 %collective-permute-start.14 = (f32[8,128]{1,0:T(8,128)S(1)}, f32[8,128]{1,0:T(8,128)S(1)}, u32[]{:S(2)}, u32[]{:S(2)}) collective-permute-start(f32[8,128]{1,0:T(8,128)S(1)} %get-tuple-element.18), channel_id=1, source_target_pairs={{0,1},{1,2},{2,3},{3,4},{4,5},{5,6},{6,7},{8,9},{9,10},{10,11},{11... | collective-permute-start | bytes 12296 | tf_op jit(solution)/shard_map/ppermute | solution.py:23
  933.7 14.0 %all-to-all-start.47 = ((f32[32,1,256]{2,1,0:T(1,128)}), f32[32,1,256]{2,1,0:T(1,128)S(1)}, u32[]{:S(2)}, u32[]{:S(2)}) async-start(f32[32,1,256]{2,1,0:T(1,128)} %broadcast_multiply_fusion), calls=%async_computation.47 | async-start | bytes 65536 | tf_op jit(solution)/shard_map/all_to_all | solution.py:33
  947.7 14.3 %all-to-all-start.46 = ((f32[32,1,256]{2,1,0:T(1,128)}), f32[32,1,256]{2,1,0:T(1,128)S(1)}, u32[]{:S(2)}, u32[]{:S(2)}) async-start(f32[32,1,256]{2,1,0:T(1,128)} %broadcast_multiply_fusion.1), calls=%async_computation.46 | async-start | bytes 65536 | tf_op jit(solution)/shard_map/all_to_all | solution.py:33
  989.4 13.7 %all-to-all-start.43 = ((f32[32,1,256]{2,1,0:T(1,128)}), f32[32,1,256]{2,1,0:T(1,128)S(1)}, u32[]{:S(2)}, u32[]{:S(2)}) async-start(f32[32,1,256]{2,1,0:T(1,128)} %broadcast_multiply_fusion.4), calls=%async_computation.43 | async-start | bytes 65536 | tf_op jit(solution)/shard_map/all_to_all | solution.py:33
  1003.2 13.7 %all-to-all-start.42 = ((f32[32,1,256]{2,1,0:T(1,128)}), f32[32,1,256]{2,1,0:T(1,128)S(1)}, u32[]{:S(2)}, u32[]{:S(2)}) async-start(f32[32,1,256]{2,1,0:T(1,128)} %broadcast_multiply_fusion.5), calls=%async_computation.42 | async-start | bytes 65536 | tf_op jit(solution)/shard_map/all_to_all | solution.py:33
  (19 other events, 619.4 us)
where the time goes:
time: 1110 us; the launch traced here: 1100 us
  waiting for transfers between devices  418 us (38%)
  blocking collectives  310 us (28%)
  starting transfers between devices  250 us (23%)
  other arithmetic  53.1 us (5%)
  matrix products  42.5 us (4%)
  local copies, waits for them, and re-layouts  21.7 us (2%)
    all_to_all x48, waiting for transfers between devices, swap_rows(): lax.all_to_all(outgoing, 'plan', split_axis=0, concat_axis=0, tiled=True)  418 us
    psum x4, blocking collectives, shards(): lax.psum((jnp.sum(gradient * gradient, axis=1), jnp.sum(gradient * image,...  310 us
    all_to_all x48, starting transfers between devices, swap_rows(): lax.all_to_all(outgoing, 'plan', split_axis=0, concat_axis=0, tiled=True)  211 us
    dot_general x8, matrix products, apply_dual(): local_term = jnp.dot(field, dual_block, precision=highest)  34.2 us
    mul x48, other arithmetic, swap_rows(): outgoing = onehot[round_id][:, None] * packed[round_id][None, :]  34.1 us
    ppermute x8, starting transfers between devices, with_halo(): before = lax.ppermute(last, axis, up)  27.6 us
  transfers between devices with their start and end apart: 64, of which 48 were waited for; matrix products, arithmetic and copies ran while one was open for 9% of the time, Pallas kernels for 0%

commit v1 on v0

v1 whole, which is shorter than its diff:
```python
import functools

import jax
import jax.numpy as jnp
from jax import lax
from jax.experimental import pallas as pl
from jax.experimental.pallas import tpu as pltpu
from jax.sharding import PartitionSpec as P

FACE = 128
JR = 32
ROUNDS = 6
ITERS = 4
LANES = 128
JW = 256
F32 = jnp.float32
BF16 = jnp.bfloat16

VMEM = pl.BlockSpec(memory_space=pltpu.VMEM)
SMEM = pl.BlockSpec(memory_space=pltpu.SMEM)


def shape(*dims, dtype=F32):
    return jax.ShapeDtypeStruct(dims, dtype)


def call(body, name, outs, specs, limit, flops=0, moved=0):
    return pl.pallas_call(
        body,
        name=name,
        out_shape=outs,
        in_specs=specs,
        out_specs=jax.tree.map(lambda _: VMEM, outs),
        compiler_params=pltpu.CompilerParams(vmem_limit_bytes=limit * 2**20),
        cost_estimate=pl.CostEstimate(flops=flops, bytes_accessed=moved, transcendentals=0),
    )


def pieces(value, count):
    parts = []
    for _ in range(count):
        part = value.astype(BF16).astype(F32)
        parts.append(part)
        value = value - part
    return parts


def dense(field, high, low):
    lhs = jnp.concatenate(pieces(field, 2), axis=0).astype(BF16)
    total = jnp.dot(lhs, high, preferred_element_type=F32)
    total = total + jnp.dot(lhs, low, preferred_element_type=F32)
    return total[:8] + total[8:]


def pick(field, onehot, *extra):
    lhs = jnp.concatenate(pieces(field, 3) + list(extra), axis=0).astype(BF16)
    out = jnp.dot(lhs, onehot, preferred_element_type=F32)
    return [out[:8] + out[8:16] + out[16:24]] + [
        out[24 + 8 * i : 32 + 8 * i] for i in range(len(extra))
    ]


def spread(jumps, onehot):
    lhs = jnp.concatenate(pieces(jumps, 3), axis=0).astype(BF16)
    out = lax.dot_general(lhs, onehot, (((1,), (1,)), ((), ())), preferred_element_type=F32)
    return out[:8] + out[8:16] + out[16:24]


def address(out_ref, partners_ref, *jumps):
    out_ref[...] = jnp.zeros_like(out_ref)
    for r in range(ROUNDS):
        group = (r * JR) // LANES
        block = jnp.concatenate(
            [jump[:, group * LANES : (group + 1) * LANES] for jump in jumps], axis=0
        )
        out_ref[pl.ds(partners_ref[0, r], 1)] = block[None]


def arrived(in_ref, partners_ref):
    height = in_ref.shape[1]
    place = lax.broadcasted_iota(jnp.int32, (height, LANES), 1) // JR
    groups = []
    for first in range(0, JW // JR, LANES // JR):
        total = jnp.zeros((height, LANES), F32)
        for r in range(first, min(first + LANES // JR, ROUNDS)):
            block = in_ref[pl.ds(partners_ref[0, r], 1)][0]
            total = jnp.where(place == r - first, block, total)
        groups.append(total)
    return jnp.concatenate(groups, axis=1)


def prepare(x_ref, contact_ref, rows_ref, partners_ref, counts_ref,
            onehot_ref, valid_ref, own_ref, out_ref, first_ref, last_ref):
    x = x_ref[...]
    rows = jnp.concatenate(
        [rows_ref[r : r + 1, :] for r in range(ROUNDS)]
        + [jnp.full((1, JW - ROUNDS * JR), -1, jnp.int32)],
        axis=1,
    )
    hit = lax.broadcasted_iota(jnp.int32, (x.shape[1], JW), 0) == rows
    onehot = jnp.where(hit, 1.0, 0.0).astype(BF16)
    onehot_ref[...] = onehot
    lane = lax.broadcasted_iota(jnp.int32, (8, JW), 1)
    valid = jnp.zeros((8, JW), F32)
    for r in range(ROUNDS):
        inside = (lane >= r * JR) & (lane < r * JR + counts_ref[0, r])
        valid = jnp.where(inside, 1.0, valid)
    valid_ref[...] = valid
    contact = jnp.broadcast_to(jnp.where(contact_ref[...] == 1, 1.0, 0.0), x.shape)
    own, own_contact = pick(x, onehot, contact)
    own_ref[...] = jnp.concatenate([own, own_contact], axis=0)
    address(out_ref, partners_ref, own, own_contact)
    both = jnp.concatenate([x, contact], axis=0)
    first_ref[...] = both[:, :FACE]
    last_ref[...] = both[:, x.shape[1] - FACE :]


def split_dense(block_ref, x_ref, high_ref, low_ref, image_ref):
    block = block_ref[...]
    high = block.astype(BF16)
    low = (block - high.astype(F32)).astype(BF16)
    high_ref[...] = high
    low_ref[...] = low
    image_ref[...] = dense(x_ref[...], high, low)


def with_coupling(image, x, load, own, far, below, above, valid, onehot):
    width = x.shape[1]
    total = image + spread(valid * (own - far), onehot) - load
    head = total[:, :FACE] + (x[:, :FACE] - below)
    tail = total[:, width - FACE :] + (x[:, width - FACE :] - above)
    return jnp.concatenate([head, total[:, FACE : width - FACE], tail], axis=1)


def give_gradient(gradient, onehot, partners_ref, g_ref, gown_ref, out_ref, first_ref, last_ref):
    width = gradient.shape[1]
    g_ref[...] = gradient
    first_ref[...] = gradient[:, :FACE]
    last_ref[...] = gradient[:, width - FACE :]
    (own,) = pick(gradient, onehot)
    gown_ref[...] = own
    address(out_ref, partners_ref, own)


def first_gradient(partners_ref, image_ref, x_ref, load_ref, own_ref, in_ref, below_ref, above_ref,
                   valid_ref, onehot_ref,
                   g_ref, gown_ref, out_ref, first_ref, last_ref, far_ref):
    far = arrived(in_ref, partners_ref)
    far_ref[...] = far
    onehot = onehot_ref[...]
    gradient = with_coupling(
        image_ref[...], x_ref[...], load_ref[...], own_ref[:8], far[:8], below_ref[:8],
        above_ref[:8], valid_ref[...], onehot,
    )
    give_gradient(gradient, onehot, partners_ref, g_ref, gown_ref, out_ref, first_ref, last_ref)


def local_sums(g_ref, high_ref, low_ref, sums_ref):
    g = g_ref[...]
    image = dense(g, high_ref[...], low_ref[...])
    square = jnp.sum(g * g, axis=1, keepdims=True)
    curvature = jnp.sum(g * image, axis=1, keepdims=True)
    sums_ref[...] = jnp.concatenate(
        [jnp.broadcast_to(square, (8, LANES)), jnp.broadcast_to(curvature, (8, LANES))], axis=0
    )


def add_coupling(partners_ref, sums_ref, gown_ref, in_ref, first_ref, last_ref, below_ref,
                 above_ref, valid_ref, all_ref, gfar_ref):
    far = arrived(in_ref, partners_ref)
    gfar_ref[...] = far
    own = gown_ref[...]
    first, last = first_ref[...], last_ref[...]
    jump = valid_ref[...] * own * (own - far)
    terms = first * (first - below_ref[...]) + last * (last - above_ref[...])
    terms = terms + jump[:, :LANES] + jump[:, LANES:]
    curvature = sums_ref[8:] + jnp.sum(terms, axis=1, keepdims=True)
    lane = lax.broadcasted_iota(jnp.int32, (8, LANES), 1)
    row = lax.broadcasted_iota(jnp.int32, (8, LANES), 0)
    both = jnp.where(lane == row, sums_ref[:8], 0.0) + jnp.where(lane == row + 8, curvature, 0.0)
    line = jnp.sum(both, axis=0, keepdims=True)
    all_ref[...] = jnp.broadcast_to(line, all_ref.shape)


def step_of(all_ref):
    line = jnp.sum(all_ref[...], axis=0, keepdims=True)
    line = jnp.broadcast_to(line, (8, LANES))
    lane = lax.broadcasted_iota(jnp.int32, (8, LANES), 1)
    row = lax.broadcasted_iota(jnp.int32, (8, LANES), 0)
    square = jnp.sum(jnp.where(lane == row, line, 0.0), axis=1, keepdims=True)
    curvature = jnp.sum(jnp.where(lane == row + 8, line, 0.0), axis=1, keepdims=True)
    return (square + 1e-6) / (curvature + 1e-6)


def moved(x, g, step, contact):
    out = x - step * g
    return jnp.where(contact == 1, jnp.maximum(out, 0.0), out)


def advance(partners_ref, all_ref, x_ref, g_ref, contact_ref, load_ref,
            own_ref, gown_ref, far_ref, gfar_ref, below_ref, gbelow_ref, above_ref, gabove_ref,
            valid_ref, onehot_ref, high_ref, low_ref,
            g_out, gown_out, out_ref, first_ref, last_ref,
            x_out, own_out, far_out, below_out, above_out):
    step = step_of(all_ref)
    x = moved(x_ref[...], g_ref[...], step, contact_ref[...])
    x_out[...] = x
    halo = []
    for held_ref, slope_ref, held_out in (
        (own_ref, gown_ref, own_out), (far_ref, gfar_ref, far_out),
        (below_ref, gbelow_ref, below_out), (above_ref, gabove_ref, above_out),
    ):
        flags = held_ref[8:]
        value = moved(held_ref[:8], slope_ref[...], step, flags)
        held_out[...] = jnp.concatenate([value, flags], axis=0)
        halo.append(value)
    onehot = onehot_ref[...]
    image = dense(x, high_ref[...], low_ref[...])
    gradient = with_coupling(image, x, load_ref[...], *halo, valid_ref[...], onehot)
    give_gradient(gradient, onehot, partners_ref, g_out, gown_out, out_ref, first_ref, last_ref)


def finish(all_ref, x_ref, g_ref, contact_ref, x_out):
    x_out[...] = moved(x_ref[...], g_ref[...], step_of(all_ref), contact_ref[...])


def swap(outgoing):
    return lax.all_to_all(outgoing, "plan", split_axis=0, concat_axis=0, tiled=True)


def neighbours(first, last):
    layers = lax.axis_size("layer")
    up = [(i, i + 1) for i in range(layers - 1)]
    down = [(j, i) for i, j in up]
    return lax.ppermute(last, "layer", up), lax.ppermute(first, "layer", down)


def shards(dual_block, start, load, partners, jump_rows, counts, contact):
    block, x, target = dual_block[0, 0], start[0, 0], load[0, 0]
    rows, amounts, flags = jump_rows[0, 0], counts[0], contact[0]
    loads, width = x.shape
    plans = lax.axis_size("plan")
    devices = plans * lax.axis_size("layer")
    field, jump, face = shape(loads, width), shape(loads, JW), shape(loads, FACE)
    parcel = shape(plans, loads, LANES)
    jump2, face2, parcel2 = shape(2 * loads, JW), shape(2 * loads, FACE), shape(plans, 2 * loads, LANES)
    half = shape(width, width, dtype=BF16)
    flops = 4 * 16 * width * width

    onehot, valid, own, out, first, last = call(
        prepare, "prepare",
        (shape(width, JW, dtype=BF16), jump, jump2, parcel2, face2, face2),
        [VMEM, VMEM, VMEM, SMEM, SMEM], 8,
    )(x, flags, rows, partners, amounts)
    incoming = swap(out)
    below, above = neighbours(first, last)
    high, low, image = call(
        split_dense, "split_dense", (half, half, field), [VMEM, VMEM], 24, flops, 12 * width * width,
    )(block, x)
    g, gown, out, first, last, far = call(
        first_gradient, "first_gradient", (field, jump, parcel, face, face, jump2),
        [SMEM] + [VMEM] * 9, 8,
    )(partners, image, x, target, own, incoming, below, above, valid, onehot)

    for iteration in range(ITERS):
        incoming = swap(out)
        gbelow, gabove = neighbours(first, last)
        sums = call(
            local_sums, "local_sums", shape(2 * loads, LANES), [VMEM] * 3, 16, flops, 4 * width * width,
        )(g, high, low)
        everyone, gfar = call(
            add_coupling, "add_coupling", (shape(devices, LANES), jump), [SMEM] + [VMEM] * 8, 8,
        )(partners, sums, gown, incoming, first, last, gbelow, gabove, valid)
        everyone = lax.all_to_all(everyone, ("plan", "layer"), split_axis=0, concat_axis=0, tiled=True)
        if iteration == ITERS - 1:
            x = call(finish, "finish", field, [VMEM] * 4, 8)(everyone, x, g, flags)
            break
        g, gown, out, first, last, x, own, far, below, above = call(
            advance, "advance",
            (field, jump, parcel, face, face, field, jump2, jump2, face2, face2),
            [SMEM] + [VMEM] * 17, 16, flops, 4 * width * width,
        )(partners, everyone, x, g, flags, target, own, gown, far, gfar, below, gbelow, above, gabove,
          valid, onehot, high, low)
    return x[None, None], g[None, None]


def solution(mesh):
    in_specs = (
        P("layer", "plan", None, None),
        P("layer", "plan", None, None),
        P("layer", "plan", None, None),
        P("plan", None),
        P("layer", "plan", None, None),
        P("layer", "plan", None),
        P("layer", "plan", None),
    )
    out_specs = (P("layer", "plan", None, None), P("layer", "plan", None, None))
    return jax.shard_map(shards, mesh=mesh, in_specs=in_specs, out_specs=out_specs, check_vma=False)
```

time: 1110 us -> 208 us (0.19)
  waiting for transfers between devices: 418 us -> 15.3 us
  blocking collectives: 310 us -> 93.6 us
  starting transfers between devices: 250 us -> 59.5 us
  other arithmetic: 53.1 us -> 0 us
  matrix products: 42.5 us -> 0 us
  Pallas kernels: 0 us -> 17.8 us
    all_to_all x48 -> x5, waiting for transfers between devices: 418 us -> 15.3 us  [swap(): lax.all_to_all(outgoing, 'plan', split_axis=0, concat_axis=0, tiled=True)]
    psum x4 -> x0, blocking collectives: 310 us -> none  [shards(): lax.psum((jnp.sum(gradient * gradient, axis=1), jnp.sum(gradient * image,...]
    all_to_all x48 -> x5, starting transfers between devices: 211 us -> 33 us  [swap(): lax.all_to_all(outgoing, 'plan', split_axis=0, concat_axis=0, tiled=True)]
    all_to_all x0 -> x4, blocking collectives: none -> 93.6 us  [shards(): lax.all_to_all(everyone, ('plan', 'layer'), split_axis=0, concat_axis=0,...]
    dot_general x56 -> x0, matrix products: 42.5 us -> none  [the longest x8 34.2 us: apply_dual(): local_term = jnp.dot(field, dual_block, precision=highest)]
    mul x56 -> x0, other arithmetic: 34.1 us -> none  [the longest x48 34.1 us: swap_rows(): outgoing = onehot[round_id][:, None] * packed[round_id][None, :]]
    unnamed x94 -> x39, local copies, waits for them, and re-layouts: 0.33 us -> 19.6 us
    pallas_call x0 -> x15, Pallas kernels: none -> 17.8 us  [the longest x3 6.9 us: shards(): call(advance, 'advance', (field, jump, parcel, face, face, field, jump2,...]
  transfers between devices with their start and end apart: 64 -> 15, of which waited for: 48 -> 5; matrix products, arithmetic and copies ran while one was open for 9% -> 0% of each run, Pallas kernels for 0% -> 2%
where the time goes in v1:
time: 208 us; the launch traced here: 207 us
  blocking collectives  93.6 us (45%)
  starting transfers between devices  59.5 us (29%)
  local copies, waits for them, and re-layouts  19.6 us (9%)
  Pallas kernels  17.8 us (9%)
  waiting for transfers between devices  15.3 us (7%)
    all_to_all x4, blocking collectives, shards(): lax.all_to_all(everyone, ('plan', 'layer'), split_axis=0, concat_axis=0,...  93.6 us
    all_to_all x5, starting transfers between devices, swap(): lax.all_to_all(outgoing, 'plan', split_axis=0, concat_axis=0, tiled=True)  33 us
    ppermute x10, starting transfers between devices, neighbours(): return (lax.ppermute(last, 'layer', up), lax.ppermute(first, 'layer', down))  26.5 us
    unnamed x39, local copies, waits for them, and re-layouts  19.6 us
    all_to_all x5, waiting for transfers between devices, swap(): lax.all_to_all(outgoing, 'plan', split_axis=0, concat_axis=0, tiled=True)  15.3 us
    pallas_call x3, Pallas kernels, shards(): call(advance, 'advance', (field, jump, parcel, face, face, field, jump2,...  6.9 us
  transfers between devices with their start and end apart: 15, of which 5 were waited for; matrix products, arithmetic and copies ran while one was open for 0% of the time, Pallas kernels for 2%

profile of v1, /device:TPU:1, one launch (start us, length us, event | category | flops | bytes accessed | tf_op | source)
XLA Modules:
  0.0 206.7 jit_solution(17793532144961834776)
XLA Ops:
  1.3 0.8 copy-done.10
  4.1 1.6 prepare.1
  5.7 12.6 %all-to-all-start = ((f32[32,16,128]{2,1,0:T(8,128)}), f32[32,16,128]{2,1,0:T(8,128)S(1)}, u32[]{:S(2)}, u32[]{:S(2)}) async-start(f32[32,16,128]{2,1,0:T(8,128)} %get-tuple-element.52), calls=%async_computation | async-start | bytes 524288 | tf_op jit(solution)/shard_map/all_to_all | solution.py:228
  18.2 3.2 %collective-permute-start = (f32[16,128]{1,0:T(8,128)S(1)}, f32[16,128]{1,0:T(8,128)S(1)}, u32[]{:S(2)}, u32[]{:S(2)}) collective-permute-start(f32[16,128]{1,0:T(8,128)S(1)} %get-tuple-element.53), channel_id=1, source_target_pairs={{0,1},{1,2},{2,3},{3,4},{4,5},{5,6},{6,7},{8,9},{9,10},{10,11},{11... | collective-permute-start | bytes 24584 | tf_op jit(solution)/shard_map/ppermute | solution.py:235
  21.5 1.3 collective-permute-start.1
  22.8 2.2 %copy-done.8 = f32[1,1,1024,1024]{3,2,1,0:T(8,128)S(1)} copy-done((f32[1,1,1024,1024]{3,2,1,0:T(8,128)S(1)}, f32[1,1,1024,1024]{3,2,1,0:T(8,128)}, u32[]{:S(2)}) %copy-start.8) | copy-done | bytes 4194328
  24.9 0.8 copy-done.11
  25.7 1.0 split_dense.1
  26.7 1.3 copy-done
  28.1 3.6 %all-to-all-done.in_ref = f32[32,16,128]{2,1,0:T(8,128)S(1)} async-done(((f32[32,16,128]{2,1,0:T(8,128)}), f32[32,16,128]{2,1,0:T(8,128)S(1)}, u32[]{:S(2)}, u32[]{:S(2)}) %all-to-all-start) | async-done | bytes 262176 | tf_op jit(solution)/shard_map/all_to_all | solution.py:228
  31.7 1.6 first_gradient.1
  33.3 6.5 %all-to-all-start.1 = ((f32[32,8,128]{2,1,0:T(8,128)}), f32[32,8,128]{2,1,0:T(8,128)S(1)}, u32[]{:S(2)}, u32[]{:S(2)}) async-start(f32[32,8,128]{2,1,0:T(8,128)} %get-tuple-element.61), calls=%async_computation.1 | async-start | bytes 262144 | tf_op jit(solution)/shard_map/all_to_all | solution.py:228
  39.8 1.3 collective-permute-start.3
  41.1 4.9 %collective-permute-start.2 = (f32[8,128]{1,0:T(8,128)S(1)}, f32[8,128]{1,0:T(8,128)S(1)}, u32[]{:S(2)}, u32[]{:S(2)}) collective-permute-start(f32[8,128]{1,0:T(8,128)S(1)} %get-tuple-element.63.last_ref), channel_id=1, source_target_pairs={{0,1},{1,2},{2,3},{3,4},{4,5},{5,6},{6,7},{8,9},{9,10},{10,11},{11... | collective-permute-start | bytes 12296 | tf_op jit(solution)/shard_map/ppermute | solution.py:235
  46.0 1.6 copy-done.1
  47.6 0.7 local_sums.4.sums_ref
  48.3 2.1 %all-to-all-done.1.in_ref = f32[32,8,128]{2,1,0:T(8,128)S(1)} async-done(((f32[32,8,128]{2,1,0:T(8,128)}), f32[32,8,128]{2,1,0:T(8,128)S(1)}, u32[]{:S(2)}, u32[]{:S(2)}) %all-to-all-start.1) | async-done | bytes 131104 | tf_op jit(solution)/shard_map/all_to_all | solution.py:228
  51.1 25.8 %all_to_all.69 = f32[256,1,128]{2,1,0:T(1,128)S(1)} all-to-all(f32[256,1,128]{2,1,0:T(1,128)S(1)} %bitcast.41), channel_id=1, replica_groups=mesh['plan'=32,'layer'=8] {'plan','layer'}, dimensions={0} | all-to-all | bytes 262144 | tf_op jit(solution)/shard_map/all_to_all | solution.py:274
  77.0 1.6 copy-done.2
  78.5 2.3 %advance.3 = (f32[8,1024]{1,0:T(8,128)S(1)}, f32[8,256]{1,0:T(8,128)S(1)}, f32[32,8,128]{2,1,0:T(8,128)}, f32[8,128]{1,0:T(8,128)S(1)}, f32[8,128]{1,0:T(8,128)S...) custom-call(s32[1,6]{1,0:T(1,128)S(1)} %copy-done.17, ...), custom_call_target="tpu_custom_call" | custom-call | flops 67108864 | bytes 4194304 | tf_op jit(solution)/shard_map/advance/pallas_call | solution.py:278
  80.8 4.6 %all-to-all-start.3 = ((f32[32,8,128]{2,1,0:T(8,128)}), f32[32,8,128]{2,1,0:T(8,128)S(1)}, u32[]{:S(2)}, u32[]{:S(2)}) async-start(f32[32,8,128]{2,1,0:T(8,128)} %get-tuple-element.69), calls=%async_computation.3 | async-start | bytes 262144 | tf_op jit(solution)/shard_map/all_to_all | solution.py:228
  85.5 1.3 collective-permute-start.5
  86.8 4.0 %collective-permute-start.4 = (f32[8,128]{1,0:T(8,128)S(1)}, f32[8,128]{1,0:T(8,128)S(1)}, u32[]{:S(2)}, u32[]{:S(2)}) collective-permute-start(f32[8,128]{1,0:T(8,128)S(1)} %get-tuple-element.71.last_ref), channel_id=1, source_target_pairs={{0,1},{1,2},{2,3},{3,4},{4,5},{5,6},{6,7},{8,9},{9,10},{10,11},{11... | collective-permute-start | bytes 12296 | tf_op jit(solution)/shard_map/ppermute | solution.py:235
  90.8 1.6 copy-done.3
  92.4 0.7 local_sums.5.sums_ref
  93.1 3.4 %all-to-all-done.3.in_ref = f32[32,8,128]{2,1,0:T(8,128)S(1)} async-done(((f32[32,8,128]{2,1,0:T(8,128)}), f32[32,8,128]{2,1,0:T(8,128)S(1)}, u32[]{:S(2)}, u32[]{:S(2)}) %all-to-all-start.3) | async-done | bytes 131104 | tf_op jit(solution)/shard_map/all_to_all | solution.py:228
  97.2 22.4 %all_to_all.70 = f32[256,1,128]{2,1,0:T(1,128)S(1)} all-to-all(f32[256,1,128]{2,1,0:T(1,128)S(1)} %bitcast.42), channel_id=1, replica_groups=mesh['plan'=32,'layer'=8] {'plan','layer'}, dimensions={0} | all-to-all | bytes 262144 | tf_op jit(solution)/shard_map/all_to_all | solution.py:274
  119.6 1.6 copy-done.4
  121.1 2.3 %advance.4 = (f32[8,1024]{1,0:T(8,128)S(1)}, f32[8,256]{1,0:T(8,128)S(1)}, f32[32,8,128]{2,1,0:T(8,128)}, f32[8,128]{1,0:T(8,128)S(1)}, f32[8,128]{1,0:T(8,128)S...) custom-call(s32[1,6]{1,0:T(1,128)S(1)} %copy-done.17, ...), custom_call_target="tpu_custom_call" | custom-call | flops 67108864 | bytes 4194304 | tf_op jit(solution)/shard_map/advance/pallas_call | solution.py:278
  123.4 4.6 %all-to-all-start.5 = ((f32[32,8,128]{2,1,0:T(8,128)}), f32[32,8,128]{2,1,0:T(8,128)S(1)}, u32[]{:S(2)}, u32[]{:S(2)}) async-start(f32[32,8,128]{2,1,0:T(8,128)} %get-tuple-element.81), calls=%async_computation.5 | async-start | bytes 262144 | tf_op jit(solution)/shard_map/all_to_all | solution.py:228
  128.1 1.3 collective-permute-start.7
  129.4 4.0 %collective-permute-start.6 = (f32[8,128]{1,0:T(8,128)S(1)}, f32[8,128]{1,0:T(8,128)S(1)}, u32[]{:S(2)}, u32[]{:S(2)}) collective-permute-start(f32[8,128]{1,0:T(8,128)S(1)} %get-tuple-element.83.last_ref), channel_id=1, source_target_pairs={{0,1},{1,2},{2,3},{3,4},{4,5},{5,6},{6,7},{8,9},{9,10},{10,11},{11... | collective-permute-start | bytes 12296 | tf_op jit(solution)/shard_map/ppermute | solution.py:235
  133.4 1.6 copy-done.5
  135.0 0.7 local_sums.6.sums_ref
  135.7 3.4 %all-to-all-done.5.in_ref = f32[32,8,128]{2,1,0:T(8,128)S(1)} async-done(((f32[32,8,128]{2,1,0:T(8,128)}), f32[32,8,128]{2,1,0:T(8,128)S(1)}, u32[]{:S(2)}, u32[]{:S(2)}) %all-to-all-start.5) | async-done | bytes 131104 | tf_op jit(solution)/shard_map/all_to_all | solution.py:228
  139.8 22.3 %all_to_all.71 = f32[256,1,128]{2,1,0:T(1,128)S(1)} all-to-all(f32[256,1,128]{2,1,0:T(1,128)S(1)} %bitcast.43), channel_id=1, replica_groups=mesh['plan'=32,'layer'=8] {'plan','layer'}, dimensions={0} | all-to-all | bytes 262144 | tf_op jit(solution)/shard_map/all_to_all | solution.py:274
  162.1 1.6 copy-done.6
  163.7 2.3 %advance.5 = (f32[8,1024]{1,0:T(8,128)}, f32[8,256]{1,0:T(8,128)S(1)}, f32[32,8,128]{2,1,0:T(8,128)}, f32[8,128]{1,0:T(8,128)S(1)}, f32[8,128]{1,0:T(8,128)S(1)}...) custom-call(s32[1,6]{1,0:T(1,128)S(1)} %copy-done.17, ...), custom_call_target="tpu_custom_call" | custom-call | flops 67108864 | bytes 4194304 | tf_op jit(solution)/shard_map/advance/pallas_call | solution.py:278
  166.0 4.6 %all-to-all-start.7 = ((f32[32,8,128]{2,1,0:T(8,128)}), f32[32,8,128]{2,1,0:T(8,128)S(1)}, u32[]{:S(2)}, u32[]{:S(2)}) async-start(f32[32,8,128]{2,1,0:T(8,128)} %get-tuple-element.93), calls=%async_computation.7 | async-start | bytes 262144 | tf_op jit(solution)/shard_map/all_to_all | solution.py:228
  170.7 1.3 collective-permute-start.9
  172.0 4.0 %collective-permute-start.8 = (f32[8,128]{1,0:T(8,128)S(1)}, f32[8,128]{1,0:T(8,128)S(1)}, u32[]{:S(2)}, u32[]{:S(2)}) collective-permute-start(f32[8,128]{1,0:T(8,128)S(1)} %get-tuple-element.95.last_ref), channel_id=1, source_target_pairs={{0,1},{1,2},{2,3},{3,4},{4,5},{5,6},{6,7},{8,9},{9,10},{10,11},{11... | collective-permute-start | bytes 12296 | tf_op jit(solution)/shard_map/ppermute | solution.py:235
  176.0 1.6 copy-done.7
  177.6 0.8 copy-done.13
  178.3 0.7 local_sums.7.sums_ref
  179.1 2.7 %all-to-all-done.7.in_ref = f32[32,8,128]{2,1,0:T(8,128)S(1)} async-done(((f32[32,8,128]{2,1,0:T(8,128)}), f32[32,8,128]{2,1,0:T(8,128)S(1)}, u32[]{:S(2)}, u32[]{:S(2)}) %all-to-all-start.7) | async-done | bytes 131104 | tf_op jit(solution)/shard_map/all_to_all | solution.py:228
  181.8 1.1 add_coupling.7
  182.9 23.1 %all_to_all.72 = f32[256,1,128]{2,1,0:T(1,128)S(1)} all-to-all(f32[256,1,128]{2,1,0:T(1,128)S(1)} %bitcast.40), channel_id=1, replica_groups=mesh['plan'=32,'layer'=8] {'plan','layer'}, dimensions={0} | all-to-all | bytes 262144 | tf_op jit(solution)/shard_map/all_to_all | solution.py:274
  206.0 0.7 finish.1
  (40 shorter events, 4.7 us)
Async XLA Ops:
  1.3 0.8 copy-start.10
  2.1 0.7 copy-start.14
  2.8 0.7 copy-start.16
  3.4 0.7 copy-start.18
  5.7 26.0 %all-to-all-start = ((f32[32,16,128]{2,1,0:T(8,128)}), f32[32,16,128]{2,1,0:T(8,128)S(1)}, u32[]{:S(2)}, u32[]{:S(2)}) async-start(f32[32,16,128]{2,1,0:T(8,128)} %get-tuple-element.52), calls=%async_computation | async-start | bytes 524288 | tf_op jit(solution)/shard_map/all_to_all | solution.py:228
  18.2 9.8 %collective-permute-start = (f32[16,128]{1,0:T(8,128)S(1)}, f32[16,128]{1,0:T(8,128)S(1)}, u32[]{:S(2)}, u32[]{:S(2)}) collective-permute-start(f32[16,128]{1,0:T(8,128)S(1)} %get-tuple-element.53), channel_id=1, source_target_pairs={{0,1},{1,2},{2,3},{3,4},{4,5},{5,6},{6,7},{8,9},{9,10},{10,11},{11... | collective-permute-start | bytes 24584 | tf_op jit(solution)/shard_map/ppermute | solution.py:235
  21.5 6.6 %collective-permute-start.1 = (f32[16,128]{1,0:T(8,128)S(1)}, f32[16,128]{1,0:T(8,128)S(1)}, u32[]{:S(2)}, u32[]{:S(2)}) collective-permute-start(f32[16,128]{1,0:T(8,128)S(1)} %get-tuple-element.54), channel_id=1, source_target_pairs={{1,0},{2,1},{3,2},{4,3},{5,4},{6,5},{7,6},{9,8},{10,9},{11,10},{12... | collective-permute-start | bytes 24584 | tf_op jit(solution)/shard_map/ppermute | solution.py:235
  22.8 2.2 %copy-start.8 = (f32[1,1,1024,1024]{3,2,1,0:T(8,128)S(1)}, f32[1,1,1024,1024]{3,2,1,0:T(8,128)}, u32[]{:S(2)}) copy-start(f32[1,1,1024,1024]{3,2,1,0:T(8,128)} %param.7) | copy-start | bytes 12582916
  24.9 0.8 copy-start.11
  25.7 5.9 %copy-start.9 = (f32[1,1,8,1024]{3,2,1,0:T(8,128)S(1)}, f32[1,1,8,1024]{3,2,1,0:T(8,128)}, u32[]{:S(2)}) copy-start(f32[1,1,8,1024]{3,2,1,0:T(8,128)} %param.9) | copy-start | bytes 98308
  25.7 6.0 %copy-start.12 = (f32[1,1,8,1024]{3,2,1,0:T(8,128)S(1)}, f32[1,1,8,1024]{3,2,1,0:T(8,128)}, u32[]{:S(2)}) copy-start(f32[1,1,8,1024]{3,2,1,0:T(8,128)} %param.8) | copy-start | bytes 98308
  25.7 6.0 %copy-start.17 = (s32[1,6]{1,0:T(1,128)S(1)}, s32[1,6]{1,0:T(1,128)}, u32[]{:S(2)}) copy-start(s32[1,6]{1,0:T(1,128)} %partners_ref.17) | copy-start | bytes 76
  26.7 1.3 copy-start
  33.3 17.1 %all-to-all-start.1 = ((f32[32,8,128]{2,1,0:T(8,128)}), f32[32,8,128]{2,1,0:T(8,128)S(1)}, u32[]{:S(2)}, u32[]{:S(2)}) async-start(f32[32,8,128]{2,1,0:T(8,128)} %get-tuple-element.61), calls=%async_computation.1 | async-start | bytes 262144 | tf_op jit(solution)/shard_map/all_to_all | solution.py:228
  39.8 8.5 %collective-permute-start.3 = (f32[8,128]{1,0:T(8,128)S(1)}, f32[8,128]{1,0:T(8,128)S(1)}, u32[]{:S(2)}, u32[]{:S(2)}) collective-permute-start(f32[8,128]{1,0:T(8,128)S(1)} %get-tuple-element.62.first_ref), channel_id=1, source_target_pairs={{1,0},{2,1},{3,2},{4,3},{5,4},{6,5},{7,6},{9,8},{10,9},{11,10},{12... | collective-permute-start | bytes 12296 | tf_op jit(solution)/shard_map/ppermute | solution.py:235
  41.1 7.2 %collective-permute-start.2 = (f32[8,128]{1,0:T(8,128)S(1)}, f32[8,128]{1,0:T(8,128)S(1)}, u32[]{:S(2)}, u32[]{:S(2)}) collective-permute-start(f32[8,128]{1,0:T(8,128)S(1)} %get-tuple-element.63.last_ref), channel_id=1, source_target_pairs={{0,1},{1,2},{2,3},{3,4},{4,5},{5,6},{6,7},{8,9},{9,10},{10,11},{11... | collective-permute-start | bytes 12296 | tf_op jit(solution)/shard_map/ppermute | solution.py:235
  46.0 1.6 copy-start.1
  47.6 29.3 %copy-start.15 = (s32[1,1,1024]{2,1,0:T(1,128)S(1)}, s32[1,1,1024]{2,1,0:T(1,128)}, u32[]{:S(2)}) copy-start(s32[1,1,1024]{2,1,0:T(1,128)} %param.13) | copy-start | bytes 12292
  77.0 1.6 copy-start.2
  80.8 15.7 %all-to-all-start.3 = ((f32[32,8,128]{2,1,0:T(8,128)}), f32[32,8,128]{2,1,0:T(8,128)S(1)}, u32[]{:S(2)}, u32[]{:S(2)}) async-start(f32[32,8,128]{2,1,0:T(8,128)} %get-tuple-element.69), calls=%async_computation.3 | async-start | bytes 262144 | tf_op jit(solution)/shard_map/all_to_all | solution.py:228
  85.5 7.6 %collective-permute-start.5 = (f32[8,128]{1,0:T(8,128)S(1)}, f32[8,128]{1,0:T(8,128)S(1)}, u32[]{:S(2)}, u32[]{:S(2)}) collective-permute-start(f32[8,128]{1,0:T(8,128)S(1)} %get-tuple-element.70.first_ref), channel_id=1, source_target_pairs={{1,0},{2,1},{3,2},{4,3},{5,4},{6,5},{7,6},{9,8},{10,9},{11,10},{12... | collective-permute-start | bytes 12296 | tf_op jit(solution)/shard_map/ppermute | solution.py:235
  86.8 6.3 %collective-permute-start.4 = (f32[8,128]{1,0:T(8,128)S(1)}, f32[8,128]{1,0:T(8,128)S(1)}, u32[]{:S(2)}, u32[]{:S(2)}) collective-permute-start(f32[8,128]{1,0:T(8,128)S(1)} %get-tuple-element.71.last_ref), channel_id=1, source_target_pairs={{0,1},{1,2},{2,3},{3,4},{4,5},{5,6},{6,7},{8,9},{9,10},{10,11},{11... | collective-permute-start | bytes 12296 | tf_op jit(solution)/shard_map/ppermute | solution.py:235
  90.8 1.6 copy-start.3
  119.6 1.6 copy-start.4
  123.4 15.7 %all-to-all-start.5 = ((f32[32,8,128]{2,1,0:T(8,128)}), f32[32,8,128]{2,1,0:T(8,128)S(1)}, u32[]{:S(2)}, u32[]{:S(2)}) async-start(f32[32,8,128]{2,1,0:T(8,128)} %get-tuple-element.81), calls=%async_computation.5 | async-start | bytes 262144 | tf_op jit(solution)/shard_map/all_to_all | solution.py:228
  128.1 7.6 %collective-permute-start.7 = (f32[8,128]{1,0:T(8,128)S(1)}, f32[8,128]{1,0:T(8,128)S(1)}, u32[]{:S(2)}, u32[]{:S(2)}) collective-permute-start(f32[8,128]{1,0:T(8,128)S(1)} %get-tuple-element.82.first_ref), channel_id=1, source_target_pairs={{1,0},{2,1},{3,2},{4,3},{5,4},{6,5},{7,6},{9,8},{10,9},{11,10},{12... | collective-permute-start | bytes 12296 | tf_op jit(solution)/shard_map/ppermute | solution.py:235
  129.4 6.3 %collective-permute-start.6 = (f32[8,128]{1,0:T(8,128)S(1)}, f32[8,128]{1,0:T(8,128)S(1)}, u32[]{:S(2)}, u32[]{:S(2)}) collective-permute-start(f32[8,128]{1,0:T(8,128)S(1)} %get-tuple-element.83.last_ref), channel_id=1, source_target_pairs={{0,1},{1,2},{2,3},{3,4},{4,5},{5,6},{6,7},{8,9},{9,10},{10,11},{11... | collective-permute-start | bytes 12296 | tf_op jit(solution)/shard_map/ppermute | solution.py:235
  133.4 1.6 copy-start.5
  162.1 1.6 copy-start.6
  166.0 15.7 %all-to-all-start.7 = ((f32[32,8,128]{2,1,0:T(8,128)}), f32[32,8,128]{2,1,0:T(8,128)S(1)}, u32[]{:S(2)}, u32[]{:S(2)}) async-start(f32[32,8,128]{2,1,0:T(8,128)} %get-tuple-element.93), calls=%async_computation.7 | async-start | bytes 262144 | tf_op jit(solution)/shard_map/all_to_all | solution.py:228
  170.7 8.4 %collective-permute-start.9 = (f32[8,128]{1,0:T(8,128)S(1)}, f32[8,128]{1,0:T(8,128)S(1)}, u32[]{:S(2)}, u32[]{:S(2)}) collective-permute-start(f32[8,128]{1,0:T(8,128)S(1)} %get-tuple-element.94.first_ref), channel_id=1, source_target_pairs={{1,0},{2,1},{3,2},{4,3},{5,4},{6,5},{7,6},{9,8},{10,9},{11,10},{12... | collective-permute-start | bytes 12296 | tf_op jit(solution)/shard_map/ppermute | solution.py:235
  172.0 7.1 %collective-permute-start.8 = (f32[8,128]{1,0:T(8,128)S(1)}, f32[8,128]{1,0:T(8,128)S(1)}, u32[]{:S(2)}, u32[]{:S(2)}) collective-permute-start(f32[8,128]{1,0:T(8,128)S(1)} %get-tuple-element.95.last_ref), channel_id=1, source_target_pairs={{0,1},{1,2},{2,3},{3,4},{4,5},{5,6},{6,7},{8,9},{9,10},{10,11},{11... | collective-permute-start | bytes 12296 | tf_op jit(solution)/shard_map/ppermute | solution.py:235
  176.0 1.6 copy-start.7
  177.6 0.8 copy-start.13

commit v2 on v1

v2 whole, which is shorter than its diff:
```python
import functools

import jax
import jax.numpy as jnp
from jax import lax
from jax.experimental import pallas as pl
from jax.experimental.pallas import tpu as pltpu
from jax.sharding import PartitionSpec as P

FACE = 128
JR = 32
ROUNDS = 6
ITERS = 4
LANES = 128
JW = 256
SQUARE, CURVATURE = 64, 65
F32 = jnp.float32
BF16 = jnp.bfloat16

VMEM = pl.BlockSpec(memory_space=pltpu.VMEM)
SMEM = pl.BlockSpec(memory_space=pltpu.SMEM)


def shape(*dims, dtype=F32):
    return jax.ShapeDtypeStruct(dims, dtype)


def call(body, name, outs, specs, limit, flops=0, moved=0):
    return pl.pallas_call(
        body,
        name=name,
        out_shape=outs,
        in_specs=specs,
        out_specs=jax.tree.map(lambda _: VMEM, outs),
        compiler_params=pltpu.CompilerParams(vmem_limit_bytes=limit * 2**20),
        cost_estimate=pl.CostEstimate(flops=flops, bytes_accessed=moved, transcendentals=0),
    )


def pieces(value, count):
    parts = []
    for _ in range(count):
        part = value.astype(BF16).astype(F32)
        parts.append(part)
        value = value - part
    return parts


def dense(field, high, low):
    lhs = jnp.concatenate(pieces(field, 2), axis=0).astype(BF16)
    total = jnp.dot(lhs, high, preferred_element_type=F32)
    total = total + jnp.dot(lhs, low, preferred_element_type=F32)
    return total[:8] + total[8:]


def pick(field, onehot, *extra):
    lhs = jnp.concatenate(pieces(field, 3) + list(extra), axis=0).astype(BF16)
    out = jnp.dot(lhs, onehot, preferred_element_type=F32)
    return [out[:8] + out[8:16] + out[16:24]] + [
        out[24 + 8 * i : 32 + 8 * i] for i in range(len(extra))
    ]


def spread(jumps, onehot):
    lhs = jnp.concatenate(pieces(jumps, 3), axis=0).astype(BF16)
    out = lax.dot_general(lhs, onehot, (((1,), (1,)), ((), ())), preferred_element_type=F32)
    return out[:8] + out[8:16] + out[16:24]


def arrived(in_ref, partners_ref, wide):
    height = in_ref.shape[1]
    place = lax.broadcasted_iota(jnp.int32, (height, LANES), 1) // JR
    groups = []
    for first in range(0, JW // JR, LANES // JR):
        total = jnp.zeros((height, LANES), F32)
        at = first * JR if wide else 0
        for r in range(first, min(first + LANES // JR, ROUNDS)):
            block = in_ref[partners_ref[0, r], :, at : at + LANES]
            total = jnp.where(place == r - first, block, total)
        groups.append(total)
    return jnp.concatenate(groups, axis=1)


def prepare(x_ref, contact_ref, rows_ref, partners_ref, counts_ref,
            onehot_ref, valid_ref, own_ref, out_ref, first_ref, last_ref):
    x = x_ref[...]
    rows = jnp.concatenate(
        [rows_ref[r : r + 1, :] for r in range(ROUNDS)]
        + [jnp.full((1, JW - ROUNDS * JR), -1, jnp.int32)],
        axis=1,
    )
    hit = lax.broadcasted_iota(jnp.int32, (x.shape[1], JW), 0) == rows
    onehot = jnp.where(hit, 1.0, 0.0).astype(BF16)
    onehot_ref[...] = onehot
    lane = lax.broadcasted_iota(jnp.int32, (8, JW), 1)
    valid = jnp.zeros((8, JW), F32)
    for r in range(ROUNDS):
        inside = (lane >= r * JR) & (lane < r * JR + counts_ref[0, r])
        valid = jnp.where(inside, 1.0, valid)
    valid_ref[...] = valid
    contact = jnp.broadcast_to(jnp.where(contact_ref[...] == 1, 1.0, 0.0), x.shape)
    own, own_contact = pick(x, onehot, contact)
    own_ref[...] = jnp.concatenate([own, own_contact], axis=0)
    short = lax.broadcasted_iota(jnp.int32, (8, LANES), 1)
    names = jnp.zeros((8, LANES), jnp.int32)
    for r in range(ROUNDS):
        names = jnp.where(short == r, partners_ref[0, r], names)
    names = names.astype(F32)
    row = lax.broadcasted_iota(jnp.int32, (8, LANES), 0)
    out_ref[...] = jnp.broadcast_to(
        jnp.concatenate([jnp.zeros((8, LANES), F32), names], axis=0)[None], out_ref.shape
    )
    for r in range(ROUNDS):
        group = (r * JR) // LANES
        at = slice(group * LANES, (group + 1) * LANES)
        low = jnp.where(row == 7, names, own_contact[:, at])
        out_ref[pl.ds(partners_ref[0, r], 1)] = jnp.concatenate([own[:, at], low], axis=0)[None]
    both = jnp.concatenate([x, contact], axis=0)
    first_ref[...] = both[:, :FACE]
    last_ref[...] = both[:, x.shape[1] - FACE :]


def split_dense(block_ref, x_ref, halves_ref, image_ref):
    block = block_ref[...]
    high = block.astype(BF16)
    low = (block - high.astype(F32)).astype(BF16)
    halves_ref[0] = high
    halves_ref[1] = low
    image_ref[...] = dense(x_ref[...], high, low)


def with_coupling(image, x, load, own, far, below, above, valid, onehot):
    width = x.shape[1]
    total = image + spread(valid * (own - far), onehot) - load
    head = total[:, :FACE] + (x[:, :FACE] - below)
    tail = total[:, width - FACE :] + (x[:, width - FACE :] - above)
    return jnp.concatenate([head, total[:, FACE : width - FACE], tail], axis=1)


def give_gradient(gradient, onehot, g_ref, gown_ref, last_ref):
    g_ref[...] = gradient
    last_ref[...] = gradient[:, gradient.shape[1] - FACE :]
    gown_ref[...] = pick(gradient, onehot)[0]


def first_gradient(partners_ref, image_ref, x_ref, load_ref, own_ref, in_ref, below_ref, above_ref,
                   valid_ref, onehot_ref, g_ref, gown_ref, last_ref, far_ref, table_ref):
    far = arrived(in_ref, partners_ref, False)
    flags = jnp.broadcast_to(far[8:9], far[8:].shape)
    far_ref[...] = jnp.concatenate([far[:8], flags], axis=0)
    for p in range(table_ref.shape[0]):
        table_ref[p : p + 1, :] = in_ref[p, 15:16, :8].astype(jnp.int32)
    onehot = onehot_ref[...]
    gradient = with_coupling(
        image_ref[...], x_ref[...], load_ref[...], own_ref[:8], far[:8], below_ref[:8],
        above_ref[:8], valid_ref[...], onehot,
    )
    give_gradient(gradient, onehot, g_ref, gown_ref, last_ref)


def local_sums(g_ref, halves_ref, sums_ref):
    g = g_ref[...]
    image = dense(g, halves_ref[0], halves_ref[1])
    width = g.shape[1]
    terms = g * image
    edges = g[:, :FACE] * g[:, :FACE] + g[:, width - FACE :] * g[:, width - FACE :]
    square = jnp.sum(g * g, axis=1, keepdims=True)
    curvature = jnp.sum(terms, axis=1, keepdims=True) + jnp.sum(edges, axis=1, keepdims=True)
    lane = lax.broadcasted_iota(jnp.int32, (8, LANES), 1)
    sums_ref[...] = jnp.where(lane == SQUARE, square, jnp.where(lane == CURVATURE, curvature, 0.0))


def announce(sums_ref, g_ref, gown_ref, valid_ref, below_ref, out_ref):
    own = valid_ref[...] * gown_ref[...]
    squares = own * own
    pairs = g_ref[:, :FACE] * below_ref[...]
    terms = squares[:, :LANES] + squares[:, LANES:] - 2.0 * pairs
    more = jnp.sum(terms, axis=1, keepdims=True)
    lane = lax.broadcasted_iota(jnp.int32, (8, LANES), 1)
    extra = sums_ref[...] + jnp.where(lane == CURVATURE, more, 0.0)
    parcel = jnp.concatenate([own[:, :LANES], own[:, LANES:] + extra], axis=1)
    out_ref[...] = jnp.broadcast_to(parcel[None], out_ref.shape)


def layer_sums(partners_ref, table_ref, in_ref, g_ref, gfar_ref, out_ref):
    gfar_ref[...] = arrived(in_ref, partners_ref, True)
    place = lax.broadcasted_iota(jnp.int32, (8, LANES), 1) // JR
    nothing = jnp.zeros((8, LANES), F32)
    products, sums = [nothing, nothing], nothing
    for p in range(in_ref.shape[0]):
        near = [in_ref[p, :, :LANES], in_ref[p, :, LANES:]]
        sums = sums + near[1]
        for group in range(2):
            far = nothing
            for r in range(4 * group, min(4 * group + 4, ROUNDS)):
                block = in_ref[table_ref[p, r], :, group * LANES : (group + 1) * LANES]
                far = jnp.where(place == r - 4 * group, block, far)
            products[group] = products[group] + near[group] * far
    cross = jnp.sum(products[0] + products[1], axis=1, keepdims=True)
    lane = lax.broadcasted_iota(jnp.int32, (8, LANES), 1)
    sums = sums - jnp.where(lane == CURVATURE, cross, 0.0)
    parcel = jnp.concatenate([g_ref[:, :FACE], sums], axis=1)
    out_ref[...] = jnp.broadcast_to(parcel[None], out_ref.shape)


def step_of(in_ref):
    total = in_ref[0, :, LANES:]
    for layer in range(1, in_ref.shape[0]):
        total = total + in_ref[layer, :, LANES:]
    square = total[:, SQUARE : SQUARE + 1]
    curvature = total[:, CURVATURE : CURVATURE + 1]
    return (square + 1e-6) / (curvature + 1e-6)


def moved(x, g, step, contact):
    out = x - step * g
    return jnp.where(contact == 1, jnp.maximum(out, 0.0), out)


def advance(layer_ref, in_ref, x_ref, g_ref, contact_ref, load_ref,
            own_ref, gown_ref, far_ref, gfar_ref, below_ref, gbelow_ref, above_ref,
            valid_ref, onehot_ref, halves_ref,
            g_out, gown_out, last_out, x_out, own_out, far_out, below_out, above_out):
    step = step_of(in_ref)
    x = moved(x_ref[...], g_ref[...], step, contact_ref[...])
    x_out[...] = x
    layers = in_ref.shape[0]
    layer = layer_ref[0, 0]
    gabove = in_ref[jnp.minimum(layer + 1, layers - 1), :, :FACE]
    gabove = jnp.where(layer < layers - 1, gabove, 0.0)
    halo = []
    for held_ref, slope, held_out in (
        (own_ref, gown_ref[...], own_out), (far_ref, gfar_ref[...], far_out),
        (below_ref, gbelow_ref[...], below_out), (above_ref, gabove, above_out),
    ):
        flags = held_ref[8:]
        value = moved(held_ref[:8], slope, step, flags)
        held_out[...] = jnp.concatenate([value, flags], axis=0)
        halo.append(value)
    onehot = onehot_ref[...]
    image = dense(x, halves_ref[0], halves_ref[1])
    gradient = with_coupling(image, x, load_ref[...], *halo, valid_ref[...], onehot)
    give_gradient(gradient, onehot, g_out, gown_out, last_out)


def finish(in_ref, x_ref, g_ref, contact_ref, x_out):
    x_out[...] = moved(x_ref[...], g_ref[...], step_of(in_ref), contact_ref[...])


def swap(outgoing, axis):
    return lax.all_to_all(outgoing, axis, split_axis=0, concat_axis=0, tiled=True)


def lift(face, step):
    layers = lax.axis_size("layer")
    return lax.ppermute(
        face, "layer", [(i, i + step) for i in range(layers) if 0 <= i + step < layers]
    )


def shards(dual_block, start, load, partners, jump_rows, counts, contact):
    block, x, target = dual_block[0, 0], start[0, 0], load[0, 0]
    rows, amounts, flags = jump_rows[0, 0], counts[0], contact[0]
    loads, width = x.shape
    plans, layers = lax.axis_size("plan"), lax.axis_size("layer")
    field, jump, face = shape(loads, width), shape(loads, JW), shape(loads, FACE)
    jump2, face2 = shape(2 * loads, JW), shape(2 * loads, FACE)
    halves_shape = shape(2, width, width, dtype=BF16)
    flops = 4 * 16 * width * width
    layer = lax.axis_index("layer").astype(jnp.int32).reshape(1, 1)

    onehot, valid, own, out, first, last = call(
        prepare, "prepare",
        (shape(width, JW, dtype=BF16), jump, jump2, shape(plans, 2 * loads, LANES), face2, face2),
        [VMEM, VMEM, VMEM, SMEM, SMEM], 8,
    )(x, flags, rows, partners, amounts)
    incoming = swap(out, "plan")
    below, above = lift(last, 1), lift(first, -1)
    halves, image = call(
        split_dense, "split_dense", (halves_shape, field), [VMEM, VMEM], 20, flops, 12 * width * width,
    )(block, x)
    g, gown, last, far, table = call(
        first_gradient, "first_gradient",
        (field, jump, face, jump2, shape(plans, 8, dtype=jnp.int32)), [SMEM] + [VMEM] * 9, 8,
    )(partners, image, x, target, own, incoming, below, above, valid, onehot)

    for iteration in range(ITERS):
        gbelow = lift(last, 1)
        sums = call(
            local_sums, "local_sums", face, [VMEM] * 2, 12, flops, 4 * width * width,
        )(g, halves)
        out = call(announce, "announce", shape(plans, loads, JW), [VMEM] * 5, 8)(
            sums, g, gown, valid, gbelow
        )
        gfar, out = call(
            layer_sums, "layer_sums", (jump, shape(layers, loads, FACE + LANES)),
            [SMEM] * 2 + [VMEM] * 2, 8,
        )(partners, table, swap(out, "plan"), g)
        incoming = swap(out, "layer")
        if iteration == ITERS - 1:
            x = call(finish, "finish", field, [VMEM] * 4, 8)(incoming, x, g, flags)
            break
        g, gown, last, x, own, far, below, above = call(
            advance, "advance", (field, jump, face, field, jump2, jump2, face2, face2),
            [SMEM] + [VMEM] * 15, 12, flops, 4 * width * width,
        )(layer, incoming, x, g, flags, target, own, gown, far, gfar, below, gbelow, above,
          valid, onehot, halves)
    return x[None, None], g[None, None]


def solution(mesh):
    in_specs = (
        P("layer", "plan", None, None),
        P("layer", "plan", None, None),
        P("layer", "plan", None, None),
        P("plan", None),
        P("layer", "plan", None, None),
        P("layer", "plan", None),
        P("layer", "plan", None),
    )
    out_specs = (P("layer", "plan", None, None), P("layer", "plan", None, None))
    return jax.shard_map(shards, mesh=mesh, in_specs=in_specs, out_specs=out_specs, check_vma=False)
```

time: 208 us -> 178 us (0.86)
  starting transfers between devices: 59.5 us -> 31.5 us
  blocking collectives: 93.6 us -> 106 us
  waiting for transfers between devices: 15.3 us -> 8.23 us
  local copies, waits for them, and re-layouts: 19.6 us -> 13.5 us
    all_to_all x5 -> x2, starting transfers between devices: 33 us -> 17.1 us  [swap(): lax.all_to_all(outgoing, axis, split_axis=0, concat_axis=0, tiled=True)]
    all_to_all x4 -> x7, blocking collectives: 93.6 us -> 106 us  [swap(): lax.all_to_all(outgoing, axis, split_axis=0, concat_axis=0, tiled=True)]
    ppermute x10 -> x6, starting transfers between devices: 26.5 us -> 14.4 us  [lift(): lax.ppermute(face, 'layer', [(i, i + step) for i in range(layers) if 0 <=...]
    all_to_all x5 -> x2, waiting for transfers between devices: 15.3 us -> 8.21 us  [swap(): lax.all_to_all(outgoing, axis, split_axis=0, concat_axis=0, tiled=True)]
    unnamed x39 -> x31, local copies, waits for them, and re-layouts: 19.6 us -> 13.5 us
    pallas_call x15 -> x19, Pallas kernels: 17.8 us -> 17.1 us  [the longest x4 5.61 us: shards(): call(layer_sums, 'layer_sums', (jump, shape(layers, loads, FACE + LANES))...]
  transfers between devices with their start and end apart: 15 -> 8, of which waited for: 5 -> 2; matrix products, arithmetic and copies ran while one was open for 0% -> 0% of each run, Pallas kernels for 2% -> 2%
where the time goes in v2:
time: 178 us; the launch traced here: 177 us
  blocking collectives  106 us (60%)
  starting transfers between devices  31.5 us (18%)
  Pallas kernels  17.1 us (10%)
  local copies, waits for them, and re-layouts  13.5 us (8%)
  waiting for transfers between devices  8.23 us (5%)
    all_to_all x7, blocking collectives, swap(): lax.all_to_all(outgoing, axis, split_axis=0, concat_axis=0, tiled=True)  106 us
    all_to_all x2, starting transfers between devices, swap(): lax.all_to_all(outgoing, axis, split_axis=0, concat_axis=0, tiled=True)  17.1 us
    ppermute x6, starting transfers between devices, lift(): lax.ppermute(face, 'layer', [(i, i + step) for i in range(layers) if 0 <=...  14.4 us
    unnamed x31, local copies, waits for them, and re-layouts  13.5 us
    all_to_all x2, waiting for transfers between devices, swap(): lax.all_to_all(outgoing, axis, split_axis=0, concat_axis=0, tiled=True)  8.21 us
    pallas_call x4, Pallas kernels, shards(): call(layer_sums, 'layer_sums', (jump, shape(layers, loads, FACE + LANES))...  5.61 us
    pallas_call x3, Pallas kernels, shards(): call(advance, 'advance', (field, jump, face, field, jump2, jump2, face2,...  3.88 us
  transfers between devices with their start and end apart: 8, of which 2 were waited for; matrix products, arithmetic and copies ran while one was open for 0% of the time, Pallas kernels for 2%

profile of v2, /device:TPU:1, one launch (start us, length us, event | category | flops | bytes accessed | tf_op | source)
XLA Modules:
  0.0 177.2 jit_solution(5877026161709463614)
XLA Ops:
  0.6 0.7 copy.11
  1.3 0.8 copy-done.6
  2.1 0.7 copy-done.10
  2.8 0.7 copy-done.12
  3.4 0.7 copy-done.14
  4.1 1.5 prepare.1
  5.6 12.6 %all-to-all-start = ((f32[32,16,128]{2,1,0:T(8,128)}), f32[32,16,128]{2,1,0:T(8,128)S(1)}, u32[]{:S(2)}, u32[]{:S(2)}) async-start(f32[32,16,128]{2,1,0:T(8,128)} %get-tuple-element.44), calls=%async_computation | async-start | bytes 524288 | tf_op jit(solution)/shard_map/all_to_all | solution.py:251
  18.2 3.2 %collective-permute-start = (f32[16,128]{1,0:T(8,128)S(1)}, f32[16,128]{1,0:T(8,128)S(1)}, u32[]{:S(2)}, u32[]{:S(2)}) collective-permute-start(f32[16,128]{1,0:T(8,128)S(1)} %get-tuple-element.45), channel_id=1, source_target_pairs={{0,1},{1,2},{2,3},{3,4},{4,5},{5,6},{6,7},{8,9},{9,10},{10,11},{11... | collective-permute-start | bytes 24584 | tf_op jit(solution)/shard_map/ppermute | solution.py:256
  21.4 1.3 collective-permute-start.1
  22.8 2.2 %copy-done.4 = f32[1,1,1024,1024]{3,2,1,0:T(8,128)S(1)} copy-done((f32[1,1,1024,1024]{3,2,1,0:T(8,128)S(1)}, f32[1,1,1024,1024]{3,2,1,0:T(8,128)}, u32[]{:S(2)}) %copy-start.4) | copy-done | bytes 4194328
  24.9 0.8 copy-done.7
  25.7 1.0 split_dense.1
  26.7 2.0 %copy-done = bf16[2,1024,1024]{2,1,0:T(8,128)(2,1)} copy-done((bf16[2,1024,1024]{2,1,0:T(8,128)(2,1)}, bf16[2,1024,1024]{2,1,0:T(8,128)(2,1)S(1)}, u32[]{:S(2)}) %copy-start) | copy-done | bytes 4194328
  28.7 3.0 %all-to-all-done.in_ref = f32[32,16,128]{2,1,0:T(8,128)S(1)} async-done(((f32[32,16,128]{2,1,0:T(8,128)}), f32[32,16,128]{2,1,0:T(8,128)S(1)}, u32[]{:S(2)}, u32[]{:S(2)}) %all-to-all-start) | async-done | bytes 262176 | tf_op jit(solution)/shard_map/all_to_all | solution.py:251
  31.6 1.0 first_gradient.1
  32.6 3.2 %collective-permute-start.2 = (f32[8,128]{1,0:T(8,128)S(1)}, f32[8,128]{1,0:T(8,128)S(1)}, u32[]{:S(2)}, u32[]{:S(2)}) collective-permute-start(f32[8,128]{1,0:T(8,128)S(1)} %get-tuple-element.53), channel_id=1, source_target_pairs={{0,1},{1,2},{2,3},{3,4},{4,5},{5,6},{6,7},{8,9},{9,10},{10,11},{11... | collective-permute-start | bytes 12296 | tf_op jit(solution)/shard_map/ppermute | solution.py:256
  35.9 2.2 %copy-done.1 = bf16[2,1024,1024]{2,1,0:T(8,128)(2,1)S(1)} copy-done((bf16[2,1024,1024]{2,1,0:T(8,128)(2,1)S(1)}, bf16[2,1024,1024]{2,1,0:T(8,128)(2,1)}, u32[]{:S(2)}) %copy-start.1) | copy-done | bytes 4194328
  38.0 0.7 local_sums.4.sums_ref
  38.7 0.2 announce.4
  38.9 21.8 %all_to_all.45.in_ref = f32[32,8,256]{2,1,0:T(8,128)S(1)} all-to-all(f32[32,8,256]{2,1,0:T(8,128)S(1)} %announce.4), channel_id=1, replica_groups=mesh['plan'=32,'layer'=8] {'plan'}, dimensions={0} | all-to-all | bytes 524288 | tf_op jit(solution)/shard_map/all_to_all | solution.py:251
  60.7 1.7 layer_sums.4
  62.4 4.5 %all-to-all-start.2 = ((f32[8,8,256]{2,1,0:T(8,128)}), f32[8,8,256]{2,1,0:T(8,128)S(1)}, u32[]{:S(2)}, u32[]{:S(2)}) async-start(f32[8,8,256]{2,1,0:T(8,128)} %get-tuple-element.54), calls=%async_computation.2 | async-start | bytes 131072 | tf_op jit(solution)/shard_map/all_to_all | solution.py:251
  66.9 5.2 %all-to-all-done.2.in_ref = f32[8,8,256]{2,1,0:T(8,128)S(1)} async-done(((f32[8,8,256]{2,1,0:T(8,128)}), f32[8,8,256]{2,1,0:T(8,128)S(1)}, u32[]{:S(2)}, u32[]{:S(2)}) %all-to-all-start.2) | async-done | bytes 65568 | tf_op jit(solution)/shard_map/all_to_all | solution.py:251
  72.2 2.2 %copy-done.2 = bf16[2,1024,1024]{2,1,0:T(8,128)(2,1)S(1)} copy-done((bf16[2,1024,1024]{2,1,0:T(8,128)(2,1)S(1)}, bf16[2,1024,1024]{2,1,0:T(8,128)(2,1)}, u32[]{:S(2)}) %copy-start.2) | copy-done | bytes 4194328
  74.3 1.1 advance.3
  75.5 2.3 %collective-permute-start.3 = (f32[8,128]{1,0:T(8,128)S(1)}, f32[8,128]{1,0:T(8,128)S(1)}, u32[]{:S(2)}, u32[]{:S(2)}) collective-permute-start(f32[8,128]{1,0:T(8,128)S(1)} %get-tuple-element.59), channel_id=1, source_target_pairs={{0,1},{1,2},{2,3},{3,4},{4,5},{5,6},{6,7},{8,9},{9,10},{10,11},{11... | collective-permute-start | bytes 12296 | tf_op jit(solution)/shard_map/ppermute | solution.py:256
  77.8 0.7 local_sums.5.sums_ref
  78.5 0.2 announce.5
  78.7 18.7 %all_to_all.46.in_ref = f32[32,8,256]{2,1,0:T(8,128)S(1)} all-to-all(f32[32,8,256]{2,1,0:T(8,128)S(1)} %announce.5), channel_id=1, replica_groups=mesh['plan'=32,'layer'=8] {'plan'}, dimensions={0} | all-to-all | bytes 524288 | tf_op jit(solution)/shard_map/all_to_all | solution.py:251
  97.3 1.1 layer_sums.5
  98.5 9.5 %all_to_all.47.in_ref = f32[8,8,256]{2,1,0:T(8,128)S(1)} all-to-all(f32[8,8,256]{2,1,0:T(8,128)S(1)} %get-tuple-element.60), channel_id=1, replica_groups=mesh['plan'=32,'layer'=8] {'layer'}, dimensions={0} | all-to-all | bytes 131072 | tf_op jit(solution)/shard_map/all_to_all | solution.py:251
  107.9 1.1 advance.4
  109.0 2.2 %collective-permute-start.4 = (f32[8,128]{1,0:T(8,128)S(1)}, f32[8,128]{1,0:T(8,128)S(1)}, u32[]{:S(2)}, u32[]{:S(2)}) collective-permute-start(f32[8,128]{1,0:T(8,128)S(1)} %get-tuple-element.69), channel_id=1, source_target_pairs={{0,1},{1,2},{2,3},{3,4},{4,5},{5,6},{6,7},{8,9},{9,10},{10,11},{11... | collective-permute-start | bytes 12296 | tf_op jit(solution)/shard_map/ppermute | solution.py:256
  111.2 0.7 local_sums.6.sums_ref
  111.9 0.2 announce.6
  112.1 19.0 %all_to_all.48.in_ref = f32[32,8,256]{2,1,0:T(8,128)S(1)} all-to-all(f32[32,8,256]{2,1,0:T(8,128)S(1)} %announce.6), channel_id=1, replica_groups=mesh['plan'=32,'layer'=8] {'plan'}, dimensions={0} | all-to-all | bytes 524288 | tf_op jit(solution)/shard_map/all_to_all | solution.py:251
  131.1 1.1 layer_sums.6
  132.2 9.5 %all_to_all.49.in_ref = f32[8,8,256]{2,1,0:T(8,128)S(1)} all-to-all(f32[8,8,256]{2,1,0:T(8,128)S(1)} %get-tuple-element.70), channel_id=1, replica_groups=mesh['plan'=32,'layer'=8] {'layer'}, dimensions={0} | all-to-all | bytes 131072 | tf_op jit(solution)/shard_map/all_to_all | solution.py:251
  141.7 1.6 advance.5
  143.3 2.2 %collective-permute-start.5 = (f32[8,128]{1,0:T(8,128)S(1)}, f32[8,128]{1,0:T(8,128)S(1)}, u32[]{:S(2)}, u32[]{:S(2)}) collective-permute-start(f32[8,128]{1,0:T(8,128)S(1)} %get-tuple-element.79), channel_id=1, source_target_pairs={{0,1},{1,2},{2,3},{3,4},{4,5},{5,6},{6,7},{8,9},{9,10},{10,11},{11... | collective-permute-start | bytes 12296 | tf_op jit(solution)/shard_map/ppermute | solution.py:256
  145.5 0.0 copy-start.9
  145.5 0.7 copy-done.9
  146.3 0.7 local_sums.7.sums_ref
  146.9 0.2 announce.7
  147.1 18.7 %all_to_all.50.in_ref = f32[32,8,256]{2,1,0:T(8,128)S(1)} all-to-all(f32[32,8,256]{2,1,0:T(8,128)S(1)} %announce.7), channel_id=1, replica_groups=mesh['plan'=32,'layer'=8] {'plan'}, dimensions={0} | all-to-all | bytes 524288 | tf_op jit(solution)/shard_map/all_to_all | solution.py:251
  165.8 1.6 layer_sums.7
  167.4 9.0 %all_to_all.51.in_ref = f32[8,8,256]{2,1,0:T(8,128)S(1)} all-to-all(f32[8,8,256]{2,1,0:T(8,128)S(1)} %get-tuple-element.80), channel_id=1, replica_groups=mesh['plan'=32,'layer'=8] {'layer'}, dimensions={0} | all-to-all | bytes 131072 | tf_op jit(solution)/shard_map/all_to_all | solution.py:251
  176.4 0.8 finish.1
  (25 shorter events, 0.1 us)
Async XLA Ops:
  0.6 31.0 %copy-start.5 = (f32[1,1,8,1024]{3,2,1,0:T(8,128)S(1)}, f32[1,1,8,1024]{3,2,1,0:T(8,128)}, u32[]{:S(2)}) copy-start(f32[1,1,8,1024]{3,2,1,0:T(8,128)} %param.9) | copy-start | bytes 98308
  1.3 0.8 copy-start.6
  2.1 0.7 copy-start.10
  2.8 0.7 copy-start.12
  3.4 0.7 copy-start.14
  4.1 27.6 %copy-start.8 = (f32[1,1,8,1024]{3,2,1,0:T(8,128)S(1)}, f32[1,1,8,1024]{3,2,1,0:T(8,128)}, u32[]{:S(2)}) copy-start(f32[1,1,8,1024]{3,2,1,0:T(8,128)} %param.8) | copy-start | bytes 98308
  4.1 27.6 %copy-start.13 = (s32[1,6]{1,0:T(1,128)S(1)}, s32[1,6]{1,0:T(1,128)}, u32[]{:S(2)}) copy-start(s32[1,6]{1,0:T(1,128)} %partners_ref.11) | copy-start | bytes 76
  5.6 26.0 %all-to-all-start = ((f32[32,16,128]{2,1,0:T(8,128)}), f32[32,16,128]{2,1,0:T(8,128)S(1)}, u32[]{:S(2)}, u32[]{:S(2)}) async-start(f32[32,16,128]{2,1,0:T(8,128)} %get-tuple-element.44), calls=%async_computation | async-start | bytes 524288 | tf_op jit(solution)/shard_map/all_to_all | solution.py:251
  18.2 10.4 %collective-permute-start = (f32[16,128]{1,0:T(8,128)S(1)}, f32[16,128]{1,0:T(8,128)S(1)}, u32[]{:S(2)}, u32[]{:S(2)}) collective-permute-start(f32[16,128]{1,0:T(8,128)S(1)} %get-tuple-element.45), channel_id=1, source_target_pairs={{0,1},{1,2},{2,3},{3,4},{4,5},{5,6},{6,7},{8,9},{9,10},{10,11},{11... | collective-permute-start | bytes 24584 | tf_op jit(solution)/shard_map/ppermute | solution.py:256
  21.4 7.2 %collective-permute-start.1 = (f32[16,128]{1,0:T(8,128)S(1)}, f32[16,128]{1,0:T(8,128)S(1)}, u32[]{:S(2)}, u32[]{:S(2)}) collective-permute-start(f32[16,128]{1,0:T(8,128)S(1)} %get-tuple-element.46), channel_id=1, source_target_pairs={{1,0},{2,1},{3,2},{4,3},{5,4},{6,5},{7,6},{9,8},{10,9},{11,10},{12... | collective-permute-start | bytes 24584 | tf_op jit(solution)/shard_map/ppermute | solution.py:256
  22.7 2.2 %copy-start.4 = (f32[1,1,1024,1024]{3,2,1,0:T(8,128)S(1)}, f32[1,1,1024,1024]{3,2,1,0:T(8,128)}, u32[]{:S(2)}) copy-start(f32[1,1,1024,1024]{3,2,1,0:T(8,128)} %param.7) | copy-start | bytes 12582916
  24.9 0.8 copy-start.7
  26.7 2.0 %copy-start = (bf16[2,1024,1024]{2,1,0:T(8,128)(2,1)}, bf16[2,1024,1024]{2,1,0:T(8,128)(2,1)S(1)}, u32[]{:S(2)}) copy-start(bf16[2,1024,1024]{2,1,0:T(8,128)(2,1)S(1)} %get-tuple-element.51.halves_ref) | copy-start | bytes 12582916
  28.6 43.5 %copy-start.11 = (s32[1,1,1024]{2,1,0:T(1,128)S(1)}, s32[1,1,1024]{2,1,0:T(1,128)}, u32[]{:S(2)}) copy-start(s32[1,1,1024]{2,1,0:T(1,128)} %param.13) | copy-start | bytes 12292
  32.6 6.1 %collective-permute-start.2 = (f32[8,128]{1,0:T(8,128)S(1)}, f32[8,128]{1,0:T(8,128)S(1)}, u32[]{:S(2)}, u32[]{:S(2)}) collective-permute-start(f32[8,128]{1,0:T(8,128)S(1)} %get-tuple-element.53), channel_id=1, source_target_pairs={{0,1},{1,2},{2,3},{3,4},{4,5},{5,6},{6,7},{8,9},{9,10},{10,11},{11... | collective-permute-start | bytes 12296 | tf_op jit(solution)/shard_map/ppermute | solution.py:256
  35.9 2.2 %copy-start.1 = (bf16[2,1024,1024]{2,1,0:T(8,128)(2,1)S(1)}, bf16[2,1024,1024]{2,1,0:T(8,128)(2,1)}, u32[]{:S(2)}) copy-start(bf16[2,1024,1024]{2,1,0:T(8,128)(2,1)} %copy-done) | copy-start | bytes 12582916
  62.4 9.7 %all-to-all-start.2 = ((f32[8,8,256]{2,1,0:T(8,128)}), f32[8,8,256]{2,1,0:T(8,128)S(1)}, u32[]{:S(2)}, u32[]{:S(2)}) async-start(f32[8,8,256]{2,1,0:T(8,128)} %get-tuple-element.54), calls=%async_computation.2 | async-start | bytes 131072 | tf_op jit(solution)/shard_map/all_to_all | solution.py:251
  72.1 2.2 %copy-start.2 = (bf16[2,1024,1024]{2,1,0:T(8,128)(2,1)S(1)}, bf16[2,1024,1024]{2,1,0:T(8,128)(2,1)}, u32[]{:S(2)}) copy-start(bf16[2,1024,1024]{2,1,0:T(8,128)(2,1)} %copy-done) | copy-start | bytes 12582916
  74.3 3.5 %copy-start.3 = (bf16[2,1024,1024]{2,1,0:T(8,128)(2,1)S(1)}, bf16[2,1024,1024]{2,1,0:T(8,128)(2,1)}, u32[]{:S(2)}) copy-start(bf16[2,1024,1024]{2,1,0:T(8,128)(2,1)} %copy-done) | copy-start | bytes 12582916
  75.5 3.0 %collective-permute-start.3 = (f32[8,128]{1,0:T(8,128)S(1)}, f32[8,128]{1,0:T(8,128)S(1)}, u32[]{:S(2)}, u32[]{:S(2)}) collective-permute-start(f32[8,128]{1,0:T(8,128)S(1)} %get-tuple-element.59), channel_id=1, source_target_pairs={{0,1},{1,2},{2,3},{3,4},{4,5},{5,6},{6,7},{8,9},{9,10},{10,11},{11... | collective-permute-start | bytes 12296 | tf_op jit(solution)/shard_map/ppermute | solution.py:256
  109.0 2.9 %collective-permute-start.4 = (f32[8,128]{1,0:T(8,128)S(1)}, f32[8,128]{1,0:T(8,128)S(1)}, u32[]{:S(2)}, u32[]{:S(2)}) collective-permute-start(f32[8,128]{1,0:T(8,128)S(1)} %get-tuple-element.69), channel_id=1, source_target_pairs={{0,1},{1,2},{2,3},{3,4},{4,5},{5,6},{6,7},{8,9},{9,10},{10,11},{11... | collective-permute-start | bytes 12296 | tf_op jit(solution)/shard_map/ppermute | solution.py:256
  143.3 3.6 %collective-permute-start.5 = (f32[8,128]{1,0:T(8,128)S(1)}, f32[8,128]{1,0:T(8,128)S(1)}, u32[]{:S(2)}, u32[]{:S(2)}) collective-permute-start(f32[8,128]{1,0:T(8,128)S(1)} %get-tuple-element.79), channel_id=1, source_target_pairs={{0,1},{1,2},{2,3},{3,4},{4,5},{5,6},{6,7},{8,9},{9,10},{10,11},{11... | collective-permute-start | bytes 12296 | tf_op jit(solution)/shard_map/ppermute | solution.py:256
  145.5 0.8 copy-start.9

commit v3 on v2

--- a/solution.py
+++ b/solution.py
@@ -1,5 +1,3 @@
-import functools
-
 import jax
 import jax.numpy as jnp
 from jax import lax
@@ -13,27 +11,31 @@
 ITERS = 4
 LANES = 128
 JW = 256
+CHUNKS = 4
+NAMES = 16
 SQUARE, CURVATURE = 64, 65
 F32 = jnp.float32
 BF16 = jnp.bfloat16
 
 VMEM = pl.BlockSpec(memory_space=pltpu.VMEM)
 SMEM = pl.BlockSpec(memory_space=pltpu.SMEM)
+HBM = pl.BlockSpec(memory_space=pltpu.HBM)
 
 
 def shape(*dims, dtype=F32):
     return jax.ShapeDtypeStruct(dims, dtype)
 
 
-def call(body, name, outs, specs, limit, flops=0, moved=0):
+def call(body, name, outs, specs, limit, flops=0, traffic=0, scratch=()):
     return pl.pallas_call(
         body,
         name=name,
         out_shape=outs,
         in_specs=specs,
+        scratch_shapes=scratch,
         out_specs=jax.tree.map(lambda _: VMEM, outs),
         compiler_params=pltpu.CompilerParams(vmem_limit_bytes=limit * 2**20),
-        cost_estimate=pl.CostEstimate(flops=flops, bytes_accessed=moved, transcendentals=0),
+        cost_estimate=pl.CostEstimate(flops=flops, bytes_accessed=traffic, transcendentals=0),
     )
 
 
@@ -67,13 +69,12 @@
     return out[:8] + out[8:16] + out[16:24]
 
 
-def arrived(in_ref, partners_ref, wide):
-    height = in_ref.shape[1]
-    place = lax.broadcasted_iota(jnp.int32, (height, LANES), 1) // JR
+def arrived(in_ref, partners_ref):
+    place = lax.broadcasted_iota(jnp.int32, (8, LANES), 1) // JR
     groups = []
     for first in range(0, JW // JR, LANES // JR):
-        total = jnp.zeros((height, LANES), F32)
-        at = first * JR if wide else 0
+        total = jnp.zeros((8, LANES), F32)
+        at = first * JR
         for r in range(first, min(first + LANES // JR, ROUNDS)):
             block = in_ref[partners_ref[0, r], :, at : at + LANES]
             total = jnp.where(place == r - first, block, total)
@@ -81,15 +82,54 @@
     return jnp.concatenate(groups, axis=1)
 
 
-def prepare(x_ref, contact_ref, rows_ref, partners_ref, counts_ref,
-            onehot_ref, valid_ref, own_ref, out_ref, first_ref, last_ref):
+def stream_dense(field, block_ref, rows_ref, sems, keep=None):
+    lhs = jnp.concatenate(pieces(field, 2), axis=0).astype(BF16)
+    depth = rows_ref.shape[0] // CHUNKS
+    total = jnp.zeros((lhs.shape[0], rows_ref.shape[1]), F32)
+    for chunk in range(CHUNKS):
+        at = slice(chunk * depth, (chunk + 1) * depth)
+        chunk_copy(block_ref, rows_ref, sems, chunk).wait()
+        rows = rows_ref[at, :]
+        high = rows.astype(BF16)
+        low = (rows - high.astype(F32)).astype(BF16)
+        if keep is not None:
+            keep[0, at, :] = high
+            keep[1, at, :] = low
+        total = total + jnp.dot(lhs[:, at], high, preferred_element_type=F32)
+        total = total + jnp.dot(lhs[:, at], low, preferred_element_type=F32)
+    return total[:8] + total[8:]
+
+
+def chunk_copy(block_ref, rows_ref, sems, chunk):
+    depth = rows_ref.shape[0] // CHUNKS
+    at = pl.ds(chunk * depth, depth)
+    return pltpu.make_async_copy(block_ref.at[at, :], rows_ref.at[at, :], sems.at[chunk])
+
+
+def prepare(block_ref, x_hbm, load_hbm, contact_hbm, rows_hbm, partners_hbm, counts_hbm,
+            onehot_ref, valid_ref, own_ref, hown_ref, h_ref, out_ref, first_ref, last_ref,
+            held_ref, x_ref, load_ref, contact_ref, rows_ref, partners_ref, counts_ref, sems, more_sems):
+    small = [
+        pltpu.make_async_copy(source, target, more_sems.at[i])
+        for i, (source, target) in enumerate((
+            (rows_hbm, rows_ref), (counts_hbm, counts_ref), (x_hbm, x_ref),
+            (contact_hbm, contact_ref), (partners_hbm, partners_ref), (load_hbm, load_ref),
+        ))
+    ]
+    for copy in small:
+        copy.start()
+    for chunk in range(CHUNKS):
+        chunk_copy(block_ref, held_ref, sems, chunk).start()
+    for copy in small:
+        copy.wait()
     x = x_ref[...]
+    width = x.shape[1]
     rows = jnp.concatenate(
         [rows_ref[r : r + 1, :] for r in range(ROUNDS)]
         + [jnp.full((1, JW - ROUNDS * JR), -1, jnp.int32)],
         axis=1,
     )
-    hit = lax.broadcasted_iota(jnp.int32, (x.shape[1], JW), 0) == rows
+    hit = lax.broadcasted_iota(jnp.int32, (width, JW), 0) == rows
     onehot = jnp.where(hit, 1.0, 0.0).astype(BF16)
     onehot_ref[...] = onehot
     lane = lax.broadcasted_iota(jnp.int32, (8, JW), 1)
@@ -101,32 +141,26 @@
     contact = jnp.broadcast_to(jnp.where(contact_ref[...] == 1, 1.0, 0.0), x.shape)
     own, own_contact = pick(x, onehot, contact)
     own_ref[...] = jnp.concatenate([own, own_contact], axis=0)
-    short = lax.broadcasted_iota(jnp.int32, (8, LANES), 1)
-    names = jnp.zeros((8, LANES), jnp.int32)
+    position = lax.broadcasted_iota(jnp.int32, x.shape, 1)
+    edge = (position < FACE) | (position >= width - FACE)
+    h = spread(valid * own, onehot) + jnp.where(edge, x, 0.0) - load_ref[...]
+    h = h + stream_dense(x, block_ref, held_ref, sems)
+    h_ref[...] = h
+    (hown,) = pick(h, onehot)
+    hown_ref[...] = hown
+    out_ref[...] = jnp.zeros_like(out_ref)
+    place = lax.broadcasted_iota(jnp.int32, (8, LANES), 1) // JR
     for r in range(ROUNDS):
-        names = jnp.where(short == r, partners_ref[0, r], names)
-    names = names.astype(F32)
-    row = lax.broadcasted_iota(jnp.int32, (8, LANES), 0)
-    out_ref[...] = jnp.broadcast_to(
-        jnp.concatenate([jnp.zeros((8, LANES), F32), names], axis=0)[None], out_ref.shape
-    )
-    for r in range(ROUNDS):
-        group = (r * JR) // LANES
+        group, slot = divmod(r * JR, LANES)
         at = slice(group * LANES, (group + 1) * LANES)
-        low = jnp.where(row == 7, names, own_contact[:, at])
-        out_ref[pl.ds(partners_ref[0, r], 1)] = jnp.concatenate([own[:, at], low], axis=0)[None]
-    both = jnp.concatenate([x, contact], axis=0)
+        parcel = jnp.zeros((8, LANES), F32)
+        for i, jump in enumerate((own, hown, own_contact)):
+            block = pltpu.roll(jump[:, at], (i * JR) % LANES, 1) if i else jump[:, at]
+            parcel = jnp.where(place == (slot // JR + i) % (LANES // JR), block, parcel)
+        out_ref[partners_ref[0, r]] = parcel
+    both = jnp.concatenate([x, h, contact], axis=0)
     first_ref[...] = both[:, :FACE]
-    last_ref[...] = both[:, x.shape[1] - FACE :]
-
-
-def split_dense(block_ref, x_ref, halves_ref, image_ref):
-    block = block_ref[...]
-    high = block.astype(BF16)
-    low = (block - high.astype(F32)).astype(BF16)
-    halves_ref[0] = high
-    halves_ref[1] = low
-    image_ref[...] = dense(x_ref[...], high, low)
+    last_ref[...] = both[:, width - FACE :]
 
 
 def with_coupling(image, x, load, own, far, below, above, valid, onehot):
@@ -137,25 +171,65 @@
     return jnp.concatenate([head, total[:, FACE : width - FACE], tail], axis=1)
 
 
+def lane_sum(value):
+    return jnp.sum(value, axis=1, keepdims=True)
+
+
+def first_gradient(partners_ref, layer_ref, block_ref, x_ref, h_ref, own_ref, hown_ref, in_ref,
+                   below_in, above_in, valid_ref, onehot_ref,
+                   g_ref, gown_ref, far_ref, gfar_ref, below_ref, gbelow_ref, above_ref, gabove_ref,
+                   halves_ref, all_ref, held_ref, sems):
+    for chunk in range(CHUNKS):
+        chunk_copy(block_ref, held_ref, sems, chunk).start()
+    width = x_ref.shape[1]
+    place = lax.broadcasted_iota(jnp.int32, (8, LANES), 1) // JR
+    parts = [[jnp.zeros((8, LANES), F32)] * 2 for _ in range(3)]
+    for r in range(ROUNDS):
+        group, slot = divmod(r * JR, LANES)
+        parcel = in_ref[partners_ref[0, r]]
+        for i in range(3):
+            block = pltpu.roll(parcel, LANES - i * JR, 1) if i else parcel
+            parts[i][group] = jnp.where(place == slot // JR, block, parts[i][group])
+    far, hfar, far_contact = (jnp.concatenate(part, axis=1) for part in parts)
+    valid = valid_ref[...]
+    own = own_ref[:8]
+    far_ref[...] = jnp.concatenate([far, far_contact], axis=0)
+    gown = hown_ref[...] - valid * far
+    gfar = hfar - valid * own
+    gown_ref[...] = gown
+    gfar_ref[...] = gfar
+    below, above = below_in[...], above_in[...]
+    below_ref[...] = jnp.concatenate([below[:8], below[16:]], axis=0)
+    above_ref[...] = jnp.concatenate([above[:8], above[16:]], axis=0)
+    layer = layer_ref[0, 0]
+    gbelow = jnp.where(layer > 0, below[8:16] - x_ref[:, :FACE], 0.0)
+    gabove = jnp.where(layer < layer_ref[0, 1] - 1, above[8:16] - x_ref[:, width - FACE :], 0.0)
+    gbelow_ref[...] = gbelow
+    gabove_ref[...] = gabove
+    h = h_ref[...] - spread(valid * far, onehot_ref[...])
+    first = h[:, :FACE] - below[:8]
+    last = h[:, width - FACE :] - above[:8]
+    g = jnp.concatenate([first, h[:, FACE : width - FACE], last], axis=1)
+    g_ref[...] = g
+    jumps = valid * gown * (gown - gfar)
+    terms = first * (first - gbelow) + last * (last - gabove) + jumps[:, :LANES] + jumps[:, LANES:]
+    square = lane_sum(g * g)
+    curvature = lane_sum(terms) + lane_sum(g * stream_dense(g, block_ref, held_ref, sems, halves_ref))
+    lane = lax.broadcasted_iota(jnp.int32, (8, LANES), 1)
+    row = lax.broadcasted_iota(jnp.int32, (8, LANES), 0)
+    line = jnp.where(lane == row, square, 0.0) + jnp.where(lane == row + 8, curvature, 0.0)
+    line = jnp.sum(line, axis=0, keepdims=True)
+    short = lax.broadcasted_iota(jnp.int32, (1, LANES), 1)
+    for r in range(ROUNDS):
+        name = jnp.full((1, LANES), partners_ref[0, r], jnp.int32).astype(F32)
+        line = jnp.where(short == NAMES + r, name, line)
+    all_ref[...] = jnp.broadcast_to(line, all_ref.shape)
+
+
 def give_gradient(gradient, onehot, g_ref, gown_ref, last_ref):
     g_ref[...] = gradient
     last_ref[...] = gradient[:, gradient.shape[1] - FACE :]
     gown_ref[...] = pick(gradient, onehot)[0]
-
-
-def first_gradient(partners_ref, image_ref, x_ref, load_ref, own_ref, in_ref, below_ref, above_ref,
-                   valid_ref, onehot_ref, g_ref, gown_ref, last_ref, far_ref, table_ref):
-    far = arrived(in_ref, partners_ref, False)
-    flags = jnp.broadcast_to(far[8:9], far[8:].shape)
-    far_ref[...] = jnp.concatenate([far[:8], flags], axis=0)
-    for p in range(table_ref.shape[0]):
-        table_ref[p : p + 1, :] = in_ref[p, 15:16, :8].astype(jnp.int32)
-    onehot = onehot_ref[...]
-    gradient = with_coupling(
-        image_ref[...], x_ref[...], load_ref[...], own_ref[:8], far[:8], below_ref[:8],
-        above_ref[:8], valid_ref[...], onehot,
-    )
-    give_gradient(gradient, onehot, g_ref, gown_ref, last_ref)
 
 
 def local_sums(g_ref, halves_ref, sums_ref):
@@ -183,7 +257,7 @@
 
 
 def layer_sums(partners_ref, table_ref, in_ref, g_ref, gfar_ref, out_ref):
-    gfar_ref[...] = arrived(in_ref, partners_ref, True)
+    gfar_ref[...] = arrived(in_ref, partners_ref)
     place = lax.broadcasted_iota(jnp.int32, (8, LANES), 1) // JR
     nothing = jnp.zeros((8, LANES), F32)
     products, sums = [nothing, nothing], nothing
@@ -217,17 +291,39 @@
     return jnp.where(contact == 1, jnp.maximum(out, 0.0), out)
 
 
-def advance(layer_ref, in_ref, x_ref, g_ref, contact_ref, load_ref,
-            own_ref, gown_ref, far_ref, gfar_ref, below_ref, gbelow_ref, above_ref,
-            valid_ref, onehot_ref, halves_ref,
-            g_out, gown_out, last_out, x_out, own_out, far_out, below_out, above_out):
-    step = step_of(in_ref)
-    x = moved(x_ref[...], g_ref[...], step, contact_ref[...])
-    x_out[...] = x
+def first_step(in_ref):
+    line = jnp.sum(in_ref[...], axis=0, keepdims=True)
+    line = jnp.broadcast_to(line, (8, LANES))
+    lane = lax.broadcasted_iota(jnp.int32, (8, LANES), 1)
+    row = lax.broadcasted_iota(jnp.int32, (8, LANES), 0)
+    square = lane_sum(jnp.where(lane == row, line, 0.0))
+    curvature = lane_sum(jnp.where(lane == row + 8, line, 0.0))
+    return (square + 1e-6) / (curvature + 1e-6)
+
+
+def first_advance(in_ref, *refs):
+    *refs, table_ref = refs
+    plans = table_ref.shape[0]
+    lines = in_ref[pl.ds(0, plans, stride=in_ref.shape[0] // plans), :]
+    table_ref[...] = pltpu.roll(lines, LANES - NAMES, 1)[:, :8].astype(jnp.int32)
+    gabove_ref, *refs = refs
+    advance_by(first_step(in_ref), gabove_ref[...], *refs)
+
+
+def advance(layer_ref, in_ref, *refs):
     layers = in_ref.shape[0]
     layer = layer_ref[0, 0]
     gabove = in_ref[jnp.minimum(layer + 1, layers - 1), :, :FACE]
     gabove = jnp.where(layer < layers - 1, gabove, 0.0)
+    advance_by(step_of(in_ref), gabove, *refs)
+
+
+def advance_by(step, gabove, x_ref, g_ref, contact_ref, load_ref,
+               own_ref, gown_ref, far_ref, gfar_ref, below_ref, gbelow_ref, above_ref,
+               valid_ref, onehot_ref, halves_ref,
+               g_out, gown_out, last_out, x_out, own_out, far_out, below_out, above_out):
+    x = moved(x_ref[...], g_ref[...], step, contact_ref[...])
+    x_out[...] = x
     halo = []
     for held_ref, slope, held_out in (
         (own_ref, gown_ref[...], own_out), (far_ref, gfar_ref[...], far_out),
@@ -264,27 +360,41 @@
     loads, width = x.shape
     plans, layers = lax.axis_size("plan"), lax.axis_size("layer")
     field, jump, face = shape(loads, width), shape(loads, JW), shape(loads, FACE)
-    jump2, face2 = shape(2 * loads, JW), shape(2 * loads, FACE)
-    halves_shape = shape(2, width, width, dtype=BF16)
+    jump2, face2, face3 = shape(2 * loads, JW), shape(2 * loads, FACE), shape(3 * loads, FACE)
     flops = 4 * 16 * width * width
-    layer = lax.axis_index("layer").astype(jnp.int32).reshape(1, 1)
-
-    onehot, valid, own, out, first, last = call(
+    layer = jnp.stack([lax.axis_index("layer"), layers]).astype(jnp.int32).reshape(1, 2)
+    held = pltpu.VMEM((width, width), F32)
+    chunk_sems = pltpu.SemaphoreType.DMA((CHUNKS,))
+
+    onehot, valid, own, hown, h, out, first, last = call(
         prepare, "prepare",
-        (shape(width, JW, dtype=BF16), jump, jump2, shape(plans, 2 * loads, LANES), face2, face2),
-        [VMEM, VMEM, VMEM, SMEM, SMEM], 8,
-    )(x, flags, rows, partners, amounts)
+        (shape(width, JW, dtype=BF16), jump, jump2, jump, field, shape(plans, loads, LANES), face3, face3),
+        [HBM] * 7, 53, flops, 4 * width * width,
+        [
+            held, pltpu.VMEM(x.shape, F32), pltpu.VMEM(target.shape, F32),
+            pltpu.VMEM(flags.shape, jnp.int32), pltpu.VMEM(rows.shape, jnp.int32),
+            pltpu.SMEM(partners.shape, jnp.int32), pltpu.SMEM(amounts.shape, jnp.int32),
+            chunk_sems, pltpu.SemaphoreType.DMA((6,)),
+        ],
+    )(block, x, target, flags, rows, partners, amounts)
     incoming = swap(out, "plan")
     below, above = lift(last, 1), lift(first, -1)
-    halves, image = call(
-        split_dense, "split_dense", (halves_shape, field), [VMEM, VMEM], 20, flops, 12 * width * width,
-    )(block, x)
-    g, gown, last, far, table = call(
+    g, gown, far, gfar, below, gbelow, above, gabove, halves, out = call(
         first_gradient, "first_gradient",
-        (field, jump, face, jump2, shape(plans, 8, dtype=jnp.int32)), [SMEM] + [VMEM] * 9, 8,
-    )(partners, image, x, target, own, incoming, below, above, valid, onehot)
-
-    for iteration in range(ITERS):
+        (field, jump, jump2, jump, face2, face, face2, face,
+         shape(2, width, width, dtype=BF16), shape(plans * layers, LANES)),
+        [SMEM] * 2 + [HBM] + [VMEM] * 9, 48, flops, 4 * width * width, [held, chunk_sems],
+    )(partners, layer, block, x, h, own, hown, incoming, below, above, valid, onehot)
+    incoming = swap(out, ("plan", "layer"))
+
+    after = (field, jump, face, field, jump2, jump2, face2, face2)
+    g, gown, last, x, own, far, below, above, table = call(
+        first_advance, "first_advance", after + (shape(plans, 8, dtype=jnp.int32),),
+        [VMEM] * 16, 12, flops, 4 * width * width,
+    )(incoming, gabove, x, g, flags, target, own, gown, far, gfar, below, gbelow, above,
+      valid, onehot, halves)
+
+    for iteration in range(1, ITERS):
         gbelow = lift(last, 1)
         sums = call(
             local_sums, "local_sums", face, [VMEM] * 2, 12, flops, 4 * width * width,
@@ -301,8 +411,7 @@
             x = call(finish, "finish", field, [VMEM] * 4, 8)(incoming, x, g, flags)
             break
         g, gown, last, x, own, far, below, above = call(
-            advance, "advance", (field, jump, face, field, jump2, jump2, face2, face2),
-            [SMEM] + [VMEM] * 15, 12, flops, 4 * width * width,
+            advance, "advance", after, [SMEM] + [VMEM] * 15, 12, flops, 4 * width * width,
         )(layer, incoming, x, g, flags, target, own, gown, far, gfar, below, gbelow, above,
           valid, onehot, halves)
     return x[None, None], g[None, None]

time: 178 us -> 164 us (0.921)
  local copies, waits for them, and re-layouts: 13.5 us -> 4.97 us
  starting transfers between devices: 31.5 us -> 23.7 us
  blocking collectives: 106 us -> 109 us
  waiting for transfers between devices: 8.23 us -> 6.41 us
  Pallas kernels: 17.1 us -> 18.9 us
    unnamed x31 -> x21, local copies, waits for them, and re-layouts: 13.5 us -> 4.97 us
    all_to_all x2 -> x1, waiting for transfers between devices: 8.21 us -> 3.05 us  [swap(): lax.all_to_all(outgoing, axis, split_axis=0, concat_axis=0, tiled=True)]
    all_to_all x2 -> x1, starting transfers between devices: 17.1 us -> 12.6 us  [swap(): lax.all_to_all(outgoing, axis, split_axis=0, concat_axis=0, tiled=True)]
    pallas_call x6 -> x5, Pallas kernels: 7.41 us -> 11.8 us  [the longest x2 3.85 us: shards(): call(advance, 'advance', after, [SMEM] + [VMEM] * 15, 12, flops, 4 * widt...]
    ppermute x6 -> x5, starting transfers between devices: 14.4 us -> 11.1 us  [lift(): lax.ppermute(face, 'layer', [(i, i + step) for i in range(layers) if 0 <=...]
    ppermute x6 -> x5, waiting for transfers between devices: 0.02 us -> 3.36 us  [lift(): lax.ppermute(face, 'layer', [(i, i + step) for i in range(layers) if 0 <=...]
    all_to_all x7, blocking collectives: 106 us -> 109 us  [swap(): lax.all_to_all(outgoing, axis, split_axis=0, concat_axis=0, tiled=True)]
    pallas_call x4 -> x3, Pallas kernels: 5.61 us -> 3.88 us  [shards(): call(layer_sums, 'layer_sums', (jump, shape(layers, loads, FACE + LANES))...]
  transfers between devices with their start and end apart: 8 -> 6, of which waited for: 2 -> 2; matrix products, arithmetic and copies ran while one was open for 0% -> 0% of each run, Pallas kernels for 2% -> 1%
where the time goes in v3:
time: 164 us; the launch traced here: 163 us
  blocking collectives  109 us (66%)
  starting transfers between devices  23.7 us (14%)
  Pallas kernels  18.9 us (12%)
  waiting for transfers between devices  6.41 us (4%)
  local copies, waits for them, and re-layouts  4.97 us (3%)
    all_to_all x7, blocking collectives, swap(): lax.all_to_all(outgoing, axis, split_axis=0, concat_axis=0, tiled=True)  109 us
    all_to_all x1, starting transfers between devices, swap(): lax.all_to_all(outgoing, axis, split_axis=0, concat_axis=0, tiled=True)  12.6 us
    ppermute x5, starting transfers between devices, lift(): lax.ppermute(face, 'layer', [(i, i + step) for i in range(layers) if 0 <=...  11.1 us
    unnamed x21, local copies, waits for them, and re-layouts  4.97 us
    pallas_call x3, Pallas kernels, shards(): call(layer_sums, 'layer_sums', (jump, shape(layers, loads, FACE + LANES))...  3.88 us
    pallas_call x2, Pallas kernels, shards(): call(advance, 'advance', after, [SMEM] + [VMEM] * 15, 12, flops, 4 * widt...  3.85 us
    pallas_call x1, Pallas kernels, shards(): call(prepare, 'prepare', (shape(width, JW, dtype=BF16), jump, jump2, jump...  3.51 us
    ppermute x5, waiting for transfers between devices, lift(): lax.ppermute(face, 'layer', [(i, i + step) for i in range(layers) if 0 <=...  3.36 us
  transfers between devices with their start and end apart: 6, of which 2 were waited for; matrix products, arithmetic and copies ran while one was open for 0% of the time, Pallas kernels for 1%

profile of v3, /device:TPU:1, one launch (start us, length us, event | category | flops | bytes accessed | tf_op | source)
XLA Modules:
  0.0 163.5 jit_solution(15726489146400155922)
XLA Ops:
  0.6 0.0 copy-start.8
  0.6 0.7 copy.12
  1.3 0.8 copy-done
  2.1 0.8 copy-done.3
  2.9 0.7 copy-done.5
  3.5 0.7 copy-done.7
  4.2 0.7 copy-done.9
  4.9 3.5 %prepare.1 = (bf16[1024,256]{1,0:T(8,128)(2,1)S(1)}, f32[8,256]{1,0:T(8,128)S(1)}, f32[16,256]{1,0:T(8,128)S(1)}, f32[8,256]{1,0:T(8,128)S(1)}, f32[8,1024]{1,0:...) custom-call(f32[1024,1024]{1,0:T(8,128)} %bitcast.34, f32[8,1024]{1,0:T(8,128)S(1)} %bitcast.23, ...), custom_call_target="tpu_custom_call" | custom-call | flops 67108864 | bytes 4194304 | tf_op jit(solution)/shard_map/prepare/pallas_call | solution.py:369
  8.4 12.6 %all-to-all-start = ((f32[32,8,128]{2,1,0:T(8,128)}), f32[32,8,128]{2,1,0:T(8,128)S(1)}, u32[]{:S(2)}, u32[]{:S(2)}) async-start(f32[32,8,128]{2,1,0:T(8,128)} %get-tuple-element.49), calls=%async_computation | async-start | bytes 262144 | tf_op jit(solution)/shard_map/all_to_all | solution.py:347
  21.0 3.2 %collective-permute-start = (f32[24,128]{1,0:T(8,128)S(1)}, f32[24,128]{1,0:T(8,128)S(1)}, u32[]{:S(2)}, u32[]{:S(2)}) collective-permute-start(f32[24,128]{1,0:T(8,128)S(1)} %get-tuple-element.50), channel_id=1, source_target_pairs={{0,1},{1,2},{2,3},{3,4},{4,5},{5,6},{6,7},{8,9},{9,10},{10,11},{11... | collective-permute-start | bytes 36872 | tf_op jit(solution)/shard_map/ppermute | solution.py:352
  24.2 1.3 collective-permute-start.1
  25.5 0.1 add_bitcast_fusion.layer_ref
  25.6 0.0 collective-permute-done.below_in
  25.6 3.4 %collective-permute-done.1.above_in = f32[24,128]{1,0:T(8,128)S(1)} collective-permute-done((f32[24,128]{1,0:T(8,128)S(1)}, f32[24,128]{1,0:T(8,128)S(1)}, u32[]{:S(2)}, u32[]{:S(2)}) %collective-permute-start.1) | collective-permute-done | bytes 12320 | tf_op jit(solution)/shard_map/ppermute | solution.py:352
  28.9 3.1 %all-to-all-done.in_ref = f32[32,8,128]{2,1,0:T(8,128)S(1)} async-done(((f32[32,8,128]{2,1,0:T(8,128)}), f32[32,8,128]{2,1,0:T(8,128)S(1)}, u32[]{:S(2)}, u32[]{:S(2)}) %all-to-all-start) | async-done | bytes 131104 | tf_op jit(solution)/shard_map/all_to_all | solution.py:347
  32.0 0.0 copy-done.8
  32.0 0.0 copy-done.4
  32.0 3.3 %first_gradient.1 = (f32[8,1024]{1,0:T(8,128)S(1)}, f32[8,256]{1,0:T(8,128)S(1)}, f32[16,256]{1,0:T(8,128)S(1)}, f32[8,256]{1,0:T(8,128)S(1)}, f32[16,128]{1,0:T...) custom-call(s32[1,6]{1,0:T(1,128)S(1)} %copy-done.8, ...), custom_call_target="tpu_custom_call" | custom-call | flops 67108864 | bytes 4194304 | tf_op jit(solution)/shard_map/first_gradient/pallas_call | solution.py:382
  35.3 24.4 %all_to_all.46 = f32[256,1,128]{2,1,0:T(1,128)S(1)} all-to-all(f32[256,1,128]{2,1,0:T(1,128)S(1)} %bitcast.26), channel_id=1, replica_groups=mesh['plan'=32,'layer'=8] {'plan','layer'}, dimensions={0} | all-to-all | bytes 262144 | tf_op jit(solution)/shard_map/all_to_all | solution.py:347
  59.7 0.0 copy-done.1
  59.7 0.0 copy-done.6
  59.7 1.1 first_advance.1
  60.9 2.2 %collective-permute-start.2 = (f32[8,128]{1,0:T(8,128)S(1)}, f32[8,128]{1,0:T(8,128)S(1)}, u32[]{:S(2)}, u32[]{:S(2)}) collective-permute-start(f32[8,128]{1,0:T(8,128)S(1)} %get-tuple-element.67), channel_id=1, source_target_pairs={{0,1},{1,2},{2,3},{3,4},{4,5},{5,6},{6,7},{8,9},{9,10},{10,11},{11... | collective-permute-start | bytes 12296 | tf_op jit(solution)/shard_map/ppermute | solution.py:352
  63.1 0.7 local_sums.3.sums_ref
  63.7 0.0 collective-permute-done.2.below_ref.refs_9_
  63.7 0.2 announce.3
  63.9 17.8 %all_to_all.47.in_ref = f32[32,8,256]{2,1,0:T(8,128)S(1)} all-to-all(f32[32,8,256]{2,1,0:T(8,128)S(1)} %announce.3), channel_id=1, replica_groups=mesh['plan'=32,'layer'=8] {'plan'}, dimensions={0} | all-to-all | bytes 524288 | tf_op jit(solution)/shard_map/all_to_all | solution.py:347
  81.7 1.1 layer_sums.3
  82.8 10.4 %all_to_all.48.in_ref = f32[8,8,256]{2,1,0:T(8,128)S(1)} all-to-all(f32[8,8,256]{2,1,0:T(8,128)S(1)} %get-tuple-element.68), channel_id=1, replica_groups=mesh['plan'=32,'layer'=8] {'layer'}, dimensions={0} | all-to-all | bytes 131072 | tf_op jit(solution)/shard_map/all_to_all | solution.py:347
  93.2 1.7 %advance.2 = (f32[8,1024]{1,0:T(8,128)S(1)}, f32[8,256]{1,0:T(8,128)S(1)}, f32[8,128]{1,0:T(8,128)S(1)}, f32[8,1024]{1,0:T(8,128)S(1)}, f32[16,256]{1,0:T(8,128)...) custom-call(s32[1,2]{1,0:T(1,128)S(1)} %add_bitcast_fusion.layer_ref, ...), custom_call_target="tpu_custom_call" | custom-call | flops 67108864 | bytes 4194304 | tf_op jit(solution)/shard_map/advance/pallas_call | solution.py:413
  94.9 2.2 %collective-permute-start.3 = (f32[8,128]{1,0:T(8,128)S(1)}, f32[8,128]{1,0:T(8,128)S(1)}, u32[]{:S(2)}, u32[]{:S(2)}) collective-permute-start(f32[8,128]{1,0:T(8,128)S(1)} %get-tuple-element.77), channel_id=1, source_target_pairs={{0,1},{1,2},{2,3},{3,4},{4,5},{5,6},{6,7},{8,9},{9,10},{10,11},{11... | collective-permute-start | bytes 12296 | tf_op jit(solution)/shard_map/ppermute | solution.py:352
  97.1 0.7 local_sums.4.sums_ref
  97.8 0.0 collective-permute-done.3.below_ref.refs_9_
  97.8 0.2 announce.4
  97.9 18.9 %all_to_all.49.in_ref = f32[32,8,256]{2,1,0:T(8,128)S(1)} all-to-all(f32[32,8,256]{2,1,0:T(8,128)S(1)} %announce.4), channel_id=1, replica_groups=mesh['plan'=32,'layer'=8] {'plan'}, dimensions={0} | all-to-all | bytes 524288 | tf_op jit(solution)/shard_map/all_to_all | solution.py:347
  116.8 1.1 layer_sums.4
  117.9 9.5 %all_to_all.50.in_ref = f32[8,8,256]{2,1,0:T(8,128)S(1)} all-to-all(f32[8,8,256]{2,1,0:T(8,128)S(1)} %get-tuple-element.78), channel_id=1, replica_groups=mesh['plan'=32,'layer'=8] {'layer'}, dimensions={0} | all-to-all | bytes 131072 | tf_op jit(solution)/shard_map/all_to_all | solution.py:347
  127.4 2.2 %advance.3 = (f32[8,1024]{1,0:T(8,128)}, f32[8,256]{1,0:T(8,128)S(1)}, f32[8,128]{1,0:T(8,128)S(1)}, f32[8,1024]{1,0:T(8,128)S(1)}, f32[16,256]{1,0:T(8,128)}, /...) custom-call(s32[1,2]{1,0:T(1,128)S(1)} %add_bitcast_fusion.layer_ref, f32[8,8,256]{2,1,0:T(8,128)S(1)} %all_to_all.50.in_ref, ...), custom_call_target="tpu_custom_call" | custom-call | flops 67108864 | bytes 4194304 | tf_op jit(solution)/shard_map/advance/pallas_call | solution.py:413
  129.6 2.2 %collective-permute-start.4 = (f32[8,128]{1,0:T(8,128)S(1)}, f32[8,128]{1,0:T(8,128)S(1)}, u32[]{:S(2)}, u32[]{:S(2)}) collective-permute-start(f32[8,128]{1,0:T(8,128)S(1)} %get-tuple-element.87), channel_id=1, source_target_pairs={{0,1},{1,2},{2,3},{3,4},{4,5},{5,6},{6,7},{8,9},{9,10},{10,11},{11... | collective-permute-start | bytes 12296 | tf_op jit(solution)/shard_map/ppermute | solution.py:352
  131.8 0.0 copy-start.2
  131.8 0.7 copy-done.2
  132.5 0.7 local_sums.5.sums_ref
  133.2 0.0 collective-permute-done.4.below_ref
  133.2 0.2 announce.5
  133.4 18.7 %all_to_all.51.in_ref = f32[32,8,256]{2,1,0:T(8,128)S(1)} all-to-all(f32[32,8,256]{2,1,0:T(8,128)S(1)} %announce.5), channel_id=1, replica_groups=mesh['plan'=32,'layer'=8] {'plan'}, dimensions={0} | all-to-all | bytes 524288 | tf_op jit(solution)/shard_map/all_to_all | solution.py:347
  152.0 1.6 %layer_sums.5 = (f32[8,256]{1,0:T(8,128)}, f32[8,8,256]{2,1,0:T(8,128)S(1)}) custom-call(s32[1,6]{1,0:T(1,128)S(1)} %copy-done.8, s32[32,8]{1,0:T(8,128)S(1)} %get-tuple-element.64.table_ref, f32[32,8,256]{2,1,0:T(8,128)S(1)} %all_to_all.51.in_ref, f32[8,1024]{1,0:T(8,128)S(1)} %copy-done.2), custom_call_target="tpu_custom_call" | custom-call | tf_op jit(solution)/shard_map/layer_sums/pallas_call | solution.py:405
  153.7 9.0 %all_to_all.52.in_ref = f32[8,8,256]{2,1,0:T(8,128)S(1)} all-to-all(f32[8,8,256]{2,1,0:T(8,128)S(1)} %get-tuple-element.88), channel_id=1, replica_groups=mesh['plan'=32,'layer'=8] {'layer'}, dimensions={0} | all-to-all | bytes 131072 | tf_op jit(solution)/shard_map/all_to_all | solution.py:347
  162.7 0.8 finish.1
  (8 shorter events, 0.0 us)
Async XLA Ops:
  0.6 31.3 %copy-start.8 = (s32[1,6]{1,0:T(1,128)S(1)}, s32[1,6]{1,0:T(1,128)}, u32[]{:S(2)}) copy-start(s32[1,6]{1,0:T(1,128)} %partners_ref.7) | copy-start | bytes 76
  1.3 0.8 copy-start
  2.1 0.8 copy-start.3
  2.9 0.7 copy-start.5
  3.5 0.7 copy-start.7
  4.2 0.7 copy-start.9
  4.8 27.1 %copy-start.4 = (f32[1,1,8,1024]{3,2,1,0:T(8,128)S(1)}, f32[1,1,8,1024]{3,2,1,0:T(8,128)}, u32[]{:S(2)}) copy-start(f32[1,1,8,1024]{3,2,1,0:T(8,128)} %param.8) | copy-start | bytes 98308
  4.9 54.9 %copy-start.1 = (f32[1,1,8,1024]{3,2,1,0:T(8,128)S(1)}, f32[1,1,8,1024]{3,2,1,0:T(8,128)}, u32[]{:S(2)}) copy-start(f32[1,1,8,1024]{3,2,1,0:T(8,128)} %param.9) | copy-start | bytes 98308
  4.9 54.9 %copy-start.6 = (s32[1,1,1024]{2,1,0:T(1,128)S(1)}, s32[1,1,1024]{2,1,0:T(1,128)}, u32[]{:S(2)}) copy-start(s32[1,1,1024]{2,1,0:T(1,128)} %param.13) | copy-start | bytes 12292
  8.4 23.6 %all-to-all-start = ((f32[32,8,128]{2,1,0:T(8,128)}), f32[32,8,128]{2,1,0:T(8,128)S(1)}, u32[]{:S(2)}, u32[]{:S(2)}) async-start(f32[32,8,128]{2,1,0:T(8,128)} %get-tuple-element.49), calls=%async_computation | async-start | bytes 262144 | tf_op jit(solution)/shard_map/all_to_all | solution.py:347
  21.0 4.6 %collective-permute-start = (f32[24,128]{1,0:T(8,128)S(1)}, f32[24,128]{1,0:T(8,128)S(1)}, u32[]{:S(2)}, u32[]{:S(2)}) collective-permute-start(f32[24,128]{1,0:T(8,128)S(1)} %get-tuple-element.50), channel_id=1, source_target_pairs={{0,1},{1,2},{2,3},{3,4},{4,5},{5,6},{6,7},{8,9},{9,10},{10,11},{11... | collective-permute-start | bytes 36872 | tf_op jit(solution)/shard_map/ppermute | solution.py:352
  24.2 4.7 %collective-permute-start.1 = (f32[24,128]{1,0:T(8,128)S(1)}, f32[24,128]{1,0:T(8,128)S(1)}, u32[]{:S(2)}, u32[]{:S(2)}) collective-permute-start(f32[24,128]{1,0:T(8,128)S(1)} %get-tuple-element.51), channel_id=1, source_target_pairs={{1,0},{2,1},{3,2},{4,3},{5,4},{6,5},{7,6},{9,8},{10,9},{11,10},{12... | collective-permute-start | bytes 36872 | tf_op jit(solution)/shard_map/ppermute | solution.py:352
  60.9 2.9 %collective-permute-start.2 = (f32[8,128]{1,0:T(8,128)S(1)}, f32[8,128]{1,0:T(8,128)S(1)}, u32[]{:S(2)}, u32[]{:S(2)}) collective-permute-start(f32[8,128]{1,0:T(8,128)S(1)} %get-tuple-element.67), channel_id=1, source_target_pairs={{0,1},{1,2},{2,3},{3,4},{4,5},{5,6},{6,7},{8,9},{9,10},{10,11},{11... | collective-permute-start | bytes 12296 | tf_op jit(solution)/shard_map/ppermute | solution.py:352
  94.9 2.9 %collective-permute-start.3 = (f32[8,128]{1,0:T(8,128)S(1)}, f32[8,128]{1,0:T(8,128)S(1)}, u32[]{:S(2)}, u32[]{:S(2)}) collective-permute-start(f32[8,128]{1,0:T(8,128)S(1)} %get-tuple-element.77), channel_id=1, source_target_pairs={{0,1},{1,2},{2,3},{3,4},{4,5},{5,6},{6,7},{8,9},{9,10},{10,11},{11... | collective-permute-start | bytes 12296 | tf_op jit(solution)/shard_map/ppermute | solution.py:352
  129.6 3.6 %collective-permute-start.4 = (f32[8,128]{1,0:T(8,128)S(1)}, f32[8,128]{1,0:T(8,128)S(1)}, u32[]{:S(2)}, u32[]{:S(2)}) collective-permute-start(f32[8,128]{1,0:T(8,128)S(1)} %get-tuple-element.87), channel_id=1, source_target_pairs={{0,1},{1,2},{2,3},{3,4},{4,5},{5,6},{6,7},{8,9},{9,10},{10,11},{11... | collective-permute-start | bytes 12296 | tf_op jit(solution)/shard_map/ppermute | solution.py:352
  131.8 0.8 copy-start.2

commit v4 on v3

--- a/solution.py
+++ b/solution.py
@@ -82,7 +82,7 @@
     return jnp.concatenate(groups, axis=1)
 
 
-def stream_dense(field, block_ref, rows_ref, sems, keep=None):
+def stream_dense(field, block_ref, rows_ref, sems, keep):
     lhs = jnp.concatenate(pieces(field, 2), axis=0).astype(BF16)
     depth = rows_ref.shape[0] // CHUNKS
     total = jnp.zeros((lhs.shape[0], rows_ref.shape[1]), F32)
@@ -92,9 +92,8 @@
         rows = rows_ref[at, :]
         high = rows.astype(BF16)
         low = (rows - high.astype(F32)).astype(BF16)
-        if keep is not None:
-            keep[0, at, :] = high
-            keep[1, at, :] = low
+        keep[0, at, :] = high
+        keep[1, at, :] = low
         total = total + jnp.dot(lhs[:, at], high, preferred_element_type=F32)
         total = total + jnp.dot(lhs[:, at], low, preferred_element_type=F32)
     return total[:8] + total[8:]
@@ -107,7 +106,7 @@
 
 
 def prepare(block_ref, x_hbm, load_hbm, contact_hbm, rows_hbm, partners_hbm, counts_hbm,
-            onehot_ref, valid_ref, own_ref, hown_ref, h_ref, out_ref, first_ref, last_ref,
+            onehot_ref, valid_ref, own_ref, hown_ref, h_ref, out_ref, first_ref, last_ref, halves_ref,
             held_ref, x_ref, load_ref, contact_ref, rows_ref, partners_ref, counts_ref, sems, more_sems):
     small = [
         pltpu.make_async_copy(source, target, more_sems.at[i])
@@ -125,7 +124,7 @@
     x = x_ref[...]
     width = x.shape[1]
     rows = jnp.concatenate(
-        [rows_ref[r : r + 1, :] for r in range(ROUNDS)]
+        [rows_ref[r] for r in range(ROUNDS)]
         + [jnp.full((1, JW - ROUNDS * JR), -1, jnp.int32)],
         axis=1,
     )
@@ -144,7 +143,7 @@
     position = lax.broadcasted_iota(jnp.int32, x.shape, 1)
     edge = (position < FACE) | (position >= width - FACE)
     h = spread(valid * own, onehot) + jnp.where(edge, x, 0.0) - load_ref[...]
-    h = h + stream_dense(x, block_ref, held_ref, sems)
+    h = h + stream_dense(x, block_ref, held_ref, sems, halves_ref)
     h_ref[...] = h
     (hown,) = pick(h, onehot)
     hown_ref[...] = hown
@@ -175,12 +174,10 @@
     return jnp.sum(value, axis=1, keepdims=True)
 
 
-def first_gradient(partners_ref, layer_ref, block_ref, x_ref, h_ref, own_ref, hown_ref, in_ref,
+def first_gradient(partners_ref, layer_ref, halves_ref, x_ref, h_ref, own_ref, hown_ref, in_ref,
                    below_in, above_in, valid_ref, onehot_ref,
                    g_ref, gown_ref, far_ref, gfar_ref, below_ref, gbelow_ref, above_ref, gabove_ref,
-                   halves_ref, all_ref, held_ref, sems):
-    for chunk in range(CHUNKS):
-        chunk_copy(block_ref, held_ref, sems, chunk).start()
+                   all_ref):
     width = x_ref.shape[1]
     place = lax.broadcasted_iota(jnp.int32, (8, LANES), 1) // JR
     parts = [[jnp.zeros((8, LANES), F32)] * 2 for _ in range(3)]
@@ -214,7 +211,7 @@
     jumps = valid * gown * (gown - gfar)
     terms = first * (first - gbelow) + last * (last - gabove) + jumps[:, :LANES] + jumps[:, LANES:]
     square = lane_sum(g * g)
-    curvature = lane_sum(terms) + lane_sum(g * stream_dense(g, block_ref, held_ref, sems, halves_ref))
+    curvature = lane_sum(terms) + lane_sum(g * dense(g, halves_ref[0], halves_ref[1]))
     lane = lax.broadcasted_iota(jnp.int32, (8, LANES), 1)
     row = lax.broadcasted_iota(jnp.int32, (8, LANES), 0)
     line = jnp.where(lane == row, square, 0.0) + jnp.where(lane == row + 8, curvature, 0.0)
@@ -256,8 +253,9 @@
     out_ref[...] = jnp.broadcast_to(parcel[None], out_ref.shape)
 
 
-def layer_sums(partners_ref, table_ref, in_ref, g_ref, gfar_ref, out_ref):
-    gfar_ref[...] = arrived(in_ref, partners_ref)
+def layer_sums(partners_ref, table_ref, in_ref, g_ref, out_ref, *gfar_refs):
+    for gfar_ref in gfar_refs:
+        gfar_ref[...] = arrived(in_ref, partners_ref)
     place = lax.broadcasted_iota(jnp.int32, (8, LANES), 1) // JR
     nothing = jnp.zeros((8, LANES), F32)
     products, sums = [nothing, nothing], nothing
@@ -321,26 +319,26 @@
 def advance_by(step, gabove, x_ref, g_ref, contact_ref, load_ref,
                own_ref, gown_ref, far_ref, gfar_ref, below_ref, gbelow_ref, above_ref,
                valid_ref, onehot_ref, halves_ref,
-               g_out, gown_out, last_out, x_out, own_out, far_out, below_out, above_out):
+               g_out, gown_out, last_out, x_out, *halo_outs):
     x = moved(x_ref[...], g_ref[...], step, contact_ref[...])
     x_out[...] = x
     halo = []
-    for held_ref, slope, held_out in (
-        (own_ref, gown_ref[...], own_out), (far_ref, gfar_ref[...], far_out),
-        (below_ref, gbelow_ref[...], below_out), (above_ref, gabove, above_out),
+    for held_ref, slope in (
+        (own_ref, gown_ref[...]), (far_ref, gfar_ref[...]), (below_ref, gbelow_ref[...]), (above_ref, gabove),
     ):
-        flags = held_ref[8:]
-        value = moved(held_ref[:8], slope, step, flags)
-        held_out[...] = jnp.concatenate([value, flags], axis=0)
-        halo.append(value)
+        halo.append(moved(held_ref[:8], slope, step, held_ref[8:]))
+    for held_ref, value, held_out in zip((own_ref, far_ref, below_ref, above_ref), halo, halo_outs):
+        held_out[...] = jnp.concatenate([value, held_ref[8:]], axis=0)
     onehot = onehot_ref[...]
     image = dense(x, halves_ref[0], halves_ref[1])
     gradient = with_coupling(image, x, load_ref[...], *halo, valid_ref[...], onehot)
     give_gradient(gradient, onehot, g_out, gown_out, last_out)
 
 
-def finish(in_ref, x_ref, g_ref, contact_ref, x_out):
-    x_out[...] = moved(x_ref[...], g_ref[...], step_of(in_ref), contact_ref[...])
+def finish(in_ref, x_ref, g_ref, contact_ref, x_out, g_out):
+    g = g_ref[...]
+    g_out[...] = g
+    x_out[...] = moved(x_ref[...], g, step_of(in_ref), contact_ref[...])
 
 
 def swap(outgoing, axis):
@@ -356,35 +354,37 @@
 
 def shards(dual_block, start, load, partners, jump_rows, counts, contact):
     block, x, target = dual_block[0, 0], start[0, 0], load[0, 0]
-    rows, amounts, flags = jump_rows[0, 0], counts[0], contact[0]
+    rows, amounts, flags = jump_rows.reshape(ROUNDS, 1, JR), counts[0], contact[0]
     loads, width = x.shape
     plans, layers = lax.axis_size("plan"), lax.axis_size("layer")
     field, jump, face = shape(loads, width), shape(loads, JW), shape(loads, FACE)
     jump2, face2, face3 = shape(2 * loads, JW), shape(2 * loads, FACE), shape(3 * loads, FACE)
     flops = 4 * 16 * width * width
     layer = jnp.stack([lax.axis_index("layer"), layers]).astype(jnp.int32).reshape(1, 2)
+    amounts, layer = lax.optimization_barrier((amounts, layer))
     held = pltpu.VMEM((width, width), F32)
     chunk_sems = pltpu.SemaphoreType.DMA((CHUNKS,))
 
-    onehot, valid, own, hown, h, out, first, last = call(
+    onehot, valid, own, hown, h, out, first, last, halves = call(
         prepare, "prepare",
-        (shape(width, JW, dtype=BF16), jump, jump2, jump, field, shape(plans, loads, LANES), face3, face3),
-        [HBM] * 7, 53, flops, 4 * width * width,
+        (shape(width, JW, dtype=BF16), jump, jump2, jump, field, shape(plans, loads, LANES), face3, face3,
+         shape(2, width, width, dtype=BF16)),
+        [HBM] * 7, 16, flops, 4 * width * width,
         [
             held, pltpu.VMEM(x.shape, F32), pltpu.VMEM(target.shape, F32),
             pltpu.VMEM(flags.shape, jnp.int32), pltpu.VMEM(rows.shape, jnp.int32),
             pltpu.SMEM(partners.shape, jnp.int32), pltpu.SMEM(amounts.shape, jnp.int32),
             chunk_sems, pltpu.SemaphoreType.DMA((6,)),
         ],
-    )(block, x, target, flags, rows, partners, amounts)
+    )(*(pltpu.with_memory_space_constraint(a, pltpu.HBM) for a in (block, x, target, flags, rows, partners, amounts)))
+    below, above, out = lax.optimization_barrier((lift(last, 1), lift(first, -1), out))
     incoming = swap(out, "plan")
-    below, above = lift(last, 1), lift(first, -1)
-    g, gown, far, gfar, below, gbelow, above, gabove, halves, out = call(
+    g, gown, far, gfar, below, gbelow, above, gabove, out = call(
         first_gradient, "first_gradient",
         (field, jump, jump2, jump, face2, face, face2, face,
-         shape(2, width, width, dtype=BF16), shape(plans * layers, LANES)),
-        [SMEM] * 2 + [HBM] + [VMEM] * 9, 48, flops, 4 * width * width, [held, chunk_sems],
-    )(partners, layer, block, x, h, own, hown, incoming, below, above, valid, onehot)
+         shape(plans * layers, LANES)),
+        [SMEM] * 2 + [VMEM] * 10, 12, flops, 4 * width * width,
+    )(partners, layer, halves, x, h, own, hown, incoming, below, above, valid, onehot)
     incoming = swap(out, ("plan", "layer"))
 
     after = (field, jump, face, field, jump2, jump2, face2, face2)
@@ -402,18 +402,21 @@
         out = call(announce, "announce", shape(plans, loads, JW), [VMEM] * 5, 8)(
             sums, g, gown, valid, gbelow
         )
-        gfar, out = call(
-            layer_sums, "layer_sums", (jump, shape(layers, loads, FACE + LANES)),
+        ending = iteration == ITERS - 1
+        out, *gfar = call(
+            layer_sums, "layer_sums", (shape(layers, loads, FACE + LANES),) + (() if ending else (jump,)),
             [SMEM] * 2 + [VMEM] * 2, 8,
         )(partners, table, swap(out, "plan"), g)
         incoming = swap(out, "layer")
-        if iteration == ITERS - 1:
-            x = call(finish, "finish", field, [VMEM] * 4, 8)(incoming, x, g, flags)
+        if ending:
+            x, g = call(finish, "finish", (field, field), [VMEM] * 4, 8)(incoming, x, g, flags)
             break
-        g, gown, last, x, own, far, below, above = call(
-            advance, "advance", after, [SMEM] + [VMEM] * 15, 12, flops, 4 * width * width,
-        )(layer, incoming, x, g, flags, target, own, gown, far, gfar, below, gbelow, above,
+        g, gown, last, x, *halo = call(
+            advance, "advance", after[:4] if iteration == ITERS - 2 else after,
+            [SMEM] + [VMEM] * 15, 12, flops, 4 * width * width,
+        )(layer, incoming, x, g, flags, target, own, gown, far, *gfar, below, gbelow, above,
           valid, onehot, halves)
+        own, far, below, above = halo or (None,) * 4
     return x[None, None], g[None, None]
 
 

time: 164 us -> 161 us (0.982)
  blocking collectives: 109 us -> 128 us
  starting transfers between devices: 23.7 us -> 11.9 us
  local copies, waits for them, and re-layouts: 4.97 us -> 0.02 us
  waiting for transfers between devices: 6.41 us -> 3.14 us
  Pallas kernels: 18.9 us -> 16.5 us
    all_to_all x7 -> x8, blocking collectives: 109 us -> 128 us  [swap(): lax.all_to_all(outgoing, axis, split_axis=0, concat_axis=0, tiled=True)]
    all_to_all x1 -> x0, starting transfers between devices: 12.6 us -> none  [swap(): lax.all_to_all(outgoing, axis, split_axis=0, concat_axis=0, tiled=True)]
    unnamed x21 -> x8, local copies, waits for them, and re-layouts: 4.97 us -> 0.02 us
    all_to_all x1 -> x0, waiting for transfers between devices: 3.05 us -> none  [swap(): lax.all_to_all(outgoing, axis, split_axis=0, concat_axis=0, tiled=True)]
    pallas_call x1, Pallas kernels: 3.33 us -> 1.47 us  [shards(): call(first_gradient, 'first_gradient', (field, jump, jump2, jump, face2,...]
  transfers between devices with their start and end apart: 6 -> 5, of which waited for: 2 -> 1; matrix products, arithmetic and copies ran while one was open for 0% -> 0% of each run, Pallas kernels for 1% -> 1%
where the time goes in v4:
time: 161 us
  blocking collectives  128 us (80%)
  Pallas kernels  16.5 us (10%)
  starting transfers between devices  11.9 us (7%)
  waiting for transfers between devices  3.14 us (2%)
    all_to_all x8, blocking collectives, swap(): lax.all_to_all(outgoing, axis, split_axis=0, concat_axis=0, tiled=True)  128 us
    ppermute x5, starting transfers between devices, lift(): lax.ppermute(face, 'layer', [(i, i + step) for i in range(layers) if 0 <=...  11.9 us
    pallas_call x1, Pallas kernels, shards(): call(prepare, 'prepare', (shape(width, JW, dtype=BF16), jump, jump2, jump...  3.97 us
    pallas_call x3, Pallas kernels, shards(): call(layer_sums, 'layer_sums', (shape(layers, loads, FACE + LANES),) + ((...  3.36 us
    pallas_call x2, Pallas kernels, shards(): call(advance, 'advance', after[:4] if iteration == ITERS - 2 else after,...  3.33 us
  transfers between devices with their start and end apart: 5, of which 1 were waited for; matrix products, arithmetic and copies ran while one was open for 0% of the time, Pallas kernels for 1%

profile of v4, /device:TPU:1, one launch (start us, length us, event | category | flops | bytes accessed | tf_op | source)
XLA Modules:
  0.0 160.7 jit_solution(11992842374659499101)
XLA Ops:
  0.6 0.0 copy-start.3
  0.6 0.0 copy-start.1
  0.7 0.1 add_bitcast_fusion.layer_ref
  0.7 0.0 copy-start
  0.7 0.0 copy-start.2
  0.7 4.0 %prepare.1 = (bf16[1024,256]{1,0:T(8,128)(2,1)S(1)}, f32[8,256]{1,0:T(8,128)S(1)}, f32[16,256]{1,0:T(8,128)S(1)}, f32[8,256]{1,0:T(8,128)S(1)}, f32[8,1024]{1,0:...) custom-call(f32[1024,1024]{1,0:T(8,128)} %bitcast.29, ...), custom_call_target="tpu_custom_call" | custom-call | flops 67108864 | bytes 4194304 | tf_op jit(solution)/shard_map/prepare/pallas_call | solution.py:368
  4.7 4.0 %collective-permute-start = (f32[24,128]{1,0:T(8,128)S(1)}, f32[24,128]{1,0:T(8,128)S(1)}, u32[]{:S(2)}, u32[]{:S(2)}) collective-permute-start(f32[24,128]{1,0:T(8,128)S(1)} %get-tuple-element.58), channel_id=1, source_target_pairs={{0,1},{1,2},{2,3},{3,4},{4,5},{5,6},{6,7},{8,9},{9,10},{10,11},{11... | collective-permute-start | bytes 36872 | tf_op jit(solution)/shard_map/ppermute | solution.py:350
  8.8 1.3 collective-permute-start.1
  10.1 0.0 collective-permute-done.below_in
  10.1 3.1 %collective-permute-done.1.above_in = f32[24,128]{1,0:T(8,128)S(1)} collective-permute-done((f32[24,128]{1,0:T(8,128)S(1)}, f32[24,128]{1,0:T(8,128)S(1)}, u32[]{:S(2)}, u32[]{:S(2)}) %collective-permute-start.1) | collective-permute-done | bytes 12320 | tf_op jit(solution)/shard_map/ppermute | solution.py:350
  13.2 24.1 %all_to_all.46.in_ref = f32[32,8,128]{2,1,0:T(8,128)S(1)} all-to-all(f32[32,8,128]{2,1,0:T(8,128)S(1)} %get-tuple-element.61), channel_id=1, replica_groups=mesh['plan'=32,'layer'=8] {'plan'}, dimensions={0} | all-to-all | bytes 262144 | tf_op jit(solution)/shard_map/all_to_all | solution.py:345
  37.3 0.0 copy-done.3
  37.3 0.0 copy-done.1
  37.3 1.5 first_gradient.1
  38.8 19.2 %all_to_all.47 = f32[256,1,128]{2,1,0:T(1,128)S(1)} all-to-all(f32[256,1,128]{2,1,0:T(1,128)S(1)} %bitcast.23), channel_id=1, replica_groups=mesh['plan'=32,'layer'=8] {'plan','layer'}, dimensions={0} | all-to-all | bytes 262144 | tf_op jit(solution)/shard_map/all_to_all | solution.py:345
  58.0 0.0 copy-done
  58.0 0.0 copy-done.2
  58.0 1.1 first_advance.1
  59.1 2.2 %collective-permute-start.2 = (f32[8,128]{1,0:T(8,128)S(1)}, f32[8,128]{1,0:T(8,128)S(1)}, u32[]{:S(2)}, u32[]{:S(2)}) collective-permute-start(f32[8,128]{1,0:T(8,128)S(1)} %get-tuple-element.78), channel_id=1, source_target_pairs={{0,1},{1,2},{2,3},{3,4},{4,5},{5,6},{6,7},{8,9},{9,10},{10,11},{11... | collective-permute-start | bytes 12296 | tf_op jit(solution)/shard_map/ppermute | solution.py:350
  61.3 0.7 local_sums.3.sums_ref
  62.0 0.0 collective-permute-done.2.below_ref.refs_9_
  62.0 0.2 announce.3
  62.2 17.8 %all_to_all.48.in_ref = f32[32,8,256]{2,1,0:T(8,128)S(1)} all-to-all(f32[32,8,256]{2,1,0:T(8,128)S(1)} %announce.3), channel_id=1, replica_groups=mesh['plan'=32,'layer'=8] {'plan'}, dimensions={0} | all-to-all | bytes 524288 | tf_op jit(solution)/shard_map/all_to_all | solution.py:345
  80.0 1.1 layer_sums.3
  81.1 10.4 %all_to_all.49.in_ref = f32[8,8,256]{2,1,0:T(8,128)S(1)} all-to-all(f32[8,8,256]{2,1,0:T(8,128)S(1)} %get-tuple-element.79), channel_id=1, replica_groups=mesh['plan'=32,'layer'=8] {'layer'}, dimensions={0} | all-to-all | bytes 131072 | tf_op jit(solution)/shard_map/all_to_all | solution.py:345
  91.5 1.7 %advance.2 = (f32[8,1024]{1,0:T(8,128)S(1)}, f32[8,256]{1,0:T(8,128)S(1)}, f32[8,128]{1,0:T(8,128)S(1)}, f32[8,1024]{1,0:T(8,128)S(1)}, f32[16,256]{1,0:T(8,128)...) custom-call(s32[1,2]{1,0:T(1,128)S(1)} %add_bitcast_fusion.layer_ref, ...), custom_call_target="tpu_custom_call" | custom-call | flops 67108864 | bytes 4194304 | tf_op jit(solution)/shard_map/advance/pallas_call | solution.py:414
  93.2 2.2 %collective-permute-start.3 = (f32[8,128]{1,0:T(8,128)S(1)}, f32[8,128]{1,0:T(8,128)S(1)}, u32[]{:S(2)}, u32[]{:S(2)}) collective-permute-start(f32[8,128]{1,0:T(8,128)S(1)} %get-tuple-element.88), channel_id=1, source_target_pairs={{0,1},{1,2},{2,3},{3,4},{4,5},{5,6},{6,7},{8,9},{9,10},{10,11},{11... | collective-permute-start | bytes 12296 | tf_op jit(solution)/shard_map/ppermute | solution.py:350
  95.4 0.7 local_sums.4.sums_ref
  96.0 0.0 collective-permute-done.3.below_ref.refs_9_
  96.0 0.2 announce.4
  96.2 18.9 %all_to_all.50.in_ref = f32[32,8,256]{2,1,0:T(8,128)S(1)} all-to-all(f32[32,8,256]{2,1,0:T(8,128)S(1)} %announce.4), channel_id=1, replica_groups=mesh['plan'=32,'layer'=8] {'plan'}, dimensions={0} | all-to-all | bytes 524288 | tf_op jit(solution)/shard_map/all_to_all | solution.py:345
  115.1 1.1 layer_sums.4
  116.2 9.5 %all_to_all.51.in_ref = f32[8,8,256]{2,1,0:T(8,128)S(1)} all-to-all(f32[8,8,256]{2,1,0:T(8,128)S(1)} %get-tuple-element.89), channel_id=1, replica_groups=mesh['plan'=32,'layer'=8] {'layer'}, dimensions={0} | all-to-all | bytes 131072 | tf_op jit(solution)/shard_map/all_to_all | solution.py:345
  125.7 1.7 %advance.3 = (f32[8,1024]{1,0:T(8,128)S(1)}, f32[8,256]{1,0:T(8,128)S(1)}, f32[8,128]{1,0:T(8,128)S(1)}, f32[8,1024]{1,0:T(8,128)S(1)}) custom-call(s32[1,2]{1,0:T(1,128)S(1)} %add_bitcast_fusion.layer_ref, f32[8,8,256]{2,1,0:T(8,128)S(1)} %all_to_all.51.in_ref, f32[8,1024]{1,0:T(8,128)S(1)} %get-tuple-element.90.refs_0_, ...), custom_call_target="tpu_custom_call" | custom-call | flops 67108864 | bytes 4194304 | tf_op jit(solution)/shard_map/advance/pallas_call | solution.py:414
  127.3 2.2 %collective-permute-start.4 = (f32[8,128]{1,0:T(8,128)S(1)}, f32[8,128]{1,0:T(8,128)S(1)}, u32[]{:S(2)}, u32[]{:S(2)}) collective-permute-start(f32[8,128]{1,0:T(8,128)S(1)} %get-tuple-element.98), channel_id=1, source_target_pairs={{0,1},{1,2},{2,3},{3,4},{4,5},{5,6},{6,7},{8,9},{9,10},{10,11},{11... | collective-permute-start | bytes 12296 | tf_op jit(solution)/shard_map/ppermute | solution.py:350
  129.5 0.7 local_sums.5.sums_ref
  130.2 0.0 collective-permute-done.4.below_ref
  130.2 0.2 announce.5
  130.4 19.0 %all_to_all.52.in_ref = f32[32,8,256]{2,1,0:T(8,128)S(1)} all-to-all(f32[32,8,256]{2,1,0:T(8,128)S(1)} %announce.5), channel_id=1, replica_groups=mesh['plan'=32,'layer'=8] {'plan'}, dimensions={0} | all-to-all | bytes 524288 | tf_op jit(solution)/shard_map/all_to_all | solution.py:345
  149.4 1.1 layer_sums.5
  150.5 9.5 %all_to_all.53.in_ref = f32[8,8,256]{2,1,0:T(8,128)S(1)} all-to-all(f32[8,8,256]{2,1,0:T(8,128)S(1)} %layer_sums.5), channel_id=1, replica_groups=mesh['plan'=32,'layer'=8] {'layer'}, dimensions={0} | all-to-all | bytes 131072 | tf_op jit(solution)/shard_map/all_to_all | solution.py:345
  160.0 0.8 finish.1
Async XLA Ops:
  0.6 36.7 %copy-start.3 = (s32[1,6]{1,0:T(1,128)S(1)}, s32[1,6]{1,0:T(1,128)}, u32[]{:S(2)}) copy-start(s32[1,6]{1,0:T(1,128)} %partners_ref.7) | copy-start | bytes 76
  0.6 36.7 %copy-start.1 = (f32[1,1,8,1024]{3,2,1,0:T(8,128)S(1)}, f32[1,1,8,1024]{3,2,1,0:T(8,128)}, u32[]{:S(2)}) copy-start(f32[1,1,8,1024]{3,2,1,0:T(8,128)} %param.8) | copy-start | bytes 98308
  0.7 57.3 %copy-start = (f32[1,1,8,1024]{3,2,1,0:T(8,128)S(1)}, f32[1,1,8,1024]{3,2,1,0:T(8,128)}, u32[]{:S(2)}) copy-start(f32[1,1,8,1024]{3,2,1,0:T(8,128)} %param.9) | copy-start | bytes 98308
  0.7 57.3 %copy-start.2 = (s32[1,1,1024]{2,1,0:T(1,128)S(1)}, s32[1,1,1024]{2,1,0:T(1,128)}, u32[]{:S(2)}) copy-start(s32[1,1,1024]{2,1,0:T(1,128)} %param.13) | copy-start | bytes 12292
  4.7 5.3 %collective-permute-start = (f32[24,128]{1,0:T(8,128)S(1)}, f32[24,128]{1,0:T(8,128)S(1)}, u32[]{:S(2)}, u32[]{:S(2)}) collective-permute-start(f32[24,128]{1,0:T(8,128)S(1)} %get-tuple-element.58), channel_id=1, source_target_pairs={{0,1},{1,2},{2,3},{3,4},{4,5},{5,6},{6,7},{8,9},{9,10},{10,11},{11... | collective-permute-start | bytes 36872 | tf_op jit(solution)/shard_map/ppermute | solution.py:350
  8.8 4.4 %collective-permute-start.1 = (f32[24,128]{1,0:T(8,128)S(1)}, f32[24,128]{1,0:T(8,128)S(1)}, u32[]{:S(2)}, u32[]{:S(2)}) collective-permute-start(f32[24,128]{1,0:T(8,128)S(1)} %get-tuple-element.59), channel_id=1, source_target_pairs={{1,0},{2,1},{3,2},{4,3},{5,4},{6,5},{7,6},{9,8},{10,9},{11,10},{12... | collective-permute-start | bytes 36872 | tf_op jit(solution)/shard_map/ppermute | solution.py:350
  59.1 2.9 %collective-permute-start.2 = (f32[8,128]{1,0:T(8,128)S(1)}, f32[8,128]{1,0:T(8,128)S(1)}, u32[]{:S(2)}, u32[]{:S(2)}) collective-permute-start(f32[8,128]{1,0:T(8,128)S(1)} %get-tuple-element.78), channel_id=1, source_target_pairs={{0,1},{1,2},{2,3},{3,4},{4,5},{5,6},{6,7},{8,9},{9,10},{10,11},{11... | collective-permute-start | bytes 12296 | tf_op jit(solution)/shard_map/ppermute | solution.py:350
  93.2 2.9 %collective-permute-start.3 = (f32[8,128]{1,0:T(8,128)S(1)}, f32[8,128]{1,0:T(8,128)S(1)}, u32[]{:S(2)}, u32[]{:S(2)}) collective-permute-start(f32[8,128]{1,0:T(8,128)S(1)} %get-tuple-element.88), channel_id=1, source_target_pairs={{0,1},{1,2},{2,3},{3,4},{4,5},{5,6},{6,7},{8,9},{9,10},{10,11},{11... | collective-permute-start | bytes 12296 | tf_op jit(solution)/shard_map/ppermute | solution.py:350
  127.3 2.9 %collective-permute-start.4 = (f32[8,128]{1,0:T(8,128)S(1)}, f32[8,128]{1,0:T(8,128)S(1)}, u32[]{:S(2)}, u32[]{:S(2)}) collective-permute-start(f32[8,128]{1,0:T(8,128)S(1)} %get-tuple-element.98), channel_id=1, source_target_pairs={{0,1},{1,2},{2,3},{3,4},{4,5},{5,6},{6,7},{8,9},{9,10},{10,11},{11... | collective-permute-start | bytes 12296 | tf_op jit(solution)/shard_map/ppermute | solution.py:350

commit v5 on v4

--- a/solution.py
+++ b/solution.py
@@ -10,10 +10,11 @@
 ROUNDS = 6
 ITERS = 4
 LANES = 128
-JW = 256
+HALF = 3
+JW = 2 * LANES
 CHUNKS = 4
 NAMES = 16
-SQUARE, CURVATURE = 64, 65
+SQUARE, CURVATURE = HALF * JR, HALF * JR + 1
 F32 = jnp.float32
 BF16 = jnp.bfloat16
 
@@ -48,6 +49,10 @@
     return parts
 
 
+def lane_sum(value):
+    return jnp.sum(value, axis=1, keepdims=True)
+
+
 def dense(field, high, low):
     lhs = jnp.concatenate(pieces(field, 2), axis=0).astype(BF16)
     total = jnp.dot(lhs, high, preferred_element_type=F32)
@@ -69,17 +74,12 @@
     return out[:8] + out[8:16] + out[16:24]
 
 
-def arrived(in_ref, partners_ref):
+def half_of(in_ref, table_ref, plan):
     place = lax.broadcasted_iota(jnp.int32, (8, LANES), 1) // JR
-    groups = []
-    for first in range(0, JW // JR, LANES // JR):
-        total = jnp.zeros((8, LANES), F32)
-        at = first * JR
-        for r in range(first, min(first + LANES // JR, ROUNDS)):
-            block = in_ref[partners_ref[0, r], :, at : at + LANES]
-            total = jnp.where(place == r - first, block, total)
-        groups.append(total)
-    return jnp.concatenate(groups, axis=1)
+    total = jnp.zeros((8, LANES), F32)
+    for r in range(HALF):
+        total = jnp.where(place == r, in_ref[table_ref[plan, r]], total)
+    return total
 
 
 def stream_dense(field, block_ref, rows_ref, sems, keep):
@@ -123,18 +123,17 @@
         copy.wait()
     x = x_ref[...]
     width = x.shape[1]
-    rows = jnp.concatenate(
-        [rows_ref[r] for r in range(ROUNDS)]
-        + [jnp.full((1, JW - ROUNDS * JR), -1, jnp.int32)],
-        axis=1,
-    )
+    spare = [jnp.full((1, LANES - HALF * JR), -1, jnp.int32)]
+    rows = [rows_ref[r] for r in range(ROUNDS)]
+    rows = jnp.concatenate(rows[:HALF] + spare + rows[HALF:] + spare, axis=1)
     hit = lax.broadcasted_iota(jnp.int32, (width, JW), 0) == rows
     onehot = jnp.where(hit, 1.0, 0.0).astype(BF16)
     onehot_ref[...] = onehot
     lane = lax.broadcasted_iota(jnp.int32, (8, JW), 1)
     valid = jnp.zeros((8, JW), F32)
     for r in range(ROUNDS):
-        inside = (lane >= r * JR) & (lane < r * JR + counts_ref[0, r])
+        start = r // HALF * LANES + r % HALF * JR
+        inside = (lane >= start) & (lane < start + counts_ref[0, r])
         valid = jnp.where(inside, 1.0, valid)
     valid_ref[...] = valid
     contact = jnp.broadcast_to(jnp.where(contact_ref[...] == 1, 1.0, 0.0), x.shape)
@@ -150,12 +149,12 @@
     out_ref[...] = jnp.zeros_like(out_ref)
     place = lax.broadcasted_iota(jnp.int32, (8, LANES), 1) // JR
     for r in range(ROUNDS):
-        group, slot = divmod(r * JR, LANES)
+        group, slot = divmod(r, HALF)
         at = slice(group * LANES, (group + 1) * LANES)
         parcel = jnp.zeros((8, LANES), F32)
         for i, jump in enumerate((own, hown, own_contact)):
             block = pltpu.roll(jump[:, at], (i * JR) % LANES, 1) if i else jump[:, at]
-            parcel = jnp.where(place == (slot // JR + i) % (LANES // JR), block, parcel)
+            parcel = jnp.where(place == (slot + i) % (LANES // JR), block, parcel)
         out_ref[partners_ref[0, r]] = parcel
     both = jnp.concatenate([x, h, contact], axis=0)
     first_ref[...] = both[:, :FACE]
@@ -170,23 +169,19 @@
     return jnp.concatenate([head, total[:, FACE : width - FACE], tail], axis=1)
 
 
-def lane_sum(value):
-    return jnp.sum(value, axis=1, keepdims=True)
-
-
-def first_gradient(partners_ref, layer_ref, halves_ref, x_ref, h_ref, own_ref, hown_ref, in_ref,
+def first_gradient(partners_ref, where_ref, halves_ref, x_ref, h_ref, own_ref, hown_ref, in_ref,
                    below_in, above_in, valid_ref, onehot_ref,
                    g_ref, gown_ref, far_ref, gfar_ref, below_ref, gbelow_ref, above_ref, gabove_ref,
-                   all_ref):
+                   all_ref, masks_ref):
     width = x_ref.shape[1]
     place = lax.broadcasted_iota(jnp.int32, (8, LANES), 1) // JR
     parts = [[jnp.zeros((8, LANES), F32)] * 2 for _ in range(3)]
     for r in range(ROUNDS):
-        group, slot = divmod(r * JR, LANES)
+        group, slot = divmod(r, HALF)
         parcel = in_ref[partners_ref[0, r]]
         for i in range(3):
             block = pltpu.roll(parcel, LANES - i * JR, 1) if i else parcel
-            parts[i][group] = jnp.where(place == slot // JR, block, parts[i][group])
+            parts[i][group] = jnp.where(place == slot, block, parts[i][group])
     far, hfar, far_contact = (jnp.concatenate(part, axis=1) for part in parts)
     valid = valid_ref[...]
     own = own_ref[:8]
@@ -198,9 +193,13 @@
     below, above = below_in[...], above_in[...]
     below_ref[...] = jnp.concatenate([below[:8], below[16:]], axis=0)
     above_ref[...] = jnp.concatenate([above[:8], above[16:]], axis=0)
-    layer = layer_ref[0, 0]
+    layer, layers, core = where_ref[0, 0], where_ref[0, 1], lax.rem(where_ref[0, 2], 2)
+    member = lax.broadcasted_iota(jnp.int32, (masks_ref.shape[1], LANES), 0)
+    masks_ref[0] = jnp.where(member == 2 * (layer + 1) + core, 1.0, 0.0)
+    masks_ref[1] = jnp.where(member == 2 * layer + 1 - core, 1.0, 0.0)
+    masks_ref[2] = jnp.where(member >= 0, core, 0).astype(F32)
     gbelow = jnp.where(layer > 0, below[8:16] - x_ref[:, :FACE], 0.0)
-    gabove = jnp.where(layer < layer_ref[0, 1] - 1, above[8:16] - x_ref[:, width - FACE :], 0.0)
+    gabove = jnp.where(layer < layers - 1, above[8:16] - x_ref[:, width - FACE :], 0.0)
     gbelow_ref[...] = gbelow
     gabove_ref[...] = gabove
     h = h_ref[...] - spread(valid * far, onehot_ref[...])
@@ -249,36 +248,32 @@
     more = jnp.sum(terms, axis=1, keepdims=True)
     lane = lax.broadcasted_iota(jnp.int32, (8, LANES), 1)
     extra = sums_ref[...] + jnp.where(lane == CURVATURE, more, 0.0)
-    parcel = jnp.concatenate([own[:, :LANES], own[:, LANES:] + extra], axis=1)
-    out_ref[...] = jnp.broadcast_to(parcel[None], out_ref.shape)
-
-
-def layer_sums(partners_ref, table_ref, in_ref, g_ref, out_ref, *gfar_refs):
+    halves = own[:, :LANES] + extra, own[:, LANES:] + extra
+    for plan in range(out_ref.shape[0]):
+        out_ref[plan] = halves[plan % 2]
+
+
+def layer_sums(where_ref, table_ref, in_ref, g_ref, out_ref, *gfar_refs):
+    plan = where_ref[0, 2]
     for gfar_ref in gfar_refs:
-        gfar_ref[...] = arrived(in_ref, partners_ref)
-    place = lax.broadcasted_iota(jnp.int32, (8, LANES), 1) // JR
-    nothing = jnp.zeros((8, LANES), F32)
-    products, sums = [nothing, nothing], nothing
+        gfar_ref[...] = half_of(in_ref, table_ref, plan)
+    products = sums = jnp.zeros((8, LANES), F32)
     for p in range(in_ref.shape[0]):
-        near = [in_ref[p, :, :LANES], in_ref[p, :, LANES:]]
-        sums = sums + near[1]
-        for group in range(2):
-            far = nothing
-            for r in range(4 * group, min(4 * group + 4, ROUNDS)):
-                block = in_ref[table_ref[p, r], :, group * LANES : (group + 1) * LANES]
-                far = jnp.where(place == r - 4 * group, block, far)
-            products[group] = products[group] + near[group] * far
-    cross = jnp.sum(products[0] + products[1], axis=1, keepdims=True)
-    lane = lax.broadcasted_iota(jnp.int32, (8, LANES), 1)
-    sums = sums - jnp.where(lane == CURVATURE, cross, 0.0)
-    parcel = jnp.concatenate([g_ref[:, :FACE], sums], axis=1)
+        near = in_ref[p]
+        sums = sums + near
+        products = products + near * half_of(in_ref, table_ref, p)
+    cross = lane_sum(products)
+    lane = lax.broadcasted_iota(jnp.int32, (8, LANES), 1)
+    sums = 0.5 * sums - jnp.where(lane == CURVATURE, cross, 0.0)
+    sibling = half_of(in_ref, table_ref, plan + 1 - 2 * lax.rem(plan, 2))
+    parcel = jnp.concatenate([g_ref[:, :FACE], jnp.where(lane < SQUARE, sibling, sums)], axis=1)
     out_ref[...] = jnp.broadcast_to(parcel[None], out_ref.shape)
 
 
 def step_of(in_ref):
     total = in_ref[0, :, LANES:]
-    for layer in range(1, in_ref.shape[0]):
-        total = total + in_ref[layer, :, LANES:]
+    for member in range(1, in_ref.shape[0]):
+        total = total + in_ref[member, :, LANES:]
     square = total[:, SQUARE : SQUARE + 1]
     curvature = total[:, CURVATURE : CURVATURE + 1]
     return (square + 1e-6) / (curvature + 1e-6)
@@ -299,32 +294,42 @@
     return (square + 1e-6) / (curvature + 1e-6)
 
 
-def first_advance(in_ref, *refs):
+def first_advance(in_ref, masks_ref, *refs):
     *refs, table_ref = refs
     plans = table_ref.shape[0]
     lines = in_ref[pl.ds(0, plans, stride=in_ref.shape[0] // plans), :]
-    table_ref[...] = pltpu.roll(lines, LANES - NAMES, 1)[:, :8].astype(jnp.int32)
-    gabove_ref, *refs = refs
-    advance_by(first_step(in_ref), gabove_ref[...], *refs)
-
-
-def advance(layer_ref, in_ref, *refs):
-    layers = in_ref.shape[0]
-    layer = layer_ref[0, 0]
-    gabove = in_ref[jnp.minimum(layer + 1, layers - 1), :, :FACE]
-    gabove = jnp.where(layer < layers - 1, gabove, 0.0)
-    advance_by(step_of(in_ref), gabove, *refs)
-
-
-def advance_by(step, gabove, x_ref, g_ref, contact_ref, load_ref,
-               own_ref, gown_ref, far_ref, gfar_ref, below_ref, gbelow_ref, above_ref,
+    names = jnp.where(
+        masks_ref[2, :1] == 0.0,
+        pltpu.roll(lines, LANES - NAMES, 1),
+        pltpu.roll(lines, LANES - NAMES - HALF, 1),
+    )
+    table_ref[...] = names[:, :8].astype(jnp.int32)
+    gabove_ref, gfar_ref, *refs = refs
+    advance_by(first_step(in_ref), gabove_ref[...], gfar_ref[...], *refs)
+
+
+def advance(in_ref, masks_ref, half_ref, *refs):
+    gabove = other = jnp.zeros((8, LANES), F32)
+    for member in range(in_ref.shape[0]):
+        at = slice(member, member + 1)
+        gabove = jnp.where(masks_ref[0, at] == 1.0, in_ref[member, :, :FACE], gabove)
+        other = jnp.where(masks_ref[1, at] == 1.0, in_ref[member, :, LANES:], other)
+    lane = lax.broadcasted_iota(jnp.int32, (8, LANES), 1)
+    half, other = half_ref[...], jnp.where(lane < SQUARE, other, 0.0)
+    even = masks_ref[2, :1] == 0.0
+    gfar = jnp.concatenate([jnp.where(even, half, other), jnp.where(even, other, half)], axis=1)
+    advance_by(step_of(in_ref), gabove, gfar, *refs)
+
+
+def advance_by(step, gabove, gfar, x_ref, g_ref, contact_ref, load_ref,
+               own_ref, gown_ref, far_ref, below_ref, gbelow_ref, above_ref,
                valid_ref, onehot_ref, halves_ref,
                g_out, gown_out, last_out, x_out, *halo_outs):
     x = moved(x_ref[...], g_ref[...], step, contact_ref[...])
     x_out[...] = x
     halo = []
     for held_ref, slope in (
-        (own_ref, gown_ref[...]), (far_ref, gfar_ref[...]), (below_ref, gbelow_ref[...]), (above_ref, gabove),
+        (own_ref, gown_ref[...]), (far_ref, gfar), (below_ref, gbelow_ref[...]), (above_ref, gabove),
     ):
         halo.append(moved(held_ref[:8], slope, step, held_ref[8:]))
     for held_ref, value, held_out in zip((own_ref, far_ref, below_ref, above_ref), halo, halo_outs):
@@ -341,8 +346,10 @@
     x_out[...] = moved(x_ref[...], g, step_of(in_ref), contact_ref[...])
 
 
-def swap(outgoing, axis):
-    return lax.all_to_all(outgoing, axis, split_axis=0, concat_axis=0, tiled=True)
+def swap(outgoing, axis, groups=None):
+    return lax.all_to_all(
+        outgoing, axis, split_axis=0, concat_axis=0, tiled=True, axis_index_groups=groups
+    )
 
 
 def lift(face, step):
@@ -360,8 +367,13 @@
     field, jump, face = shape(loads, width), shape(loads, JW), shape(loads, FACE)
     jump2, face2, face3 = shape(2 * loads, JW), shape(2 * loads, FACE), shape(3 * loads, FACE)
     flops = 4 * 16 * width * width
-    layer = jnp.stack([lax.axis_index("layer"), layers]).astype(jnp.int32).reshape(1, 2)
-    amounts, layer = lax.optimization_barrier((amounts, layer))
+    position = jnp.stack([lax.axis_index("layer"), layers, lax.axis_index("plan")])
+    position = position.astype(jnp.int32).reshape(1, 3)
+    amounts, position = lax.optimization_barrier((amounts, position))
+    columns = [
+        [(chip + core) * layers + layer for layer in range(layers) for core in range(2)]
+        for chip in range(0, plans, 2)
+    ]
     held = pltpu.VMEM((width, width), F32)
     chunk_sems = pltpu.SemaphoreType.DMA((CHUNKS,))
 
@@ -379,19 +391,19 @@
     )(*(pltpu.with_memory_space_constraint(a, pltpu.HBM) for a in (block, x, target, flags, rows, partners, amounts)))
     below, above, out = lax.optimization_barrier((lift(last, 1), lift(first, -1), out))
     incoming = swap(out, "plan")
-    g, gown, far, gfar, below, gbelow, above, gabove, out = call(
+    g, gown, far, gfar, below, gbelow, above, gabove, out, masks = call(
         first_gradient, "first_gradient",
         (field, jump, jump2, jump, face2, face, face2, face,
-         shape(plans * layers, LANES)),
+         shape(plans * layers, LANES), shape(3, 2 * layers, LANES)),
         [SMEM] * 2 + [VMEM] * 10, 12, flops, 4 * width * width,
-    )(partners, layer, halves, x, h, own, hown, incoming, below, above, valid, onehot)
+    )(partners, position, halves, x, h, own, hown, incoming, below, above, valid, onehot)
     incoming = swap(out, ("plan", "layer"))
 
     after = (field, jump, face, field, jump2, jump2, face2, face2)
     g, gown, last, x, own, far, below, above, table = call(
         first_advance, "first_advance", after + (shape(plans, 8, dtype=jnp.int32),),
-        [VMEM] * 16, 12, flops, 4 * width * width,
-    )(incoming, gabove, x, g, flags, target, own, gown, far, gfar, below, gbelow, above,
+        [VMEM] * 17, 12, flops, 4 * width * width,
+    )(incoming, masks, gabove, gfar, x, g, flags, target, own, gown, far, below, gbelow, above,
       valid, onehot, halves)
 
     for iteration in range(1, ITERS):
@@ -399,22 +411,23 @@
         sums = call(
             local_sums, "local_sums", face, [VMEM] * 2, 12, flops, 4 * width * width,
         )(g, halves)
-        out = call(announce, "announce", shape(plans, loads, JW), [VMEM] * 5, 8)(
+        out = call(announce, "announce", shape(plans, loads, LANES), [VMEM] * 5, 8)(
             sums, g, gown, valid, gbelow
         )
         ending = iteration == ITERS - 1
-        out, *gfar = call(
-            layer_sums, "layer_sums", (shape(layers, loads, FACE + LANES),) + (() if ending else (jump,)),
+        out, *half = call(
+            layer_sums, "layer_sums",
+            (shape(2 * layers, loads, FACE + LANES),) + (() if ending else (shape(loads, LANES),)),
             [SMEM] * 2 + [VMEM] * 2, 8,
-        )(partners, table, swap(out, "plan"), g)
-        incoming = swap(out, "layer")
+        )(position, table, swap(out, "plan"), g)
+        incoming = swap(out, ("plan", "layer"), columns)
         if ending:
             x, g = call(finish, "finish", (field, field), [VMEM] * 4, 8)(incoming, x, g, flags)
             break
         g, gown, last, x, *halo = call(
             advance, "advance", after[:4] if iteration == ITERS - 2 else after,
-            [SMEM] + [VMEM] * 15, 12, flops, 4 * width * width,
-        )(layer, incoming, x, g, flags, target, own, gown, far, *gfar, below, gbelow, above,
+            [VMEM] * 16, 12, flops, 4 * width * width,
+        )(incoming, masks, *half, x, g, flags, target, own, gown, far, below, gbelow, above,
           valid, onehot, halves)
         own, far, below, above = halo or (None,) * 4
     return x[None, None], g[None, None]

time: 161 us -> 156 us (0.969)
  blocking collectives: 128 us -> 125 us
    all_to_all x8, blocking collectives: 128 us -> 125 us  [swap(): lax.all_to_all(outgoing, axis, split_axis=0, concat_axis=0, tiled=True, a...]
where the time goes in v5:
time: 156 us
  blocking collectives  125 us (80%)
  Pallas kernels  14.9 us (10%)
  starting transfers between devices  11.8 us (8%)
  waiting for transfers between devices  3.14 us (2%)
    all_to_all x8, blocking collectives, swap(): lax.all_to_all(outgoing, axis, split_axis=0, concat_axis=0, tiled=True, a...  125 us
    ppermute x5, starting transfers between devices, lift(): lax.ppermute(face, 'layer', [(i, i + step) for i in range(layers) if 0 <=...  11.8 us
    pallas_call x1, Pallas kernels, shards(): call(prepare, 'prepare', (shape(width, JW, dtype=BF16), jump, jump2, jump...  3.97 us
    ppermute x5, waiting for transfers between devices, lift(): lax.ppermute(face, 'layer', [(i, i + step) for i in range(layers) if 0 <=...  3.14 us
  transfers between devices with their start and end apart: 5, of which 1 were waited for; matrix products, arithmetic and copies ran while one was open for 0% of the time, Pallas kernels for 1%

profile of v5, /device:TPU:1, one launch (start us, length us, event | category | flops | bytes accessed | tf_op | source)
XLA Modules:
  0.0 155.8 jit_solution(17265366541085993949)
XLA Ops:
  0.6 0.0 copy-start.3
  0.6 0.0 copy-start.1
  0.7 0.1 add_bitcast_fusion.where_ref
  0.7 0.0 copy-start
  0.7 0.0 copy-start.2
  0.7 4.0 %prepare.1 = (bf16[1024,256]{1,0:T(8,128)(2,1)S(1)}, f32[8,256]{1,0:T(8,128)S(1)}, f32[16,256]{1,0:T(8,128)S(1)}, f32[8,256]{1,0:T(8,128)S(1)}, f32[8,1024]{1,0:...) custom-call(f32[1024,1024]{1,0:T(8,128)} %bitcast.30, ...), custom_call_target="tpu_custom_call" | custom-call | flops 67108864 | bytes 4194304 | tf_op jit(solution)/shard_map/prepare/pallas_call | solution.py:380
  4.7 4.0 %collective-permute-start = (f32[24,128]{1,0:T(8,128)S(1)}, f32[24,128]{1,0:T(8,128)S(1)}, u32[]{:S(2)}, u32[]{:S(2)}) collective-permute-start(f32[24,128]{1,0:T(8,128)S(1)} %get-tuple-element.59), channel_id=1, source_target_pairs={{0,1},{1,2},{2,3},{3,4},{4,5},{5,6},{6,7},{8,9},{9,10},{10,11},{11... | collective-permute-start | bytes 36872 | tf_op jit(solution)/shard_map/ppermute | solution.py:357
  8.8 1.3 collective-permute-start.1
  10.1 0.0 collective-permute-done.below_in
  10.1 3.1 %collective-permute-done.1.above_in = f32[24,128]{1,0:T(8,128)S(1)} collective-permute-done((f32[24,128]{1,0:T(8,128)S(1)}, f32[24,128]{1,0:T(8,128)S(1)}, u32[]{:S(2)}, u32[]{:S(2)}) %collective-permute-start.1) | collective-permute-done | bytes 12320 | tf_op jit(solution)/shard_map/ppermute | solution.py:357
  13.2 24.1 %all_to_all.46.in_ref = f32[32,8,128]{2,1,0:T(8,128)S(1)} all-to-all(f32[32,8,128]{2,1,0:T(8,128)S(1)} %get-tuple-element.62), channel_id=1, replica_groups=mesh['plan'=32,'layer'=8] {'plan'}, dimensions={0} | all-to-all | bytes 262144 | tf_op jit(solution)/shard_map/all_to_all | solution.py:350
  37.3 0.0 copy-done.3
  37.3 0.0 copy-done.1
  37.4 1.5 first_gradient.1
  38.8 19.2 %all_to_all.47 = f32[256,1,128]{2,1,0:T(1,128)S(1)} all-to-all(f32[256,1,128]{2,1,0:T(1,128)S(1)} %bitcast.24), channel_id=1, replica_groups=mesh['plan'=32,'layer'=8] {'plan','layer'}, dimensions={0} | all-to-all | bytes 262144 | tf_op jit(solution)/shard_map/all_to_all | solution.py:350
  58.0 0.0 copy-done
  58.0 0.0 copy-done.2
  58.0 1.1 first_advance.1
  59.1 2.2 %collective-permute-start.2 = (f32[8,128]{1,0:T(8,128)S(1)}, f32[8,128]{1,0:T(8,128)S(1)}, u32[]{:S(2)}, u32[]{:S(2)}) collective-permute-start(f32[8,128]{1,0:T(8,128)S(1)} %get-tuple-element.80), channel_id=1, source_target_pairs={{0,1},{1,2},{2,3},{3,4},{4,5},{5,6},{6,7},{8,9},{9,10},{10,11},{11... | collective-permute-start | bytes 12296 | tf_op jit(solution)/shard_map/ppermute | solution.py:357
  61.3 0.7 local_sums.3.sums_ref
  62.0 0.0 collective-permute-done.2.below_ref.refs_8_
  62.0 0.2 announce.3
  62.2 15.6 %all_to_all.48.in_ref = f32[32,8,128]{2,1,0:T(8,128)S(1)} all-to-all(f32[32,8,128]{2,1,0:T(8,128)S(1)} %announce.3), channel_id=1, replica_groups=mesh['plan'=32,'layer'=8] {'plan'}, dimensions={0} | all-to-all | bytes 262144 | tf_op jit(solution)/shard_map/all_to_all | solution.py:350
  77.8 1.0 layer_sums.3
  78.8 12.2 %all_to_all.49.in_ref = f32[16,8,256]{2,1,0:T(8,128)S(1)} all-to-all(f32[16,8,256]{2,1,0:T(8,128)S(1)} %get-tuple-element.81), channel_id=1, replica_groups={{0,8,1,9,2,10,3,11,4,12,5,13,6,14,7,15},{16,24,17,25,18,26,19,27,20,28,..., dimensions={0} | all-to-all | bytes 262144 | tf_op jit(solution)/shard_map/all_to_all | solution.py:350
  91.0 1.1 advance.2
  92.1 2.1 %collective-permute-start.3 = (f32[8,128]{1,0:T(8,128)S(1)}, f32[8,128]{1,0:T(8,128)S(1)}, u32[]{:S(2)}, u32[]{:S(2)}) collective-permute-start(f32[8,128]{1,0:T(8,128)S(1)} %get-tuple-element.90), channel_id=1, source_target_pairs={{0,1},{1,2},{2,3},{3,4},{4,5},{5,6},{6,7},{8,9},{9,10},{10,11},{11... | collective-permute-start | bytes 12296 | tf_op jit(solution)/shard_map/ppermute | solution.py:357
  94.3 0.7 local_sums.4.sums_ref
  94.9 0.0 collective-permute-done.3.below_ref.refs_8_
  94.9 0.2 announce.4
  95.1 14.7 %all_to_all.50.in_ref = f32[32,8,128]{2,1,0:T(8,128)S(1)} all-to-all(f32[32,8,128]{2,1,0:T(8,128)S(1)} %announce.4), channel_id=1, replica_groups=mesh['plan'=32,'layer'=8] {'plan'}, dimensions={0} | all-to-all | bytes 262144 | tf_op jit(solution)/shard_map/all_to_all | solution.py:350
  109.8 1.0 layer_sums.4
  110.8 12.2 %all_to_all.51.in_ref = f32[16,8,256]{2,1,0:T(8,128)S(1)} all-to-all(f32[16,8,256]{2,1,0:T(8,128)S(1)} %get-tuple-element.91), channel_id=1, replica_groups={{0,8,1,9,2,10,3,11,4,12,5,13,6,14,7,15},{16,24,17,25,18,26,19,27,20,28,..., dimensions={0} | all-to-all | bytes 262144 | tf_op jit(solution)/shard_map/all_to_all | solution.py:350
  123.0 1.1 advance.3
  124.1 2.1 %collective-permute-start.4 = (f32[8,128]{1,0:T(8,128)S(1)}, f32[8,128]{1,0:T(8,128)S(1)}, u32[]{:S(2)}, u32[]{:S(2)}) collective-permute-start(f32[8,128]{1,0:T(8,128)S(1)} %get-tuple-element.100), channel_id=1, source_target_pairs={{0,1},{1,2},{2,3},{3,4},{4,5},{5,6},{6,7},{8,9},{9,10},{10,11},{11... | collective-permute-start | bytes 12296 | tf_op jit(solution)/shard_map/ppermute | solution.py:357
  126.3 0.7 local_sums.5.sums_ref
  126.9 0.0 collective-permute-done.4.below_ref
  126.9 0.2 announce.5
  127.1 14.7 %all_to_all.52.in_ref = f32[32,8,128]{2,1,0:T(8,128)S(1)} all-to-all(f32[32,8,128]{2,1,0:T(8,128)S(1)} %announce.5), channel_id=1, replica_groups=mesh['plan'=32,'layer'=8] {'plan'}, dimensions={0} | all-to-all | bytes 262144 | tf_op jit(solution)/shard_map/all_to_all | solution.py:350
  141.8 1.0 layer_sums.5
  142.8 12.2 %all_to_all.53.in_ref = f32[16,8,256]{2,1,0:T(8,128)S(1)} all-to-all(f32[16,8,256]{2,1,0:T(8,128)S(1)} %layer_sums.5), channel_id=1, replica_groups={{0,8,1,9,2,10,3,11,4,12,5,13,6,14,7,15},{16,24,17,25,18,26,19,27,20,28,..., dimensions={0} | all-to-all | bytes 262144 | tf_op jit(solution)/shard_map/all_to_all | solution.py:350
  155.0 0.8 finish.1
Async XLA Ops:
  0.6 36.7 %copy-start.3 = (s32[1,6]{1,0:T(1,128)S(1)}, s32[1,6]{1,0:T(1,128)}, u32[]{:S(2)}) copy-start(s32[1,6]{1,0:T(1,128)} %partners_ref.1) | copy-start | bytes 76
  0.6 36.7 %copy-start.1 = (f32[1,1,8,1024]{3,2,1,0:T(8,128)S(1)}, f32[1,1,8,1024]{3,2,1,0:T(8,128)}, u32[]{:S(2)}) copy-start(f32[1,1,8,1024]{3,2,1,0:T(8,128)} %param.8) | copy-start | bytes 98308
  0.7 57.3 %copy-start = (f32[1,1,8,1024]{3,2,1,0:T(8,128)S(1)}, f32[1,1,8,1024]{3,2,1,0:T(8,128)}, u32[]{:S(2)}) copy-start(f32[1,1,8,1024]{3,2,1,0:T(8,128)} %param.9) | copy-start | bytes 98308
  0.7 57.3 %copy-start.2 = (s32[1,1,1024]{2,1,0:T(1,128)S(1)}, s32[1,1,1024]{2,1,0:T(1,128)}, u32[]{:S(2)}) copy-start(s32[1,1,1024]{2,1,0:T(1,128)} %param.13) | copy-start | bytes 12292
  4.7 5.3 %collective-permute-start = (f32[24,128]{1,0:T(8,128)S(1)}, f32[24,128]{1,0:T(8,128)S(1)}, u32[]{:S(2)}, u32[]{:S(2)}) collective-permute-start(f32[24,128]{1,0:T(8,128)S(1)} %get-tuple-element.59), channel_id=1, source_target_pairs={{0,1},{1,2},{2,3},{3,4},{4,5},{5,6},{6,7},{8,9},{9,10},{10,11},{11... | collective-permute-start | bytes 36872 | tf_op jit(solution)/shard_map/ppermute | solution.py:357
  8.8 4.4 %collective-permute-start.1 = (f32[24,128]{1,0:T(8,128)S(1)}, f32[24,128]{1,0:T(8,128)S(1)}, u32[]{:S(2)}, u32[]{:S(2)}) collective-permute-start(f32[24,128]{1,0:T(8,128)S(1)} %get-tuple-element.60), channel_id=1, source_target_pairs={{1,0},{2,1},{3,2},{4,3},{5,4},{6,5},{7,6},{9,8},{10,9},{11,10},{12... | collective-permute-start | bytes 36872 | tf_op jit(solution)/shard_map/ppermute | solution.py:357
  59.1 2.9 %collective-permute-start.2 = (f32[8,128]{1,0:T(8,128)S(1)}, f32[8,128]{1,0:T(8,128)S(1)}, u32[]{:S(2)}, u32[]{:S(2)}) collective-permute-start(f32[8,128]{1,0:T(8,128)S(1)} %get-tuple-element.80), channel_id=1, source_target_pairs={{0,1},{1,2},{2,3},{3,4},{4,5},{5,6},{6,7},{8,9},{9,10},{10,11},{11... | collective-permute-start | bytes 12296 | tf_op jit(solution)/shard_map/ppermute | solution.py:357
  92.1 2.8 %collective-permute-start.3 = (f32[8,128]{1,0:T(8,128)S(1)}, f32[8,128]{1,0:T(8,128)S(1)}, u32[]{:S(2)}, u32[]{:S(2)}) collective-permute-start(f32[8,128]{1,0:T(8,128)S(1)} %get-tuple-element.90), channel_id=1, source_target_pairs={{0,1},{1,2},{2,3},{3,4},{4,5},{5,6},{6,7},{8,9},{9,10},{10,11},{11... | collective-permute-start | bytes 12296 | tf_op jit(solution)/shard_map/ppermute | solution.py:357
  124.1 2.8 %collective-permute-start.4 = (f32[8,128]{1,0:T(8,128)S(1)}, f32[8,128]{1,0:T(8,128)S(1)}, u32[]{:S(2)}, u32[]{:S(2)}) collective-permute-start(f32[8,128]{1,0:T(8,128)S(1)} %get-tuple-element.100), channel_id=1, source_target_pairs={{0,1},{1,2},{2,3},{3,4},{4,5},{5,6},{6,7},{8,9},{9,10},{10,11},{11... | collective-permute-start | bytes 12296 | tf_op jit(solution)/shard_map/ppermute | solution.py:357

commit v6 on v5

--- a/solution.py
+++ b/solution.py
@@ -53,10 +53,10 @@
     return jnp.sum(value, axis=1, keepdims=True)
 
 
-def dense(field, high, low):
+def dense(field, halves_ref, columns=slice(None)):
     lhs = jnp.concatenate(pieces(field, 2), axis=0).astype(BF16)
-    total = jnp.dot(lhs, high, preferred_element_type=F32)
-    total = total + jnp.dot(lhs, low, preferred_element_type=F32)
+    total = jnp.dot(lhs, halves_ref[0, :, columns], preferred_element_type=F32)
+    total = total + jnp.dot(lhs, halves_ref[1, :, columns], preferred_element_type=F32)
     return total[:8] + total[8:]
 
 
@@ -161,14 +161,6 @@
     last_ref[...] = both[:, width - FACE :]
 
 
-def with_coupling(image, x, load, own, far, below, above, valid, onehot):
-    width = x.shape[1]
-    total = image + spread(valid * (own - far), onehot) - load
-    head = total[:, :FACE] + (x[:, :FACE] - below)
-    tail = total[:, width - FACE :] + (x[:, width - FACE :] - above)
-    return jnp.concatenate([head, total[:, FACE : width - FACE], tail], axis=1)
-
-
 def first_gradient(partners_ref, where_ref, halves_ref, x_ref, h_ref, own_ref, hown_ref, in_ref,
                    below_in, above_in, valid_ref, onehot_ref,
                    g_ref, gown_ref, far_ref, gfar_ref, below_ref, gbelow_ref, above_ref, gabove_ref,
@@ -210,7 +202,7 @@
     jumps = valid * gown * (gown - gfar)
     terms = first * (first - gbelow) + last * (last - gabove) + jumps[:, :LANES] + jumps[:, LANES:]
     square = lane_sum(g * g)
-    curvature = lane_sum(terms) + lane_sum(g * dense(g, halves_ref[0], halves_ref[1]))
+    curvature = lane_sum(terms) + lane_sum(g * dense(g, halves_ref))
     lane = lax.broadcasted_iota(jnp.int32, (8, LANES), 1)
     row = lax.broadcasted_iota(jnp.int32, (8, LANES), 0)
     line = jnp.where(lane == row, square, 0.0) + jnp.where(lane == row + 8, curvature, 0.0)
@@ -222,22 +214,13 @@
     all_ref[...] = jnp.broadcast_to(line, all_ref.shape)
 
 
-def give_gradient(gradient, onehot, g_ref, gown_ref, last_ref):
-    g_ref[...] = gradient
-    last_ref[...] = gradient[:, gradient.shape[1] - FACE :]
-    gown_ref[...] = pick(gradient, onehot)[0]
-
-
-def local_sums(g_ref, halves_ref, sums_ref):
-    g = g_ref[...]
-    image = dense(g, halves_ref[0], halves_ref[1])
+def local_sums(g, halves_ref):
     width = g.shape[1]
-    terms = g * image
-    edges = g[:, :FACE] * g[:, :FACE] + g[:, width - FACE :] * g[:, width - FACE :]
-    square = jnp.sum(g * g, axis=1, keepdims=True)
-    curvature = jnp.sum(terms, axis=1, keepdims=True) + jnp.sum(edges, axis=1, keepdims=True)
-    lane = lax.broadcasted_iota(jnp.int32, (8, LANES), 1)
-    sums_ref[...] = jnp.where(lane == SQUARE, square, jnp.where(lane == CURVATURE, curvature, 0.0))
+    first, last = g[:, :FACE], g[:, width - FACE :]
+    square = lane_sum(g * g)
+    curvature = lane_sum(g * dense(g, halves_ref)) + lane_sum(first * first + last * last)
+    lane = lax.broadcasted_iota(jnp.int32, (8, LANES), 1)
+    return jnp.where(lane == SQUARE, square, jnp.where(lane == CURVATURE, curvature, 0.0))
 
 
 def announce(sums_ref, g_ref, gown_ref, valid_ref, below_ref, out_ref):
@@ -265,15 +248,16 @@
     cross = lane_sum(products)
     lane = lax.broadcasted_iota(jnp.int32, (8, LANES), 1)
     sums = 0.5 * sums - jnp.where(lane == CURVATURE, cross, 0.0)
-    sibling = half_of(in_ref, table_ref, plan + 1 - 2 * lax.rem(plan, 2))
-    parcel = jnp.concatenate([g_ref[:, :FACE], jnp.where(lane < SQUARE, sibling, sums)], axis=1)
-    out_ref[...] = jnp.broadcast_to(parcel[None], out_ref.shape)
+    if gfar_refs:
+        sibling = half_of(in_ref, table_ref, plan + 1 - 2 * lax.rem(plan, 2))
+        sums = jnp.concatenate([jnp.where(lane < SQUARE, sibling, sums), g_ref[:, :FACE]], axis=1)
+    out_ref[...] = jnp.broadcast_to(sums[None], out_ref.shape)
 
 
 def step_of(in_ref):
-    total = in_ref[0, :, LANES:]
+    total = in_ref[0, :, :LANES]
     for member in range(1, in_ref.shape[0]):
-        total = total + in_ref[member, :, LANES:]
+        total = total + in_ref[member, :, :LANES]
     square = total[:, SQUARE : SQUARE + 1]
     curvature = total[:, CURVATURE : CURVATURE + 1]
     return (square + 1e-6) / (curvature + 1e-6)
@@ -294,7 +278,33 @@
     return (square + 1e-6) / (curvature + 1e-6)
 
 
-def first_advance(in_ref, masks_ref, *refs):
+def chosen(in_ref, mask, columns):
+    total = jnp.zeros((8, LANES), F32)
+    for member in range(in_ref.shape[0]):
+        total = jnp.where(mask[member : member + 1] == 1.0, in_ref[member, :, columns], total)
+    return total
+
+
+def first_face(in_ref, gabove_ref, *refs):
+    face_by(first_step(in_ref), gabove_ref[...], *refs)
+
+
+def next_face(in_ref, masks_ref, *refs):
+    face_by(step_of(in_ref), chosen(in_ref, masks_ref[0], slice(LANES, None)), *refs)
+
+
+def face_by(step, gabove, x_ref, g_ref, contact_ref, load_ref, above_ref, halves_ref,
+            x_out, last_out, step_out, above_out):
+    x = moved(x_ref[...], g_ref[...], step, contact_ref[...])
+    x_out[...] = x
+    step_out[...] = jnp.broadcast_to(step, step_out.shape)
+    above = moved(above_ref[:8], gabove, step, above_ref[8:])
+    above_out[...] = jnp.concatenate([above, above_ref[8:]], axis=0)
+    at = slice(x.shape[1] - FACE, x.shape[1])
+    last_out[...] = dense(x, halves_ref, at) - load_ref[:, at] + (x[:, at] - above)
+
+
+def first_rest(in_ref, masks_ref, gfar_ref, *refs):
     *refs, table_ref = refs
     plans = table_ref.shape[0]
     lines = in_ref[pl.ds(0, plans, stride=in_ref.shape[0] // plans), :]
@@ -304,40 +314,38 @@
         pltpu.roll(lines, LANES - NAMES - HALF, 1),
     )
     table_ref[...] = names[:, :8].astype(jnp.int32)
-    gabove_ref, gfar_ref, *refs = refs
-    advance_by(first_step(in_ref), gabove_ref[...], gfar_ref[...], *refs)
-
-
-def advance(in_ref, masks_ref, half_ref, *refs):
-    gabove = other = jnp.zeros((8, LANES), F32)
-    for member in range(in_ref.shape[0]):
-        at = slice(member, member + 1)
-        gabove = jnp.where(masks_ref[0, at] == 1.0, in_ref[member, :, :FACE], gabove)
-        other = jnp.where(masks_ref[1, at] == 1.0, in_ref[member, :, LANES:], other)
-    lane = lax.broadcasted_iota(jnp.int32, (8, LANES), 1)
+    rest_by(gfar_ref[...], *refs)
+
+
+def next_rest(in_ref, masks_ref, half_ref, *refs):
+    lane = lax.broadcasted_iota(jnp.int32, (8, LANES), 1)
+    other = chosen(in_ref, masks_ref[1], slice(LANES))
     half, other = half_ref[...], jnp.where(lane < SQUARE, other, 0.0)
     even = masks_ref[2, :1] == 0.0
-    gfar = jnp.concatenate([jnp.where(even, half, other), jnp.where(even, other, half)], axis=1)
-    advance_by(step_of(in_ref), gabove, gfar, *refs)
-
-
-def advance_by(step, gabove, gfar, x_ref, g_ref, contact_ref, load_ref,
-               own_ref, gown_ref, far_ref, below_ref, gbelow_ref, above_ref,
-               valid_ref, onehot_ref, halves_ref,
-               g_out, gown_out, last_out, x_out, *halo_outs):
-    x = moved(x_ref[...], g_ref[...], step, contact_ref[...])
-    x_out[...] = x
+    rest_by(
+        jnp.concatenate([jnp.where(even, half, other), jnp.where(even, other, half)], axis=1), *refs
+    )
+
+
+def rest_by(gfar, step_ref, x_ref, last_ref, load_ref, own_ref, gown_ref, far_ref,
+            below_ref, gbelow_ref, valid_ref, onehot_ref, halves_ref,
+            g_out, gown_out, sums_out, *halo_outs):
+    step, x = step_ref[:, :1], x_ref[...]
+    inner = x.shape[1] - FACE
     halo = []
-    for held_ref, slope in (
-        (own_ref, gown_ref[...]), (far_ref, gfar), (below_ref, gbelow_ref[...]), (above_ref, gabove),
-    ):
+    for held_ref, slope in ((own_ref, gown_ref[...]), (far_ref, gfar), (below_ref, gbelow_ref[...])):
         halo.append(moved(held_ref[:8], slope, step, held_ref[8:]))
-    for held_ref, value, held_out in zip((own_ref, far_ref, below_ref, above_ref), halo, halo_outs):
+    for held_ref, value, held_out in zip((own_ref, far_ref, below_ref), halo, halo_outs):
         held_out[...] = jnp.concatenate([value, held_ref[8:]], axis=0)
+    own, far, below = halo
     onehot = onehot_ref[...]
-    image = dense(x, halves_ref[0], halves_ref[1])
-    gradient = with_coupling(image, x, load_ref[...], *halo, valid_ref[...], onehot)
-    give_gradient(gradient, onehot, g_out, gown_out, last_out)
+    jumps = spread(valid_ref[...] * (own - far), onehot)
+    total = dense(x, halves_ref, slice(inner)) + jumps[:, :inner] - load_ref[:, :inner]
+    head = total[:, :FACE] + (x[:, :FACE] - below)
+    g = jnp.concatenate([head, total[:, FACE:], last_ref[...]], axis=1)
+    g_out[...] = g
+    gown_out[...] = pick(g, onehot)[0]
+    sums_out[...] = local_sums(g, halves_ref)
 
 
 def finish(in_ref, x_ref, g_ref, contact_ref, x_out, g_out):
@@ -399,37 +407,42 @@
     )(partners, position, halves, x, h, own, hown, incoming, below, above, valid, onehot)
     incoming = swap(out, ("plan", "layer"))
 
-    after = (field, jump, face, field, jump2, jump2, face2, face2)
-    g, gown, last, x, own, far, below, above, table = call(
-        first_advance, "first_advance", after + (shape(plans, 8, dtype=jnp.int32),),
-        [VMEM] * 17, 12, flops, 4 * width * width,
-    )(incoming, masks, gabove, gfar, x, g, flags, target, own, gown, far, below, gbelow, above,
-      valid, onehot, halves)
+    early = (field, face, face, face2)
+    x, last, step, above = call(
+        first_face, "first_face", early, [VMEM] * 8, 12, flops // 8, width * width // 2,
+    )(incoming, gabove, x, g, flags, target, above, halves)
+    late = (field, jump, face, jump2, jump2, face2)
+    below_next = lift(last, 1)
+    g, gown, sums, own, far, below, table = call(
+        first_rest, "first_rest", late + (shape(plans, 8, dtype=jnp.int32),),
+        [VMEM] * 15, 12, 2 * flops, 8 * width * width,
+    )(incoming, masks, gfar, step, x, last, target, own, gown, far, below, gbelow, valid, onehot, halves)
 
     for iteration in range(1, ITERS):
-        gbelow = lift(last, 1)
-        sums = call(
-            local_sums, "local_sums", face, [VMEM] * 2, 12, flops, 4 * width * width,
-        )(g, halves)
+        gbelow = below_next
         out = call(announce, "announce", shape(plans, loads, LANES), [VMEM] * 5, 8)(
             sums, g, gown, valid, gbelow
         )
         ending = iteration == ITERS - 1
+        parcel = shape(2 * layers, loads, LANES if ending else LANES + FACE)
         out, *half = call(
-            layer_sums, "layer_sums",
-            (shape(2 * layers, loads, FACE + LANES),) + (() if ending else (shape(loads, LANES),)),
+            layer_sums, "layer_sums", (parcel,) + (() if ending else (shape(loads, LANES),)),
             [SMEM] * 2 + [VMEM] * 2, 8,
         )(position, table, swap(out, "plan"), g)
         incoming = swap(out, ("plan", "layer"), columns)
         if ending:
             x, g = call(finish, "finish", (field, field), [VMEM] * 4, 8)(incoming, x, g, flags)
             break
-        g, gown, last, x, *halo = call(
-            advance, "advance", after[:4] if iteration == ITERS - 2 else after,
-            [VMEM] * 16, 12, flops, 4 * width * width,
-        )(incoming, masks, *half, x, g, flags, target, own, gown, far, below, gbelow, above,
+        x, last, step, above = call(
+            next_face, "next_face", early, [VMEM] * 8, 12, flops // 8, width * width // 2,
+        )(incoming, masks, x, g, flags, target, above, halves)
+        below_next = lift(last, 1)
+        g, gown, sums, *halo = call(
+            next_rest, "next_rest", late[:3] if iteration == ITERS - 2 else late,
+            [VMEM] * 15, 12, 2 * flops, 8 * width * width,
+        )(incoming, masks, *half, step, x, last, target, own, gown, far, below, gbelow,
           valid, onehot, halves)
-        own, far, below, above = halo or (None,) * 4
+        own, far, below = halo or (None,) * 3
     return x[None, None], g[None, None]
 
 

time: 156 us -> 154 us (0.987)
  blocking collectives: 125 us -> 122 us
    all_to_all x8, blocking collectives: 125 us -> 122 us  [swap(): lax.all_to_all(outgoing, axis, split_axis=0, concat_axis=0, tiled=True, a...]
  transfers between devices with their start and end apart: 5 -> 5, of which waited for: 1 -> 1; matrix products, arithmetic and copies ran while one was open for 0% -> 0% of each run, Pallas kernels for 1% -> 3%
where the time goes in v6:
time: 154 us
  blocking collectives  122 us (79%)
  Pallas kernels  15.8 us (10%)
  starting transfers between devices  11.8 us (8%)
  waiting for transfers between devices  3.14 us (2%)
    all_to_all x8, blocking collectives, swap(): lax.all_to_all(outgoing, axis, split_axis=0, concat_axis=0, tiled=True, a...  122 us
    ppermute x5, starting transfers between devices, lift(): lax.ppermute(face, 'layer', [(i, i + step) for i in range(layers) if 0 <=...  11.8 us
    pallas_call x1, Pallas kernels, shards(): call(prepare, 'prepare', (shape(width, JW, dtype=BF16), jump, jump2, jump...  3.97 us
    pallas_call x2, Pallas kernels, shards(): call(next_rest, 'next_rest', late[:3] if iteration == ITERS - 2 else late...  3.19 us
    ppermute x5, waiting for transfers between devices, lift(): lax.ppermute(face, 'layer', [(i, i + step) for i in range(layers) if 0 <=...  3.14 us
  transfers between devices with their start and end apart: 5, of which 1 were waited for; matrix products, arithmetic and copies ran while one was open for 0% of the time, Pallas kernels for 3%

profile of v6, /device:TPU:1, one launch (start us, length us, event | category | flops | bytes accessed | tf_op | source)
XLA Modules:
  0.0 153.6 jit_solution(6713343243944543984)
XLA Ops:
  0.6 0.0 copy-start.3
  0.6 0.0 copy-start.1
  0.7 0.1 add_bitcast_fusion.where_ref
  0.7 0.0 copy-start
  0.7 0.0 copy-start.2
  0.7 4.0 %prepare.1 = (bf16[1024,256]{1,0:T(8,128)(2,1)S(1)}, f32[8,256]{1,0:T(8,128)S(1)}, f32[16,256]{1,0:T(8,128)S(1)}, f32[8,256]{1,0:T(8,128)S(1)}, f32[8,1024]{1,0:...) custom-call(f32[1024,1024]{1,0:T(8,128)} %bitcast.34, ...), custom_call_target="tpu_custom_call" | custom-call | flops 67108864 | bytes 4194304 | tf_op jit(solution)/shard_map/prepare/pallas_call | solution.py:388
  4.7 4.0 %collective-permute-start = (f32[24,128]{1,0:T(8,128)S(1)}, f32[24,128]{1,0:T(8,128)S(1)}, u32[]{:S(2)}, u32[]{:S(2)}) collective-permute-start(f32[24,128]{1,0:T(8,128)S(1)} %get-tuple-element.65), channel_id=1, source_target_pairs={{0,1},{1,2},{2,3},{3,4},{4,5},{5,6},{6,7},{8,9},{9,10},{10,11},{11... | collective-permute-start | bytes 36872 | tf_op jit(solution)/shard_map/ppermute | solution.py:365
  8.8 1.3 collective-permute-start.1
  10.1 0.0 collective-permute-done.below_in
  10.1 3.1 %collective-permute-done.1.above_in = f32[24,128]{1,0:T(8,128)S(1)} collective-permute-done((f32[24,128]{1,0:T(8,128)S(1)}, f32[24,128]{1,0:T(8,128)S(1)}, u32[]{:S(2)}, u32[]{:S(2)}) %collective-permute-start.1) | collective-permute-done | bytes 12320 | tf_op jit(solution)/shard_map/ppermute | solution.py:365
  13.2 24.1 %all_to_all.46.in_ref = f32[32,8,128]{2,1,0:T(8,128)S(1)} all-to-all(f32[32,8,128]{2,1,0:T(8,128)S(1)} %get-tuple-element.68), channel_id=1, replica_groups=mesh['plan'=32,'layer'=8] {'plan'}, dimensions={0} | all-to-all | bytes 262144 | tf_op jit(solution)/shard_map/all_to_all | solution.py:358
  37.3 0.0 copy-done.3
  37.3 0.0 copy-done.1
  37.4 1.5 first_gradient.1
  38.8 19.2 %all_to_all.47 = f32[256,1,128]{2,1,0:T(1,128)S(1)} all-to-all(f32[256,1,128]{2,1,0:T(1,128)S(1)} %bitcast.28), channel_id=1, replica_groups=mesh['plan'=32,'layer'=8] {'plan','layer'}, dimensions={0} | all-to-all | bytes 262144 | tf_op jit(solution)/shard_map/all_to_all | solution.py:358
  58.0 0.0 copy-done
  58.0 0.0 copy-done.2
  58.0 0.3 first_face.1
  58.4 2.2 %collective-permute-start.2 = (f32[8,128]{1,0:T(8,128)S(1)}, f32[8,128]{1,0:T(8,128)S(1)}, u32[]{:S(2)}, u32[]{:S(2)}) collective-permute-start(f32[8,128]{1,0:T(8,128)S(1)} %get-tuple-element.81.refs_2_), channel_id=1, source_target_pairs={{0,1},{1,2},{2,3},{3,4},{4,5},{5,6},{6,7},{8,9},{9,10},{10,11},{11... | collective-permute-start | bytes 12296 | tf_op jit(solution)/shard_map/ppermute | solution.py:365
  60.6 1.6 %first_rest.1 = (f32[8,1024]{1,0:T(8,128)S(1)}, f32[8,256]{1,0:T(8,128)S(1)}, f32[8,128]{1,0:T(8,128)S(1)}, f32[16,256]{1,0:T(8,128)S(1)}, f32[16,256]{1,0:T(8,1...) custom-call(f32[256,128]{1,0:T(8,128)S(1)} %bitcast.24, f32[3,16,128]{2,1,0:T(8,128)S(1)} %get-tuple-element.74.masks_ref, ...), custom_call_target="tpu_custom_call" | custom-call | flops 134217728 | bytes 8388608 | tf_op jit(solution)/shard_map/first_rest/pallas_call | solution.py:416
  62.2 0.0 collective-permute-done.2.below_ref.refs_8_
  62.2 0.1 announce.3
  62.3 15.0 %all_to_all.48.in_ref = f32[32,8,128]{2,1,0:T(8,128)S(1)} all-to-all(f32[32,8,128]{2,1,0:T(8,128)S(1)} %announce.3), channel_id=1, replica_groups=mesh['plan'=32,'layer'=8] {'plan'}, dimensions={0} | all-to-all | bytes 262144 | tf_op jit(solution)/shard_map/all_to_all | solution.py:358
  77.3 1.0 layer_sums.3
  78.3 11.9 %all_to_all.49.in_ref = f32[16,8,256]{2,1,0:T(8,128)S(1)} all-to-all(f32[16,8,256]{2,1,0:T(8,128)S(1)} %get-tuple-element.90), channel_id=1, replica_groups={{0,8,1,9,2,10,3,11,4,12,5,13,6,14,7,15},{16,24,17,25,18,26,19,27,20,28,..., dimensions={0} | all-to-all | bytes 262144 | tf_op jit(solution)/shard_map/all_to_all | solution.py:358
  90.2 0.4 next_face.2
  90.6 2.1 %collective-permute-start.3 = (f32[8,128]{1,0:T(8,128)S(1)}, f32[8,128]{1,0:T(8,128)S(1)}, u32[]{:S(2)}, u32[]{:S(2)}) collective-permute-start(f32[8,128]{1,0:T(8,128)S(1)} %get-tuple-element.95.refs_2_), channel_id=1, source_target_pairs={{0,1},{1,2},{2,3},{3,4},{4,5},{5,6},{6,7},{8,9},{9,10},{10,11},{11... | collective-permute-start | bytes 12296 | tf_op jit(solution)/shard_map/ppermute | solution.py:365
  92.7 1.6 %next_rest.2 = (f32[8,1024]{1,0:T(8,128)S(1)}, f32[8,256]{1,0:T(8,128)S(1)}, f32[8,128]{1,0:T(8,128)S(1)}, f32[16,256]{1,0:T(8,128)S(1)}, f32[16,256]{1,0:T(8,128)S(1)}, /*index=5*/f32[16,128]{1,0:T(8,128)S(1)}) custom-call(f32[16,8,256]{2,1,0:T(8,128)S(1)} %all_to_all.49.in_ref, f32[3,16,128]{2,1,0:T(8,128)S(1)} %get-tuple-element.74.masks_ref, ...), custom_call_target="tpu_custom_call" | custom-call | flops 134217728 | bytes 8388608 | tf_op jit(solution)/shard_map/next_rest/pallas_call | solution.py:440
  94.3 0.0 collective-permute-done.3.below_ref.refs_8_
  94.3 0.1 announce.4
  94.5 14.1 %all_to_all.50.in_ref = f32[32,8,128]{2,1,0:T(8,128)S(1)} all-to-all(f32[32,8,128]{2,1,0:T(8,128)S(1)} %announce.4), channel_id=1, replica_groups=mesh['plan'=32,'layer'=8] {'plan'}, dimensions={0} | all-to-all | bytes 262144 | tf_op jit(solution)/shard_map/all_to_all | solution.py:358
  108.6 1.0 layer_sums.4
  109.5 11.9 %all_to_all.51.in_ref = f32[16,8,256]{2,1,0:T(8,128)S(1)} all-to-all(f32[16,8,256]{2,1,0:T(8,128)S(1)} %get-tuple-element.102), channel_id=1, replica_groups={{0,8,1,9,2,10,3,11,4,12,5,13,6,14,7,15},{16,24,17,25,18,26,19,27,20,28,..., dimensions={0} | all-to-all | bytes 262144 | tf_op jit(solution)/shard_map/all_to_all | solution.py:358
  121.5 0.9 next_face.3
  122.3 2.1 %collective-permute-start.4 = (f32[8,128]{1,0:T(8,128)S(1)}, f32[8,128]{1,0:T(8,128)S(1)}, u32[]{:S(2)}, u32[]{:S(2)}) collective-permute-start(f32[8,128]{1,0:T(8,128)S(1)} %get-tuple-element.107.refs_2_), channel_id=1, source_target_pairs={{0,1},{1,2},{2,3},{3,4},{4,5},{5,6},{6,7},{8,9},{9,10},{10,11},{11... | collective-permute-start | bytes 12296 | tf_op jit(solution)/shard_map/ppermute | solution.py:365
  124.5 1.6 %next_rest.3 = (f32[8,1024]{1,0:T(8,128)S(1)}, f32[8,256]{1,0:T(8,128)S(1)}, f32[8,128]{1,0:T(8,128)S(1)}) custom-call(f32[16,8,256]{2,1,0:T(8,128)S(1)} %all_to_all.51.in_ref, f32[3,16,128]{2,1,0:T(8,128)S(1)} %get-tuple-element.74.masks_ref, f32[8,128]{1,0:T(8,128)S(1)} %get-tuple-element.103.half_ref, f32[8,128]{1,0:T(8,128)S(1)} %get-tuple-element.105.refs_0_, ...), custom_call_target="tpu_custom_call" | custom-call | flops 134217728 | bytes 8388608 | tf_op jit(solution)/shard_map/next_rest/pallas_call | solution.py:440
  126.0 0.0 collective-permute-done.4.below_ref
  126.1 0.1 announce.5
  126.2 14.1 %all_to_all.52.in_ref = f32[32,8,128]{2,1,0:T(8,128)S(1)} all-to-all(f32[32,8,128]{2,1,0:T(8,128)S(1)} %announce.5), channel_id=1, replica_groups=mesh['plan'=32,'layer'=8] {'plan'}, dimensions={0} | all-to-all | bytes 262144 | tf_op jit(solution)/shard_map/all_to_all | solution.py:358
  140.3 1.0 layer_sums.5
  141.2 11.6 %all_to_all.53.in_ref = f32[16,8,128]{2,1,0:T(8,128)S(1)} all-to-all(f32[16,8,128]{2,1,0:T(8,128)S(1)} %layer_sums.5), channel_id=1, replica_groups={{0,8,1,9,2,10,3,11,4,12,5,13,6,14,7,15},{16,24,17,25,18,26,19,27,20,28,..., dimensions={0} | all-to-all | bytes 131072 | tf_op jit(solution)/shard_map/all_to_all | solution.py:358
  152.9 0.8 finish.1
Async XLA Ops:
  0.6 36.7 %copy-start.3 = (s32[1,6]{1,0:T(1,128)S(1)}, s32[1,6]{1,0:T(1,128)}, u32[]{:S(2)}) copy-start(s32[1,6]{1,0:T(1,128)} %partners_ref.1) | copy-start | bytes 76
  0.6 36.7 %copy-start.1 = (f32[1,1,8,1024]{3,2,1,0:T(8,128)S(1)}, f32[1,1,8,1024]{3,2,1,0:T(8,128)}, u32[]{:S(2)}) copy-start(f32[1,1,8,1024]{3,2,1,0:T(8,128)} %param.8) | copy-start | bytes 98308
  0.7 57.3 %copy-start = (f32[1,1,8,1024]{3,2,1,0:T(8,128)S(1)}, f32[1,1,8,1024]{3,2,1,0:T(8,128)}, u32[]{:S(2)}) copy-start(f32[1,1,8,1024]{3,2,1,0:T(8,128)} %param.9) | copy-start | bytes 98308
  0.7 57.3 %copy-start.2 = (s32[1,1,1024]{2,1,0:T(1,128)S(1)}, s32[1,1,1024]{2,1,0:T(1,128)}, u32[]{:S(2)}) copy-start(s32[1,1,1024]{2,1,0:T(1,128)} %param.13) | copy-start | bytes 12292
  4.7 5.3 %collective-permute-start = (f32[24,128]{1,0:T(8,128)S(1)}, f32[24,128]{1,0:T(8,128)S(1)}, u32[]{:S(2)}, u32[]{:S(2)}) collective-permute-start(f32[24,128]{1,0:T(8,128)S(1)} %get-tuple-element.65), channel_id=1, source_target_pairs={{0,1},{1,2},{2,3},{3,4},{4,5},{5,6},{6,7},{8,9},{9,10},{10,11},{11... | collective-permute-start | bytes 36872 | tf_op jit(solution)/shard_map/ppermute | solution.py:365
  8.8 4.4 %collective-permute-start.1 = (f32[24,128]{1,0:T(8,128)S(1)}, f32[24,128]{1,0:T(8,128)S(1)}, u32[]{:S(2)}, u32[]{:S(2)}) collective-permute-start(f32[24,128]{1,0:T(8,128)S(1)} %get-tuple-element.66), channel_id=1, source_target_pairs={{1,0},{2,1},{3,2},{4,3},{5,4},{6,5},{7,6},{9,8},{10,9},{11,10},{12... | collective-permute-start | bytes 36872 | tf_op jit(solution)/shard_map/ppermute | solution.py:365
  58.4 3.8 %collective-permute-start.2 = (f32[8,128]{1,0:T(8,128)S(1)}, f32[8,128]{1,0:T(8,128)S(1)}, u32[]{:S(2)}, u32[]{:S(2)}) collective-permute-start(f32[8,128]{1,0:T(8,128)S(1)} %get-tuple-element.81.refs_2_), channel_id=1, source_target_pairs={{0,1},{1,2},{2,3},{3,4},{4,5},{5,6},{6,7},{8,9},{9,10},{10,11},{11... | collective-permute-start | bytes 12296 | tf_op jit(solution)/shard_map/ppermute | solution.py:365
  90.6 3.7 %collective-permute-start.3 = (f32[8,128]{1,0:T(8,128)S(1)}, f32[8,128]{1,0:T(8,128)S(1)}, u32[]{:S(2)}, u32[]{:S(2)}) collective-permute-start(f32[8,128]{1,0:T(8,128)S(1)} %get-tuple-element.95.refs_2_), channel_id=1, source_target_pairs={{0,1},{1,2},{2,3},{3,4},{4,5},{5,6},{6,7},{8,9},{9,10},{10,11},{11... | collective-permute-start | bytes 12296 | tf_op jit(solution)/shard_map/ppermute | solution.py:365
  122.3 3.7 %collective-permute-start.4 = (f32[8,128]{1,0:T(8,128)S(1)}, f32[8,128]{1,0:T(8,128)S(1)}, u32[]{:S(2)}, u32[]{:S(2)}) collective-permute-start(f32[8,128]{1,0:T(8,128)S(1)} %get-tuple-element.107.refs_2_), channel_id=1, source_target_pairs={{0,1},{1,2},{2,3},{3,4},{4,5},{5,6},{6,7},{8,9},{9,10},{10,11},{11... | collective-permute-start | bytes 12296 | tf_op jit(solution)/shard_map/ppermute | solution.py:365

commit v7 on v6

--- a/solution.py
+++ b/solution.py
@@ -1,3 +1,5 @@
+import functools
+
 import jax
 import jax.numpy as jnp
 from jax import lax
@@ -34,7 +36,7 @@
         out_shape=outs,
         in_specs=specs,
         scratch_shapes=scratch,
-        out_specs=jax.tree.map(lambda _: VMEM, outs),
+        out_specs=jax.tree.map(lambda out: VMEM if isinstance(out, jax.ShapeDtypeStruct) else HBM, outs),
         compiler_params=pltpu.CompilerParams(vmem_limit_bytes=limit * 2**20),
         cost_estimate=pl.CostEstimate(flops=flops, bytes_accessed=traffic, transcendentals=0),
     )
@@ -53,10 +55,12 @@
     return jnp.sum(value, axis=1, keepdims=True)
 
 
-def dense(field, halves_ref, columns=slice(None)):
+def dense(field, high_ref, low_ref, columns=slice(None), before_low=None):
     lhs = jnp.concatenate(pieces(field, 2), axis=0).astype(BF16)
-    total = jnp.dot(lhs, halves_ref[0, :, columns], preferred_element_type=F32)
-    total = total + jnp.dot(lhs, halves_ref[1, :, columns], preferred_element_type=F32)
+    total = jnp.dot(lhs, high_ref[:, columns], preferred_element_type=F32)
+    if before_low is not None:
+        before_low()
+    total = total + jnp.dot(lhs, low_ref[:, columns], preferred_element_type=F32)
     return total[:8] + total[8:]
 
 
@@ -82,7 +86,7 @@
     return total
 
 
-def stream_dense(field, block_ref, rows_ref, sems, keep):
+def stream_dense(field, block_ref, rows_ref, sems, high_ref, low_ref, give):
     lhs = jnp.concatenate(pieces(field, 2), axis=0).astype(BF16)
     depth = rows_ref.shape[0] // CHUNKS
     total = jnp.zeros((lhs.shape[0], rows_ref.shape[1]), F32)
@@ -92,22 +96,24 @@
         rows = rows_ref[at, :]
         high = rows.astype(BF16)
         low = (rows - high.astype(F32)).astype(BF16)
-        keep[0, at, :] = high
-        keep[1, at, :] = low
+        high_ref[at, :] = high
+        low_ref[at, :] = low
+        give(chunk).start()
         total = total + jnp.dot(lhs[:, at], high, preferred_element_type=F32)
         total = total + jnp.dot(lhs[:, at], low, preferred_element_type=F32)
     return total[:8] + total[8:]
 
 
-def chunk_copy(block_ref, rows_ref, sems, chunk):
-    depth = rows_ref.shape[0] // CHUNKS
+def chunk_copy(source_ref, target_ref, sems, chunk):
+    depth = source_ref.shape[0] // CHUNKS
     at = pl.ds(chunk * depth, depth)
-    return pltpu.make_async_copy(block_ref.at[at, :], rows_ref.at[at, :], sems.at[chunk])
+    return pltpu.make_async_copy(source_ref.at[at, :], target_ref.at[at, :], sems.at[chunk])
 
 
 def prepare(block_ref, x_hbm, load_hbm, contact_hbm, rows_hbm, partners_hbm, counts_hbm,
-            onehot_ref, valid_ref, own_ref, hown_ref, h_ref, out_ref, first_ref, last_ref, halves_ref,
-            held_ref, x_ref, load_ref, contact_ref, rows_ref, partners_ref, counts_ref, sems, more_sems):
+            onehot_ref, valid_ref, own_ref, hown_ref, h_ref, out_ref, first_ref, last_ref, high_ref,
+            low_hbm, held_ref, low_ref, x_ref, load_ref, contact_ref, rows_ref, partners_ref, counts_ref,
+            sems, low_sems, more_sems):
     small = [
         pltpu.make_async_copy(source, target, more_sems.at[i])
         for i, (source, target) in enumerate((
@@ -142,7 +148,8 @@
     position = lax.broadcasted_iota(jnp.int32, x.shape, 1)
     edge = (position < FACE) | (position >= width - FACE)
     h = spread(valid * own, onehot) + jnp.where(edge, x, 0.0) - load_ref[...]
-    h = h + stream_dense(x, block_ref, held_ref, sems, halves_ref)
+    low_copy = functools.partial(chunk_copy, low_ref, low_hbm, low_sems)
+    h = h + stream_dense(x, block_ref, held_ref, sems, high_ref, low_ref, low_copy)
     h_ref[...] = h
     (hown,) = pick(h, onehot)
     hown_ref[...] = hown
@@ -159,12 +166,16 @@
     both = jnp.concatenate([x, h, contact], axis=0)
     first_ref[...] = both[:, :FACE]
     last_ref[...] = both[:, width - FACE :]
-
-
-def first_gradient(partners_ref, where_ref, halves_ref, x_ref, h_ref, own_ref, hown_ref, in_ref,
+    for chunk in range(CHUNKS):
+        low_copy(chunk).wait()
+
+
+def first_gradient(partners_ref, where_ref, low_hbm, high_ref, x_ref, h_ref, own_ref, hown_ref, in_ref,
                    below_in, above_in, valid_ref, onehot_ref,
                    g_ref, gown_ref, far_ref, gfar_ref, below_ref, gbelow_ref, above_ref, gabove_ref,
-                   all_ref, masks_ref):
+                   all_ref, masks_ref, low_ref, sem):
+    low_copy = pltpu.make_async_copy(low_hbm, low_ref, sem)
+    low_copy.start()
     width = x_ref.shape[1]
     place = lax.broadcasted_iota(jnp.int32, (8, LANES), 1) // JR
     parts = [[jnp.zeros((8, LANES), F32)] * 2 for _ in range(3)]
@@ -202,7 +213,8 @@
     jumps = valid * gown * (gown - gfar)
     terms = first * (first - gbelow) + last * (last - gabove) + jumps[:, :LANES] + jumps[:, LANES:]
     square = lane_sum(g * g)
-    curvature = lane_sum(terms) + lane_sum(g * dense(g, halves_ref))
+    image = dense(g, high_ref, low_ref, before_low=low_copy.wait)
+    curvature = lane_sum(terms) + lane_sum(g * image)
     lane = lax.broadcasted_iota(jnp.int32, (8, LANES), 1)
     row = lax.broadcasted_iota(jnp.int32, (8, LANES), 0)
     line = jnp.where(lane == row, square, 0.0) + jnp.where(lane == row + 8, curvature, 0.0)
@@ -214,11 +226,11 @@
     all_ref[...] = jnp.broadcast_to(line, all_ref.shape)
 
 
-def local_sums(g, halves_ref):
+def local_sums(g, high_ref, low_ref):
     width = g.shape[1]
     first, last = g[:, :FACE], g[:, width - FACE :]
     square = lane_sum(g * g)
-    curvature = lane_sum(g * dense(g, halves_ref)) + lane_sum(first * first + last * last)
+    curvature = lane_sum(g * dense(g, high_ref, low_ref)) + lane_sum(first * first + last * last)
     lane = lax.broadcasted_iota(jnp.int32, (8, LANES), 1)
     return jnp.where(lane == SQUARE, square, jnp.where(lane == CURVATURE, curvature, 0.0))
 
@@ -293,15 +305,16 @@
     face_by(step_of(in_ref), chosen(in_ref, masks_ref[0], slice(LANES, None)), *refs)
 
 
-def face_by(step, gabove, x_ref, g_ref, contact_ref, load_ref, above_ref, halves_ref,
-            x_out, last_out, step_out, above_out):
+def face_by(step, gabove, x_ref, g_ref, contact_ref, load_ref, above_ref, high_ref, low_ref,
+            x_out, last_out, step_out, *above_outs):
     x = moved(x_ref[...], g_ref[...], step, contact_ref[...])
     x_out[...] = x
     step_out[...] = jnp.broadcast_to(step, step_out.shape)
     above = moved(above_ref[:8], gabove, step, above_ref[8:])
-    above_out[...] = jnp.concatenate([above, above_ref[8:]], axis=0)
+    for above_out in above_outs:
+        above_out[...] = jnp.concatenate([above, above_ref[8:]], axis=0)
     at = slice(x.shape[1] - FACE, x.shape[1])
-    last_out[...] = dense(x, halves_ref, at) - load_ref[:, at] + (x[:, at] - above)
+    last_out[...] = dense(x, high_ref, low_ref, at) - load_ref[:, at] + (x[:, at] - above)
 
 
 def first_rest(in_ref, masks_ref, gfar_ref, *refs):
@@ -328,7 +341,7 @@
 
 
 def rest_by(gfar, step_ref, x_ref, last_ref, load_ref, own_ref, gown_ref, far_ref,
-            below_ref, gbelow_ref, valid_ref, onehot_ref, halves_ref,
+            below_ref, gbelow_ref, valid_ref, onehot_ref, high_ref, low_ref,
             g_out, gown_out, sums_out, *halo_outs):
     step, x = step_ref[:, :1], x_ref[...]
     inner = x.shape[1] - FACE
@@ -340,12 +353,12 @@
     own, far, below = halo
     onehot = onehot_ref[...]
     jumps = spread(valid_ref[...] * (own - far), onehot)
-    total = dense(x, halves_ref, slice(inner)) + jumps[:, :inner] - load_ref[:, :inner]
+    total = dense(x, high_ref, low_ref, slice(inner)) + jumps[:, :inner] - load_ref[:, :inner]
     head = total[:, :FACE] + (x[:, :FACE] - below)
     g = jnp.concatenate([head, total[:, FACE:], last_ref[...]], axis=1)
     g_out[...] = g
     gown_out[...] = pick(g, onehot)[0]
-    sums_out[...] = local_sums(g, halves_ref)
+    sums_out[...] = local_sums(g, high_ref, low_ref)
 
 
 def finish(in_ref, x_ref, g_ref, contact_ref, x_out, g_out):
@@ -382,41 +395,42 @@
         [(chip + core) * layers + layer for layer in range(layers) for core in range(2)]
         for chip in range(0, plans, 2)
     ]
+    half_shape = shape(width, width, dtype=BF16)
     held = pltpu.VMEM((width, width), F32)
     chunk_sems = pltpu.SemaphoreType.DMA((CHUNKS,))
 
-    onehot, valid, own, hown, h, out, first, last, halves = call(
+    onehot, valid, own, hown, h, out, first, last, high, low = call(
         prepare, "prepare",
         (shape(width, JW, dtype=BF16), jump, jump2, jump, field, shape(plans, loads, LANES), face3, face3,
-         shape(2, width, width, dtype=BF16)),
+         half_shape, pltpu.HBM(half_shape.shape, BF16)),
         [HBM] * 7, 16, flops, 4 * width * width,
         [
-            held, pltpu.VMEM(x.shape, F32), pltpu.VMEM(target.shape, F32),
+            held, pltpu.VMEM((width, width), BF16), pltpu.VMEM(x.shape, F32), pltpu.VMEM(target.shape, F32),
             pltpu.VMEM(flags.shape, jnp.int32), pltpu.VMEM(rows.shape, jnp.int32),
             pltpu.SMEM(partners.shape, jnp.int32), pltpu.SMEM(amounts.shape, jnp.int32),
-            chunk_sems, pltpu.SemaphoreType.DMA((6,)),
+            chunk_sems, chunk_sems, pltpu.SemaphoreType.DMA((6,)),
         ],
     )(*(pltpu.with_memory_space_constraint(a, pltpu.HBM) for a in (block, x, target, flags, rows, partners, amounts)))
-    below, above, out = lax.optimization_barrier((lift(last, 1), lift(first, -1), out))
     incoming = swap(out, "plan")
-    g, gown, far, gfar, below, gbelow, above, gabove, out, masks = call(
+    below, above = lift(last, 1), lift(first, -1)
+    g, gown, far, gfar, below, gbelow, above, gabove, out, masks, low = call(
         first_gradient, "first_gradient",
         (field, jump, jump2, jump, face2, face, face2, face,
-         shape(plans * layers, LANES), shape(3, 2 * layers, LANES)),
-        [SMEM] * 2 + [VMEM] * 10, 12, flops, 4 * width * width,
-    )(partners, position, halves, x, h, own, hown, incoming, below, above, valid, onehot)
+         shape(plans * layers, LANES), shape(3, 2 * layers, LANES), half_shape),
+        [SMEM] * 2 + [HBM] + [VMEM] * 10, 12, flops, 4 * width * width, [pltpu.SemaphoreType.DMA],
+    )(partners, position, pltpu.with_memory_space_constraint(low, pltpu.HBM), high, x, h, own, hown, incoming, below, above, valid, onehot)
     incoming = swap(out, ("plan", "layer"))
 
     early = (field, face, face, face2)
     x, last, step, above = call(
-        first_face, "first_face", early, [VMEM] * 8, 12, flops // 8, width * width // 2,
-    )(incoming, gabove, x, g, flags, target, above, halves)
+        first_face, "first_face", early, [VMEM] * 9, 12, flops // 8, width * width // 2,
+    )(incoming, gabove, x, g, flags, target, above, high, low)
     late = (field, jump, face, jump2, jump2, face2)
     below_next = lift(last, 1)
     g, gown, sums, own, far, below, table = call(
         first_rest, "first_rest", late + (shape(plans, 8, dtype=jnp.int32),),
-        [VMEM] * 15, 12, 2 * flops, 8 * width * width,
-    )(incoming, masks, gfar, step, x, last, target, own, gown, far, below, gbelow, valid, onehot, halves)
+        [VMEM] * 16, 12, 2 * flops, 8 * width * width,
+    )(incoming, masks, gfar, step, x, last, target, own, gown, far, below, gbelow, valid, onehot, high, low)
 
     for iteration in range(1, ITERS):
         gbelow = below_next
@@ -433,16 +447,16 @@
         if ending:
             x, g = call(finish, "finish", (field, field), [VMEM] * 4, 8)(incoming, x, g, flags)
             break
-        x, last, step, above = call(
-            next_face, "next_face", early, [VMEM] * 8, 12, flops // 8, width * width // 2,
-        )(incoming, masks, x, g, flags, target, above, halves)
+        x, last, step, *above = call(
+            next_face, "next_face", early[:3] if iteration == ITERS - 2 else early, [VMEM] * 9, 12, flops // 8, width * width // 2,
+        )(incoming, masks, x, g, flags, target, above, high, low)
         below_next = lift(last, 1)
         g, gown, sums, *halo = call(
             next_rest, "next_rest", late[:3] if iteration == ITERS - 2 else late,
-            [VMEM] * 15, 12, 2 * flops, 8 * width * width,
+            [VMEM] * 16, 12, 2 * flops, 8 * width * width,
         )(incoming, masks, *half, step, x, last, target, own, gown, far, below, gbelow,
-          valid, onehot, halves)
-        own, far, below = halo or (None,) * 3
+          valid, onehot, high, low)
+        (above,), (own, far, below) = above or (None,), halo or (None,) * 3
     return x[None, None], g[None, None]
 
 

time: 154 us -> 152 us (0.987)
  blocking collectives: 122 us -> 103 us
  starting transfers between devices: 11.8 us -> 23.5 us
  waiting for transfers between devices: 3.14 us -> 6.49 us
  Pallas kernels: 15.8 us -> 17.9 us
    all_to_all x8 -> x7, blocking collectives: 122 us -> 103 us  [swap(): lax.all_to_all(outgoing, axis, split_axis=0, concat_axis=0, tiled=True, a...]
    all_to_all x0 -> x1, starting transfers between devices: none -> 12.6 us  [swap(): lax.all_to_all(outgoing, axis, split_axis=0, concat_axis=0, tiled=True, a...]
    all_to_all x0 -> x1, waiting for transfers between devices: none -> 3.05 us  [swap(): lax.all_to_all(outgoing, axis, split_axis=0, concat_axis=0, tiled=True, a...]
    pallas_call x1, Pallas kernels: 1.47 us -> 3.11 us  [shards(): call(first_gradient, 'first_gradient', (field, jump, jump2, jump, face2,...]
  transfers between devices with their start and end apart: 5 -> 6, of which waited for: 1 -> 2; matrix products, arithmetic and copies ran while one was open for 0% -> 0% of each run, Pallas kernels for 3% -> 3%
where the time goes in v7:
time: 152 us
  blocking collectives  103 us (68%)
  starting transfers between devices  23.5 us (15%)
  Pallas kernels  17.9 us (12%)
  waiting for transfers between devices  6.49 us (4%)
    all_to_all x7, blocking collectives, swap(): lax.all_to_all(outgoing, axis, split_axis=0, concat_axis=0, tiled=True, a...  103 us
    all_to_all x1, starting transfers between devices, swap(): lax.all_to_all(outgoing, axis, split_axis=0, concat_axis=0, tiled=True, a...  12.6 us
    ppermute x5, starting transfers between devices, lift(): lax.ppermute(face, 'layer', [(i, i + step) for i in range(layers) if 0 <=...  10.9 us
    pallas_call x1, Pallas kernels, shards(): call(prepare, 'prepare', (shape(width, JW, dtype=BF16), jump, jump2, jump...  4.87 us
    ppermute x5, waiting for transfers between devices, lift(): lax.ppermute(face, 'layer', [(i, i + step) for i in range(layers) if 0 <=...  3.43 us
    pallas_call x2, Pallas kernels, shards(): call(next_rest, 'next_rest', late[:3] if iteration == ITERS - 2 else late...  3.21 us
    pallas_call x1, Pallas kernels, shards(): call(first_gradient, 'first_gradient', (field, jump, jump2, jump, face2,...  3.11 us
    all_to_all x1, waiting for transfers between devices, swap(): lax.all_to_all(outgoing, axis, split_axis=0, concat_axis=0, tiled=True, a...  3.05 us
  transfers between devices with their start and end apart: 6, of which 2 were waited for; matrix products, arithmetic and copies ran while one was open for 0% of the time, Pallas kernels for 3%

profile of v7, /device:TPU:1, one launch (start us, length us, event | category | flops | bytes accessed | tf_op | source)
XLA Modules:
  0.0 151.9 jit_solution(18370117117606053416)
XLA Ops:
  0.6 0.1 add_bitcast_fusion.where_ref
  0.7 0.0 copy-start.1
  0.7 0.0 copy-start.3
  0.7 4.9 %prepare.1 = (bf16[1024,256]{1,0:T(8,128)(2,1)S(1)}, f32[8,256]{1,0:T(8,128)S(1)}, f32[16,256]{1,0:T(8,128)S(1)}, f32[8,256]{1,0:T(8,128)S(1)}, f32[8,1024]{1,0:...) custom-call(f32[1024,1024]{1,0:T(8,128)} %bitcast.34, ...), custom_call_target="tpu_custom_call" | custom-call | flops 67108864 | bytes 4194304 | tf_op jit(solution)/shard_map/prepare/pallas_call | solution.py:402
  5.6 12.6 %all-to-all-start = ((f32[32,8,128]{2,1,0:T(8,128)}), f32[32,8,128]{2,1,0:T(8,128)S(1)}, u32[]{:S(2)}, u32[]{:S(2)}) async-start(f32[32,8,128]{2,1,0:T(8,128)} %get-tuple-element.65), calls=%async_computation | async-start | bytes 262144 | tf_op jit(solution)/shard_map/all_to_all | solution.py:371
  18.2 3.2 %collective-permute-start = (f32[24,128]{1,0:T(8,128)S(1)}, f32[24,128]{1,0:T(8,128)S(1)}, u32[]{:S(2)}, u32[]{:S(2)}) collective-permute-start(f32[24,128]{1,0:T(8,128)S(1)} %get-tuple-element.66), channel_id=1, source_target_pairs={{0,1},{1,2},{2,3},{3,4},{4,5},{5,6},{6,7},{8,9},{9,10},{10,11},{11... | collective-permute-start | bytes 36872 | tf_op jit(solution)/shard_map/ppermute | solution.py:378
  21.4 1.3 collective-permute-start.1
  22.7 0.0 collective-permute-done.below_in
  22.7 3.4 %collective-permute-done.1.above_in = f32[24,128]{1,0:T(8,128)S(1)} collective-permute-done((f32[24,128]{1,0:T(8,128)S(1)}, f32[24,128]{1,0:T(8,128)S(1)}, u32[]{:S(2)}, u32[]{:S(2)}) %collective-permute-start.1) | collective-permute-done | bytes 12320 | tf_op jit(solution)/shard_map/ppermute | solution.py:378
  26.1 3.1 %all-to-all-done.in_ref = f32[32,8,128]{2,1,0:T(8,128)S(1)} async-done(((f32[32,8,128]{2,1,0:T(8,128)}), f32[32,8,128]{2,1,0:T(8,128)S(1)}, u32[]{:S(2)}, u32[]{:S(2)}) %all-to-all-start) | async-done | bytes 131104 | tf_op jit(solution)/shard_map/all_to_all | solution.py:371
  29.2 0.0 copy-done.1
  29.2 0.0 copy-done.3
  29.2 0.0 copy-start
  29.2 0.0 copy-start.2
  29.2 3.1 %first_gradient.1 = (f32[8,1024]{1,0:T(8,128)S(1)}, f32[8,256]{1,0:T(8,128)S(1)}, f32[16,256]{1,0:T(8,128)S(1)}, f32[8,256]{1,0:T(8,128)S(1)}, f32[16,128]{1,0:T...) custom-call(s32[1,6]{1,0:T(1,128)S(1)} %copy-done.3, ...), custom_call_target="tpu_custom_call" | custom-call | flops 67108864 | bytes 4194304 | tf_op jit(solution)/shard_map/first_gradient/pallas_call | solution.py:416
  32.3 24.4 %all_to_all.46 = f32[256,1,128]{2,1,0:T(1,128)S(1)} all-to-all(f32[256,1,128]{2,1,0:T(1,128)S(1)} %bitcast.28), channel_id=1, replica_groups=mesh['plan'=32,'layer'=8] {'plan','layer'}, dimensions={0} | all-to-all | bytes 262144 | tf_op jit(solution)/shard_map/all_to_all | solution.py:371
  56.7 0.0 copy-done
  56.7 0.0 copy-done.2
  56.7 0.3 first_face.1
  57.1 2.2 %collective-permute-start.2 = (f32[8,128]{1,0:T(8,128)S(1)}, f32[8,128]{1,0:T(8,128)S(1)}, u32[]{:S(2)}, u32[]{:S(2)}) collective-permute-start(f32[8,128]{1,0:T(8,128)S(1)} %get-tuple-element.79.refs_2_), channel_id=1, source_target_pairs={{0,1},{1,2},{2,3},{3,4},{4,5},{5,6},{6,7},{8,9},{9,10},{10,11},{11... | collective-permute-start | bytes 12296 | tf_op jit(solution)/shard_map/ppermute | solution.py:378
  59.3 1.6 %first_rest.1 = (f32[8,1024]{1,0:T(8,128)S(1)}, f32[8,256]{1,0:T(8,128)S(1)}, f32[8,128]{1,0:T(8,128)S(1)}, f32[16,256]{1,0:T(8,128)S(1)}, f32[16,256]{1,0:T(8,1...) custom-call(f32[256,128]{1,0:T(8,128)S(1)} %bitcast.24, f32[3,16,128]{2,1,0:T(8,128)S(1)} %get-tuple-element.71.masks_ref, ...), custom_call_target="tpu_custom_call" | custom-call | flops 134217728 | bytes 8388608 | tf_op jit(solution)/shard_map/first_rest/pallas_call | solution.py:430
  60.9 0.0 collective-permute-done.2.below_ref.refs_8_
  60.9 0.1 announce.3
  61.0 15.0 %all_to_all.47.in_ref = f32[32,8,128]{2,1,0:T(8,128)S(1)} all-to-all(f32[32,8,128]{2,1,0:T(8,128)S(1)} %announce.3), channel_id=1, replica_groups=mesh['plan'=32,'layer'=8] {'plan'}, dimensions={0} | all-to-all | bytes 262144 | tf_op jit(solution)/shard_map/all_to_all | solution.py:371
  76.1 1.0 layer_sums.3
  77.0 11.9 %all_to_all.48.in_ref = f32[16,8,256]{2,1,0:T(8,128)S(1)} all-to-all(f32[16,8,256]{2,1,0:T(8,128)S(1)} %get-tuple-element.88), channel_id=1, replica_groups={{0,8,1,9,2,10,3,11,4,12,5,13,6,14,7,15},{16,24,17,25,18,26,19,27,20,28,..., dimensions={0} | all-to-all | bytes 262144 | tf_op jit(solution)/shard_map/all_to_all | solution.py:371
  89.0 0.4 next_face.2
  89.3 2.1 %collective-permute-start.3 = (f32[8,128]{1,0:T(8,128)S(1)}, f32[8,128]{1,0:T(8,128)S(1)}, u32[]{:S(2)}, u32[]{:S(2)}) collective-permute-start(f32[8,128]{1,0:T(8,128)S(1)} %get-tuple-element.93.refs_2_), channel_id=1, source_target_pairs={{0,1},{1,2},{2,3},{3,4},{4,5},{5,6},{6,7},{8,9},{9,10},{10,11},{11... | collective-permute-start | bytes 12296 | tf_op jit(solution)/shard_map/ppermute | solution.py:378
  91.5 1.6 %next_rest.2 = (f32[8,1024]{1,0:T(8,128)S(1)}, f32[8,256]{1,0:T(8,128)S(1)}, f32[8,128]{1,0:T(8,128)S(1)}, f32[16,256]{1,0:T(8,128)S(1)}, f32[16,256]{1,0:T(8,128)S(1)}, /*index=5*/f32[16,128]{1,0:T(8,128)S(1)}) custom-call(f32[16,8,256]{2,1,0:T(8,128)S(1)} %all_to_all.48.in_ref, f32[3,16,128]{2,1,0:T(8,128)S(1)} %get-tuple-element.71.masks_ref, ...), custom_call_target="tpu_custom_call" | custom-call | flops 134217728 | bytes 8388608 | tf_op jit(solution)/shard_map/next_rest/pallas_call | solution.py:454
  93.1 0.0 collective-permute-done.3.below_ref.refs_8_
  93.1 0.1 announce.4
  93.2 14.1 %all_to_all.49.in_ref = f32[32,8,128]{2,1,0:T(8,128)S(1)} all-to-all(f32[32,8,128]{2,1,0:T(8,128)S(1)} %announce.4), channel_id=1, replica_groups=mesh['plan'=32,'layer'=8] {'plan'}, dimensions={0} | all-to-all | bytes 262144 | tf_op jit(solution)/shard_map/all_to_all | solution.py:371
  107.3 1.0 layer_sums.4
  108.3 11.9 %all_to_all.50.in_ref = f32[16,8,256]{2,1,0:T(8,128)S(1)} all-to-all(f32[16,8,256]{2,1,0:T(8,128)S(1)} %get-tuple-element.100), channel_id=1, replica_groups={{0,8,1,9,2,10,3,11,4,12,5,13,6,14,7,15},{16,24,17,25,18,26,19,27,20,28,..., dimensions={0} | all-to-all | bytes 262144 | tf_op jit(solution)/shard_map/all_to_all | solution.py:371
  120.2 0.4 next_face.3
  120.6 2.1 %collective-permute-start.4 = (f32[8,128]{1,0:T(8,128)S(1)}, f32[8,128]{1,0:T(8,128)S(1)}, u32[]{:S(2)}, u32[]{:S(2)}) collective-permute-start(f32[8,128]{1,0:T(8,128)S(1)} %get-tuple-element.105.refs_2_), channel_id=1, source_target_pairs={{0,1},{1,2},{2,3},{3,4},{4,5},{5,6},{6,7},{8,9},{9,10},{10,11},{11... | collective-permute-start | bytes 12296 | tf_op jit(solution)/shard_map/ppermute | solution.py:378
  122.7 1.6 %next_rest.3 = (f32[8,1024]{1,0:T(8,128)S(1)}, f32[8,256]{1,0:T(8,128)S(1)}, f32[8,128]{1,0:T(8,128)S(1)}) custom-call(f32[16,8,256]{2,1,0:T(8,128)S(1)} %all_to_all.50.in_ref, f32[3,16,128]{2,1,0:T(8,128)S(1)} %get-tuple-element.71.masks_ref, f32[8,128]{1,0:T(8,128)S(1)} %get-tuple-element.101.half_ref, f32[8,128]{1,0:T(8,128)S(1)} %get-tuple-element.103.refs_0_, ...), custom_call_target="tpu_custom_call" | custom-call | flops 134217728 | bytes 8388608 | tf_op jit(solution)/shard_map/next_rest/pallas_call | solution.py:454
  124.3 0.0 collective-permute-done.4.below_ref
  124.3 0.1 announce.5
  124.4 14.1 %all_to_all.51.in_ref = f32[32,8,128]{2,1,0:T(8,128)S(1)} all-to-all(f32[32,8,128]{2,1,0:T(8,128)S(1)} %announce.5), channel_id=1, replica_groups=mesh['plan'=32,'layer'=8] {'plan'}, dimensions={0} | all-to-all | bytes 262144 | tf_op jit(solution)/shard_map/all_to_all | solution.py:371
  138.5 1.0 layer_sums.5
  139.5 11.6 %all_to_all.52.in_ref = f32[16,8,128]{2,1,0:T(8,128)S(1)} all-to-all(f32[16,8,128]{2,1,0:T(8,128)S(1)} %layer_sums.5), channel_id=1, replica_groups={{0,8,1,9,2,10,3,11,4,12,5,13,6,14,7,15},{16,24,17,25,18,26,19,27,20,28,..., dimensions={0} | all-to-all | bytes 131072 | tf_op jit(solution)/shard_map/all_to_all | solution.py:371
  151.1 0.8 finish.1
Async XLA Ops:
  0.7 28.5 %copy-start.1 = (f32[1,1,8,1024]{3,2,1,0:T(8,128)S(1)}, f32[1,1,8,1024]{3,2,1,0:T(8,128)}, u32[]{:S(2)}) copy-start(f32[1,1,8,1024]{3,2,1,0:T(8,128)} %param.8) | copy-start | bytes 98308
  0.7 28.5 %copy-start.3 = (s32[1,6]{1,0:T(1,128)S(1)}, s32[1,6]{1,0:T(1,128)}, u32[]{:S(2)}) copy-start(s32[1,6]{1,0:T(1,128)} %partners_ref.1) | copy-start | bytes 76
  5.6 23.6 %all-to-all-start = ((f32[32,8,128]{2,1,0:T(8,128)}), f32[32,8,128]{2,1,0:T(8,128)S(1)}, u32[]{:S(2)}, u32[]{:S(2)}) async-start(f32[32,8,128]{2,1,0:T(8,128)} %get-tuple-element.65), calls=%async_computation | async-start | bytes 262144 | tf_op jit(solution)/shard_map/all_to_all | solution.py:371
  18.2 4.5 %collective-permute-start = (f32[24,128]{1,0:T(8,128)S(1)}, f32[24,128]{1,0:T(8,128)S(1)}, u32[]{:S(2)}, u32[]{:S(2)}) collective-permute-start(f32[24,128]{1,0:T(8,128)S(1)} %get-tuple-element.66), channel_id=1, source_target_pairs={{0,1},{1,2},{2,3},{3,4},{4,5},{5,6},{6,7},{8,9},{9,10},{10,11},{11... | collective-permute-start | bytes 36872 | tf_op jit(solution)/shard_map/ppermute | solution.py:378
  21.4 4.7 %collective-permute-start.1 = (f32[24,128]{1,0:T(8,128)S(1)}, f32[24,128]{1,0:T(8,128)S(1)}, u32[]{:S(2)}, u32[]{:S(2)}) collective-permute-start(f32[24,128]{1,0:T(8,128)S(1)} %get-tuple-element.67), channel_id=1, source_target_pairs={{1,0},{2,1},{3,2},{4,3},{5,4},{6,5},{7,6},{9,8},{10,9},{11,10},{12... | collective-permute-start | bytes 36872 | tf_op jit(solution)/shard_map/ppermute | solution.py:378
  29.2 27.5 %copy-start = (f32[1,1,8,1024]{3,2,1,0:T(8,128)S(1)}, f32[1,1,8,1024]{3,2,1,0:T(8,128)}, u32[]{:S(2)}) copy-start(f32[1,1,8,1024]{3,2,1,0:T(8,128)} %param.9) | copy-start | bytes 98308
  29.2 27.5 %copy-start.2 = (s32[1,1,1024]{2,1,0:T(1,128)S(1)}, s32[1,1,1024]{2,1,0:T(1,128)}, u32[]{:S(2)}) copy-start(s32[1,1,1024]{2,1,0:T(1,128)} %param.13) | copy-start | bytes 12292
  57.1 3.8 %collective-permute-start.2 = (f32[8,128]{1,0:T(8,128)S(1)}, f32[8,128]{1,0:T(8,128)S(1)}, u32[]{:S(2)}, u32[]{:S(2)}) collective-permute-start(f32[8,128]{1,0:T(8,128)S(1)} %get-tuple-element.79.refs_2_), channel_id=1, source_target_pairs={{0,1},{1,2},{2,3},{3,4},{4,5},{5,6},{6,7},{8,9},{9,10},{10,11},{11... | collective-permute-start | bytes 12296 | tf_op jit(solution)/shard_map/ppermute | solution.py:378
  89.3 3.8 %collective-permute-start.3 = (f32[8,128]{1,0:T(8,128)S(1)}, f32[8,128]{1,0:T(8,128)S(1)}, u32[]{:S(2)}, u32[]{:S(2)}) collective-permute-start(f32[8,128]{1,0:T(8,128)S(1)} %get-tuple-element.93.refs_2_), channel_id=1, source_target_pairs={{0,1},{1,2},{2,3},{3,4},{4,5},{5,6},{6,7},{8,9},{9,10},{10,11},{11... | collective-permute-start | bytes 12296 | tf_op jit(solution)/shard_map/ppermute | solution.py:378
  120.6 3.7 %collective-permute-start.4 = (f32[8,128]{1,0:T(8,128)S(1)}, f32[8,128]{1,0:T(8,128)S(1)}, u32[]{:S(2)}, u32[]{:S(2)}) collective-permute-start(f32[8,128]{1,0:T(8,128)S(1)} %get-tuple-element.105.refs_2_), channel_id=1, source_target_pairs={{0,1},{1,2},{2,3},{3,4},{4,5},{5,6},{6,7},{8,9},{9,10},{10,11},{11... | collective-permute-start | bytes 12296 | tf_op jit(solution)/shard_map/ppermute | solution.py:378

commit v8 on v7

--- a/solution.py
+++ b/solution.py
@@ -1,5 +1,3 @@
-import functools
-
 import jax
 import jax.numpy as jnp
 from jax import lax
@@ -15,6 +13,7 @@
 HALF = 3
 JW = 2 * LANES
 CHUNKS = 4
+LOW_CHUNKS = 8
 NAMES = 16
 SQUARE, CURVATURE = HALF * JR, HALF * JR + 1
 F32 = jnp.float32
@@ -55,11 +54,11 @@
     return jnp.sum(value, axis=1, keepdims=True)
 
 
-def dense(field, high_ref, low_ref, columns=slice(None), before_low=None):
+def dense(field, high_ref, low_ref, columns=slice(None), copies=()):
     lhs = jnp.concatenate(pieces(field, 2), axis=0).astype(BF16)
     total = jnp.dot(lhs, high_ref[:, columns], preferred_element_type=F32)
-    if before_low is not None:
-        before_low()
+    for copy in copies:
+        copy.wait()
     total = total + jnp.dot(lhs, low_ref[:, columns], preferred_element_type=F32)
     return total[:8] + total[8:]
 
@@ -86,45 +85,47 @@
     return total
 
 
-def stream_dense(field, block_ref, rows_ref, sems, high_ref, low_ref, give):
+def stream_dense(field, block_ref, rows_ref, sems, high_ref, low_ref):
     lhs = jnp.concatenate(pieces(field, 2), axis=0).astype(BF16)
     depth = rows_ref.shape[0] // CHUNKS
     total = jnp.zeros((lhs.shape[0], rows_ref.shape[1]), F32)
     for chunk in range(CHUNKS):
         at = slice(chunk * depth, (chunk + 1) * depth)
-        chunk_copy(block_ref, rows_ref, sems, chunk).wait()
+        chunk_copy(block_ref, rows_ref, sems, chunk, CHUNKS).wait()
         rows = rows_ref[at, :]
         high = rows.astype(BF16)
         low = (rows - high.astype(F32)).astype(BF16)
         high_ref[at, :] = high
         low_ref[at, :] = low
-        give(chunk).start()
         total = total + jnp.dot(lhs[:, at], high, preferred_element_type=F32)
         total = total + jnp.dot(lhs[:, at], low, preferred_element_type=F32)
     return total[:8] + total[8:]
 
 
-def chunk_copy(source_ref, target_ref, sems, chunk):
-    depth = source_ref.shape[0] // CHUNKS
+def chunk_copy(source_ref, target_ref, sems, chunk, chunks):
+    depth = source_ref.shape[0] // chunks
     at = pl.ds(chunk * depth, depth)
     return pltpu.make_async_copy(source_ref.at[at, :], target_ref.at[at, :], sems.at[chunk])
 
 
-def prepare(block_ref, x_hbm, load_hbm, contact_hbm, rows_hbm, partners_hbm, counts_hbm,
-            onehot_ref, valid_ref, own_ref, hown_ref, h_ref, out_ref, first_ref, last_ref, high_ref,
-            low_hbm, held_ref, low_ref, x_ref, load_ref, contact_ref, rows_ref, partners_ref, counts_ref,
-            sems, low_sems, more_sems):
+def low_copies(source_ref, target_ref, sems):
+    return [chunk_copy(source_ref, target_ref, sems, chunk, LOW_CHUNKS) for chunk in range(LOW_CHUNKS)]
+
+
+def prepare(block_ref, x_hbm, load_hbm, contact_hbm, rows_hbm, counts_hbm,
+            onehot_ref, valid_ref, own_ref, h_ref, first_ref, last_ref, high_ref, low_ref,
+            held_ref, x_ref, load_ref, contact_ref, rows_ref, counts_ref, sems, more_sems):
     small = [
         pltpu.make_async_copy(source, target, more_sems.at[i])
         for i, (source, target) in enumerate((
             (rows_hbm, rows_ref), (counts_hbm, counts_ref), (x_hbm, x_ref),
-            (contact_hbm, contact_ref), (partners_hbm, partners_ref), (load_hbm, load_ref),
+            (contact_hbm, contact_ref), (load_hbm, load_ref),
         ))
     ]
     for copy in small:
         copy.start()
     for chunk in range(CHUNKS):
-        chunk_copy(block_ref, held_ref, sems, chunk).start()
+        chunk_copy(block_ref, held_ref, sems, chunk, CHUNKS).start()
     for copy in small:
         copy.wait()
     x = x_ref[...]
@@ -148,11 +149,24 @@
     position = lax.broadcasted_iota(jnp.int32, x.shape, 1)
     edge = (position < FACE) | (position >= width - FACE)
     h = spread(valid * own, onehot) + jnp.where(edge, x, 0.0) - load_ref[...]
-    low_copy = functools.partial(chunk_copy, low_ref, low_hbm, low_sems)
-    h = h + stream_dense(x, block_ref, held_ref, sems, high_ref, low_ref, low_copy)
+    h = h + stream_dense(x, block_ref, held_ref, sems, high_ref, low_ref)
     h_ref[...] = h
-    (hown,) = pick(h, onehot)
+    both = jnp.concatenate([x, h, contact], axis=0)
+    first_ref[...] = both[:, :FACE]
+    last_ref[...] = both[:, width - FACE :]
+
+
+def address(partners_hbm, own_ref, h_ref, onehot_ref, low_ref,
+            hown_ref, out_ref, low_hbm, partners_ref, sem, low_sems):
+    names = pltpu.make_async_copy(partners_hbm, partners_ref, sem)
+    names.start()
+    copies = low_copies(low_ref, low_hbm, low_sems)
+    for copy in copies:
+        copy.start()
+    own, own_contact = own_ref[:8], own_ref[8:]
+    (hown,) = pick(h_ref[...], onehot_ref[...])
     hown_ref[...] = hown
+    names.wait()
     out_ref[...] = jnp.zeros_like(out_ref)
     place = lax.broadcasted_iota(jnp.int32, (8, LANES), 1) // JR
     for r in range(ROUNDS):
@@ -163,19 +177,17 @@
             block = pltpu.roll(jump[:, at], (i * JR) % LANES, 1) if i else jump[:, at]
             parcel = jnp.where(place == (slot + i) % (LANES // JR), block, parcel)
         out_ref[partners_ref[0, r]] = parcel
-    both = jnp.concatenate([x, h, contact], axis=0)
-    first_ref[...] = both[:, :FACE]
-    last_ref[...] = both[:, width - FACE :]
-    for chunk in range(CHUNKS):
-        low_copy(chunk).wait()
+    for copy in copies:
+        copy.wait()
 
 
 def first_gradient(partners_ref, where_ref, low_hbm, high_ref, x_ref, h_ref, own_ref, hown_ref, in_ref,
                    below_in, above_in, valid_ref, onehot_ref,
                    g_ref, gown_ref, far_ref, gfar_ref, below_ref, gbelow_ref, above_ref, gabove_ref,
-                   all_ref, masks_ref, low_ref, sem):
-    low_copy = pltpu.make_async_copy(low_hbm, low_ref, sem)
-    low_copy.start()
+                   all_ref, masks_ref, low_ref, sems):
+    copies = low_copies(low_hbm, low_ref, sems)
+    for copy in copies:
+        copy.start()
     width = x_ref.shape[1]
     place = lax.broadcasted_iota(jnp.int32, (8, LANES), 1) // JR
     parts = [[jnp.zeros((8, LANES), F32)] * 2 for _ in range(3)]
@@ -213,7 +225,7 @@
     jumps = valid * gown * (gown - gfar)
     terms = first * (first - gbelow) + last * (last - gabove) + jumps[:, :LANES] + jumps[:, LANES:]
     square = lane_sum(g * g)
-    image = dense(g, high_ref, low_ref, before_low=low_copy.wait)
+    image = dense(g, high_ref, low_ref, copies=copies)
     curvature = lane_sum(terms) + lane_sum(g * image)
     lane = lax.broadcasted_iota(jnp.int32, (8, LANES), 1)
     row = lax.broadcasted_iota(jnp.int32, (8, LANES), 0)
@@ -397,28 +409,36 @@
     ]
     half_shape = shape(width, width, dtype=BF16)
     held = pltpu.VMEM((width, width), F32)
-    chunk_sems = pltpu.SemaphoreType.DMA((CHUNKS,))
-
-    onehot, valid, own, hown, h, out, first, last, high, low = call(
+
+    low_sems = pltpu.SemaphoreType.DMA((LOW_CHUNKS,))
+    hbm = lambda *arrays: tuple(pltpu.with_memory_space_constraint(a, pltpu.HBM) for a in arrays)
+
+    onehot, valid, own, h, first, last, high, low = call(
         prepare, "prepare",
-        (shape(width, JW, dtype=BF16), jump, jump2, jump, field, shape(plans, loads, LANES), face3, face3,
-         half_shape, pltpu.HBM(half_shape.shape, BF16)),
-        [HBM] * 7, 16, flops, 4 * width * width,
+        (shape(width, JW, dtype=BF16), jump, jump2, field, face3, face3, half_shape, half_shape),
+        [HBM] * 6, 16, flops, 4 * width * width,
         [
-            held, pltpu.VMEM((width, width), BF16), pltpu.VMEM(x.shape, F32), pltpu.VMEM(target.shape, F32),
+            held, pltpu.VMEM(x.shape, F32), pltpu.VMEM(target.shape, F32),
             pltpu.VMEM(flags.shape, jnp.int32), pltpu.VMEM(rows.shape, jnp.int32),
-            pltpu.SMEM(partners.shape, jnp.int32), pltpu.SMEM(amounts.shape, jnp.int32),
-            chunk_sems, chunk_sems, pltpu.SemaphoreType.DMA((6,)),
+            pltpu.SMEM(amounts.shape, jnp.int32), pltpu.SemaphoreType.DMA((CHUNKS,)),
+            pltpu.SemaphoreType.DMA((5,)),
         ],
-    )(*(pltpu.with_memory_space_constraint(a, pltpu.HBM) for a in (block, x, target, flags, rows, partners, amounts)))
+    )(*hbm(block, x, target, flags, rows, amounts))
+    below, above = lift(last, 1), lift(first, -1)
+    below, h_then = lax.optimization_barrier((below, h))
+    hown, out, low = call(
+        address, "address",
+        (jump, shape(plans, loads, LANES), pltpu.HBM(half_shape.shape, BF16)),
+        [HBM] + [VMEM] * 4, 8, 2**28, 4 * width * width,
+        [pltpu.SMEM(partners.shape, jnp.int32), pltpu.SemaphoreType.DMA, low_sems],
+    )(*hbm(partners), own, h_then, onehot, low)
     incoming = swap(out, "plan")
-    below, above = lift(last, 1), lift(first, -1)
     g, gown, far, gfar, below, gbelow, above, gabove, out, masks, low = call(
         first_gradient, "first_gradient",
         (field, jump, jump2, jump, face2, face, face2, face,
          shape(plans * layers, LANES), shape(3, 2 * layers, LANES), half_shape),
-        [SMEM] * 2 + [HBM] + [VMEM] * 10, 12, flops, 4 * width * width, [pltpu.SemaphoreType.DMA],
-    )(partners, position, pltpu.with_memory_space_constraint(low, pltpu.HBM), high, x, h, own, hown, incoming, below, above, valid, onehot)
+        [SMEM] * 2 + [HBM] + [VMEM] * 10, 12, flops, 4 * width * width, [low_sems],
+    )(partners, position, *hbm(low), high, x, h, own, hown, incoming, below, above, valid, onehot)
     incoming = swap(out, ("plan", "layer"))
 
     early = (field, face, face, face2)

time: 152 us -> 156 us (1.026)
  waiting for transfers between devices: 6.49 us -> 10.2 us
    all_to_all x1, waiting for transfers between devices: 3.05 us -> 5.35 us  [swap(): lax.all_to_all(outgoing, axis, split_axis=0, concat_axis=0, tiled=True, a...]
    pallas_call x1 -> x2, Pallas kernels: 4.87 us -> 5.54 us  [the longest x1 3.41 us: shards(): call(prepare, 'prepare', (shape(width, JW, dtype=BF16), jump, jump2, fiel...]
  transfers between devices with their start and end apart: 6 -> 6, of which waited for: 2 -> 3; matrix products, arithmetic and copies ran while one was open for 0% -> 0% of each run, Pallas kernels for 3% -> 3%
where the time goes in v8:
time: 156 us
  blocking collectives  102 us (65%)
  starting transfers between devices  24.4 us (16%)
  Pallas kernels  18.5 us (12%)
  waiting for transfers between devices  10.2 us (7%)
    all_to_all x7, blocking collectives, swap(): lax.all_to_all(outgoing, axis, split_axis=0, concat_axis=0, tiled=True, a...  102 us
    all_to_all x1, starting transfers between devices, swap(): lax.all_to_all(outgoing, axis, split_axis=0, concat_axis=0, tiled=True, a...  12.6 us
    ppermute x5, starting transfers between devices, lift(): lax.ppermute(face, 'layer', [(i, i + step) for i in range(layers) if 0 <=...  11.8 us
    all_to_all x1, waiting for transfers between devices, swap(): lax.all_to_all(outgoing, axis, split_axis=0, concat_axis=0, tiled=True, a...  5.35 us
    ppermute x5, waiting for transfers between devices, lift(): lax.ppermute(face, 'layer', [(i, i + step) for i in range(layers) if 0 <=...  4.81 us
    pallas_call x1, Pallas kernels, shards(): call(prepare, 'prepare', (shape(width, JW, dtype=BF16), jump, jump2, fiel...  3.41 us
    pallas_call x2, Pallas kernels, shards(): call(next_rest, 'next_rest', late[:3] if iteration == ITERS - 2 else late...  3.21 us
  transfers between devices with their start and end apart: 6, of which 3 were waited for; matrix products, arithmetic and copies ran while one was open for 0% of the time, Pallas kernels for 3%

profile of v8, /device:TPU:1, one launch (start us, length us, event | category | flops | bytes accessed | tf_op | source)
XLA Modules:
  0.0 155.6 jit_solution(3264577696304009212)
XLA Ops:
  0.6 0.1 add_bitcast_fusion.where_ref
  0.7 3.4 %prepare.1 = (bf16[1024,256]{1,0:T(8,128)(2,1)S(1)}, f32[8,256]{1,0:T(8,128)S(1)}, f32[16,256]{1,0:T(8,128)S(1)}, f32[8,1024]{1,0:T(8,128)S(1)}, f32[24,128]{1,0...) custom-call(f32[1024,1024]{1,0:T(8,128)} %bitcast.34, ...), custom_call_target="tpu_custom_call" | custom-call | flops 67108864 | bytes 4194304 | tf_op jit(solution)/shard_map/prepare/pallas_call | solution.py:416
  4.1 0.0 copy-start.1
  4.1 0.0 copy-start.3
  4.2 4.0 %collective-permute-start = (f32[24,128]{1,0:T(8,128)S(1)}, f32[24,128]{1,0:T(8,128)S(1)}, u32[]{:S(2)}, u32[]{:S(2)}) collective-permute-start(f32[24,128]{1,0:T(8,128)S(1)} %get-tuple-element.64), channel_id=1, source_target_pairs={{0,1},{1,2},{2,3},{3,4},{4,5},{5,6},{6,7},{8,9},{9,10},{10,11},{11... | collective-permute-start | bytes 36872 | tf_op jit(solution)/shard_map/ppermute | solution.py:390
  8.2 0.8 collective-permute-done.below_in
  9.0 2.1 %address.1 = (f32[8,256]{1,0:T(8,128)S(1)}, f32[32,8,128]{2,1,0:T(8,128)}, bf16[1024,1024]{1,0:T(8,128)(2,1)}) custom-call(s32[1,6]{1,0:T(1,128)} %partners_ref.1, f32[16,256]{1,0:T(8,128)S(1)} %get-tuple-element.63.own_ref.refs_4_, f32[8,1024]{1,0:T(8,128)S(1)} %get-tuple-element.66.h_ref, bf16[1024,256]{1,0:T(8,128)(2,1)S(1)} %get-tuple-element.67.onehot_ref.refs_10_, ...), custom_call_target="tpu_custom_call" | custom-call | flops 268435456 | bytes 4194304 | tf_op jit(solution)/shard_map/address/pallas_call | solution.py:429
  11.1 12.6 %all-to-all-start = ((f32[32,8,128]{2,1,0:T(8,128)}), f32[32,8,128]{2,1,0:T(8,128)S(1)}, u32[]{:S(2)}, u32[]{:S(2)}) async-start(f32[32,8,128]{2,1,0:T(8,128)} %get-tuple-element.72), calls=%async_computation | async-start | bytes 262144 | tf_op jit(solution)/shard_map/all_to_all | solution.py:383
  23.8 1.3 collective-permute-start.1
  25.1 4.0 %collective-permute-done.1.above_in = f32[24,128]{1,0:T(8,128)S(1)} collective-permute-done((f32[24,128]{1,0:T(8,128)S(1)}, f32[24,128]{1,0:T(8,128)S(1)}, u32[]{:S(2)}, u32[]{:S(2)}) %collective-permute-start.1) | collective-permute-done | bytes 12320 | tf_op jit(solution)/shard_map/ppermute | solution.py:390
  29.1 5.4 %all-to-all-done.in_ref = f32[32,8,128]{2,1,0:T(8,128)S(1)} async-done(((f32[32,8,128]{2,1,0:T(8,128)}), f32[32,8,128]{2,1,0:T(8,128)S(1)}, u32[]{:S(2)}, u32[]{:S(2)}) %all-to-all-start) | async-done | bytes 131104 | tf_op jit(solution)/shard_map/all_to_all | solution.py:383
  34.4 0.0 copy-done.1
  34.4 0.0 copy-done.3
  34.4 0.0 copy-start
  34.4 0.0 copy-start.2
  34.4 3.1 %first_gradient.1 = (f32[8,1024]{1,0:T(8,128)S(1)}, f32[8,256]{1,0:T(8,128)S(1)}, f32[16,256]{1,0:T(8,128)S(1)}, f32[8,256]{1,0:T(8,128)S(1)}, f32[16,128]{1,0:T...) custom-call(s32[1,6]{1,0:T(1,128)S(1)} %copy-done.3, ...), custom_call_target="tpu_custom_call" | custom-call | flops 67108864 | bytes 4194304 | tf_op jit(solution)/shard_map/first_gradient/pallas_call | solution.py:436
  37.5 22.9 %all_to_all.46 = f32[256,1,128]{2,1,0:T(1,128)S(1)} all-to-all(f32[256,1,128]{2,1,0:T(1,128)S(1)} %bitcast.28), channel_id=1, replica_groups=mesh['plan'=32,'layer'=8] {'plan','layer'}, dimensions={0} | all-to-all | bytes 262144 | tf_op jit(solution)/shard_map/all_to_all | solution.py:383
  60.4 0.0 copy-done
  60.4 0.0 copy-done.2
  60.4 0.3 first_face.1
  60.8 2.2 %collective-permute-start.2 = (f32[8,128]{1,0:T(8,128)S(1)}, f32[8,128]{1,0:T(8,128)S(1)}, u32[]{:S(2)}, u32[]{:S(2)}) collective-permute-start(f32[8,128]{1,0:T(8,128)S(1)} %get-tuple-element.85.refs_2_), channel_id=1, source_target_pairs={{0,1},{1,2},{2,3},{3,4},{4,5},{5,6},{6,7},{8,9},{9,10},{10,11},{11... | collective-permute-start | bytes 12296 | tf_op jit(solution)/shard_map/ppermute | solution.py:390
  63.0 1.6 %first_rest.1 = (f32[8,1024]{1,0:T(8,128)S(1)}, f32[8,256]{1,0:T(8,128)S(1)}, f32[8,128]{1,0:T(8,128)S(1)}, f32[16,256]{1,0:T(8,128)S(1)}, f32[16,256]{1,0:T(8,1...) custom-call(f32[256,128]{1,0:T(8,128)S(1)} %bitcast.24, f32[3,16,128]{2,1,0:T(8,128)S(1)} %get-tuple-element.77.masks_ref, ...), custom_call_target="tpu_custom_call" | custom-call | flops 134217728 | bytes 8388608 | tf_op jit(solution)/shard_map/first_rest/pallas_call | solution.py:450
  64.6 0.0 collective-permute-done.2.below_ref.refs_8_
  64.6 0.1 announce.3
  64.7 15.0 %all_to_all.47.in_ref = f32[32,8,128]{2,1,0:T(8,128)S(1)} all-to-all(f32[32,8,128]{2,1,0:T(8,128)S(1)} %announce.3), channel_id=1, replica_groups=mesh['plan'=32,'layer'=8] {'plan'}, dimensions={0} | all-to-all | bytes 262144 | tf_op jit(solution)/shard_map/all_to_all | solution.py:383
  79.7 1.0 layer_sums.3
  80.7 11.9 %all_to_all.48.in_ref = f32[16,8,256]{2,1,0:T(8,128)S(1)} all-to-all(f32[16,8,256]{2,1,0:T(8,128)S(1)} %get-tuple-element.94), channel_id=1, replica_groups={{0,8,1,9,2,10,3,11,4,12,5,13,6,14,7,15},{16,24,17,25,18,26,19,27,20,28,..., dimensions={0} | all-to-all | bytes 262144 | tf_op jit(solution)/shard_map/all_to_all | solution.py:383
  92.6 0.4 next_face.2
  93.0 2.1 %collective-permute-start.3 = (f32[8,128]{1,0:T(8,128)S(1)}, f32[8,128]{1,0:T(8,128)S(1)}, u32[]{:S(2)}, u32[]{:S(2)}) collective-permute-start(f32[8,128]{1,0:T(8,128)S(1)} %get-tuple-element.99.refs_2_), channel_id=1, source_target_pairs={{0,1},{1,2},{2,3},{3,4},{4,5},{5,6},{6,7},{8,9},{9,10},{10,11},{11... | collective-permute-start | bytes 12296 | tf_op jit(solution)/shard_map/ppermute | solution.py:390
  95.1 1.6 %next_rest.2 = (f32[8,1024]{1,0:T(8,128)S(1)}, f32[8,256]{1,0:T(8,128)S(1)}, f32[8,128]{1,0:T(8,128)S(1)}, f32[16,256]{1,0:T(8,128)S(1)}, f32[16,256]{1,0:T(8,128)S(1)}, /*index=5*/f32[16,128]{1,0:T(8,128)S(1)}) custom-call(f32[16,8,256]{2,1,0:T(8,128)S(1)} %all_to_all.48.in_ref, f32[3,16,128]{2,1,0:T(8,128)S(1)} %get-tuple-element.77.masks_ref, ...), custom_call_target="tpu_custom_call" | custom-call | flops 134217728 | bytes 8388608 | tf_op jit(solution)/shard_map/next_rest/pallas_call | solution.py:474
  96.7 0.0 collective-permute-done.3.below_ref.refs_8_
  96.8 0.1 announce.4
  96.9 14.1 %all_to_all.49.in_ref = f32[32,8,128]{2,1,0:T(8,128)S(1)} all-to-all(f32[32,8,128]{2,1,0:T(8,128)S(1)} %announce.4), channel_id=1, replica_groups=mesh['plan'=32,'layer'=8] {'plan'}, dimensions={0} | all-to-all | bytes 262144 | tf_op jit(solution)/shard_map/all_to_all | solution.py:383
  111.0 1.0 layer_sums.4
  111.9 11.9 %all_to_all.50.in_ref = f32[16,8,256]{2,1,0:T(8,128)S(1)} all-to-all(f32[16,8,256]{2,1,0:T(8,128)S(1)} %get-tuple-element.106), channel_id=1, replica_groups={{0,8,1,9,2,10,3,11,4,12,5,13,6,14,7,15},{16,24,17,25,18,26,19,27,20,28,..., dimensions={0} | all-to-all | bytes 262144 | tf_op jit(solution)/shard_map/all_to_all | solution.py:383
  123.9 0.4 next_face.3
  124.2 2.1 %collective-permute-start.4 = (f32[8,128]{1,0:T(8,128)S(1)}, f32[8,128]{1,0:T(8,128)S(1)}, u32[]{:S(2)}, u32[]{:S(2)}) collective-permute-start(f32[8,128]{1,0:T(8,128)S(1)} %get-tuple-element.111.refs_2_), channel_id=1, source_target_pairs={{0,1},{1,2},{2,3},{3,4},{4,5},{5,6},{6,7},{8,9},{9,10},{10,11},{11... | collective-permute-start | bytes 12296 | tf_op jit(solution)/shard_map/ppermute | solution.py:390
  126.4 1.6 %next_rest.3 = (f32[8,1024]{1,0:T(8,128)S(1)}, f32[8,256]{1,0:T(8,128)S(1)}, f32[8,128]{1,0:T(8,128)S(1)}) custom-call(f32[16,8,256]{2,1,0:T(8,128)S(1)} %all_to_all.50.in_ref, f32[3,16,128]{2,1,0:T(8,128)S(1)} %get-tuple-element.77.masks_ref, f32[8,128]{1,0:T(8,128)S(1)} %get-tuple-element.107.half_ref, f32[8,128]{1,0:T(8,128)S(1)} %get-tuple-element.109.refs_0_, ...), custom_call_target="tpu_custom_call" | custom-call | flops 134217728 | bytes 8388608 | tf_op jit(solution)/shard_map/next_rest/pallas_call | solution.py:474
  128.0 0.0 collective-permute-done.4.below_ref
  128.0 0.1 announce.5
  128.1 14.1 %all_to_all.51.in_ref = f32[32,8,128]{2,1,0:T(8,128)S(1)} all-to-all(f32[32,8,128]{2,1,0:T(8,128)S(1)} %announce.5), channel_id=1, replica_groups=mesh['plan'=32,'layer'=8] {'plan'}, dimensions={0} | all-to-all | bytes 262144 | tf_op jit(solution)/shard_map/all_to_all | solution.py:383
  142.2 1.0 layer_sums.5
  143.2 11.6 %all_to_all.52.in_ref = f32[16,8,128]{2,1,0:T(8,128)S(1)} all-to-all(f32[16,8,128]{2,1,0:T(8,128)S(1)} %layer_sums.5), channel_id=1, replica_groups={{0,8,1,9,2,10,3,11,4,12,5,13,6,14,7,15},{16,24,17,25,18,26,19,27,20,28,..., dimensions={0} | all-to-all | bytes 131072 | tf_op jit(solution)/shard_map/all_to_all | solution.py:383
  154.8 0.8 finish.1
Async XLA Ops:
  4.1 30.3 %copy-start.1 = (f32[1,1,8,1024]{3,2,1,0:T(8,128)S(1)}, f32[1,1,8,1024]{3,2,1,0:T(8,128)}, u32[]{:S(2)}) copy-start(f32[1,1,8,1024]{3,2,1,0:T(8,128)} %param.8) | copy-start | bytes 98308
  4.1 30.3 %copy-start.3 = (s32[1,6]{1,0:T(1,128)S(1)}, s32[1,6]{1,0:T(1,128)}, u32[]{:S(2)}) copy-start(s32[1,6]{1,0:T(1,128)} %partners_ref.1) | copy-start | bytes 76
  4.2 4.9 %collective-permute-start = (f32[24,128]{1,0:T(8,128)S(1)}, f32[24,128]{1,0:T(8,128)S(1)}, u32[]{:S(2)}, u32[]{:S(2)}) collective-permute-start(f32[24,128]{1,0:T(8,128)S(1)} %get-tuple-element.64), channel_id=1, source_target_pairs={{0,1},{1,2},{2,3},{3,4},{4,5},{5,6},{6,7},{8,9},{9,10},{10,11},{11... | collective-permute-start | bytes 36872 | tf_op jit(solution)/shard_map/ppermute | solution.py:390
  11.1 23.3 %all-to-all-start = ((f32[32,8,128]{2,1,0:T(8,128)}), f32[32,8,128]{2,1,0:T(8,128)S(1)}, u32[]{:S(2)}, u32[]{:S(2)}) async-start(f32[32,8,128]{2,1,0:T(8,128)} %get-tuple-element.72), calls=%async_computation | async-start | bytes 262144 | tf_op jit(solution)/shard_map/all_to_all | solution.py:383
  23.8 5.3 %collective-permute-start.1 = (f32[24,128]{1,0:T(8,128)S(1)}, f32[24,128]{1,0:T(8,128)S(1)}, u32[]{:S(2)}, u32[]{:S(2)}) collective-permute-start(f32[24,128]{1,0:T(8,128)S(1)} %get-tuple-element.74), channel_id=1, source_target_pairs={{1,0},{2,1},{3,2},{4,3},{5,4},{6,5},{7,6},{9,8},{10,9},{11,10},{12... | collective-permute-start | bytes 36872 | tf_op jit(solution)/shard_map/ppermute | solution.py:390
  34.4 26.0 %copy-start = (f32[1,1,8,1024]{3,2,1,0:T(8,128)S(1)}, f32[1,1,8,1024]{3,2,1,0:T(8,128)}, u32[]{:S(2)}) copy-start(f32[1,1,8,1024]{3,2,1,0:T(8,128)} %param.9) | copy-start | bytes 98308
  34.4 26.0 %copy-start.2 = (s32[1,1,1024]{2,1,0:T(1,128)S(1)}, s32[1,1,1024]{2,1,0:T(1,128)}, u32[]{:S(2)}) copy-start(s32[1,1,1024]{2,1,0:T(1,128)} %param.13) | copy-start | bytes 12292
  60.8 3.8 %collective-permute-start.2 = (f32[8,128]{1,0:T(8,128)S(1)}, f32[8,128]{1,0:T(8,128)S(1)}, u32[]{:S(2)}, u32[]{:S(2)}) collective-permute-start(f32[8,128]{1,0:T(8,128)S(1)} %get-tuple-element.85.refs_2_), channel_id=1, source_target_pairs={{0,1},{1,2},{2,3},{3,4},{4,5},{5,6},{6,7},{8,9},{9,10},{10,11},{11... | collective-permute-start | bytes 12296 | tf_op jit(solution)/shard_map/ppermute | solution.py:390
  93.0 3.7 %collective-permute-start.3 = (f32[8,128]{1,0:T(8,128)S(1)}, f32[8,128]{1,0:T(8,128)S(1)}, u32[]{:S(2)}, u32[]{:S(2)}) collective-permute-start(f32[8,128]{1,0:T(8,128)S(1)} %get-tuple-element.99.refs_2_), channel_id=1, source_target_pairs={{0,1},{1,2},{2,3},{3,4},{4,5},{5,6},{6,7},{8,9},{9,10},{10,11},{11... | collective-permute-start | bytes 12296 | tf_op jit(solution)/shard_map/ppermute | solution.py:390
  124.2 3.7 %collective-permute-start.4 = (f32[8,128]{1,0:T(8,128)S(1)}, f32[8,128]{1,0:T(8,128)S(1)}, u32[]{:S(2)}, u32[]{:S(2)}) collective-permute-start(f32[8,128]{1,0:T(8,128)S(1)} %get-tuple-element.111.refs_2_), channel_id=1, source_target_pairs={{0,1},{1,2},{2,3},{3,4},{4,5},{5,6},{6,7},{8,9},{9,10},{10,11},{11... | collective-permute-start | bytes 12296 | tf_op jit(solution)/shard_map/ppermute | solution.py:390

commit v9 on v7

--- a/solution.py
+++ b/solution.py
@@ -14,6 +14,7 @@
 LANES = 128
 HALF = 3
 JW = 2 * LANES
+STRIP = 32
 CHUNKS = 4
 NAMES = 16
 SQUARE, CURVATURE = HALF * JR, HALF * JR + 1
@@ -55,12 +56,16 @@
     return jnp.sum(value, axis=1, keepdims=True)
 
 
-def dense(field, high_ref, low_ref, columns=slice(None), before_low=None):
+def dense(field, high_ref, low_ref, columns=slice(None), copies=()):
     lhs = jnp.concatenate(pieces(field, 2), axis=0).astype(BF16)
-    total = jnp.dot(lhs, high_ref[:, columns], preferred_element_type=F32)
-    if before_low is not None:
-        before_low()
-    total = total + jnp.dot(lhs, low_ref[:, columns], preferred_element_type=F32)
+    depth = field.shape[1] // CHUNKS
+    total = 0.0
+    for half_ref, arrivals in ((high_ref, ()), (low_ref, copies)):
+        for chunk in range(CHUNKS):
+            for copy in arrivals[chunk : chunk + 1]:
+                copy.wait()
+            at = slice(chunk * depth, (chunk + 1) * depth)
+            total = total + jnp.dot(lhs[:, at], half_ref[at, columns], preferred_element_type=F32)
     return total[:8] + total[8:]
 
 
@@ -93,14 +98,15 @@
     for chunk in range(CHUNKS):
         at = slice(chunk * depth, (chunk + 1) * depth)
         chunk_copy(block_ref, rows_ref, sems, chunk).wait()
-        rows = rows_ref[at, :]
-        high = rows.astype(BF16)
-        low = (rows - high.astype(F32)).astype(BF16)
-        high_ref[at, :] = high
-        low_ref[at, :] = low
+        for first in range(at.start, at.stop, STRIP):
+            strip = slice(first, first + STRIP)
+            rows = rows_ref[strip, :]
+            high = rows.astype(BF16)
+            high_ref[strip, :] = high
+            low_ref[strip, :] = (rows - high.astype(F32)).astype(BF16)
         give(chunk).start()
-        total = total + jnp.dot(lhs[:, at], high, preferred_element_type=F32)
-        total = total + jnp.dot(lhs[:, at], low, preferred_element_type=F32)
+        total = total + jnp.dot(lhs[:, at], high_ref[at, :], preferred_element_type=F32)
+        total = total + jnp.dot(lhs[:, at], low_ref[at, :], preferred_element_type=F32)
     return total[:8] + total[8:]
 
 
@@ -133,8 +139,7 @@
     rows = [rows_ref[r] for r in range(ROUNDS)]
     rows = jnp.concatenate(rows[:HALF] + spare + rows[HALF:] + spare, axis=1)
     hit = lax.broadcasted_iota(jnp.int32, (width, JW), 0) == rows
-    onehot = jnp.where(hit, 1.0, 0.0).astype(BF16)
-    onehot_ref[...] = onehot
+    onehot_ref[...] = jnp.where(hit, 1.0, 0.0).astype(BF16)
     lane = lax.broadcasted_iota(jnp.int32, (8, JW), 1)
     valid = jnp.zeros((8, JW), F32)
     for r in range(ROUNDS):
@@ -143,15 +148,15 @@
         valid = jnp.where(inside, 1.0, valid)
     valid_ref[...] = valid
     contact = jnp.broadcast_to(jnp.where(contact_ref[...] == 1, 1.0, 0.0), x.shape)
-    own, own_contact = pick(x, onehot, contact)
+    own, own_contact = pick(x, onehot_ref[...], contact)
     own_ref[...] = jnp.concatenate([own, own_contact], axis=0)
     position = lax.broadcasted_iota(jnp.int32, x.shape, 1)
     edge = (position < FACE) | (position >= width - FACE)
-    h = spread(valid * own, onehot) + jnp.where(edge, x, 0.0) - load_ref[...]
+    h = spread(valid * own, onehot_ref[...]) + jnp.where(edge, x, 0.0) - load_ref[...]
     low_copy = functools.partial(chunk_copy, low_ref, low_hbm, low_sems)
     h = h + stream_dense(x, block_ref, held_ref, sems, high_ref, low_ref, low_copy)
     h_ref[...] = h
-    (hown,) = pick(h, onehot)
+    (hown,) = pick(h, onehot_ref[...])
     hown_ref[...] = hown
     out_ref[...] = jnp.zeros_like(out_ref)
     place = lax.broadcasted_iota(jnp.int32, (8, LANES), 1) // JR
@@ -173,9 +178,10 @@
 def first_gradient(partners_ref, where_ref, low_hbm, high_ref, x_ref, h_ref, own_ref, hown_ref, in_ref,
                    below_in, above_in, valid_ref, onehot_ref,
                    g_ref, gown_ref, far_ref, gfar_ref, below_ref, gbelow_ref, above_ref, gabove_ref,
-                   all_ref, masks_ref, low_ref, sem):
-    low_copy = pltpu.make_async_copy(low_hbm, low_ref, sem)
-    low_copy.start()
+                   all_ref, masks_ref, low_ref, sems):
+    copies = [chunk_copy(low_hbm, low_ref, sems, chunk) for chunk in range(CHUNKS)]
+    for copy in copies:
+        copy.start()
     width = x_ref.shape[1]
     place = lax.broadcasted_iota(jnp.int32, (8, LANES), 1) // JR
     parts = [[jnp.zeros((8, LANES), F32)] * 2 for _ in range(3)]
@@ -213,7 +219,7 @@
     jumps = valid * gown * (gown - gfar)
     terms = first * (first - gbelow) + last * (last - gabove) + jumps[:, :LANES] + jumps[:, LANES:]
     square = lane_sum(g * g)
-    image = dense(g, high_ref, low_ref, before_low=low_copy.wait)
+    image = dense(g, high_ref, low_ref, copies=copies)
     curvature = lane_sum(terms) + lane_sum(g * image)
     lane = lax.broadcasted_iota(jnp.int32, (8, LANES), 1)
     row = lax.broadcasted_iota(jnp.int32, (8, LANES), 0)
@@ -417,7 +423,7 @@
         first_gradient, "first_gradient",
         (field, jump, jump2, jump, face2, face, face2, face,
          shape(plans * layers, LANES), shape(3, 2 * layers, LANES), half_shape),
-        [SMEM] * 2 + [HBM] + [VMEM] * 10, 12, flops, 4 * width * width, [pltpu.SemaphoreType.DMA],
+        [SMEM] * 2 + [HBM] + [VMEM] * 10, 12, flops, 4 * width * width, [chunk_sems],
     )(partners, position, pltpu.with_memory_space_constraint(low, pltpu.HBM), high, x, h, own, hown, incoming, below, above, valid, onehot)
     incoming = swap(out, ("plan", "layer"))
 

time: 152 us -> 152 us (level)
  no operation moved by 1% of the time
where the time goes in v9:
time: 152 us; the launch traced here: 151 us
  blocking collectives  103 us (68%)
  starting transfers between devices  23.5 us (15%)
  Pallas kernels  17.5 us (12%)
  waiting for transfers between devices  6.49 us (4%)
    all_to_all x7, blocking collectives, swap(): lax.all_to_all(outgoing, axis, split_axis=0, concat_axis=0, tiled=True, a...  103 us
    all_to_all x1, starting transfers between devices, swap(): lax.all_to_all(outgoing, axis, split_axis=0, concat_axis=0, tiled=True, a...  12.6 us
    ppermute x5, starting transfers between devices, lift(): lax.ppermute(face, 'layer', [(i, i + step) for i in range(layers) if 0 <=...  10.9 us
    pallas_call x1, Pallas kernels, shards(): call(prepare, 'prepare', (shape(width, JW, dtype=BF16), jump, jump2, jump...  4.87 us
    ppermute x5, waiting for transfers between devices, lift(): lax.ppermute(face, 'layer', [(i, i + step) for i in range(layers) if 0 <=...  3.43 us
    pallas_call x2, Pallas kernels, shards(): call(next_rest, 'next_rest', late[:3] if iteration == ITERS - 2 else late...  3.26 us
    all_to_all x1, waiting for transfers between devices, swap(): lax.all_to_all(outgoing, axis, split_axis=0, concat_axis=0, tiled=True, a...  3.05 us
  transfers between devices with their start and end apart: 6, of which 2 were waited for; matrix products, arithmetic and copies ran while one was open for 0% of the time, Pallas kernels for 3%

profile of v9, /device:TPU:1, one launch (start us, length us, event | category | flops | bytes accessed | tf_op | source)
XLA Modules:
  0.0 151.5 jit_solution(7347889852102947091)
XLA Ops:
  0.6 0.1 add_bitcast_fusion.where_ref
  0.7 0.0 copy-start.1
  0.7 0.0 copy-start.3
  0.7 4.9 %prepare.1 = (bf16[1024,256]{1,0:T(8,128)(2,1)S(1)}, f32[8,256]{1,0:T(8,128)S(1)}, f32[16,256]{1,0:T(8,128)S(1)}, f32[8,256]{1,0:T(8,128)S(1)}, f32[8,1024]{1,0:...) custom-call(f32[1024,1024]{1,0:T(8,128)} %bitcast.34, ...), custom_call_target="tpu_custom_call" | custom-call | flops 67108864 | bytes 4194304 | tf_op jit(solution)/shard_map/prepare/pallas_call | solution.py:408
  5.6 12.6 %all-to-all-start = ((f32[32,8,128]{2,1,0:T(8,128)}), f32[32,8,128]{2,1,0:T(8,128)S(1)}, u32[]{:S(2)}, u32[]{:S(2)}) async-start(f32[32,8,128]{2,1,0:T(8,128)} %get-tuple-element.65), calls=%async_computation | async-start | bytes 262144 | tf_op jit(solution)/shard_map/all_to_all | solution.py:377
  18.2 3.2 %collective-permute-start = (f32[24,128]{1,0:T(8,128)S(1)}, f32[24,128]{1,0:T(8,128)S(1)}, u32[]{:S(2)}, u32[]{:S(2)}) collective-permute-start(f32[24,128]{1,0:T(8,128)S(1)} %get-tuple-element.66), channel_id=1, source_target_pairs={{0,1},{1,2},{2,3},{3,4},{4,5},{5,6},{6,7},{8,9},{9,10},{10,11},{11... | collective-permute-start | bytes 36872 | tf_op jit(solution)/shard_map/ppermute | solution.py:384
  21.4 1.3 collective-permute-start.1
  22.7 0.0 collective-permute-done.below_in
  22.7 3.4 %collective-permute-done.1.above_in = f32[24,128]{1,0:T(8,128)S(1)} collective-permute-done((f32[24,128]{1,0:T(8,128)S(1)}, f32[24,128]{1,0:T(8,128)S(1)}, u32[]{:S(2)}, u32[]{:S(2)}) %collective-permute-start.1) | collective-permute-done | bytes 12320 | tf_op jit(solution)/shard_map/ppermute | solution.py:384
  26.1 3.1 %all-to-all-done.in_ref = f32[32,8,128]{2,1,0:T(8,128)S(1)} async-done(((f32[32,8,128]{2,1,0:T(8,128)}), f32[32,8,128]{2,1,0:T(8,128)S(1)}, u32[]{:S(2)}, u32[]{:S(2)}) %all-to-all-start) | async-done | bytes 131104 | tf_op jit(solution)/shard_map/all_to_all | solution.py:377
  29.2 0.0 copy-done.1
  29.2 0.0 copy-done.3
  29.2 0.0 copy-start
  29.2 0.0 copy-start.2
  29.2 2.7 %first_gradient.1 = (f32[8,1024]{1,0:T(8,128)S(1)}, f32[8,256]{1,0:T(8,128)S(1)}, f32[16,256]{1,0:T(8,128)S(1)}, f32[8,256]{1,0:T(8,128)S(1)}, f32[16,128]{1,0:T...) custom-call(s32[1,6]{1,0:T(1,128)S(1)} %copy-done.3, ...), custom_call_target="tpu_custom_call" | custom-call | flops 67108864 | bytes 4194304 | tf_op jit(solution)/shard_map/first_gradient/pallas_call | solution.py:422
  31.9 24.4 %all_to_all.46 = f32[256,1,128]{2,1,0:T(1,128)S(1)} all-to-all(f32[256,1,128]{2,1,0:T(1,128)S(1)} %bitcast.28), channel_id=1, replica_groups=mesh['plan'=32,'layer'=8] {'plan','layer'}, dimensions={0} | all-to-all | bytes 262144 | tf_op jit(solution)/shard_map/all_to_all | solution.py:377
  56.3 0.0 copy-done
  56.3 0.0 copy-done.2
  56.3 0.3 first_face.1
  56.7 2.2 %collective-permute-start.2 = (f32[8,128]{1,0:T(8,128)S(1)}, f32[8,128]{1,0:T(8,128)S(1)}, u32[]{:S(2)}, u32[]{:S(2)}) collective-permute-start(f32[8,128]{1,0:T(8,128)S(1)} %get-tuple-element.79.refs_2_), channel_id=1, source_target_pairs={{0,1},{1,2},{2,3},{3,4},{4,5},{5,6},{6,7},{8,9},{9,10},{10,11},{11... | collective-permute-start | bytes 12296 | tf_op jit(solution)/shard_map/ppermute | solution.py:384
  58.9 1.6 %first_rest.1 = (f32[8,1024]{1,0:T(8,128)S(1)}, f32[8,256]{1,0:T(8,128)S(1)}, f32[8,128]{1,0:T(8,128)S(1)}, f32[16,256]{1,0:T(8,128)S(1)}, f32[16,256]{1,0:T(8,1...) custom-call(f32[256,128]{1,0:T(8,128)S(1)} %bitcast.24, f32[3,16,128]{2,1,0:T(8,128)S(1)} %get-tuple-element.71.masks_ref, ...), custom_call_target="tpu_custom_call" | custom-call | flops 134217728 | bytes 8388608 | tf_op jit(solution)/shard_map/first_rest/pallas_call | solution.py:436
  60.5 0.0 collective-permute-done.2.below_ref.refs_8_
  60.5 0.1 announce.3
  60.6 15.0 %all_to_all.47.in_ref = f32[32,8,128]{2,1,0:T(8,128)S(1)} all-to-all(f32[32,8,128]{2,1,0:T(8,128)S(1)} %announce.3), channel_id=1, replica_groups=mesh['plan'=32,'layer'=8] {'plan'}, dimensions={0} | all-to-all | bytes 262144 | tf_op jit(solution)/shard_map/all_to_all | solution.py:377
  75.7 1.0 layer_sums.3
  76.6 11.9 %all_to_all.48.in_ref = f32[16,8,256]{2,1,0:T(8,128)S(1)} all-to-all(f32[16,8,256]{2,1,0:T(8,128)S(1)} %get-tuple-element.88), channel_id=1, replica_groups={{0,8,1,9,2,10,3,11,4,12,5,13,6,14,7,15},{16,24,17,25,18,26,19,27,20,28,..., dimensions={0} | all-to-all | bytes 262144 | tf_op jit(solution)/shard_map/all_to_all | solution.py:377
  88.5 0.4 next_face.2
  88.9 2.1 %collective-permute-start.3 = (f32[8,128]{1,0:T(8,128)S(1)}, f32[8,128]{1,0:T(8,128)S(1)}, u32[]{:S(2)}, u32[]{:S(2)}) collective-permute-start(f32[8,128]{1,0:T(8,128)S(1)} %get-tuple-element.93.refs_2_), channel_id=1, source_target_pairs={{0,1},{1,2},{2,3},{3,4},{4,5},{5,6},{6,7},{8,9},{9,10},{10,11},{11... | collective-permute-start | bytes 12296 | tf_op jit(solution)/shard_map/ppermute | solution.py:384
  91.0 1.6 %next_rest.2 = (f32[8,1024]{1,0:T(8,128)S(1)}, f32[8,256]{1,0:T(8,128)S(1)}, f32[8,128]{1,0:T(8,128)S(1)}, f32[16,256]{1,0:T(8,128)S(1)}, f32[16,256]{1,0:T(8,128)S(1)}, /*index=5*/f32[16,128]{1,0:T(8,128)S(1)}) custom-call(f32[16,8,256]{2,1,0:T(8,128)S(1)} %all_to_all.48.in_ref, f32[3,16,128]{2,1,0:T(8,128)S(1)} %get-tuple-element.71.masks_ref, ...), custom_call_target="tpu_custom_call" | custom-call | flops 134217728 | bytes 8388608 | tf_op jit(solution)/shard_map/next_rest/pallas_call | solution.py:460
  92.7 0.0 collective-permute-done.3.below_ref.refs_8_
  92.7 0.1 announce.4
  92.8 14.1 %all_to_all.49.in_ref = f32[32,8,128]{2,1,0:T(8,128)S(1)} all-to-all(f32[32,8,128]{2,1,0:T(8,128)S(1)} %announce.4), channel_id=1, replica_groups=mesh['plan'=32,'layer'=8] {'plan'}, dimensions={0} | all-to-all | bytes 262144 | tf_op jit(solution)/shard_map/all_to_all | solution.py:377
  106.9 1.0 layer_sums.4
  107.9 11.9 %all_to_all.50.in_ref = f32[16,8,256]{2,1,0:T(8,128)S(1)} all-to-all(f32[16,8,256]{2,1,0:T(8,128)S(1)} %get-tuple-element.100), channel_id=1, replica_groups={{0,8,1,9,2,10,3,11,4,12,5,13,6,14,7,15},{16,24,17,25,18,26,19,27,20,28,..., dimensions={0} | all-to-all | bytes 262144 | tf_op jit(solution)/shard_map/all_to_all | solution.py:377
  119.8 0.4 next_face.3
  120.1 2.1 %collective-permute-start.4 = (f32[8,128]{1,0:T(8,128)S(1)}, f32[8,128]{1,0:T(8,128)S(1)}, u32[]{:S(2)}, u32[]{:S(2)}) collective-permute-start(f32[8,128]{1,0:T(8,128)S(1)} %get-tuple-element.105.refs_2_), channel_id=1, source_target_pairs={{0,1},{1,2},{2,3},{3,4},{4,5},{5,6},{6,7},{8,9},{9,10},{10,11},{11... | collective-permute-start | bytes 12296 | tf_op jit(solution)/shard_map/ppermute | solution.py:384
  122.3 1.6 %next_rest.3 = (f32[8,1024]{1,0:T(8,128)S(1)}, f32[8,256]{1,0:T(8,128)S(1)}, f32[8,128]{1,0:T(8,128)S(1)}) custom-call(f32[16,8,256]{2,1,0:T(8,128)S(1)} %all_to_all.50.in_ref, f32[3,16,128]{2,1,0:T(8,128)S(1)} %get-tuple-element.71.masks_ref, f32[8,128]{1,0:T(8,128)S(1)} %get-tuple-element.101.half_ref, f32[8,128]{1,0:T(8,128)S(1)} %get-tuple-element.103.refs_0_, ...), custom_call_target="tpu_custom_call" | custom-call | flops 134217728 | bytes 8388608 | tf_op jit(solution)/shard_map/next_rest/pallas_call | solution.py:460
  123.9 0.0 collective-permute-done.4.below_ref
  123.9 0.1 announce.5
  124.0 14.1 %all_to_all.51.in_ref = f32[32,8,128]{2,1,0:T(8,128)S(1)} all-to-all(f32[32,8,128]{2,1,0:T(8,128)S(1)} %announce.5), channel_id=1, replica_groups=mesh['plan'=32,'layer'=8] {'plan'}, dimensions={0} | all-to-all | bytes 262144 | tf_op jit(solution)/shard_map/all_to_all | solution.py:377
  138.1 1.0 layer_sums.5
  139.1 11.6 %all_to_all.52.in_ref = f32[16,8,128]{2,1,0:T(8,128)S(1)} all-to-all(f32[16,8,128]{2,1,0:T(8,128)S(1)} %layer_sums.5), channel_id=1, replica_groups={{0,8,1,9,2,10,3,11,4,12,5,13,6,14,7,15},{16,24,17,25,18,26,19,27,20,28,..., dimensions={0} | all-to-all | bytes 131072 | tf_op jit(solution)/shard_map/all_to_all | solution.py:377
  150.7 0.8 finish.1
Async XLA Ops:
  0.7 28.5 %copy-start.1 = (f32[1,1,8,1024]{3,2,1,0:T(8,128)S(1)}, f32[1,1,8,1024]{3,2,1,0:T(8,128)}, u32[]{:S(2)}) copy-start(f32[1,1,8,1024]{3,2,1,0:T(8,128)} %param.8) | copy-start | bytes 98308
  0.7 28.5 %copy-start.3 = (s32[1,6]{1,0:T(1,128)S(1)}, s32[1,6]{1,0:T(1,128)}, u32[]{:S(2)}) copy-start(s32[1,6]{1,0:T(1,128)} %partners_ref.1) | copy-start | bytes 76
  5.6 23.6 %all-to-all-start = ((f32[32,8,128]{2,1,0:T(8,128)}), f32[32,8,128]{2,1,0:T(8,128)S(1)}, u32[]{:S(2)}, u32[]{:S(2)}) async-start(f32[32,8,128]{2,1,0:T(8,128)} %get-tuple-element.65), calls=%async_computation | async-start | bytes 262144 | tf_op jit(solution)/shard_map/all_to_all | solution.py:377
  18.2 4.5 %collective-permute-start = (f32[24,128]{1,0:T(8,128)S(1)}, f32[24,128]{1,0:T(8,128)S(1)}, u32[]{:S(2)}, u32[]{:S(2)}) collective-permute-start(f32[24,128]{1,0:T(8,128)S(1)} %get-tuple-element.66), channel_id=1, source_target_pairs={{0,1},{1,2},{2,3},{3,4},{4,5},{5,6},{6,7},{8,9},{9,10},{10,11},{11... | collective-permute-start | bytes 36872 | tf_op jit(solution)/shard_map/ppermute | solution.py:384
  21.4 4.7 %collective-permute-start.1 = (f32[24,128]{1,0:T(8,128)S(1)}, f32[24,128]{1,0:T(8,128)S(1)}, u32[]{:S(2)}, u32[]{:S(2)}) collective-permute-start(f32[24,128]{1,0:T(8,128)S(1)} %get-tuple-element.67), channel_id=1, source_target_pairs={{1,0},{2,1},{3,2},{4,3},{5,4},{6,5},{7,6},{9,8},{10,9},{11,10},{12... | collective-permute-start | bytes 36872 | tf_op jit(solution)/shard_map/ppermute | solution.py:384
  29.2 27.1 %copy-start = (f32[1,1,8,1024]{3,2,1,0:T(8,128)S(1)}, f32[1,1,8,1024]{3,2,1,0:T(8,128)}, u32[]{:S(2)}) copy-start(f32[1,1,8,1024]{3,2,1,0:T(8,128)} %param.9) | copy-start | bytes 98308
  29.2 27.1 %copy-start.2 = (s32[1,1,1024]{2,1,0:T(1,128)S(1)}, s32[1,1,1024]{2,1,0:T(1,128)}, u32[]{:S(2)}) copy-start(s32[1,1,1024]{2,1,0:T(1,128)} %param.13) | copy-start | bytes 12292
  56.7 3.8 %collective-permute-start.2 = (f32[8,128]{1,0:T(8,128)S(1)}, f32[8,128]{1,0:T(8,128)S(1)}, u32[]{:S(2)}, u32[]{:S(2)}) collective-permute-start(f32[8,128]{1,0:T(8,128)S(1)} %get-tuple-element.79.refs_2_), channel_id=1, source_target_pairs={{0,1},{1,2},{2,3},{3,4},{4,5},{5,6},{6,7},{8,9},{9,10},{10,11},{11... | collective-permute-start | bytes 12296 | tf_op jit(solution)/shard_map/ppermute | solution.py:384
  88.9 3.8 %collective-permute-start.3 = (f32[8,128]{1,0:T(8,128)S(1)}, f32[8,128]{1,0:T(8,128)S(1)}, u32[]{:S(2)}, u32[]{:S(2)}) collective-permute-start(f32[8,128]{1,0:T(8,128)S(1)} %get-tuple-element.93.refs_2_), channel_id=1, source_target_pairs={{0,1},{1,2},{2,3},{3,4},{4,5},{5,6},{6,7},{8,9},{9,10},{10,11},{11... | collective-permute-start | bytes 12296 | tf_op jit(solution)/shard_map/ppermute | solution.py:384
  120.1 3.8 %collective-permute-start.4 = (f32[8,128]{1,0:T(8,128)S(1)}, f32[8,128]{1,0:T(8,128)S(1)}, u32[]{:S(2)}, u32[]{:S(2)}) collective-permute-start(f32[8,128]{1,0:T(8,128)S(1)} %get-tuple-element.105.refs_2_), channel_id=1, source_target_pairs={{0,1},{1,2},{2,3},{3,4},{4,5},{5,6},{6,7},{8,9},{9,10},{10,11},{11... | collective-permute-start | bytes 12296 | tf_op jit(solution)/shard_map/ppermute | solution.py:384

commit v10 on v9

--- a/solution.py
+++ b/solution.py
@@ -241,33 +241,34 @@
     return jnp.where(lane == SQUARE, square, jnp.where(lane == CURVATURE, curvature, 0.0))
 
 
-def announce(sums_ref, g_ref, gown_ref, valid_ref, below_ref, out_ref):
+def add_pairs(sums_ref, g_ref, gown_ref, valid_ref, below_ref, out_ref):
     own = valid_ref[...] * gown_ref[...]
     squares = own * own
     pairs = g_ref[:, :FACE] * below_ref[...]
     terms = squares[:, :LANES] + squares[:, LANES:] - 2.0 * pairs
-    more = jnp.sum(terms, axis=1, keepdims=True)
-    lane = lax.broadcasted_iota(jnp.int32, (8, LANES), 1)
-    extra = sums_ref[...] + jnp.where(lane == CURVATURE, more, 0.0)
-    halves = own[:, :LANES] + extra, own[:, LANES:] + extra
-    for plan in range(out_ref.shape[0]):
-        out_ref[plan] = halves[plan % 2]
+    lane = lax.broadcasted_iota(jnp.int32, (8, LANES), 1)
+    out_ref[...] = sums_ref[...] + jnp.where(lane == CURVATURE, lane_sum(terms), 0.0)
+
+
+def announce(sums_ref, keep_ref, swapped_ref, out_ref):
+    parcel = jnp.concatenate([keep_ref[...] + sums_ref[...], swapped_ref[...]], axis=0)
+    out_ref[...] = jnp.broadcast_to(parcel[None], out_ref.shape)
 
 
 def layer_sums(where_ref, table_ref, in_ref, g_ref, out_ref, *gfar_refs):
     plan = where_ref[0, 2]
+    core = lax.rem(plan, 2)
     for gfar_ref in gfar_refs:
         gfar_ref[...] = half_of(in_ref, table_ref, plan)
     products = sums = jnp.zeros((8, LANES), F32)
     for p in range(in_ref.shape[0]):
-        near = in_ref[p]
+        near = in_ref[p + core if p % 2 == 0 else p - core]
         sums = sums + near
         products = products + near * half_of(in_ref, table_ref, p)
-    cross = lane_sum(products)
-    lane = lax.broadcasted_iota(jnp.int32, (8, LANES), 1)
-    sums = 0.5 * sums - jnp.where(lane == CURVATURE, cross, 0.0)
+    lane = lax.broadcasted_iota(jnp.int32, (8, LANES), 1)
+    sums = sums - jnp.where(lane == CURVATURE, lane_sum(products), 0.0)
     if gfar_refs:
-        sibling = half_of(in_ref, table_ref, plan + 1 - 2 * lax.rem(plan, 2))
+        sibling = half_of(in_ref, table_ref, plan + 1 - 2 * core)
         sums = jnp.concatenate([jnp.where(lane < SQUARE, sibling, sums), g_ref[:, :FACE]], axis=1)
     out_ref[...] = jnp.broadcast_to(sums[None], out_ref.shape)
 
@@ -332,8 +333,10 @@
         pltpu.roll(lines, LANES - NAMES, 1),
         pltpu.roll(lines, LANES - NAMES - HALF, 1),
     )
-    table_ref[...] = names[:, :8].astype(jnp.int32)
-    rest_by(gfar_ref[...], *refs)
+    names = names[:, :8].astype(jnp.int32)
+    other = names + 1 - 2 * (names & 1)
+    table_ref[...] = jnp.where(masks_ref[2, :1, :8] == 0.0, names, other)
+    rest_by(gfar_ref[...], masks_ref, *refs)
 
 
 def next_rest(in_ref, masks_ref, half_ref, *refs):
@@ -342,13 +345,14 @@
     half, other = half_ref[...], jnp.where(lane < SQUARE, other, 0.0)
     even = masks_ref[2, :1] == 0.0
     rest_by(
-        jnp.concatenate([jnp.where(even, half, other), jnp.where(even, other, half)], axis=1), *refs
-    )
-
-
-def rest_by(gfar, step_ref, x_ref, last_ref, load_ref, own_ref, gown_ref, far_ref,
+        jnp.concatenate([jnp.where(even, half, other), jnp.where(even, other, half)], axis=1),
+        masks_ref, *refs,
+    )
+
+
+def rest_by(gfar, masks_ref, step_ref, x_ref, last_ref, load_ref, own_ref, gown_ref, far_ref,
             below_ref, gbelow_ref, valid_ref, onehot_ref, high_ref, low_ref,
-            g_out, gown_out, sums_out, *halo_outs):
+            g_out, gown_out, sums_out, keep_out, give_out, *halo_outs):
     step, x = step_ref[:, :1], x_ref[...]
     inner = x.shape[1] - FACE
     halo = []
@@ -363,7 +367,12 @@
     head = total[:, :FACE] + (x[:, :FACE] - below)
     g = jnp.concatenate([head, total[:, FACE:], last_ref[...]], axis=1)
     g_out[...] = g
-    gown_out[...] = pick(g, onehot)[0]
+    gown = pick(g, onehot)[0]
+    gown_out[...] = gown
+    jumps = valid_ref[...] * gown
+    even = masks_ref[2, :1] == 0.0
+    keep_out[...] = jnp.where(even, jumps[:, :LANES], jumps[:, LANES:])
+    give_out[...] = jnp.where(even, jumps[:, LANES:], jumps[:, :LANES])
     sums_out[...] = local_sums(g, high_ref, low_ref)
 
 
@@ -397,6 +406,7 @@
     position = jnp.stack([lax.axis_index("layer"), layers, lax.axis_index("plan")])
     position = position.astype(jnp.int32).reshape(1, 3)
     amounts, position = lax.optimization_barrier((amounts, position))
+    cores = [list(range(core, plans, 2)) for core in range(2)]
     columns = [
         [(chip + core) * layers + layer for layer in range(layers) for core in range(2)]
         for chip in range(0, plans, 2)
@@ -431,24 +441,27 @@
     x, last, step, above = call(
         first_face, "first_face", early, [VMEM] * 9, 12, flops // 8, width * width // 2,
     )(incoming, gabove, x, g, flags, target, above, high, low)
-    late = (field, jump, face, jump2, jump2, face2)
+    late = (field, jump, face, face, face, jump2, jump2, face2)
     below_next = lift(last, 1)
-    g, gown, sums, own, far, below, table = call(
+    g, gown, sums, keep, give, own, far, below, table = call(
         first_rest, "first_rest", late + (shape(plans, 8, dtype=jnp.int32),),
         [VMEM] * 16, 12, 2 * flops, 8 * width * width,
     )(incoming, masks, gfar, step, x, last, target, own, gown, far, below, gbelow, valid, onehot, high, low)
 
     for iteration in range(1, ITERS):
         gbelow = below_next
-        out = call(announce, "announce", shape(plans, loads, LANES), [VMEM] * 5, 8)(
-            sums, g, gown, valid, gbelow
+        sums = call(add_pairs, "add_pairs", face, [VMEM] * 5, 8)(sums, g, gown, valid, gbelow)
+        swapped = lax.ppermute(give, "plan", [(p, p ^ 1) for p in range(plans)])
+        out = call(announce, "announce", shape(plans // 2, 2 * loads, LANES), [VMEM] * 3, 8)(
+            sums, keep, swapped
         )
+        everyone = swap(out, "plan", cores).reshape(plans, loads, LANES)
         ending = iteration == ITERS - 1
         parcel = shape(2 * layers, loads, LANES if ending else LANES + FACE)
         out, *half = call(
             layer_sums, "layer_sums", (parcel,) + (() if ending else (shape(loads, LANES),)),
             [SMEM] * 2 + [VMEM] * 2, 8,
-        )(position, table, swap(out, "plan"), g)
+        )(position, table, everyone, g)
         incoming = swap(out, ("plan", "layer"), columns)
         if ending:
             x, g = call(finish, "finish", (field, field), [VMEM] * 4, 8)(incoming, x, g, flags)
@@ -457,8 +470,8 @@
             next_face, "next_face", early[:3] if iteration == ITERS - 2 else early, [VMEM] * 9, 12, flops // 8, width * width // 2,
         )(incoming, masks, x, g, flags, target, above, high, low)
         below_next = lift(last, 1)
-        g, gown, sums, *halo = call(
-            next_rest, "next_rest", late[:3] if iteration == ITERS - 2 else late,
+        g, gown, sums, keep, give, *halo = call(
+            next_rest, "next_rest", late[:5] if iteration == ITERS - 2 else late,
             [VMEM] * 16, 12, 2 * flops, 8 * width * width,
         )(incoming, masks, *half, step, x, last, target, own, gown, far, below, gbelow,
           valid, onehot, high, low)

time: 152 us -> 151 us (level)
  blocking collectives: 103 us -> 97.2 us
  starting transfers between devices: 23.5 us -> 26.2 us
  waiting for transfers between devices: 6.49 us -> 8.7 us
    all_to_all x7, blocking collectives: 103 us -> 97.2 us  [swap(): lax.all_to_all(outgoing, axis, split_axis=0, concat_axis=0, tiled=True, a...]
    ppermute x0 -> x3, starting transfers between devices: none -> 2.61 us  [shards(): swapped = lax.ppermute(give, 'plan', [(p, p ^ 1) for p in range(plans)])]
    ppermute x0 -> x3, waiting for transfers between devices: none -> 2.21 us  [shards(): swapped = lax.ppermute(give, 'plan', [(p, p ^ 1) for p in range(plans)])]
    pallas_call x5 -> x8, Pallas kernels: 3.59 us -> 3.54 us  [the longest x2 3.26 us: shards(): call(next_rest, 'next_rest', late[:5] if iteration == ITERS - 2 else late...]
  transfers between devices with their start and end apart: 6 -> 9, of which waited for: 2 -> 5; matrix products, arithmetic and copies ran while one was open for 0% -> 0% of each run, Pallas kernels for 3% -> 3%
where the time goes in v10:
time: 151 us; the launch traced here: 150 us
  blocking collectives  97.2 us (64%)
  starting transfers between devices  26.2 us (17%)
  Pallas kernels  17.6 us (12%)
  waiting for transfers between devices  8.7 us (6%)
    all_to_all x7, blocking collectives, swap(): lax.all_to_all(outgoing, axis, split_axis=0, concat_axis=0, tiled=True, a...  97.2 us
    all_to_all x1, starting transfers between devices, swap(): lax.all_to_all(outgoing, axis, split_axis=0, concat_axis=0, tiled=True, a...  12.6 us
    ppermute x5, starting transfers between devices, lift(): lax.ppermute(face, 'layer', [(i, i + step) for i in range(layers) if 0 <=...  10.9 us
    pallas_call x1, Pallas kernels, shards(): call(prepare, 'prepare', (shape(width, JW, dtype=BF16), jump, jump2, jump...  4.88 us
    ppermute x5, waiting for transfers between devices, lift(): lax.ppermute(face, 'layer', [(i, i + step) for i in range(layers) if 0 <=...  3.43 us
    pallas_call x2, Pallas kernels, shards(): call(next_rest, 'next_rest', late[:5] if iteration == ITERS - 2 else late...  3.26 us
    all_to_all x1, waiting for transfers between devices, swap(): lax.all_to_all(outgoing, axis, split_axis=0, concat_axis=0, tiled=True, a...  3.05 us
  transfers between devices with their start and end apart: 9, of which 5 were waited for; matrix products, arithmetic and copies ran while one was open for 0% of the time, Pallas kernels for 3%

profile of v10, /device:TPU:1, one launch (start us, length us, event | category | flops | bytes accessed | tf_op | source)
XLA Modules:
  0.0 150.4 jit_solution(785686358567087512)
XLA Ops:
  0.6 0.1 add_bitcast_fusion.where_ref
  0.7 0.0 copy-start.1
  0.7 0.0 copy-start.3
  0.7 4.9 %prepare.1 = (bf16[1024,256]{1,0:T(8,128)(2,1)S(1)}, f32[8,256]{1,0:T(8,128)S(1)}, f32[16,256]{1,0:T(8,128)S(1)}, f32[8,256]{1,0:T(8,128)S(1)}, f32[8,1024]{1,0:...) custom-call(f32[1024,1024]{1,0:T(8,128)} %bitcast.40, ...), custom_call_target="tpu_custom_call" | custom-call | flops 67108864 | bytes 4194304 | tf_op jit(solution)/shard_map/prepare/pallas_call | solution.py:418
  5.6 12.6 %all-to-all-start = ((f32[32,8,128]{2,1,0:T(8,128)}), f32[32,8,128]{2,1,0:T(8,128)S(1)}, u32[]{:S(2)}, u32[]{:S(2)}) async-start(f32[32,8,128]{2,1,0:T(8,128)} %get-tuple-element.71), calls=%async_computation | async-start | bytes 262144 | tf_op jit(solution)/shard_map/all_to_all | solution.py:386
  18.2 3.2 %collective-permute-start = (f32[24,128]{1,0:T(8,128)S(1)}, f32[24,128]{1,0:T(8,128)S(1)}, u32[]{:S(2)}, u32[]{:S(2)}) collective-permute-start(f32[24,128]{1,0:T(8,128)S(1)} %get-tuple-element.72), channel_id=1, source_target_pairs={{0,1},{1,2},{2,3},{3,4},{4,5},{5,6},{6,7},{8,9},{9,10},{10,11},{11... | collective-permute-start | bytes 36872 | tf_op jit(solution)/shard_map/ppermute | solution.py:393
  21.4 1.3 collective-permute-start.1
  22.7 0.0 collective-permute-done.below_in
  22.7 3.4 %collective-permute-done.1.above_in = f32[24,128]{1,0:T(8,128)S(1)} collective-permute-done((f32[24,128]{1,0:T(8,128)S(1)}, f32[24,128]{1,0:T(8,128)S(1)}, u32[]{:S(2)}, u32[]{:S(2)}) %collective-permute-start.1) | collective-permute-done | bytes 12320 | tf_op jit(solution)/shard_map/ppermute | solution.py:393
  26.1 3.1 %all-to-all-done.in_ref = f32[32,8,128]{2,1,0:T(8,128)S(1)} async-done(((f32[32,8,128]{2,1,0:T(8,128)}), f32[32,8,128]{2,1,0:T(8,128)S(1)}, u32[]{:S(2)}, u32[]{:S(2)}) %all-to-all-start) | async-done | bytes 131104 | tf_op jit(solution)/shard_map/all_to_all | solution.py:386
  29.2 0.0 copy-done.1
  29.2 0.0 copy-done.3
  29.2 0.0 copy-start
  29.2 2.7 %first_gradient.1 = (f32[8,1024]{1,0:T(8,128)S(1)}, f32[8,256]{1,0:T(8,128)S(1)}, f32[16,256]{1,0:T(8,128)S(1)}, f32[8,256]{1,0:T(8,128)S(1)}, f32[16,128]{1,0:T...) custom-call(s32[1,6]{1,0:T(1,128)S(1)} %copy-done.3, ...), custom_call_target="tpu_custom_call" | custom-call | flops 67108864 | bytes 4194304 | tf_op jit(solution)/shard_map/first_gradient/pallas_call | solution.py:432
  31.9 24.4 %all_to_all.46 = f32[256,1,128]{2,1,0:T(1,128)S(1)} all-to-all(f32[256,1,128]{2,1,0:T(1,128)S(1)} %bitcast.34), channel_id=1, replica_groups=mesh['plan'=32,'layer'=8] {'plan','layer'}, dimensions={0} | all-to-all | bytes 262144 | tf_op jit(solution)/shard_map/all_to_all | solution.py:386
  56.3 0.0 copy-done
  56.3 0.0 copy-done.2
  56.3 0.3 first_face.1
  56.7 2.2 %collective-permute-start.2 = (f32[8,128]{1,0:T(8,128)S(1)}, f32[8,128]{1,0:T(8,128)S(1)}, u32[]{:S(2)}, u32[]{:S(2)}) collective-permute-start(f32[8,128]{1,0:T(8,128)S(1)} %get-tuple-element.85.refs_2_), channel_id=1, source_target_pairs={{0,1},{1,2},{2,3},{3,4},{4,5},{5,6},{6,7},{8,9},{9,10},{10,11},{11... | collective-permute-start | bytes 12296 | tf_op jit(solution)/shard_map/ppermute | solution.py:393
  58.9 1.6 %first_rest.1 = (f32[8,1024]{1,0:T(8,128)S(1)}, f32[8,256]{1,0:T(8,128)S(1)}, f32[8,128]{1,0:T(8,128)S(1)}, f32[8,128]{1,0:T(8,128)S(1)}, f32[8,128]{1,0:T(8,128...) custom-call(f32[256,128]{1,0:T(8,128)S(1)} %bitcast.27, ...), custom_call_target="tpu_custom_call" | custom-call | flops 134217728 | bytes 8388608 | tf_op jit(solution)/shard_map/first_rest/pallas_call | solution.py:446
  60.5 1.5 collective-permute-start.3
  62.0 0.0 collective-permute-done.2.below_ref.refs_8_
  62.0 0.1 add_pairs.3.sums_ref
  62.1 0.7 collective-permute-done.3.swapped_ref
  62.8 11.9 %all_to_all.47 = f32[16,16,128]{2,1,0:T(8,128)S(1)} all-to-all(f32[16,16,128]{2,1,0:T(8,128)S(1)} %announce.3), channel_id=1, replica_groups={{0,16,32,48,64,80,96,112,128,144,160,176,192,208,224,240},{8,24,40,56,7..., dimensions={0} | all-to-all | bytes 262144 | tf_op jit(solution)/shard_map/all_to_all | solution.py:386
  74.7 1.0 layer_sums.3
  75.7 12.3 %all_to_all.48.in_ref = f32[16,8,256]{2,1,0:T(8,128)S(1)} all-to-all(f32[16,8,256]{2,1,0:T(8,128)S(1)} %get-tuple-element.96), channel_id=1, replica_groups={{0,8,1,9,2,10,3,11,4,12,5,13,6,14,7,15},{16,24,17,25,18,26,19,27,20,28,..., dimensions={0} | all-to-all | bytes 262144 | tf_op jit(solution)/shard_map/all_to_all | solution.py:386
  88.0 0.4 next_face.2
  88.4 2.1 %collective-permute-start.4 = (f32[8,128]{1,0:T(8,128)S(1)}, f32[8,128]{1,0:T(8,128)S(1)}, u32[]{:S(2)}, u32[]{:S(2)}) collective-permute-start(f32[8,128]{1,0:T(8,128)S(1)} %get-tuple-element.101.refs_2_), channel_id=1, source_target_pairs={{0,1},{1,2},{2,3},{3,4},{4,5},{5,6},{6,7},{8,9},{9,10},{10,11},{11... | collective-permute-start | bytes 12296 | tf_op jit(solution)/shard_map/ppermute | solution.py:393
  90.5 1.6 %next_rest.2 = (f32[8,1024]{1,0:T(8,128)S(1)}, f32[8,256]{1,0:T(8,128)S(1)}, f32[8,128]{1,0:T(8,128)S(1)}, f32[8,128]{1,0:T(8,128)S(1)}, f32[8,128]{1,0:T(8,128)...) custom-call(f32[16,8,256]{2,1,0:T(8,128)S(1)} %all_to_all.48.in_ref, ...), custom_call_target="tpu_custom_call" | custom-call | flops 134217728 | bytes 8388608 | tf_op jit(solution)/shard_map/next_rest/pallas_call | solution.py:473
  92.1 0.6 collective-permute-start.5
  92.7 0.0 collective-permute-done.4.below_ref.refs_8_
  92.7 0.1 add_pairs.4.sums_ref
  92.8 0.7 collective-permute-done.5.swapped_ref
  93.5 12.2 %all_to_all.49 = f32[16,16,128]{2,1,0:T(8,128)S(1)} all-to-all(f32[16,16,128]{2,1,0:T(8,128)S(1)} %announce.4), channel_id=1, replica_groups={{0,16,32,48,64,80,96,112,128,144,160,176,192,208,224,240},{8,24,40,56,7..., dimensions={0} | all-to-all | bytes 262144 | tf_op jit(solution)/shard_map/all_to_all | solution.py:386
  105.7 1.0 layer_sums.4
  106.7 12.3 %all_to_all.50.in_ref = f32[16,8,256]{2,1,0:T(8,128)S(1)} all-to-all(f32[16,8,256]{2,1,0:T(8,128)S(1)} %get-tuple-element.110), channel_id=1, replica_groups={{0,8,1,9,2,10,3,11,4,12,5,13,6,14,7,15},{16,24,17,25,18,26,19,27,20,28,..., dimensions={0} | all-to-all | bytes 262144 | tf_op jit(solution)/shard_map/all_to_all | solution.py:386
  119.1 0.4 next_face.3
  119.4 2.1 %collective-permute-start.6 = (f32[8,128]{1,0:T(8,128)S(1)}, f32[8,128]{1,0:T(8,128)S(1)}, u32[]{:S(2)}, u32[]{:S(2)}) collective-permute-start(f32[8,128]{1,0:T(8,128)S(1)} %get-tuple-element.115.refs_2_), channel_id=1, source_target_pairs={{0,1},{1,2},{2,3},{3,4},{4,5},{5,6},{6,7},{8,9},{9,10},{10,11},{11... | collective-permute-start | bytes 12296 | tf_op jit(solution)/shard_map/ppermute | solution.py:393
  121.6 1.6 %next_rest.3 = (f32[8,1024]{1,0:T(8,128)S(1)}, f32[8,256]{1,0:T(8,128)S(1)}, f32[8,128]{1,0:T(8,128)S(1)}, f32[8,128]{1,0:T(8,128)S(1)}, f32[8,128]{1,0:T(8,128)S(1)}) custom-call(f32[16,8,256]{2,1,0:T(8,128)S(1)} %all_to_all.50.in_ref, f32[3,16,128]{2,1,0:T(8,128)S(1)} %get-tuple-element.77.masks_ref, f32[8,128]{1,0:T(8,128)S(1)} %get-tuple-element.111.half_ref, ...), custom_call_target="tpu_custom_call" | custom-call | flops 134217728 | bytes 8388608 | tf_op jit(solution)/shard_map/next_rest/pallas_call | solution.py:473
  123.2 0.6 collective-permute-start.7
  123.7 0.0 collective-permute-done.6.below_ref
  123.8 0.1 add_pairs.5.sums_ref
  123.8 0.7 collective-permute-done.7.swapped_ref
  124.6 12.0 %all_to_all.51 = f32[16,16,128]{2,1,0:T(8,128)S(1)} all-to-all(f32[16,16,128]{2,1,0:T(8,128)S(1)} %announce.5), channel_id=1, replica_groups={{0,16,32,48,64,80,96,112,128,144,160,176,192,208,224,240},{8,24,40,56,7..., dimensions={0} | all-to-all | bytes 262144 | tf_op jit(solution)/shard_map/all_to_all | solution.py:386
  136.6 1.0 layer_sums.5
  137.6 12.0 %all_to_all.52.in_ref = f32[16,8,128]{2,1,0:T(8,128)S(1)} all-to-all(f32[16,8,128]{2,1,0:T(8,128)S(1)} %layer_sums.5), channel_id=1, replica_groups={{0,8,1,9,2,10,3,11,4,12,5,13,6,14,7,15},{16,24,17,25,18,26,19,27,20,28,..., dimensions={0} | all-to-all | bytes 131072 | tf_op jit(solution)/shard_map/all_to_all | solution.py:386
  149.6 0.8 finish.1
  (4 shorter events, 0.0 us)
Async XLA Ops:
  0.7 28.5 %copy-start.1 = (f32[1,1,8,1024]{3,2,1,0:T(8,128)S(1)}, f32[1,1,8,1024]{3,2,1,0:T(8,128)}, u32[]{:S(2)}) copy-start(f32[1,1,8,1024]{3,2,1,0:T(8,128)} %param.8) | copy-start | bytes 98308
  0.7 28.5 %copy-start.3 = (s32[1,6]{1,0:T(1,128)S(1)}, s32[1,6]{1,0:T(1,128)}, u32[]{:S(2)}) copy-start(s32[1,6]{1,0:T(1,128)} %partners_ref.1) | copy-start | bytes 76
  5.6 23.6 %all-to-all-start = ((f32[32,8,128]{2,1,0:T(8,128)}), f32[32,8,128]{2,1,0:T(8,128)S(1)}, u32[]{:S(2)}, u32[]{:S(2)}) async-start(f32[32,8,128]{2,1,0:T(8,128)} %get-tuple-element.71), calls=%async_computation | async-start | bytes 262144 | tf_op jit(solution)/shard_map/all_to_all | solution.py:386
  18.2 4.5 %collective-permute-start = (f32[24,128]{1,0:T(8,128)S(1)}, f32[24,128]{1,0:T(8,128)S(1)}, u32[]{:S(2)}, u32[]{:S(2)}) collective-permute-start(f32[24,128]{1,0:T(8,128)S(1)} %get-tuple-element.72), channel_id=1, source_target_pairs={{0,1},{1,2},{2,3},{3,4},{4,5},{5,6},{6,7},{8,9},{9,10},{10,11},{11... | collective-permute-start | bytes 36872 | tf_op jit(solution)/shard_map/ppermute | solution.py:393
  21.4 4.7 %collective-permute-start.1 = (f32[24,128]{1,0:T(8,128)S(1)}, f32[24,128]{1,0:T(8,128)S(1)}, u32[]{:S(2)}, u32[]{:S(2)}) collective-permute-start(f32[24,128]{1,0:T(8,128)S(1)} %get-tuple-element.73), channel_id=1, source_target_pairs={{1,0},{2,1},{3,2},{4,3},{5,4},{6,5},{7,6},{9,8},{10,9},{11,10},{12... | collective-permute-start | bytes 36872 | tf_op jit(solution)/shard_map/ppermute | solution.py:393
  29.2 27.1 %copy-start = (f32[1,1,8,1024]{3,2,1,0:T(8,128)S(1)}, f32[1,1,8,1024]{3,2,1,0:T(8,128)}, u32[]{:S(2)}) copy-start(f32[1,1,8,1024]{3,2,1,0:T(8,128)} %param.9) | copy-start | bytes 98308
  29.2 27.1 %copy-start.2 = (s32[1,1,1024]{2,1,0:T(1,128)S(1)}, s32[1,1,1024]{2,1,0:T(1,128)}, u32[]{:S(2)}) copy-start(s32[1,1,1024]{2,1,0:T(1,128)} %param.13) | copy-start | bytes 12292
  56.7 5.3 %collective-permute-start.2 = (f32[8,128]{1,0:T(8,128)S(1)}, f32[8,128]{1,0:T(8,128)S(1)}, u32[]{:S(2)}, u32[]{:S(2)}) collective-permute-start(f32[8,128]{1,0:T(8,128)S(1)} %get-tuple-element.85.refs_2_), channel_id=1, source_target_pairs={{0,1},{1,2},{2,3},{3,4},{4,5},{5,6},{6,7},{8,9},{9,10},{10,11},{11... | collective-permute-start | bytes 12296 | tf_op jit(solution)/shard_map/ppermute | solution.py:393
  60.5 2.3 %collective-permute-start.3 = (f32[8,128]{1,0:T(8,128)S(1)}, f32[8,128]{1,0:T(8,128)S(1)}, u32[]{:S(2)}, u32[]{:S(2)}) collective-permute-start(f32[8,128]{1,0:T(8,128)S(1)} %get-tuple-element.95), channel_id=1, source_target_pairs={{0,8},{8,0},{16,24},{24,16},{32,40},{40,32},{48,56},{56,48},{64,72... | collective-permute-start | bytes 12296 | tf_op jit(solution)/shard_map/ppermute | solution.py:454
  88.4 4.3 %collective-permute-start.4 = (f32[8,128]{1,0:T(8,128)S(1)}, f32[8,128]{1,0:T(8,128)S(1)}, u32[]{:S(2)}, u32[]{:S(2)}) collective-permute-start(f32[8,128]{1,0:T(8,128)S(1)} %get-tuple-element.101.refs_2_), channel_id=1, source_target_pairs={{0,1},{1,2},{2,3},{3,4},{4,5},{5,6},{6,7},{8,9},{9,10},{10,11},{11... | collective-permute-start | bytes 12296 | tf_op jit(solution)/shard_map/ppermute | solution.py:393
  92.1 1.4 collective-permute-start.5
  119.4 4.3 %collective-permute-start.6 = (f32[8,128]{1,0:T(8,128)S(1)}, f32[8,128]{1,0:T(8,128)S(1)}, u32[]{:S(2)}, u32[]{:S(2)}) collective-permute-start(f32[8,128]{1,0:T(8,128)S(1)} %get-tuple-element.115.refs_2_), channel_id=1, source_target_pairs={{0,1},{1,2},{2,3},{3,4},{4,5},{5,6},{6,7},{8,9},{9,10},{10,11},{11... | collective-permute-start | bytes 12296 | tf_op jit(solution)/shard_map/ppermute | solution.py:393
  123.2 1.4 collective-permute-start.7

commit v11 on v10

--- a/solution.py
+++ b/solution.py
@@ -1,5 +1,3 @@
-import functools
-
 import jax
 import jax.numpy as jnp
 from jax import lax
@@ -37,7 +35,7 @@
         out_shape=outs,
         in_specs=specs,
         scratch_shapes=scratch,
-        out_specs=jax.tree.map(lambda out: VMEM if isinstance(out, jax.ShapeDtypeStruct) else HBM, outs),
+        out_specs=jax.tree.map(lambda _: VMEM, outs),
         compiler_params=pltpu.CompilerParams(vmem_limit_bytes=limit * 2**20),
         cost_estimate=pl.CostEstimate(flops=flops, bytes_accessed=traffic, transcendentals=0),
     )
@@ -56,14 +54,14 @@
     return jnp.sum(value, axis=1, keepdims=True)
 
 
-def dense(field, high_ref, low_ref, columns=slice(None), copies=()):
+def dense(field, high_ref, low_ref, columns=slice(None), arrive=None):
     lhs = jnp.concatenate(pieces(field, 2), axis=0).astype(BF16)
     depth = field.shape[1] // CHUNKS
     total = 0.0
-    for half_ref, arrivals in ((high_ref, ()), (low_ref, copies)):
+    for half_ref in (high_ref, low_ref):
         for chunk in range(CHUNKS):
-            for copy in arrivals[chunk : chunk + 1]:
-                copy.wait()
+            if half_ref is low_ref and arrive is not None:
+                arrive(chunk)
             at = slice(chunk * depth, (chunk + 1) * depth)
             total = total + jnp.dot(lhs[:, at], half_ref[at, columns], preferred_element_type=F32)
     return total[:8] + total[8:]
@@ -87,11 +85,11 @@
     place = lax.broadcasted_iota(jnp.int32, (8, LANES), 1) // JR
     total = jnp.zeros((8, LANES), F32)
     for r in range(HALF):
-        total = jnp.where(place == r, in_ref[table_ref[plan, r]], total)
+        total = jnp.where(place == r, in_ref[table_ref[0, HALF * plan + r]], total)
     return total
 
 
-def stream_dense(field, block_ref, rows_ref, sems, high_ref, low_ref, give):
+def stream_dense(field, block_ref, rows_ref, sems, high_ref, low_ref):
     lhs = jnp.concatenate(pieces(field, 2), axis=0).astype(BF16)
     depth = rows_ref.shape[0] // CHUNKS
     total = jnp.zeros((lhs.shape[0], rows_ref.shape[1]), F32)
@@ -104,7 +102,6 @@
             high = rows.astype(BF16)
             high_ref[strip, :] = high
             low_ref[strip, :] = (rows - high.astype(F32)).astype(BF16)
-        give(chunk).start()
         total = total + jnp.dot(lhs[:, at], high_ref[at, :], preferred_element_type=F32)
         total = total + jnp.dot(lhs[:, at], low_ref[at, :], preferred_element_type=F32)
     return total[:8] + total[8:]
@@ -118,8 +115,8 @@
 
 def prepare(block_ref, x_hbm, load_hbm, contact_hbm, rows_hbm, partners_hbm, counts_hbm,
             onehot_ref, valid_ref, own_ref, hown_ref, h_ref, out_ref, first_ref, last_ref, high_ref,
-            low_hbm, held_ref, low_ref, x_ref, load_ref, contact_ref, rows_ref, partners_ref, counts_ref,
-            sems, low_sems, more_sems):
+            held_ref, low_ref, x_ref, load_ref, contact_ref, rows_ref, partners_ref, counts_ref,
+            sems, more_sems):
     small = [
         pltpu.make_async_copy(source, target, more_sems.at[i])
         for i, (source, target) in enumerate((
@@ -153,8 +150,7 @@
     position = lax.broadcasted_iota(jnp.int32, x.shape, 1)
     edge = (position < FACE) | (position >= width - FACE)
     h = spread(valid * own, onehot_ref[...]) + jnp.where(edge, x, 0.0) - load_ref[...]
-    low_copy = functools.partial(chunk_copy, low_ref, low_hbm, low_sems)
-    h = h + stream_dense(x, block_ref, held_ref, sems, high_ref, low_ref, low_copy)
+    h = h + stream_dense(x, block_ref, held_ref, sems, high_ref, low_ref)
     h_ref[...] = h
     (hown,) = pick(h, onehot_ref[...])
     hown_ref[...] = hown
@@ -171,17 +167,23 @@
     both = jnp.concatenate([x, h, contact], axis=0)
     first_ref[...] = both[:, :FACE]
     last_ref[...] = both[:, width - FACE :]
-    for chunk in range(CHUNKS):
-        low_copy(chunk).wait()
-
-
-def first_gradient(partners_ref, where_ref, low_hbm, high_ref, x_ref, h_ref, own_ref, hown_ref, in_ref,
+
+
+def first_gradient(partners_ref, where_ref, block_ref, high_ref, x_ref, h_ref, own_ref, hown_ref, in_ref,
                    below_in, above_in, valid_ref, onehot_ref,
                    g_ref, gown_ref, far_ref, gfar_ref, below_ref, gbelow_ref, above_ref, gabove_ref,
-                   all_ref, masks_ref, low_ref, sems):
-    copies = [chunk_copy(low_hbm, low_ref, sems, chunk) for chunk in range(CHUNKS)]
-    for copy in copies:
-        copy.start()
+                   all_ref, masks_ref, low_ref, held_ref, sems):
+    for chunk in range(CHUNKS):
+        chunk_copy(block_ref, held_ref, sems, chunk).start()
+
+    def arrive(chunk):
+        chunk_copy(block_ref, held_ref, sems, chunk).wait()
+        depth = held_ref.shape[0] // CHUNKS
+        for first in range(chunk * depth, (chunk + 1) * depth, STRIP):
+            strip = slice(first, first + STRIP)
+            rest = held_ref[strip, :] - high_ref[strip, :].astype(F32)
+            low_ref[strip, :] = rest.astype(BF16)
+
     width = x_ref.shape[1]
     place = lax.broadcasted_iota(jnp.int32, (8, LANES), 1) // JR
     parts = [[jnp.zeros((8, LANES), F32)] * 2 for _ in range(3)]
@@ -207,6 +209,7 @@
     masks_ref[0] = jnp.where(member == 2 * (layer + 1) + core, 1.0, 0.0)
     masks_ref[1] = jnp.where(member == 2 * layer + 1 - core, 1.0, 0.0)
     masks_ref[2] = jnp.where(member >= 0, core, 0).astype(F32)
+    masks_ref[3] = jnp.where(member >= 0, where_ref[0, 2], 0).astype(F32)
     gbelow = jnp.where(layer > 0, below[8:16] - x_ref[:, :FACE], 0.0)
     gabove = jnp.where(layer < layers - 1, above[8:16] - x_ref[:, width - FACE :], 0.0)
     gbelow_ref[...] = gbelow
@@ -219,7 +222,7 @@
     jumps = valid * gown * (gown - gfar)
     terms = first * (first - gbelow) + last * (last - gabove) + jumps[:, :LANES] + jumps[:, LANES:]
     square = lane_sum(g * g)
-    image = dense(g, high_ref, low_ref, copies=copies)
+    image = dense(g, high_ref, low_ref, arrive=arrive)
     curvature = lane_sum(terms) + lane_sum(g * image)
     lane = lax.broadcasted_iota(jnp.int32, (8, LANES), 1)
     row = lax.broadcasted_iota(jnp.int32, (8, LANES), 0)
@@ -255,8 +258,8 @@
     out_ref[...] = jnp.broadcast_to(parcel[None], out_ref.shape)
 
 
-def layer_sums(where_ref, table_ref, in_ref, g_ref, out_ref, *gfar_refs):
-    plan = where_ref[0, 2]
+def layer_sums(table_ref, in_ref, g_ref, out_ref, *gfar_refs):
+    plan = table_ref[0, HALF * in_ref.shape[0]]
     core = lax.rem(plan, 2)
     for gfar_ref in gfar_refs:
         gfar_ref[...] = half_of(in_ref, table_ref, plan)
@@ -326,16 +329,21 @@
 
 def first_rest(in_ref, masks_ref, gfar_ref, *refs):
     *refs, table_ref = refs
-    plans = table_ref.shape[0]
+    plans = in_ref.shape[0] * 2 // masks_ref.shape[1]
     lines = in_ref[pl.ds(0, plans, stride=in_ref.shape[0] // plans), :]
+    even = masks_ref[2, :1] == 0.0
     names = jnp.where(
-        masks_ref[2, :1] == 0.0,
-        pltpu.roll(lines, LANES - NAMES, 1),
-        pltpu.roll(lines, LANES - NAMES - HALF, 1),
-    )
-    names = names[:, :8].astype(jnp.int32)
-    other = names + 1 - 2 * (names & 1)
-    table_ref[...] = jnp.where(masks_ref[2, :1, :8] == 0.0, names, other)
+        even, pltpu.roll(lines, LANES - NAMES, 1), pltpu.roll(lines, LANES - NAMES - HALF, 1)
+    ).astype(jnp.int32)
+    names = jnp.where(even, names, names + 1 - 2 * (names & 1)).astype(F32)
+    lane = lax.broadcasted_iota(jnp.int32, (plans, LANES), 1)
+    plan = lax.broadcasted_iota(jnp.int32, (plans, LANES), 0)
+    table = jnp.zeros((plans, LANES), F32)
+    for r in range(HALF):
+        table = jnp.where(lane == HALF * plan + r, names[:, r : r + 1], table)
+    table = jnp.sum(table, axis=0, keepdims=True)
+    table = jnp.where(lane[:1] == HALF * plans, masks_ref[3, :1], table)
+    table_ref[...] = table.astype(jnp.int32)
     rest_by(gfar_ref[...], masks_ref, *refs)
 
 
@@ -415,16 +423,16 @@
     held = pltpu.VMEM((width, width), F32)
     chunk_sems = pltpu.SemaphoreType.DMA((CHUNKS,))
 
-    onehot, valid, own, hown, h, out, first, last, high, low = call(
+    onehot, valid, own, hown, h, out, first, last, high = call(
         prepare, "prepare",
         (shape(width, JW, dtype=BF16), jump, jump2, jump, field, shape(plans, loads, LANES), face3, face3,
-         half_shape, pltpu.HBM(half_shape.shape, BF16)),
+         half_shape),
         [HBM] * 7, 16, flops, 4 * width * width,
         [
             held, pltpu.VMEM((width, width), BF16), pltpu.VMEM(x.shape, F32), pltpu.VMEM(target.shape, F32),
             pltpu.VMEM(flags.shape, jnp.int32), pltpu.VMEM(rows.shape, jnp.int32),
             pltpu.SMEM(partners.shape, jnp.int32), pltpu.SMEM(amounts.shape, jnp.int32),
-            chunk_sems, chunk_sems, pltpu.SemaphoreType.DMA((6,)),
+            chunk_sems, pltpu.SemaphoreType.DMA((6,)),
         ],
     )(*(pltpu.with_memory_space_constraint(a, pltpu.HBM) for a in (block, x, target, flags, rows, partners, amounts)))
     incoming = swap(out, "plan")
@@ -432,9 +440,9 @@
     g, gown, far, gfar, below, gbelow, above, gabove, out, masks, low = call(
         first_gradient, "first_gradient",
         (field, jump, jump2, jump, face2, face, face2, face,
-         shape(plans * layers, LANES), shape(3, 2 * layers, LANES), half_shape),
-        [SMEM] * 2 + [HBM] + [VMEM] * 10, 12, flops, 4 * width * width, [chunk_sems],
-    )(partners, position, pltpu.with_memory_space_constraint(low, pltpu.HBM), high, x, h, own, hown, incoming, below, above, valid, onehot)
+         shape(plans * layers, LANES), shape(4, 2 * layers, LANES), half_shape),
+        [SMEM] * 2 + [HBM] + [VMEM] * 10, 12, flops, 4 * width * width, [held, chunk_sems],
+    )(partners, position, pltpu.with_memory_space_constraint(block, pltpu.HBM), high, x, h, own, hown, incoming, below, above, valid, onehot)
     incoming = swap(out, ("plan", "layer"))
 
     early = (field, face, face, face2)
@@ -444,7 +452,7 @@
     late = (field, jump, face, face, face, jump2, jump2, face2)
     below_next = lift(last, 1)
     g, gown, sums, keep, give, own, far, below, table = call(
-        first_rest, "first_rest", late + (shape(plans, 8, dtype=jnp.int32),),
+        first_rest, "first_rest", late + (shape(1, LANES, dtype=jnp.int32),),
         [VMEM] * 16, 12, 2 * flops, 8 * width * width,
     )(incoming, masks, gfar, step, x, last, target, own, gown, far, below, gbelow, valid, onehot, high, low)
 
@@ -460,8 +468,8 @@
         parcel = shape(2 * layers, loads, LANES if ending else LANES + FACE)
         out, *half = call(
             layer_sums, "layer_sums", (parcel,) + (() if ending else (shape(loads, LANES),)),
-            [SMEM] * 2 + [VMEM] * 2, 8,
-        )(position, table, everyone, g)
+            [SMEM] + [VMEM] * 2, 8,
+        )(table, everyone, g)
         incoming = swap(out, ("plan", "layer"), columns)
         if ending:
             x, g = call(finish, "finish", (field, field), [VMEM] * 4, 8)(incoming, x, g, flags)

time: 151 us -> 150 us (level)
  no operation moved by 1% of the time
where the time goes in v11:
time: 150 us
  blocking collectives  97.1 us (65%)
  starting transfers between devices  26.1 us (17%)
  Pallas kernels  17 us (11%)
  waiting for transfers between devices  8.7 us (6%)
    all_to_all x7, blocking collectives, swap(): lax.all_to_all(outgoing, axis, split_axis=0, concat_axis=0, tiled=True, a...  97.1 us
    all_to_all x1, starting transfers between devices, swap(): lax.all_to_all(outgoing, axis, split_axis=0, concat_axis=0, tiled=True, a...  12.6 us
    ppermute x5, starting transfers between devices, lift(): lax.ppermute(face, 'layer', [(i, i + step) for i in range(layers) if 0 <=...  10.9 us
    pallas_call x1, Pallas kernels, shards(): call(prepare, 'prepare', (shape(width, JW, dtype=BF16), jump, jump2, jump...  4.36 us
    ppermute x5, waiting for transfers between devices, lift(): lax.ppermute(face, 'layer', [(i, i + step) for i in range(layers) if 0 <=...  3.43 us
    pallas_call x1, Pallas kernels, shards(): call(first_gradient, 'first_gradient', (field, jump, jump2, jump, face2,...  3.37 us
    pallas_call x2, Pallas kernels, shards(): call(next_rest, 'next_rest', late[:5] if iteration == ITERS - 2 else late...  3.3 us
    all_to_all x1, waiting for transfers between devices, swap(): lax.all_to_all(outgoing, axis, split_axis=0, concat_axis=0, tiled=True, a...  3.05 us
  transfers between devices with their start and end apart: 9, of which 5 were waited for; matrix products, arithmetic and copies ran while one was open for 0% of the time, Pallas kernels for 3%

profile of v11, /device:TPU:1, one launch (start us, length us, event | category | flops | bytes accessed | tf_op | source)
XLA Modules:
  0.0 149.8 jit_solution(16871266479227115897)
XLA Ops:
  0.6 0.1 add_bitcast_fusion.where_ref
  0.7 0.0 copy-start.1
  0.7 0.0 copy-start.3
  0.7 4.4 %prepare.1 = (bf16[1024,256]{1,0:T(8,128)(2,1)S(1)}, f32[8,256]{1,0:T(8,128)S(1)}, f32[16,256]{1,0:T(8,128)S(1)}, f32[8,256]{1,0:T(8,128)S(1)}, f32[8,1024]{1,0:...) custom-call(f32[1024,1024]{1,0:T(8,128)} %bitcast.40, ...), custom_call_target="tpu_custom_call" | custom-call | flops 67108864 | bytes 4194304 | tf_op jit(solution)/shard_map/prepare/pallas_call | solution.py:426
  5.1 12.6 %all-to-all-start = ((f32[32,8,128]{2,1,0:T(8,128)}), f32[32,8,128]{2,1,0:T(8,128)S(1)}, u32[]{:S(2)}, u32[]{:S(2)}) async-start(f32[32,8,128]{2,1,0:T(8,128)} %get-tuple-element.69), calls=%async_computation | async-start | bytes 262144 | tf_op jit(solution)/shard_map/all_to_all | solution.py:394
  17.7 3.2 %collective-permute-start = (f32[24,128]{1,0:T(8,128)S(1)}, f32[24,128]{1,0:T(8,128)S(1)}, u32[]{:S(2)}, u32[]{:S(2)}) collective-permute-start(f32[24,128]{1,0:T(8,128)S(1)} %get-tuple-element.70), channel_id=1, source_target_pairs={{0,1},{1,2},{2,3},{3,4},{4,5},{5,6},{6,7},{8,9},{9,10},{10,11},{11... | collective-permute-start | bytes 36872 | tf_op jit(solution)/shard_map/ppermute | solution.py:401
  20.9 1.3 collective-permute-start.1
  22.2 0.0 collective-permute-done.below_in
  22.2 3.4 %collective-permute-done.1.above_in = f32[24,128]{1,0:T(8,128)S(1)} collective-permute-done((f32[24,128]{1,0:T(8,128)S(1)}, f32[24,128]{1,0:T(8,128)S(1)}, u32[]{:S(2)}, u32[]{:S(2)}) %collective-permute-start.1) | collective-permute-done | bytes 12320 | tf_op jit(solution)/shard_map/ppermute | solution.py:401
  25.6 3.1 %all-to-all-done.in_ref = f32[32,8,128]{2,1,0:T(8,128)S(1)} async-done(((f32[32,8,128]{2,1,0:T(8,128)}), f32[32,8,128]{2,1,0:T(8,128)S(1)}, u32[]{:S(2)}, u32[]{:S(2)}) %all-to-all-start) | async-done | bytes 131104 | tf_op jit(solution)/shard_map/all_to_all | solution.py:394
  28.7 0.0 copy-done.1
  28.7 0.0 copy-done.3
  28.7 0.0 copy-start
  28.7 3.4 %first_gradient.1 = (f32[8,1024]{1,0:T(8,128)S(1)}, f32[8,256]{1,0:T(8,128)S(1)}, f32[16,256]{1,0:T(8,128)S(1)}, f32[8,256]{1,0:T(8,128)S(1)}, f32[16,128]{1,0:T...) custom-call(s32[1,6]{1,0:T(1,128)S(1)} %copy-done.3, ...), custom_call_target="tpu_custom_call" | custom-call | flops 67108864 | bytes 4194304 | tf_op jit(solution)/shard_map/first_gradient/pallas_call | solution.py:440
  32.1 24.4 %all_to_all.46 = f32[256,1,128]{2,1,0:T(1,128)S(1)} all-to-all(f32[256,1,128]{2,1,0:T(1,128)S(1)} %bitcast.34), channel_id=1, replica_groups=mesh['plan'=32,'layer'=8] {'plan','layer'}, dimensions={0} | all-to-all | bytes 262144 | tf_op jit(solution)/shard_map/all_to_all | solution.py:394
  56.5 0.0 copy-done
  56.5 0.0 copy-done.2
  56.5 0.3 first_face.1
  56.8 2.2 %collective-permute-start.2 = (f32[8,128]{1,0:T(8,128)S(1)}, f32[8,128]{1,0:T(8,128)S(1)}, u32[]{:S(2)}, u32[]{:S(2)}) collective-permute-start(f32[8,128]{1,0:T(8,128)S(1)} %get-tuple-element.83.refs_2_), channel_id=1, source_target_pairs={{0,1},{1,2},{2,3},{3,4},{4,5},{5,6},{6,7},{8,9},{9,10},{10,11},{11... | collective-permute-start | bytes 12296 | tf_op jit(solution)/shard_map/ppermute | solution.py:401
  59.0 1.7 %first_rest.1 = (f32[8,1024]{1,0:T(8,128)S(1)}, f32[8,256]{1,0:T(8,128)S(1)}, f32[8,128]{1,0:T(8,128)S(1)}, f32[8,128]{1,0:T(8,128)S(1)}, f32[8,128]{1,0:T(8,128...) custom-call(f32[256,128]{1,0:T(8,128)S(1)} %bitcast.27, ...), custom_call_target="tpu_custom_call" | custom-call | flops 134217728 | bytes 8388608 | tf_op jit(solution)/shard_map/first_rest/pallas_call | solution.py:454
  60.7 1.5 collective-permute-start.3
  62.2 0.0 collective-permute-done.2.below_ref.refs_8_
  62.2 0.1 add_pairs.3.sums_ref
  62.3 0.7 collective-permute-done.3.swapped_ref
  63.0 11.9 %all_to_all.47 = f32[16,16,128]{2,1,0:T(8,128)S(1)} all-to-all(f32[16,16,128]{2,1,0:T(8,128)S(1)} %announce.3), channel_id=1, replica_groups={{0,16,32,48,64,80,96,112,128,144,160,176,192,208,224,240},{8,24,40,56,7..., dimensions={0} | all-to-all | bytes 262144 | tf_op jit(solution)/shard_map/all_to_all | solution.py:394
  74.9 0.7 layer_sums.3
  75.6 12.3 %all_to_all.48.in_ref = f32[16,8,256]{2,1,0:T(8,128)S(1)} all-to-all(f32[16,8,256]{2,1,0:T(8,128)S(1)} %get-tuple-element.94), channel_id=1, replica_groups={{0,8,1,9,2,10,3,11,4,12,5,13,6,14,7,15},{16,24,17,25,18,26,19,27,20,28,..., dimensions={0} | all-to-all | bytes 262144 | tf_op jit(solution)/shard_map/all_to_all | solution.py:394
  87.9 0.4 next_face.2
  88.3 2.1 %collective-permute-start.4 = (f32[8,128]{1,0:T(8,128)S(1)}, f32[8,128]{1,0:T(8,128)S(1)}, u32[]{:S(2)}, u32[]{:S(2)}) collective-permute-start(f32[8,128]{1,0:T(8,128)S(1)} %get-tuple-element.99.refs_2_), channel_id=1, source_target_pairs={{0,1},{1,2},{2,3},{3,4},{4,5},{5,6},{6,7},{8,9},{9,10},{10,11},{11... | collective-permute-start | bytes 12296 | tf_op jit(solution)/shard_map/ppermute | solution.py:401
  90.4 1.7 %next_rest.2 = (f32[8,1024]{1,0:T(8,128)S(1)}, f32[8,256]{1,0:T(8,128)S(1)}, f32[8,128]{1,0:T(8,128)S(1)}, f32[8,128]{1,0:T(8,128)S(1)}, f32[8,128]{1,0:T(8,128)...) custom-call(f32[16,8,256]{2,1,0:T(8,128)S(1)} %all_to_all.48.in_ref, ...), custom_call_target="tpu_custom_call" | custom-call | flops 134217728 | bytes 8388608 | tf_op jit(solution)/shard_map/next_rest/pallas_call | solution.py:481
  92.1 0.6 collective-permute-start.5
  92.6 0.0 collective-permute-done.4.below_ref.refs_8_
  92.6 0.1 add_pairs.4.sums_ref
  92.7 0.7 collective-permute-done.5.swapped_ref
  93.5 12.2 %all_to_all.49 = f32[16,16,128]{2,1,0:T(8,128)S(1)} all-to-all(f32[16,16,128]{2,1,0:T(8,128)S(1)} %announce.4), channel_id=1, replica_groups={{0,16,32,48,64,80,96,112,128,144,160,176,192,208,224,240},{8,24,40,56,7..., dimensions={0} | all-to-all | bytes 262144 | tf_op jit(solution)/shard_map/all_to_all | solution.py:394
  105.7 0.7 layer_sums.4
  106.4 12.3 %all_to_all.50.in_ref = f32[16,8,256]{2,1,0:T(8,128)S(1)} all-to-all(f32[16,8,256]{2,1,0:T(8,128)S(1)} %get-tuple-element.108), channel_id=1, replica_groups={{0,8,1,9,2,10,3,11,4,12,5,13,6,14,7,15},{16,24,17,25,18,26,19,27,20,28,..., dimensions={0} | all-to-all | bytes 262144 | tf_op jit(solution)/shard_map/all_to_all | solution.py:394
  118.7 0.4 next_face.3
  119.1 2.1 %collective-permute-start.6 = (f32[8,128]{1,0:T(8,128)S(1)}, f32[8,128]{1,0:T(8,128)S(1)}, u32[]{:S(2)}, u32[]{:S(2)}) collective-permute-start(f32[8,128]{1,0:T(8,128)S(1)} %get-tuple-element.113.refs_2_), channel_id=1, source_target_pairs={{0,1},{1,2},{2,3},{3,4},{4,5},{5,6},{6,7},{8,9},{9,10},{10,11},{11... | collective-permute-start | bytes 12296 | tf_op jit(solution)/shard_map/ppermute | solution.py:401
  121.2 1.7 %next_rest.3 = (f32[8,1024]{1,0:T(8,128)S(1)}, f32[8,256]{1,0:T(8,128)S(1)}, f32[8,128]{1,0:T(8,128)S(1)}, f32[8,128]{1,0:T(8,128)S(1)}, f32[8,128]{1,0:T(8,128)S(1)}) custom-call(f32[16,8,256]{2,1,0:T(8,128)S(1)} %all_to_all.50.in_ref, f32[4,16,128]{2,1,0:T(8,128)S(1)} %get-tuple-element.75.masks_ref, f32[8,128]{1,0:T(8,128)S(1)} %get-tuple-element.109.half_ref, ...), custom_call_target="tpu_custom_call" | custom-call | flops 134217728 | bytes 8388608 | tf_op jit(solution)/shard_map/next_rest/pallas_call | solution.py:481
  122.9 0.6 collective-permute-start.7
  123.4 0.0 collective-permute-done.6.below_ref
  123.4 0.1 add_pairs.5.sums_ref
  123.5 0.7 collective-permute-done.7.swapped_ref
  124.3 12.0 %all_to_all.51 = f32[16,16,128]{2,1,0:T(8,128)S(1)} all-to-all(f32[16,16,128]{2,1,0:T(8,128)S(1)} %announce.5), channel_id=1, replica_groups={{0,16,32,48,64,80,96,112,128,144,160,176,192,208,224,240},{8,24,40,56,7..., dimensions={0} | all-to-all | bytes 262144 | tf_op jit(solution)/shard_map/all_to_all | solution.py:394
  136.3 0.7 layer_sums.5
  137.0 12.0 %all_to_all.52.in_ref = f32[16,8,128]{2,1,0:T(8,128)S(1)} all-to-all(f32[16,8,128]{2,1,0:T(8,128)S(1)} %layer_sums.5), channel_id=1, replica_groups={{0,8,1,9,2,10,3,11,4,12,5,13,6,14,7,15},{16,24,17,25,18,26,19,27,20,28,..., dimensions={0} | all-to-all | bytes 131072 | tf_op jit(solution)/shard_map/all_to_all | solution.py:394
  149.0 0.8 finish.1
  (4 shorter events, 0.0 us)
Async XLA Ops:
  0.7 28.0 %copy-start.1 = (f32[1,1,8,1024]{3,2,1,0:T(8,128)S(1)}, f32[1,1,8,1024]{3,2,1,0:T(8,128)}, u32[]{:S(2)}) copy-start(f32[1,1,8,1024]{3,2,1,0:T(8,128)} %param.8) | copy-start | bytes 98308
  0.7 28.0 %copy-start.3 = (s32[1,6]{1,0:T(1,128)S(1)}, s32[1,6]{1,0:T(1,128)}, u32[]{:S(2)}) copy-start(s32[1,6]{1,0:T(1,128)} %partners_ref.1) | copy-start | bytes 76
  5.1 23.6 %all-to-all-start = ((f32[32,8,128]{2,1,0:T(8,128)}), f32[32,8,128]{2,1,0:T(8,128)S(1)}, u32[]{:S(2)}, u32[]{:S(2)}) async-start(f32[32,8,128]{2,1,0:T(8,128)} %get-tuple-element.69), calls=%async_computation | async-start | bytes 262144 | tf_op jit(solution)/shard_map/all_to_all | solution.py:394
  17.7 4.5 %collective-permute-start = (f32[24,128]{1,0:T(8,128)S(1)}, f32[24,128]{1,0:T(8,128)S(1)}, u32[]{:S(2)}, u32[]{:S(2)}) collective-permute-start(f32[24,128]{1,0:T(8,128)S(1)} %get-tuple-element.70), channel_id=1, source_target_pairs={{0,1},{1,2},{2,3},{3,4},{4,5},{5,6},{6,7},{8,9},{9,10},{10,11},{11... | collective-permute-start | bytes 36872 | tf_op jit(solution)/shard_map/ppermute | solution.py:401
  20.9 4.7 %collective-permute-start.1 = (f32[24,128]{1,0:T(8,128)S(1)}, f32[24,128]{1,0:T(8,128)S(1)}, u32[]{:S(2)}, u32[]{:S(2)}) collective-permute-start(f32[24,128]{1,0:T(8,128)S(1)} %get-tuple-element.71), channel_id=1, source_target_pairs={{1,0},{2,1},{3,2},{4,3},{5,4},{6,5},{7,6},{9,8},{10,9},{11,10},{12... | collective-permute-start | bytes 36872 | tf_op jit(solution)/shard_map/ppermute | solution.py:401
  28.7 27.8 %copy-start = (f32[1,1,8,1024]{3,2,1,0:T(8,128)S(1)}, f32[1,1,8,1024]{3,2,1,0:T(8,128)}, u32[]{:S(2)}) copy-start(f32[1,1,8,1024]{3,2,1,0:T(8,128)} %param.9) | copy-start | bytes 98308
  28.7 27.8 %copy-start.2 = (s32[1,1,1024]{2,1,0:T(1,128)S(1)}, s32[1,1,1024]{2,1,0:T(1,128)}, u32[]{:S(2)}) copy-start(s32[1,1,1024]{2,1,0:T(1,128)} %param.13) | copy-start | bytes 12292
  56.8 5.4 %collective-permute-start.2 = (f32[8,128]{1,0:T(8,128)S(1)}, f32[8,128]{1,0:T(8,128)S(1)}, u32[]{:S(2)}, u32[]{:S(2)}) collective-permute-start(f32[8,128]{1,0:T(8,128)S(1)} %get-tuple-element.83.refs_2_), channel_id=1, source_target_pairs={{0,1},{1,2},{2,3},{3,4},{4,5},{5,6},{6,7},{8,9},{9,10},{10,11},{11... | collective-permute-start | bytes 12296 | tf_op jit(solution)/shard_map/ppermute | solution.py:401
  60.7 2.3 %collective-permute-start.3 = (f32[8,128]{1,0:T(8,128)S(1)}, f32[8,128]{1,0:T(8,128)S(1)}, u32[]{:S(2)}, u32[]{:S(2)}) collective-permute-start(f32[8,128]{1,0:T(8,128)S(1)} %get-tuple-element.93), channel_id=1, source_target_pairs={{0,8},{8,0},{16,24},{24,16},{32,40},{40,32},{48,56},{56,48},{64,72... | collective-permute-start | bytes 12296 | tf_op jit(solution)/shard_map/ppermute | solution.py:462
  88.3 4.3 %collective-permute-start.4 = (f32[8,128]{1,0:T(8,128)S(1)}, f32[8,128]{1,0:T(8,128)S(1)}, u32[]{:S(2)}, u32[]{:S(2)}) collective-permute-start(f32[8,128]{1,0:T(8,128)S(1)} %get-tuple-element.99.refs_2_), channel_id=1, source_target_pairs={{0,1},{1,2},{2,3},{3,4},{4,5},{5,6},{6,7},{8,9},{9,10},{10,11},{11... | collective-permute-start | bytes 12296 | tf_op jit(solution)/shard_map/ppermute | solution.py:401
  92.1 1.4 collective-permute-start.5
  119.1 4.3 %collective-permute-start.6 = (f32[8,128]{1,0:T(8,128)S(1)}, f32[8,128]{1,0:T(8,128)S(1)}, u32[]{:S(2)}, u32[]{:S(2)}) collective-permute-start(f32[8,128]{1,0:T(8,128)S(1)} %get-tuple-element.113.refs_2_), channel_id=1, source_target_pairs={{0,1},{1,2},{2,3},{3,4},{4,5},{5,6},{6,7},{8,9},{9,10},{10,11},{11... | collective-permute-start | bytes 12296 | tf_op jit(solution)/shard_map/ppermute | solution.py:401
  122.9 1.4 collective-permute-start.7

commit v12 on v11

--- a/solution.py
+++ b/solution.py
@@ -13,7 +13,7 @@
 HALF = 3
 JW = 2 * LANES
 STRIP = 32
-CHUNKS = 4
+CHUNKS = 8
 NAMES = 16
 SQUARE, CURVATURE = HALF * JR, HALF * JR + 1
 F32 = jnp.float32
@@ -56,11 +56,12 @@
 
 def dense(field, high_ref, low_ref, columns=slice(None), arrive=None):
     lhs = jnp.concatenate(pieces(field, 2), axis=0).astype(BF16)
-    depth = field.shape[1] // CHUNKS
     total = 0.0
     for half_ref in (high_ref, low_ref):
-        for chunk in range(CHUNKS):
-            if half_ref is low_ref and arrive is not None:
+        chunks = 1 if arrive is None else CHUNKS
+        depth = field.shape[1] // chunks
+        for chunk in range(chunks):
+            if chunks > 1 and half_ref is low_ref:
                 arrive(chunk)
             at = slice(chunk * depth, (chunk + 1) * depth)
             total = total + jnp.dot(lhs[:, at], half_ref[at, columns], preferred_element_type=F32)

time: 150 us -> 151 us (level)
  no operation moved by 1% of the time
where the time goes in v12:
time: 151 us; the launch traced here: 150 us
  blocking collectives  97.2 us (64%)
  starting transfers between devices  26.1 us (17%)
  Pallas kernels  17.3 us (11%)
  waiting for transfers between devices  8.7 us (6%)
    all_to_all x7, blocking collectives, swap(): lax.all_to_all(outgoing, axis, split_axis=0, concat_axis=0, tiled=True, a...  97.2 us
    all_to_all x1, starting transfers between devices, swap(): lax.all_to_all(outgoing, axis, split_axis=0, concat_axis=0, tiled=True, a...  12.6 us
    ppermute x5, starting transfers between devices, lift(): lax.ppermute(face, 'layer', [(i, i + step) for i in range(layers) if 0 <=...  10.9 us
    pallas_call x1, Pallas kernels, shards(): call(prepare, 'prepare', (shape(width, JW, dtype=BF16), jump, jump2, jump...  4.76 us
    ppermute x5, waiting for transfers between devices, lift(): lax.ppermute(face, 'layer', [(i, i + step) for i in range(layers) if 0 <=...  3.43 us
    pallas_call x1, Pallas kernels, shards(): call(first_gradient, 'first_gradient', (field, jump, jump2, jump, face2,...  3.34 us
    pallas_call x2, Pallas kernels, shards(): call(next_rest, 'next_rest', late[:5] if iteration == ITERS - 2 else late...  3.23 us
    all_to_all x1, waiting for transfers between devices, swap(): lax.all_to_all(outgoing, axis, split_axis=0, concat_axis=0, tiled=True, a...  3.05 us
  transfers between devices with their start and end apart: 9, of which 5 were waited for; matrix products, arithmetic and copies ran while one was open for 0% of the time, Pallas kernels for 3%

profile of v12, /device:TPU:1, one launch (start us, length us, event | category | flops | bytes accessed | tf_op | source)
XLA Modules:
  0.0 150.2 jit_solution(12907753716147784865)
XLA Ops:
  0.6 0.1 add_bitcast_fusion.where_ref
  0.7 0.0 copy-start.1
  0.7 0.0 copy-start.3
  0.7 4.8 %prepare.1 = (bf16[1024,256]{1,0:T(8,128)(2,1)S(1)}, f32[8,256]{1,0:T(8,128)S(1)}, f32[16,256]{1,0:T(8,128)S(1)}, f32[8,256]{1,0:T(8,128)S(1)}, f32[8,1024]{1,0:...) custom-call(f32[1024,1024]{1,0:T(8,128)} %bitcast.40, ...), custom_call_target="tpu_custom_call" | custom-call | flops 67108864 | bytes 4194304 | tf_op jit(solution)/shard_map/prepare/pallas_call | solution.py:427
  5.5 12.6 %all-to-all-start = ((f32[32,8,128]{2,1,0:T(8,128)}), f32[32,8,128]{2,1,0:T(8,128)S(1)}, u32[]{:S(2)}, u32[]{:S(2)}) async-start(f32[32,8,128]{2,1,0:T(8,128)} %get-tuple-element.69), calls=%async_computation | async-start | bytes 262144 | tf_op jit(solution)/shard_map/all_to_all | solution.py:395
  18.1 3.2 %collective-permute-start = (f32[24,128]{1,0:T(8,128)S(1)}, f32[24,128]{1,0:T(8,128)S(1)}, u32[]{:S(2)}, u32[]{:S(2)}) collective-permute-start(f32[24,128]{1,0:T(8,128)S(1)} %get-tuple-element.70), channel_id=1, source_target_pairs={{0,1},{1,2},{2,3},{3,4},{4,5},{5,6},{6,7},{8,9},{9,10},{10,11},{11... | collective-permute-start | bytes 36872 | tf_op jit(solution)/shard_map/ppermute | solution.py:402
  21.3 1.3 collective-permute-start.1
  22.6 0.0 collective-permute-done.below_in
  22.6 3.4 %collective-permute-done.1.above_in = f32[24,128]{1,0:T(8,128)S(1)} collective-permute-done((f32[24,128]{1,0:T(8,128)S(1)}, f32[24,128]{1,0:T(8,128)S(1)}, u32[]{:S(2)}, u32[]{:S(2)}) %collective-permute-start.1) | collective-permute-done | bytes 12320 | tf_op jit(solution)/shard_map/ppermute | solution.py:402
  26.0 3.1 %all-to-all-done.in_ref = f32[32,8,128]{2,1,0:T(8,128)S(1)} async-done(((f32[32,8,128]{2,1,0:T(8,128)}), f32[32,8,128]{2,1,0:T(8,128)S(1)}, u32[]{:S(2)}, u32[]{:S(2)}) %all-to-all-start) | async-done | bytes 131104 | tf_op jit(solution)/shard_map/all_to_all | solution.py:395
  29.1 0.0 copy-done.1
  29.1 0.0 copy-done.3
  29.1 0.0 copy-start
  29.1 3.3 %first_gradient.1 = (f32[8,1024]{1,0:T(8,128)S(1)}, f32[8,256]{1,0:T(8,128)S(1)}, f32[16,256]{1,0:T(8,128)S(1)}, f32[8,256]{1,0:T(8,128)S(1)}, f32[16,128]{1,0:T...) custom-call(s32[1,6]{1,0:T(1,128)S(1)} %copy-done.3, ...), custom_call_target="tpu_custom_call" | custom-call | flops 67108864 | bytes 4194304 | tf_op jit(solution)/shard_map/first_gradient/pallas_call | solution.py:441
  32.5 24.4 %all_to_all.46 = f32[256,1,128]{2,1,0:T(1,128)S(1)} all-to-all(f32[256,1,128]{2,1,0:T(1,128)S(1)} %bitcast.34), channel_id=1, replica_groups=mesh['plan'=32,'layer'=8] {'plan','layer'}, dimensions={0} | all-to-all | bytes 262144 | tf_op jit(solution)/shard_map/all_to_all | solution.py:395
  56.9 0.0 copy-done
  56.9 0.0 copy-done.2
  56.9 0.3 first_face.1
  57.2 2.2 %collective-permute-start.2 = (f32[8,128]{1,0:T(8,128)S(1)}, f32[8,128]{1,0:T(8,128)S(1)}, u32[]{:S(2)}, u32[]{:S(2)}) collective-permute-start(f32[8,128]{1,0:T(8,128)S(1)} %get-tuple-element.83.refs_2_), channel_id=1, source_target_pairs={{0,1},{1,2},{2,3},{3,4},{4,5},{5,6},{6,7},{8,9},{9,10},{10,11},{11... | collective-permute-start | bytes 12296 | tf_op jit(solution)/shard_map/ppermute | solution.py:402
  59.4 1.6 %first_rest.1 = (f32[8,1024]{1,0:T(8,128)S(1)}, f32[8,256]{1,0:T(8,128)S(1)}, f32[8,128]{1,0:T(8,128)S(1)}, f32[8,128]{1,0:T(8,128)S(1)}, f32[8,128]{1,0:T(8,128...) custom-call(f32[256,128]{1,0:T(8,128)S(1)} %bitcast.27, ...), custom_call_target="tpu_custom_call" | custom-call | flops 134217728 | bytes 8388608 | tf_op jit(solution)/shard_map/first_rest/pallas_call | solution.py:455
  61.0 1.5 collective-permute-start.3
  62.5 0.0 collective-permute-done.2.below_ref.refs_8_
  62.5 0.1 add_pairs.3.sums_ref
  62.6 0.7 collective-permute-done.3.swapped_ref
  63.4 11.9 %all_to_all.47 = f32[16,16,128]{2,1,0:T(8,128)S(1)} all-to-all(f32[16,16,128]{2,1,0:T(8,128)S(1)} %announce.3), channel_id=1, replica_groups={{0,16,32,48,64,80,96,112,128,144,160,176,192,208,224,240},{8,24,40,56,7..., dimensions={0} | all-to-all | bytes 262144 | tf_op jit(solution)/shard_map/all_to_all | solution.py:395
  75.2 0.7 layer_sums.3
  76.0 12.3 %all_to_all.48.in_ref = f32[16,8,256]{2,1,0:T(8,128)S(1)} all-to-all(f32[16,8,256]{2,1,0:T(8,128)S(1)} %get-tuple-element.94), channel_id=1, replica_groups={{0,8,1,9,2,10,3,11,4,12,5,13,6,14,7,15},{16,24,17,25,18,26,19,27,20,28,..., dimensions={0} | all-to-all | bytes 262144 | tf_op jit(solution)/shard_map/all_to_all | solution.py:395
  88.3 0.4 next_face.2
  88.6 2.1 %collective-permute-start.4 = (f32[8,128]{1,0:T(8,128)S(1)}, f32[8,128]{1,0:T(8,128)S(1)}, u32[]{:S(2)}, u32[]{:S(2)}) collective-permute-start(f32[8,128]{1,0:T(8,128)S(1)} %get-tuple-element.99.refs_2_), channel_id=1, source_target_pairs={{0,1},{1,2},{2,3},{3,4},{4,5},{5,6},{6,7},{8,9},{9,10},{10,11},{11... | collective-permute-start | bytes 12296 | tf_op jit(solution)/shard_map/ppermute | solution.py:402
  90.8 1.6 %next_rest.2 = (f32[8,1024]{1,0:T(8,128)S(1)}, f32[8,256]{1,0:T(8,128)S(1)}, f32[8,128]{1,0:T(8,128)S(1)}, f32[8,128]{1,0:T(8,128)S(1)}, f32[8,128]{1,0:T(8,128)...) custom-call(f32[16,8,256]{2,1,0:T(8,128)S(1)} %all_to_all.48.in_ref, ...), custom_call_target="tpu_custom_call" | custom-call | flops 134217728 | bytes 8388608 | tf_op jit(solution)/shard_map/next_rest/pallas_call | solution.py:482
  92.4 0.6 collective-permute-start.5
  92.9 0.0 collective-permute-done.4.below_ref.refs_8_
  93.0 0.1 add_pairs.4.sums_ref
  93.0 0.7 collective-permute-done.5.swapped_ref
  93.8 12.2 %all_to_all.49 = f32[16,16,128]{2,1,0:T(8,128)S(1)} all-to-all(f32[16,16,128]{2,1,0:T(8,128)S(1)} %announce.4), channel_id=1, replica_groups={{0,16,32,48,64,80,96,112,128,144,160,176,192,208,224,240},{8,24,40,56,7..., dimensions={0} | all-to-all | bytes 262144 | tf_op jit(solution)/shard_map/all_to_all | solution.py:395
  106.0 0.7 layer_sums.4
  106.7 12.3 %all_to_all.50.in_ref = f32[16,8,256]{2,1,0:T(8,128)S(1)} all-to-all(f32[16,8,256]{2,1,0:T(8,128)S(1)} %get-tuple-element.108), channel_id=1, replica_groups={{0,8,1,9,2,10,3,11,4,12,5,13,6,14,7,15},{16,24,17,25,18,26,19,27,20,28,..., dimensions={0} | all-to-all | bytes 262144 | tf_op jit(solution)/shard_map/all_to_all | solution.py:395
  119.1 0.4 next_face.3
  119.4 2.1 %collective-permute-start.6 = (f32[8,128]{1,0:T(8,128)S(1)}, f32[8,128]{1,0:T(8,128)S(1)}, u32[]{:S(2)}, u32[]{:S(2)}) collective-permute-start(f32[8,128]{1,0:T(8,128)S(1)} %get-tuple-element.113.refs_2_), channel_id=1, source_target_pairs={{0,1},{1,2},{2,3},{3,4},{4,5},{5,6},{6,7},{8,9},{9,10},{10,11},{11... | collective-permute-start | bytes 12296 | tf_op jit(solution)/shard_map/ppermute | solution.py:402
  121.6 1.6 %next_rest.3 = (f32[8,1024]{1,0:T(8,128)S(1)}, f32[8,256]{1,0:T(8,128)S(1)}, f32[8,128]{1,0:T(8,128)S(1)}, f32[8,128]{1,0:T(8,128)S(1)}, f32[8,128]{1,0:T(8,128)S(1)}) custom-call(f32[16,8,256]{2,1,0:T(8,128)S(1)} %all_to_all.50.in_ref, f32[4,16,128]{2,1,0:T(8,128)S(1)} %get-tuple-element.75.masks_ref, f32[8,128]{1,0:T(8,128)S(1)} %get-tuple-element.109.half_ref, ...), custom_call_target="tpu_custom_call" | custom-call | flops 134217728 | bytes 8388608 | tf_op jit(solution)/shard_map/next_rest/pallas_call | solution.py:482
  123.2 0.6 collective-permute-start.7
  123.7 0.0 collective-permute-done.6.below_ref
  123.7 0.1 add_pairs.5.sums_ref
  123.8 0.7 collective-permute-done.7.swapped_ref
  124.6 12.0 %all_to_all.51 = f32[16,16,128]{2,1,0:T(8,128)S(1)} all-to-all(f32[16,16,128]{2,1,0:T(8,128)S(1)} %announce.5), channel_id=1, replica_groups={{0,16,32,48,64,80,96,112,128,144,160,176,192,208,224,240},{8,24,40,56,7..., dimensions={0} | all-to-all | bytes 262144 | tf_op jit(solution)/shard_map/all_to_all | solution.py:395
  136.6 0.7 layer_sums.5
  137.3 12.0 %all_to_all.52.in_ref = f32[16,8,128]{2,1,0:T(8,128)S(1)} all-to-all(f32[16,8,128]{2,1,0:T(8,128)S(1)} %layer_sums.5), channel_id=1, replica_groups={{0,8,1,9,2,10,3,11,4,12,5,13,6,14,7,15},{16,24,17,25,18,26,19,27,20,28,..., dimensions={0} | all-to-all | bytes 131072 | tf_op jit(solution)/shard_map/all_to_all | solution.py:395
  149.4 0.8 finish.1
  (4 shorter events, 0.0 us)
Async XLA Ops:
  0.7 28.4 %copy-start.1 = (f32[1,1,8,1024]{3,2,1,0:T(8,128)S(1)}, f32[1,1,8,1024]{3,2,1,0:T(8,128)}, u32[]{:S(2)}) copy-start(f32[1,1,8,1024]{3,2,1,0:T(8,128)} %param.8) | copy-start | bytes 98308
  0.7 28.4 %copy-start.3 = (s32[1,6]{1,0:T(1,128)S(1)}, s32[1,6]{1,0:T(1,128)}, u32[]{:S(2)}) copy-start(s32[1,6]{1,0:T(1,128)} %partners_ref.1) | copy-start | bytes 76
  5.5 23.6 %all-to-all-start = ((f32[32,8,128]{2,1,0:T(8,128)}), f32[32,8,128]{2,1,0:T(8,128)S(1)}, u32[]{:S(2)}, u32[]{:S(2)}) async-start(f32[32,8,128]{2,1,0:T(8,128)} %get-tuple-element.69), calls=%async_computation | async-start | bytes 262144 | tf_op jit(solution)/shard_map/all_to_all | solution.py:395
  18.1 4.5 %collective-permute-start = (f32[24,128]{1,0:T(8,128)S(1)}, f32[24,128]{1,0:T(8,128)S(1)}, u32[]{:S(2)}, u32[]{:S(2)}) collective-permute-start(f32[24,128]{1,0:T(8,128)S(1)} %get-tuple-element.70), channel_id=1, source_target_pairs={{0,1},{1,2},{2,3},{3,4},{4,5},{5,6},{6,7},{8,9},{9,10},{10,11},{11... | collective-permute-start | bytes 36872 | tf_op jit(solution)/shard_map/ppermute | solution.py:402
  21.3 4.7 %collective-permute-start.1 = (f32[24,128]{1,0:T(8,128)S(1)}, f32[24,128]{1,0:T(8,128)S(1)}, u32[]{:S(2)}, u32[]{:S(2)}) collective-permute-start(f32[24,128]{1,0:T(8,128)S(1)} %get-tuple-element.71), channel_id=1, source_target_pairs={{1,0},{2,1},{3,2},{4,3},{5,4},{6,5},{7,6},{9,8},{10,9},{11,10},{12... | collective-permute-start | bytes 36872 | tf_op jit(solution)/shard_map/ppermute | solution.py:402
  29.1 27.8 %copy-start = (f32[1,1,8,1024]{3,2,1,0:T(8,128)S(1)}, f32[1,1,8,1024]{3,2,1,0:T(8,128)}, u32[]{:S(2)}) copy-start(f32[1,1,8,1024]{3,2,1,0:T(8,128)} %param.9) | copy-start | bytes 98308
  29.1 27.8 %copy-start.2 = (s32[1,1,1024]{2,1,0:T(1,128)S(1)}, s32[1,1,1024]{2,1,0:T(1,128)}, u32[]{:S(2)}) copy-start(s32[1,1,1024]{2,1,0:T(1,128)} %param.13) | copy-start | bytes 12292
  57.2 5.3 %collective-permute-start.2 = (f32[8,128]{1,0:T(8,128)S(1)}, f32[8,128]{1,0:T(8,128)S(1)}, u32[]{:S(2)}, u32[]{:S(2)}) collective-permute-start(f32[8,128]{1,0:T(8,128)S(1)} %get-tuple-element.83.refs_2_), channel_id=1, source_target_pairs={{0,1},{1,2},{2,3},{3,4},{4,5},{5,6},{6,7},{8,9},{9,10},{10,11},{11... | collective-permute-start | bytes 12296 | tf_op jit(solution)/shard_map/ppermute | solution.py:402
  61.0 2.3 %collective-permute-start.3 = (f32[8,128]{1,0:T(8,128)S(1)}, f32[8,128]{1,0:T(8,128)S(1)}, u32[]{:S(2)}, u32[]{:S(2)}) collective-permute-start(f32[8,128]{1,0:T(8,128)S(1)} %get-tuple-element.93), channel_id=1, source_target_pairs={{0,8},{8,0},{16,24},{24,16},{32,40},{40,32},{48,56},{56,48},{64,72... | collective-permute-start | bytes 12296 | tf_op jit(solution)/shard_map/ppermute | solution.py:463
  88.6 4.3 %collective-permute-start.4 = (f32[8,128]{1,0:T(8,128)S(1)}, f32[8,128]{1,0:T(8,128)S(1)}, u32[]{:S(2)}, u32[]{:S(2)}) collective-permute-start(f32[8,128]{1,0:T(8,128)S(1)} %get-tuple-element.99.refs_2_), channel_id=1, source_target_pairs={{0,1},{1,2},{2,3},{3,4},{4,5},{5,6},{6,7},{8,9},{9,10},{10,11},{11... | collective-permute-start | bytes 12296 | tf_op jit(solution)/shard_map/ppermute | solution.py:402
  92.4 1.4 collective-permute-start.5
  119.4 4.3 %collective-permute-start.6 = (f32[8,128]{1,0:T(8,128)S(1)}, f32[8,128]{1,0:T(8,128)S(1)}, u32[]{:S(2)}, u32[]{:S(2)}) collective-permute-start(f32[8,128]{1,0:T(8,128)S(1)} %get-tuple-element.113.refs_2_), channel_id=1, source_target_pairs={{0,1},{1,2},{2,3},{3,4},{4,5},{5,6},{6,7},{8,9},{9,10},{10,11},{11... | collective-permute-start | bytes 12296 | tf_op jit(solution)/shard_map/ppermute | solution.py:402
  123.2 1.4 collective-permute-start.7
